TPU v7x, 32 devices: a whole 2x2x4 slice. The times are simulated.
32 devices in a mesh: grp: 2 (over y), blk: 4 (over z), rhs: 2 (over x), sub: 2 (over core).
Axes of the slice: x: 2, y: 2, z: 4, core: 2. Of those that a mesh axis runs over, the one named last changes fastest.
Arguments:
- x_panels: bfloat16 [32, 128, 2, 128], P(('grp', 'blk', 'sub'), None, None, 'rhs'), parts along dimension 0, may hold values from -6 to 6
- leaf_basis: bfloat16 [16, 32, 64, 2, 128], P(('blk', 'sub'), 'rhs'), may hold values from -0.375 to 0.375
- leaf_count: int32 [16], P(('blk', 'sub')), may hold values from 1 to 32, as said below
- parent_map: int32 [64], P('rhs'), may hold values from 0 to 15
- up_transfer: bfloat16 [8, 64, 64, 256], P(('blk', 'sub'), 'rhs'), may hold values from -0.375 to 0.375
- mid_perm: int32 [8], replicated, may hold values from 0 to 7, each once
- down_transfer: bfloat16 [4, 2, 32, 2, 64, 256], P(None, 'rhs', ('blk', 'sub')), may hold values from -0.375 to 0.375
- row_basis: bfloat16 [2, 32, 2, 4, 128, 128], P('rhs', ('blk', 'sub')), may hold values from -0.25 to 0.25
Outputs:
- field_out: bfloat16 [4, 32, 2, 128, 2, 128], P(('grp', 'rhs'), ('blk', 'sub')), parts along dimension 0
There are 2 independent parts, one for each index of `grp`. A program takes and returns all parts, laid end to end along the dimension named above; an argument that names none is the same for every part. Nothing has to cross between parts.
Inputs may be any that keep to these rules, and one draw needn't show every extreme that they name: Level-0 directions d >= leaf_count[b] of leaf box b are padding and contribute nothing; in every draw some box has all 32 directions live and some box has one. Level-1 direction j draws from level-0 direction (j // 32) * 16 + parent_map[j]. `mid_perm`: A permutation of the 8 level-1 column groups; entries 2q and 2q + 1 are the children of level-2 column group q.
All inputs are finite; a program needn't handle non-finite values.
Results may differ from a plain program's by a relative error of at most 0.0064.
Values may be sent and summed in bfloat16 or wider, within the bound.
No kernel may reach another device: no remote copies, remote signals or barrier semaphores. Data moves between devices by JAX's collectives and lax.ppermute only.
A program may use at most 64 MiB of HBM per device.

v0:
```python
import jax
import jax.numpy as jnp
from jax import lax
from jax.sharding import PartitionSpec as P

NRHS = 128


def twisted(values):
    real_part = values[..., 0, :]
    imag_part = values[..., 1, :]
    turned = jnp.stack([-imag_part, real_part], axis=-2)
    return jnp.stack([values, turned], axis=-4)


def on_device(
    x_panels, leaf_basis, leaf_count, parent_map, up_transfer, mid_perm, down_transfer, row_basis
):
    boxes = leaf_basis.shape[0]
    directions = leaf_basis.shape[1]
    rank_size = leaf_basis.shape[2]
    leaf_size = leaf_basis.shape[4]
    ncols = NRHS
    group = lax.axis_index("rhs")
    basis_flat = leaf_basis.reshape(boxes, directions, rank_size, 2 * leaf_size)
    global_dir = group * directions + jnp.arange(directions, dtype=jnp.int32)
    live = global_dir[None, :] < leaf_count[:, None]
    piece = lax.all_gather(x_panels, "rhs", axis=3, tiled=True)
    width = piece.shape[3]
    spread = twisted(piece).reshape(boxes, 2 * leaf_size, 2 * width)
    coeffs = jnp.einsum("bdmk,bkn->bdmn", basis_flat, spread, preferred_element_type=jnp.float32)
    coeffs = jnp.where(live[:, :, None, None], coeffs, jnp.zeros_like(coeffs)).astype(jnp.bfloat16)
    leaf_coef = coeffs.reshape(boxes, directions, rank_size, 2, width)
    chosen = jnp.take(leaf_coef, parent_map, axis=1)
    pairs = boxes // 2
    dirs_up = chosen.shape[1]
    chosen = chosen.reshape(pairs, 2, dirs_up, rank_size, 2, ncols)
    spread_up = jnp.transpose(twisted(chosen), (0, 2, 1, 3, 4, 5, 6)).reshape(
        pairs, dirs_up, 4 * rank_size, 2 * ncols
    )
    mid_coef = jnp.einsum(
        "pjmx,pjxn->pjmn", up_transfer, spread_up, preferred_element_type=jnp.float32
    )
    mid_coef = mid_coef.astype(jnp.bfloat16).reshape(pairs, dirs_up, rank_size, 2, ncols)
    switched = lax.all_to_all(mid_coef, ("blk", "sub"), split_axis=1, concat_axis=0, tiled=True)
    local_dirs = switched.shape[1]
    top_groups = switched.shape[0] // 2
    ordered = jnp.take(switched, mid_perm, axis=0).reshape(
        top_groups, 2, local_dirs, rank_size, 2, ncols
    )
    spread_down = jnp.transpose(twisted(ordered), (0, 2, 1, 3, 4, 5, 6)).reshape(
        top_groups, local_dirs, 4 * rank_size, 2 * ncols
    )
    down_local = down_transfer.reshape(top_groups, local_dirs, 2, rank_size, 4 * rank_size)
    top_coef = jnp.einsum(
        "qjtmx,qjxn->qjtmn", down_local, spread_down, preferred_element_type=jnp.float32
    )
    top_coef = top_coef.astype(jnp.bfloat16).reshape(top_groups, local_dirs, 2, rank_size, 2, ncols)
    spread_row = twisted(top_coef).reshape(top_groups, local_dirs, 2, 2 * rank_size, 2 * ncols)
    rows_local = row_basis.reshape(local_dirs, 2, top_groups, leaf_size, 2 * rank_size)
    result = jnp.einsum(
        "jtqlx,qjtxn->jtln", rows_local, spread_row, preferred_element_type=jnp.float32
    )
    return result.astype(jnp.bfloat16).reshape(1, local_dirs, 2, leaf_size, 2, ncols)


def solution(mesh):
    return jax.shard_map(
        on_device,
        mesh=mesh,
        in_specs=(
            P(("grp", "blk", "sub"), None, None, "rhs"),
            P(("blk", "sub"), "rhs", None, None, None),
            P(("blk", "sub")),
            P("rhs"),
            P(("blk", "sub"), "rhs", None, None),
            P(),
            P(None, "rhs", ("blk", "sub"), None, None, None),
            P("rhs", ("blk", "sub"), None, None, None, None),
        ),
        out_specs=P(("grp", "rhs"), ("blk", "sub"), None, None, None, None),
        check_vma=False,
    )
```

profile of v0, /device:TPU:0, one launch (start us, length us, event | category | flops | bytes accessed | tf_op | source)
XLA Modules:
  0.0 115.1 jit_solution(215822143500802356)
XLA Ops:
  0.0 0.8 compare_select_fusion
  0.8 0.7 compare_and_fusion
  1.5 6.1 %all_gather.3 = bf16[2,128,2,128]{1,3,2,0:T(8,128)(2,1)S(1)} all-gather(bf16[2,128,2,64]{1,3,2,0:T(8,128)(2,1)} %param.8), channel_id=1, replica_groups=mesh['grp'=2,'blk'=4,'rhs'=2,'sub'=2] {'rhs'}, dimensions={3}, use_global_device_ids=true | all-gather | bytes 196608 | tf_op jit(solution)/shard_map/all_gather | solution.py:28
  8.0 0.7 reshape.120
  8.8 0.4 fusion.11
  9.3 1.1 reshape.121
  10.4 6.7 %gather_fusion = bf16[32,2,64,2,128]{4,3,2,1,0:T(2,128)(2,1)S(1)} fusion(bf16[2,16,64,2,128]{4,3,2,1,0:T(2,128)(2,1)} %reshape.121, s32[1024]{0:T(1024)S(1)} %pad_clamp_fusion.1), kind=kCustom, calls=%fused_computation | custom fusion | bytes 4194432 | tf_op jit(solution)/shard_map/jit(_take)/gather | solution.py:34
  17.1 1.9 %broadcast_select_fusion = bf16[1,2,32,64,2,128]{5,4,3,1,2,0:T(2,128)(2,1)S(1)} fusion(pred[32]{0:T(512)(128)(4,1)S(1)} %compare_and_fusion, bf16[32,2,64,2,128]{4,3,2,1,0:T(2,128)(2,1)S(1)} %gather_fusion), kind=kLoop, calls=%fused_computation.3 | loop fusion | flops 1048576 | bytes 4194336 | tf_op jit(solution)/shard_map/jit(_take)/select_n | solution.py:34
  19.0 3.2 %broadcast_select_fusion.1 = bf16[1,2,32,1,64,2,128]{6,5,4,1,2,3,0:T(2,128)(2,1)} fusion(pred[32]{0:T(512)(128)(4,1)S(1)} %compare_and_fusion, bf16[32,2,64,2,128]{4,3,2,1,0:T(2,128)(2,1)S(1)} %gather_fusion), kind=kLoop, calls=%fused_computation.4 | loop fusion | flops 1048576 | bytes 4194336 | tf_op jit(solution)/shard_map/jit(_take)/select_n | solution.py:34
  22.3 4.6 %slice_negate_fusion = (bf16[1,2,32,64,1,128]{5,4,3,1,2,0:T(2,128)(2,1)S(1)}, bf16[1,2,32,64,1,128]{5,4,3,1,2,0:T(2,128)(2,1)S(1)}) fusion(bf16[1,2,32,64,2,128]{5,4,3,1,2,0:T(2,128)(2,1)S(1)} %broadcast_select_fusion), kind=kLoop, calls=%fused_computation.5 | loop fusion | flops 524288 | bytes 4194304 | tf_op jit(solution)/shard_map/neg | solution.py:12
  26.9 5.6 %maximum_bitcast_fusion.1 = bf16[1,2,32,1,64,2,128]{6,5,4,1,2,3,0:T(2,128)(2,1)} fusion(bf16[1,2,32,64,1,128]{5,4,3,1,2,0:T(2,128)(2,1)S(1)} %get-tuple-element.6, bf16[1,2,32,64,1,128]{5,4,3,1,2,0:T(2,128)(2,1)S(1)} %get-tuple-element.5), kind=kLoop, calls=%fused_computation.6 | loop fusion | flops 4194304 | bytes 4194304 | tf_op jit(solution)/shard_map/stack | solution.py:13
  32.5 8.5 %maximum_bitcast_fusion = bf16[1,32,2,2,64,2,128]{6,5,4,2,1,3,0:T(2,128)(2,1)S(1)} fusion(bf16[1,2,32,1,64,2,128]{6,5,4,1,2,3,0:T(2,128)(2,1)} %maximum_bitcast_fusion.1, bf16[1,2,32,1,64,2,128]{6,5,4,1,2,3,0:T(2,128)(2,1)} %broadcast_select_fusion.1), kind=kLoop, calls=%fused_computation.2 | loop fusion | flops 2097152 | bytes 8388608 | tf_op jit(solution)/shard_map/transpose | solution.py:38
  41.0 5.9 %copy.28 = bf16[1,32,2,2,64,2,128]{6,5,4,3,2,1,0:T(2,128)(2,1)} copy(bf16[1,32,2,2,64,2,128]{6,5,4,2,1,3,0:T(2,128)(2,1)S(1)} %maximum_bitcast_fusion) | data formatting | bytes 8388608 | tf_op jit(solution)/shard_map/transpose | solution.py:38
  47.0 7.7 %reshape.122 = bf16[32,256,256]{2,1,0:T(8,128)(2,1)} reshape(bf16[1,32,2,2,64,2,128]{6,5,4,3,2,1,0:T(2,128)(2,1)} %copy.28) | data formatting | bytes 8388608 | tf_op jit(solution)/shard_map/reshape.3
  54.6 3.0 %fusion.7 = bf16[32,64,256]{2,1,0:T(8,128)(2,1)S(1)} fusion(bf16[32,256,256]{2,1,0:T(8,128)(2,1)} %reshape.122, bf16[1,32,64,256]{3,2,1,0:T(8,128)(2,1)S(1)} %copy-done), kind=kOutput, calls=%fused_computation.16 | convolution fusion | flops 268959744 | bytes 6291456 | tf_op jit(solution)/shard_map/pjmx,pjxn->pjmn/dot_general | solution.py:41
  57.7 1.1 reshape.124
  58.8 5.4 %all-to-all-start = ((bf16[1,32,64,2,128]{4,3,2,0,1:T(2,128)(2,1)}), bf16[1,32,64,2,128]{4,3,2,0,1:T(2,128)(2,1)S(1)}, u32[]{:S(2)}, u32[]{:S(2)}) async-start(bf16[1,32,64,2,128]{4,3,2,0,1:T(2,128)(2,1)} %bitcast.11), calls=%async_computation | async-start | bytes 2097152 | tf_op jit(solution)/shard_map/all_to_all | solution.py:45
  64.3 26.5 %all-to-all-done = bf16[1,32,64,2,128]{4,3,2,0,1:T(2,128)(2,1)S(1)} async-done(((bf16[1,32,64,2,128]{4,3,2,0,1:T(2,128)(2,1)}), bf16[1,32,64,2,128]{4,3,2,0,1:T(2,128)(2,1)S(1)}, u32[]{:S(2)}, u32[]{:S(2)}) %all-to-all-start) | async-done | bytes 1048608 | tf_op jit(solution)/shard_map/all_to_all | solution.py:45
  90.8 0.3 copy.30
  91.0 0.8 gather_fusion.1
  92.4 0.2 maximum_bitcast_fusion.2
  92.6 2.2 %copy.31 = bf16[4,4,2,2,64,2,128]{6,5,4,3,2,1,0:T(2,128)(2,1)S(1)} copy(bf16[4,4,2,2,64,2,128]{6,4,5,3,1,2,0:T(8,128)(2,1)S(1)} %maximum_bitcast_fusion.2) | data formatting | bytes 4194304 | tf_op jit(solution)/shard_map/transpose | solution.py:51
  94.7 2.6 %reshape.150 = bf16[4,4,256,256,1]{3,2,1,0,4:T(8,128)(2,1)} reshape(bf16[4,4,2,2,64,2,128]{6,5,4,3,2,1,0:T(2,128)(2,1)S(1)} %copy.31) | data formatting | bytes 4194304 | tf_op jit(solution)/shard_map/reshape | solution.py:51
  97.3 2.3 %fusion.8 = bf16[4,4,2,64,256]{4,3,2,1,0:T(8,128)(2,1)S(1)} fusion(bf16[4,4,256,256,1]{3,2,1,0,4:T(8,128)(2,1)} %reshape.150, bf16[4,1,4,2,64,256]{5,4,3,2,1,0:T(8,128)(2,1)} %param.14), kind=kOutput, calls=%fused_computation.17 | convolution fusion | flops 268959744 | bytes 4194304 | tf_op jit(solution)/shard_map/qjtmx,qjxn->qjtmn/dot_general | solution.py:55
  99.7 0.3 reshape.127
  100.0 1.1 stack_reshape.2
  101.1 2.3 %slice_negate_fusion.1 = (bf16[4,4,2,64,1,128]{5,4,3,2,1,0:T(2,128)(2,1)S(1)}, bf16[4,4,2,64,1,128]{5,4,3,2,1,0:T(2,128)(2,1)S(1)}) fusion(bf16[4,4,2,64,2,128]{5,4,3,2,1,0:T(2,128)(2,1)S(1)} %reshape.127), kind=kLoop, calls=%fused_computation.19 | loop fusion | flops 262144 | bytes 2097152 | tf_op jit(solution)/shard_map/neg | solution.py:12
  103.4 2.4 %maximum_bitcast_fusion.4 = bf16[4,4,2,1,64,2,128]{6,5,4,3,2,1,0:T(2,128)(2,1)S(1)} fusion(bf16[4,4,2,64,1,128]{5,4,3,2,1,0:T(2,128)(2,1)S(1)} %get-tuple-element.8, bf16[4,4,2,64,1,128]{5,4,3,2,1,0:T(2,128)(2,1)S(1)} %get-tuple-element.7), kind=kLoop, calls=%fused_computation.21 | loop fusion | flops 2097152 | bytes 2097152 | tf_op jit(solution)/shard_map/stack | solution.py:13
  105.9 2.8 %pad_maximum_fusion = bf16[4,4,2,2,64,2,128]{6,5,4,3,2,1,0:T(2,128)(2,1)S(1)} fusion(bf16[4,4,2,1,64,2,128]{6,5,4,3,2,1,0:T(2,128)(2,1)S(1)} %maximum_bitcast_fusion.4, bf16[4,4,2,1,64,2,128]{6,5,4,3,2,1,0:T(2,128)(2,1)S(1)} %bitcast.68), kind=kLoop, calls=%fused_computation.8 | loop fusion | flops 1048576 | bytes 4194304 | tf_op jit(solution)/shard_map/stack | solution.py:13
  108.6 2.6 %reshape.128 = bf16[4,4,2,128,256]{4,3,2,1,0:T(8,128)(2,1)} reshape(bf16[4,4,2,2,64,2,128]{6,5,4,3,2,1,0:T(2,128)(2,1)S(1)} %pad_maximum_fusion) | data formatting | bytes 4194304 | tf_op jit(solution)/shard_map/reshape | solution.py:59
  111.3 2.6 %fusion = bf16[4,2,256,128,1]{3,2,0,1,4:T(8,128)(2,1)S(1)} fusion(bf16[4,4,2,128,256]{4,3,2,1,0:T(8,128)(2,1)} %reshape.128, bf16[1,4,2,4,128,128]{5,4,3,2,1,0:T(8,128)(2,1)} %param.15), kind=kOutput, calls=%fused_computation.9 | convolution fusion | flops 268435456 | bytes 3670016 | tf_op jit(solution)/shard_map/jtqlx,qjtxn->jtln/dot_general | solution.py:61
  114.0 1.1 copy.35
  (27 shorter events, 1.2 us)
Async XLA Ops:
  0.0 54.6 %copy-start = (bf16[1,32,64,256]{3,2,1,0:T(8,128)(2,1)S(1)}, bf16[1,32,64,256]{3,2,1,0:T(8,128)(2,1)}, u32[]{:S(2)}) copy-start(bf16[1,32,64,256]{3,2,1,0:T(8,128)(2,1)} %param.12) | copy-start | bytes 3145732
  0.0 8.0 %copy-start.2 = (bf16[2,16,64,2,128]{4,3,2,1,0:T(2,128)(2,1)S(1)}, bf16[2,16,64,2,128]{4,3,2,1,0:T(2,128)(2,1)}, u32[]{:S(2)}) copy-start(bf16[2,16,64,2,128]{4,3,2,1,0:T(2,128)(2,1)} %param.9) | copy-start | bytes 3145732
  7.6 1.2 %copy-start.3 = (s32[2]{0:T(128)S(1)}, s32[2]{0:T(128)}, u32[]{:S(2)}) copy-start(s32[2]{0:T(128)} %param.10) | copy-start | bytes 28
  57.7 6.5 %copy-start.4 = (s32[8]{0:T(128)S(1)}, s32[8]{0:T(128)}, u32[]{:S(2)}) copy-start(s32[8]{0:T(128)} %param.13) | copy-start | bytes 100
  58.8 32.0 %all-to-all-start = ((bf16[1,32,64,2,128]{4,3,2,0,1:T(2,128)(2,1)}), bf16[1,32,64,2,128]{4,3,2,0,1:T(2,128)(2,1)S(1)}, u32[]{:S(2)}, u32[]{:S(2)}) async-start(bf16[1,32,64,2,128]{4,3,2,0,1:T(2,128)(2,1)} %bitcast.11), calls=%async_computation | async-start | bytes 2097152 | tf_op jit(solution)/shard_map/all_to_all | solution.py:45
  103.4 2.5 %copy-start.1 = (bf16[4,4,2,1,64,2,128]{6,5,4,2,1,0,3:T(2,128)(2,1)S(1)}, bf16[4,4,2,1,64,2,128]{6,5,4,2,1,0,3:T(2,128)(2,1)}, u32[]{:S(2)}) copy-start(bf16[4,4,2,1,64,2,128]{6,5,4,2,1,0,3:T(2,128)(2,1)} %stack_reshape.2) | copy-start | bytes 3145732
where the time goes:
time: 116 us; the launch traced here: 115 us
  local copies, waits for them, and re-layouts  34.6 us (30%)
  other arithmetic  33.8 us (29%)
  waiting for transfers between devices  26.5 us (23%)
  matrix products  8.42 us (7%)
  blocking collectives  6.1 us (5%)
  starting transfers between devices  5.36 us (5%)
    all_to_all x1, waiting for transfers between devices, on_device(): lax.all_to_all(mid_coef, ('blk', 'sub'), split_axis=1, concat_axis=0, til...  26.5 us
    another operation x6, other arithmetic, twisted(): return jnp.stack([values, turned], axis=-4)  11 us
    transpose x1, other arithmetic, on_device(): jnp.transpose(twisted(chosen), (0, 2, 1, 3, 4, 5, 6))  8.51 us
    another operation x1, local copies, waits for them, and re-layouts  7.65 us
    neg x4, other arithmetic, twisted(): turned = jnp.stack([-imag_part, real_part], axis=-2)  7.08 us
    gather x1, local copies, waits for them, and re-layouts, on_device(): chosen = jnp.take(leaf_coef, parent_map, axis=1)  6.66 us
    all_gather x1, blocking collectives, on_device(): piece = lax.all_gather(x_panels, 'rhs', axis=3, tiled=True)  6.1 us
    select_n x3, other arithmetic, on_device(): chosen = jnp.take(leaf_coef, parent_map, axis=1)  5.98 us
  transfers between devices with their start and end apart: 1, of which 1 were waited for; matrix products, arithmetic and copies ran while one was open for 0% of the time, Pallas kernels for 0%

commit v1 on v0

v1 whole, which is shorter than its diff:
```python
import functools

import jax
import jax.numpy as jnp
from jax import lax
from jax.experimental import pallas as pl
from jax.experimental.pallas import tpu as pltpu
from jax.sharding import PartitionSpec as P

NRHS = 128
HALF = 64
F32 = jnp.float32
BF16 = jnp.bfloat16


def turn(values):
    lane = lax.broadcasted_iota(jnp.int32, values.shape, 1)
    rolled = pltpu.roll(values, HALF, 1)
    return jnp.where(lane < HALF, -rolled, rolled)


def lower_kernel(count_ref, parent_ref, x_ref, basis_ref, up_ref, out_ref, g_ref, leaf_ref):
    boxes, dirs, rows, _ = basis_ref.shape
    rank = rows // 2
    pairs, dirs_up = up_ref.shape[0], up_ref.shape[1]
    dests, _, local, _, _ = out_ref.shape
    first = lax.axis_index("rhs") * dirs
    for b in range(boxes):
        x = x_ref[b]
        spread = jnp.concatenate([x, -x[HALF:], x[:HALF]], axis=0)
        for d in range(dirs):
            slot = b * dirs + d
            g = lax.dot_general(
                basis_ref[b, d], spread, (((1,), (1,)), ((), ())), preferred_element_type=F32
            )
            g_ref[slot, 0] = g[:, :NRHS]
            g_ref[slot, 1] = g[:, NRHS:]
            even = pl.ds(0, rank, stride=2)
            odd = pl.ds(1, rank, stride=2)
            plain = g_ref[slot, 0, even, :] + g_ref[slot, 1, odd, :]
            turned = g_ref[slot, 1, even, :] - g_ref[slot, 0, odd, :]
            live = first + d < count_ref[b]
            plain = jnp.where(live, plain, jnp.zeros_like(plain)).astype(BF16)
            turned = jnp.where(live, turned, jnp.zeros_like(turned)).astype(BF16)
            base = (b % 2) * 2 * rank
            leaf_ref[b // 2, d, base : base + rank, :] = plain
            leaf_ref[b // 2, d, base + rank : base + 2 * rank, :] = turned
    for p in range(pairs):
        for j in range(dirs_up):
            mid = jnp.dot(
                up_ref[p, j], leaf_ref[p, parent_ref[j]], preferred_element_type=F32
            )
            out_ref[j // local, p, j % local] = mid.astype(BF16)


def lower(count, parents, x, basis, up, dests):
    boxes, dirs, rows, _ = basis.shape
    pairs, dirs_up, rank, _ = up.shape
    smem = pl.BlockSpec(memory_space=pltpu.SMEM)
    vmem = pl.BlockSpec(memory_space=pltpu.VMEM)
    return pl.pallas_call(
        lower_kernel,
        out_shape=jax.ShapeDtypeStruct((dests, pairs, dirs_up // dests, rank, NRHS), BF16),
        in_specs=[smem, smem, vmem, vmem, vmem],
        out_specs=vmem,
        scratch_shapes=[
            pltpu.VMEM((boxes * dirs, 2, rows, NRHS), F32),
            pltpu.VMEM((pairs, dirs, 4 * rank, NRHS), BF16),
        ],
        compiler_params=pltpu.CompilerParams(vmem_limit_bytes=32 * 1024 * 1024),
        cost_estimate=pl.CostEstimate(
            flops=400_000_000, bytes_accessed=2_800_000, transcendentals=0
        ),
        name="lower",
    )(count, parents, x, basis, up)


def upper_half(perm_ref, mid_ref, down_ref, row_ref, h):
    groups = down_ref.shape[0]
    rank = mid_ref.shape[2]
    tops = ([], [])
    for q in range(groups):
        parts = []
        for s in range(2):
            mid = mid_ref[perm_ref[2 * q + s], h]
            parts += [mid, turn(mid.astype(F32)).astype(BF16)]
        top = jnp.dot(
            down_ref[q, h], jnp.concatenate(parts, axis=0), preferred_element_type=F32
        )
        for t in range(2):
            piece = top[t * rank : (t + 1) * rank]
            tops[t].extend([piece.astype(BF16), turn(piece).astype(BF16)])
    results = []
    for t in range(2):
        rows = jnp.concatenate([row_ref[h, t, q] for q in range(groups)], axis=1)
        results.append(
            jnp.dot(rows, jnp.concatenate(tops[t], axis=0), preferred_element_type=F32)
        )
    return results


def upper_first_kernel(perm_ref, mid_ref, down_ref, row_ref, out_ref):
    for h in range(out_ref.shape[0]):
        results = upper_half(perm_ref, mid_ref, down_ref, row_ref, h)
        for t in range(2):
            out_ref[h, t] = results[t].astype(BF16)


def upper_last_kernel(own_first, perm_ref, mid_ref, down_ref, row_ref, held_ref, out_ref, mix_ref):
    leaf = held_ref.shape[2]
    if own_first:
        swap = lax.axis_index("rhs") == 1
    for h in range(out_ref.shape[0]):
        results = upper_half(perm_ref, mid_ref, down_ref, row_ref, h)
        for t in range(2):
            low = held_ref[h, t].astype(F32)
            high = results[t]
            if own_first:
                low, high = jnp.where(swap, high, low), jnp.where(swap, low, high)
            lane = lax.broadcasted_iota(jnp.int32, low.shape, 1)
            left = lane < HALF
            real = jnp.where(left, low, pltpu.roll(high, HALF, 1))
            imag = jnp.where(left, pltpu.roll(low, HALF, 1), high)
            mix_ref[h, t, pl.ds(0, leaf, stride=2), :] = real
            mix_ref[h, t, pl.ds(1, leaf, stride=2), :] = imag
            out_ref[h, t] = mix_ref[h, t].astype(BF16)


def upper(perm, mid, down, row, held, own_first):
    groups, local, _, _ = down.shape
    leaf = row.shape[3]
    smem = pl.BlockSpec(memory_space=pltpu.SMEM)
    vmem = pl.BlockSpec(memory_space=pltpu.VMEM)
    params = dict(
        out_specs=vmem,
        compiler_params=pltpu.CompilerParams(vmem_limit_bytes=32 * 1024 * 1024),
        cost_estimate=pl.CostEstimate(
            flops=400_000_000, bytes_accessed=2_800_000, transcendentals=0
        ),
    )
    if held is None:
        return pl.pallas_call(
            upper_first_kernel,
            out_shape=jax.ShapeDtypeStruct((local, 2, leaf, NRHS), BF16),
            in_specs=[smem, vmem, vmem, vmem],
            name="upper_first",
            **params,
        )(perm, mid, down, row)
    return pl.pallas_call(
        functools.partial(upper_last_kernel, own_first),
        out_shape=jax.ShapeDtypeStruct((local, 2, 2 * leaf, NRHS), BF16),
        in_specs=[smem, vmem, vmem, vmem, vmem],
        scratch_shapes=[pltpu.VMEM((local, 2, 2 * leaf, NRHS), F32)],
        name="upper_last",
        **params,
    )(perm, mid, down, row, held)


def on_device(
    dests, x_panels, leaf_basis, leaf_count, parent_map, up_transfer, mid_perm, down_transfer, row_basis
):
    boxes, directions, rank, _, leaf = leaf_basis.shape
    basis = leaf_basis.reshape(boxes, directions, rank * 2, leaf)
    groups, _, local = down_transfer.shape[:3]
    down = down_transfer.reshape(groups, local, 2 * rank, 4 * rank)
    row = row_basis.reshape(local, 2, groups, leaf, 2 * rank)
    flipped = jnp.transpose(x_panels, (0, 2, 3, 1))
    own_first = flipped.shape[2] == HALF
    if own_first:
        other = lax.ppermute(flipped, "rhs", [(0, 1), (1, 0)])
        halves = [flipped, other]
    else:
        whole = lax.all_gather(flipped, "rhs", axis=2, tiled=True)
        halves = [whole[:, :, :HALF], whole[:, :, HALF:]]
    arrived = []
    for half in halves:
        x = half.reshape(boxes, 2 * HALF, leaf)
        mid = lower(leaf_count, parent_map, x, basis, up_transfer, dests)
        moved = lax.all_to_all(mid, ("blk", "sub"), split_axis=0, concat_axis=0, tiled=True)
        arrived.append(moved.reshape(-1, local, rank, NRHS))
    held = upper(mid_perm, arrived[0], down, row, None, own_first)
    result = upper(mid_perm, arrived[1], down, row, held, own_first)
    return result.reshape(1, local, 2, leaf, 2, NRHS)


def solution(mesh):
    dests = mesh.shape["blk"] * mesh.shape["sub"]
    return jax.shard_map(
        functools.partial(on_device, dests),
        mesh=mesh,
        in_specs=(
            P(("grp", "blk", "sub"), None, None, "rhs"),
            P(("blk", "sub"), "rhs", None, None, None),
            P(("blk", "sub")),
            P("rhs"),
            P(("blk", "sub"), "rhs", None, None),
            P(),
            P(None, "rhs", ("blk", "sub"), None, None, None),
            P("rhs", ("blk", "sub"), None, None, None, None),
        ),
        out_specs=P(("grp", "rhs"), ("blk", "sub"), None, None, None, None),
        check_vma=False,
    )
```

time: 116 us -> 50.9 us (0.44)
  other arithmetic: 33.8 us -> 0 us
  local copies, waits for them, and re-layouts: 34.6 us -> 5.39 us
  Pallas kernels: 0 us -> 10.3 us
  matrix products: 8.42 us -> 0 us
  starting transfers between devices: 5.36 us -> 11.5 us
  blocking collectives: 6.1 us -> 0 us
  waiting for transfers between devices: 26.5 us -> 23.2 us
    another operation x6 -> x0, other arithmetic: 11 us -> none  [twisted(): return jnp.stack([values, turned], axis=-4)]
    pallas_call x0 -> x4, Pallas kernels: none -> 10.3 us  [the longest x2 4.66 us: lower(): pl.pallas_call(lower_kernel, out_shape=jax.ShapeDtypeStruct((dests, pairs...]
    reshape x8 -> x0, local copies, waits for them, and re-layouts: 9.75 us -> none  [the longest x1 2.62 us: on_device(): jnp.transpose(twisted(ordered), (0, 2, 1, 3, 4, 5, 6))]
    another operation x3 -> x0, local copies, waits for them, and re-layouts: 8.95 us -> none
    transpose x2 -> x0, other arithmetic: 8.71 us -> none  [the longest x1 8.51 us: on_device(): jnp.transpose(twisted(chosen), (0, 2, 1, 3, 4, 5, 6))]
    dot_general x4 -> x0, matrix products: 8.42 us -> none  [the longest x1 3.03 us: on_device(): jnp.einsum('pjmx,pjxn->pjmn', up_transfer, spread_up, preferred_element_t...]
    transpose x2 -> x0, local copies, waits for them, and re-layouts: 8.09 us -> none  [the longest x1 5.93 us: on_device(): jnp.transpose(twisted(chosen), (0, 2, 1, 3, 4, 5, 6))]
    gather x2 -> x0, local copies, waits for them, and re-layouts: 7.41 us -> none  [the longest x1 6.66 us: on_device(): chosen = jnp.take(leaf_coef, parent_map, axis=1)]
  transfers between devices with their start and end apart: 1 -> 3, of which waited for: 1 -> 3; matrix products, arithmetic and copies ran while one was open for 0% -> 0% of each run, Pallas kernels for 0% -> 9%
where the time goes in v1:
time: 50.9 us; the launch traced here: 50.5 us
  waiting for transfers between devices  23.2 us (46%)
  starting transfers between devices  11.5 us (23%)
  Pallas kernels  10.3 us (20%)
  local copies, waits for them, and re-layouts  5.39 us (11%)
    all_to_all x2, waiting for transfers between devices, on_device(): lax.all_to_all(mid, ('blk', 'sub'), split_axis=0, concat_axis=0, tiled=True)  20.2 us
    all_to_all x2, starting transfers between devices, on_device(): lax.all_to_all(mid, ('blk', 'sub'), split_axis=0, concat_axis=0, tiled=True)  9.95 us
    unnamed x24, local copies, waits for them, and re-layouts  5.39 us
    pallas_call x2, Pallas kernels, lower(): pl.pallas_call(lower_kernel, out_shape=jax.ShapeDtypeStruct((dests, pairs...  4.66 us
    pallas_call x1, Pallas kernels, upper(): pl.pallas_call(functools.partial(upper_last_kernel, own_first), out_shape...  3.07 us
    ppermute x1, waiting for transfers between devices, on_device(): other = lax.ppermute(flipped, 'rhs', [(0, 1), (1, 0)])  2.94 us
    pallas_call x1, Pallas kernels, upper(): pl.pallas_call(upper_first_kernel, out_shape=jax.ShapeDtypeStruct((local,...  2.61 us
    ppermute x1, starting transfers between devices, on_device(): other = lax.ppermute(flipped, 'rhs', [(0, 1), (1, 0)])  1.56 us
  transfers between devices with their start and end apart: 3, of which 3 were waited for; matrix products, arithmetic and copies ran while one was open for 0% of the time, Pallas kernels for 9%

profile of v1, /device:TPU:0, one launch (start us, length us, event | category | flops | bytes accessed | tf_op | source)
XLA Modules:
  0.0 50.5 jit_solution(749439720767863511)
XLA Ops:
  0.0 0.0 copy-start.9
  0.0 0.0 copy-start.10
  0.0 0.7 %copy-done.9 = s32[2]{0:T(128)S(1)} copy-done((s32[2]{0:T(128)S(1)}, s32[2]{0:T(128)}, u32[]{:S(2)}) %copy-start.9) | copy-done | bytes 32
  0.7 0.0 copy-done.10
  0.7 0.0 copy-start
  0.7 1.2 %copy-done = bf16[2,16,64,2,128]{4,3,2,1,0:T(2,128)(2,1)S(1)} copy-done((bf16[2,16,64,2,128]{4,3,2,1,0:T(2,128)(2,1)S(1)}, bf16[2,16,64,2,128]{4,3,2,1,0:T(2,128)(2,1)}, u32[]{:S(2)}) %copy-start) | copy-done | bytes 1048600
  1.9 0.0 copy-start.2
  1.9 1.2 %copy-done.2 = bf16[1,32,64,256]{3,2,1,0:T(8,128)(2,1)S(1)} copy-done((bf16[1,32,64,256]{3,2,1,0:T(8,128)(2,1)S(1)}, bf16[1,32,64,256]{3,2,1,0:T(8,128)(2,1)}, u32[]{:S(2)}) %copy-start.2) | copy-done | bytes 1048600
  3.1 0.0 copy-start.7
  3.1 0.8 %copy-done.7 = bf16[2,128,2,64]{1,3,2,0:T(8,128)(2,1)S(1)} copy-done((bf16[2,128,2,64]{1,3,2,0:T(8,128)(2,1)S(1)}, bf16[2,128,2,64]{1,3,2,0:T(8,128)(2,1)}, u32[]{:S(2)}) %copy-start.7) | copy-done | bytes 65560
  4.0 0.0 copy-start.8
  4.0 0.0 copy-start.3
  4.0 2.7 %lower.3 = bf16[8,1,4,64,128]{4,3,2,1,0:T(8,128)(2,1)} custom-call(s32[2]{0:T(128)S(1)} %copy-done.9, s32[32]{0:T(128)S(1)} %copy-done.10, bf16[2,128,128]{2,1,0:T(8,128)(2,1)S(1)} %bitcast.17, bf16[2,16,128,128]{3,2,1,0:T(8,128)(2,1)S(1)} %bitcast.10, bf16[1,32,64,256]{3,2,1,0:T(8,128)(2,1)S(1)} %copy-done.2), custom_call_target="tpu_custom_call" | custom-call | flops 400000000 | bytes 2800000 | tf_op jit(solution)/shard_map/lower/pallas_call | solution.py:61
  6.7 0.0 copy-start.1
  6.7 6.5 %all-to-all-start.1 = ((bf16[8,1,4,64,128]{4,3,2,1,0:T(8,128)(2,1)}), bf16[8,1,4,64,128]{4,3,2,1,0:T(8,128)(2,1)}, u32[]{:S(2)}, u32[]{:S(2)}) async-start(bf16[8,1,4,64,128]{4,3,2,1,0:T(8,128)(2,1)} %lower.3), calls=%async_computation.1 | async-start | bytes 1048576 | tf_op jit(solution)/shard_map/all_to_all | solution.py:179
  13.2 0.0 copy-done.8
  13.2 1.6 %collective-permute-start = (bf16[2,2,64,128]{3,2,1,0:T(8,128)(2,1)S(1)}, bf16[2,2,64,128]{3,2,1,0:T(8,128)(2,1)S(1)}, u32[]{:S(2)}, u32[]{:S(2)}) collective-permute-start(bf16[2,2,64,128]{3,2,1,0:T(8,128)(2,1)S(1)} %bitcast.18), channel_id=1, source_target_pairs={{0,2},{2,0},{1,3},{3,1},{4,6},{6,4},{5,7},{7,5},{8,10},{10,8},{9,1... | collective-permute-start | bytes 196616 | tf_op jit(solution)/shard_map/ppermute | solution.py:170
  14.7 2.9 %collective-permute-done = bf16[2,2,64,128]{3,2,1,0:T(8,128)(2,1)S(1)} collective-permute-done((bf16[2,2,64,128]{3,2,1,0:T(8,128)(2,1)S(1)}, bf16[2,2,64,128]{3,2,1,0:T(8,128)(2,1)S(1)}, u32[]{:S(2)}, u32[]{:S(2)}) %collective-permute-start) | collective-permute-done | bytes 65568 | tf_op jit(solution)/shard_map/ppermute | solution.py:170
  17.7 0.0 copy-done.3
  17.7 0.0 copy-done.1
  17.7 1.9 %lower.2 = bf16[8,1,4,64,128]{4,3,2,1,0:T(8,128)(2,1)S(1)} custom-call(s32[2]{0:T(128)S(1)} %copy-done.9, s32[32]{0:T(128)S(1)} %copy-done.10, bf16[2,128,128]{2,1,0:T(8,128)(2,1)S(1)} %bitcast.19, bf16[2,16,128,128]{3,2,1,0:T(8,128)(2,1)S(1)} %bitcast.11, bf16[1,32,64,256]{3,2,1,0:T(8,128)(2,1)S(1)} %copy-done.3), custom_call_target="tpu_custom_call" | custom-call | flops 400000000 | bytes 2800000 | tf_op jit(solution)/shard_map/lower/pallas_call | solution.py:61
  19.6 0.0 copy-start.6
  19.6 0.8 %copy-done.6 = bf16[8,1,4,64,128]{4,3,2,1,0:T(8,128)(2,1)} copy-done((bf16[8,1,4,64,128]{4,3,2,1,0:T(8,128)(2,1)}, bf16[8,1,4,64,128]{4,3,2,1,0:T(8,128)(2,1)S(1)}, u32[]{:S(2)}) %copy-start.6) | copy-done | bytes 524312
  20.4 8.2 %all-to-all-done.1 = bf16[8,1,4,64,128]{4,3,2,1,0:T(8,128)(2,1)} async-done(((bf16[8,1,4,64,128]{4,3,2,1,0:T(8,128)(2,1)}), bf16[8,1,4,64,128]{4,3,2,1,0:T(8,128)(2,1)}, u32[]{:S(2)}, u32[]{:S(2)}) %all-to-all-start.1) | async-done | bytes 524320 | tf_op jit(solution)/shard_map/all_to_all | solution.py:179
  28.6 3.5 %all-to-all-start = ((bf16[8,1,4,64,128]{4,3,2,1,0:T(8,128)(2,1)}), bf16[8,1,4,64,128]{4,3,2,1,0:T(8,128)(2,1)S(1)}, u32[]{:S(2)}, u32[]{:S(2)}) async-start(bf16[8,1,4,64,128]{4,3,2,1,0:T(8,128)(2,1)} %copy-done.6), calls=%async_computation | async-start | bytes 1048576 | tf_op jit(solution)/shard_map/all_to_all | solution.py:179
  32.1 0.0 copy-start.11
  32.1 0.0 copy-done.5
  32.1 0.0 copy-done.4
  32.2 0.6 %copy-done.11 = s32[8]{0:T(128)S(1)} copy-done((s32[8]{0:T(128)S(1)}, s32[8]{0:T(128)}, u32[]{:S(2)}) %copy-start.11) | copy-done | bytes 56
  32.8 2.6 %upper_first.1.held_ref = bf16[4,2,128,128]{3,2,1,0:T(8,128)(2,1)S(1)} custom-call(s32[8]{0:T(128)S(1)} %copy-done.11, bf16[8,4,64,128]{3,2,1,0:T(8,128)(2,1)} %bitcast.7.mid_ref, bf16[4,4,128,256]{3,2,1,0:T(8,128)(2,1)S(1)} %bitcast.12, bf16[4,2,4,128,128]{4,3,2,1,0:T(8,128)(2,1)S(1)} %bitcast.14), custom_call_target="tpu_custom_call" | custom-call | flops 400000000 | bytes 2800000 | tf_op jit(solution)/shard_map/upper_first/pallas_call | solution.py:142
  35.4 12.0 %all-to-all-done = bf16[8,1,4,64,128]{4,3,2,1,0:T(8,128)(2,1)S(1)} async-done(((bf16[8,1,4,64,128]{4,3,2,1,0:T(8,128)(2,1)}), bf16[8,1,4,64,128]{4,3,2,1,0:T(8,128)(2,1)S(1)}, u32[]{:S(2)}, u32[]{:S(2)}) %all-to-all-start) | async-done | bytes 524320 | tf_op jit(solution)/shard_map/all_to_all | solution.py:179
  47.4 3.1 %upper_last.1 = bf16[4,2,256,128]{3,2,1,0:T(8,128)(2,1)} custom-call(s32[8]{0:T(128)S(1)} %copy-done.11, bf16[8,4,64,128]{3,2,1,0:T(8,128)(2,1)S(1)} %bitcast.16, bf16[4,4,128,256]{3,2,1,0:T(8,128)(2,1)S(1)} %bitcast.13, bf16[4,2,4,128,128]{4,3,2,1,0:T(8,128)(2,1)S(1)} %bitcast.15, bf16[4,2,128,128]{3,2,1,0:T(8,128)(2,1)S(1)} %upper_first.1.held_ref), custom_call_target="tpu_custom_call" | custom-call | flops 400000000 | bytes 2800000 | tf_op jit(solution)/shard_map/upper_last/pallas_call | solution.py:149
  (2 shorter events, 0.0 us)
Async XLA Ops:
  0.0 0.7 %copy-start.9 = (s32[2]{0:T(128)S(1)}, s32[2]{0:T(128)}, u32[]{:S(2)}) copy-start(s32[2]{0:T(128)} %count_ref.3) | copy-start | bytes 28
  0.0 0.7 %copy-start.10 = (s32[32]{0:T(128)S(1)}, s32[32]{0:T(128)}, u32[]{:S(2)}) copy-start(s32[32]{0:T(128)} %parent_ref.3) | copy-start | bytes 388
  0.7 1.2 %copy-start = (bf16[2,16,64,2,128]{4,3,2,1,0:T(2,128)(2,1)S(1)}, bf16[2,16,64,2,128]{4,3,2,1,0:T(2,128)(2,1)}, u32[]{:S(2)}) copy-start(bf16[2,16,64,2,128]{4,3,2,1,0:T(2,128)(2,1)} %param.9) | copy-start | bytes 3145732
  1.9 1.2 %copy-start.2 = (bf16[1,32,64,256]{3,2,1,0:T(8,128)(2,1)S(1)}, bf16[1,32,64,256]{3,2,1,0:T(8,128)(2,1)}, u32[]{:S(2)}) copy-start(bf16[1,32,64,256]{3,2,1,0:T(8,128)(2,1)} %up_ref.3) | copy-start | bytes 3145732
  3.1 0.8 %copy-start.7 = (bf16[2,128,2,64]{1,3,2,0:T(8,128)(2,1)S(1)}, bf16[2,128,2,64]{1,3,2,0:T(8,128)(2,1)}, u32[]{:S(2)}) copy-start(bf16[2,128,2,64]{1,3,2,0:T(8,128)(2,1)} %param.8) | copy-start | bytes 196612
  4.0 9.2 %copy-start.8 = (bf16[2,128,2,64]{1,3,2,0:T(8,128)(2,1)S(1)}, bf16[2,128,2,64]{1,3,2,0:T(8,128)(2,1)}, u32[]{:S(2)}) copy-start(bf16[2,128,2,64]{1,3,2,0:T(8,128)(2,1)} %param.8) | copy-start | bytes 196612
  4.0 13.7 %copy-start.3 = (bf16[1,32,64,256]{3,2,1,0:T(8,128)(2,1)S(1)}, bf16[1,32,64,256]{3,2,1,0:T(8,128)(2,1)}, u32[]{:S(2)}) copy-start(bf16[1,32,64,256]{3,2,1,0:T(8,128)(2,1)} %up_ref.3) | copy-start | bytes 3145732
  6.7 11.0 %copy-start.1 = (bf16[2,16,64,2,128]{4,3,2,1,0:T(2,128)(2,1)S(1)}, bf16[2,16,64,2,128]{4,3,2,1,0:T(2,128)(2,1)}, u32[]{:S(2)}) copy-start(bf16[2,16,64,2,128]{4,3,2,1,0:T(2,128)(2,1)} %param.9) | copy-start | bytes 3145732
  6.7 21.9 %all-to-all-start.1 = ((bf16[8,1,4,64,128]{4,3,2,1,0:T(8,128)(2,1)}), bf16[8,1,4,64,128]{4,3,2,1,0:T(8,128)(2,1)}, u32[]{:S(2)}, u32[]{:S(2)}) async-start(bf16[8,1,4,64,128]{4,3,2,1,0:T(8,128)(2,1)} %lower.3), calls=%async_computation.1 | async-start | bytes 1048576 | tf_op jit(solution)/shard_map/all_to_all | solution.py:179
  13.2 4.5 %collective-permute-start = (bf16[2,2,64,128]{3,2,1,0:T(8,128)(2,1)S(1)}, bf16[2,2,64,128]{3,2,1,0:T(8,128)(2,1)S(1)}, u32[]{:S(2)}, u32[]{:S(2)}) collective-permute-start(bf16[2,2,64,128]{3,2,1,0:T(8,128)(2,1)S(1)} %bitcast.18), channel_id=1, source_target_pairs={{0,2},{2,0},{1,3},{3,1},{4,6},{6,4},{5,7},{7,5},{8,10},{10,8},{9,1... | collective-permute-start | bytes 196616 | tf_op jit(solution)/shard_map/ppermute | solution.py:170
  17.7 14.5 %copy-start.5 = (bf16[1,4,2,4,128,128]{5,4,3,2,1,0:T(8,128)(2,1)S(1)}, bf16[1,4,2,4,128,128]{5,4,3,2,1,0:T(8,128)(2,1)}, u32[]{:S(2)}) copy-start(bf16[1,4,2,4,128,128]{5,4,3,2,1,0:T(8,128)(2,1)} %param.15) | copy-start | bytes 3145732
  19.6 0.8 %copy-start.6 = (bf16[8,1,4,64,128]{4,3,2,1,0:T(8,128)(2,1)}, bf16[8,1,4,64,128]{4,3,2,1,0:T(8,128)(2,1)S(1)}, u32[]{:S(2)}) copy-start(bf16[8,1,4,64,128]{4,3,2,1,0:T(8,128)(2,1)S(1)} %lower.2) | copy-start | bytes 1572868
  20.4 11.7 %copy-start.4 = (bf16[4,1,4,2,64,256]{5,4,3,2,1,0:T(8,128)(2,1)S(1)}, bf16[4,1,4,2,64,256]{5,4,3,2,1,0:T(8,128)(2,1)}, u32[]{:S(2)}) copy-start(bf16[4,1,4,2,64,256]{5,4,3,2,1,0:T(8,128)(2,1)} %param.14) | copy-start | bytes 3145732
  28.6 18.8 %all-to-all-start = ((bf16[8,1,4,64,128]{4,3,2,1,0:T(8,128)(2,1)}), bf16[8,1,4,64,128]{4,3,2,1,0:T(8,128)(2,1)S(1)}, u32[]{:S(2)}, u32[]{:S(2)}) async-start(bf16[8,1,4,64,128]{4,3,2,1,0:T(8,128)(2,1)} %copy-done.6), calls=%async_computation | async-start | bytes 1048576 | tf_op jit(solution)/shard_map/all_to_all | solution.py:179
  32.1 0.7 %copy-start.11 = (s32[8]{0:T(128)S(1)}, s32[8]{0:T(128)}, u32[]{:S(2)}) copy-start(s32[8]{0:T(128)} %perm_ref.3) | copy-start | bytes 100

commit v2 on v1

v2 whole, which is shorter than its diff:
```python
import functools

import jax
import jax.numpy as jnp
from jax import lax
from jax.experimental import pallas as pl
from jax.experimental.pallas import tpu as pltpu
from jax.sharding import PartitionSpec as P

NRHS = 128
HALF = 64
F32 = jnp.float32
BF16 = jnp.bfloat16


def turn(values):
    lane = lax.broadcasted_iota(jnp.int32, values.shape, 1)
    rolled = pltpu.roll(values, HALF, 1)
    return jnp.where(lane < HALF, -rolled, rolled)


def lower_body(me, order, count_ref, parent_ref, x_ref, basis_ref, up_ref, outs, g_ref, leaf_ref, ready):
    boxes, dirs, rows, _ = basis_ref.shape
    rank = rows // 2
    pairs = up_ref.shape[0]
    local = outs[0].shape[1]
    first = lax.axis_index("rhs") * dirs
    even = pl.ds(0, rank, stride=2)
    odd = pl.ds(1, rank, stride=2)
    ready("start")
    for b in range(boxes):
        ready(b)
        x = x_ref[b]
        spread = jnp.concatenate([x, -x[HALF:], x[:HALF]], axis=0)
        for d in range(dirs):
            slot = b * dirs + d
            g = lax.dot_general(
                basis_ref[b, d], spread, (((1,), (1,)), ((), ())), preferred_element_type=F32
            )
            g_ref[slot, 0] = g[:, :NRHS]
            g_ref[slot, 1] = g[:, NRHS:]
            plain = g_ref[slot, 0, even, :] + g_ref[slot, 1, odd, :]
            turned = g_ref[slot, 1, even, :] - g_ref[slot, 0, odd, :]
            live = first + d < count_ref[b]
            plain = jnp.where(live, plain, jnp.zeros_like(plain)).astype(BF16)
            turned = jnp.where(live, turned, jnp.zeros_like(turned)).astype(BF16)
            base = (b % 2) * 2 * rank
            leaf_ref[b // 2, d, base : base + rank, :] = plain
            leaf_ref[b // 2, d, base + rank : base + 2 * rank, :] = turned
    ready("up")
    for out_ref, k in zip(outs, order):
        dest = jnp.bitwise_xor(me, k)
        for p in range(pairs):
            for h in range(local):
                j = dest * local + h
                mid = jnp.dot(
                    up_ref[p, j], leaf_ref[p, parent_ref[j]], preferred_element_type=F32
                )
                out_ref[p, h] = mid.astype(BF16)


def position():
    return lax.axis_index("blk") * lax.axis_size("sub") + lax.axis_index("sub")


def lower_cold_kernel(order, count_hbm, parent_hbm, x_hbm, basis_hbm, up_hbm, *refs):
    n = len(order)
    outs = refs[:n]
    g_ref, leaf_ref, count_ref, parent_ref, x_ref, basis_ref, up_ref, sems = refs[n:]
    boxes = basis_ref.shape[0]
    copies = {
        "x": pltpu.make_async_copy(x_hbm, x_ref, sems.at[0]),
        "count": pltpu.make_async_copy(count_hbm, count_ref, sems.at[1]),
        "parent": pltpu.make_async_copy(parent_hbm, parent_ref, sems.at[2]),
        "up": pltpu.make_async_copy(up_hbm, up_ref, sems.at[3]),
    }
    for b in range(boxes):
        copies[b] = pltpu.make_async_copy(basis_hbm.at[b], basis_ref.at[b], sems.at[4 + b])
    for name in ["x", 0, "count"] + list(range(1, boxes)) + ["up", "parent"]:
        copies[name].start()

    def ready(name):
        for other in {"start": ["x", "count"], "up": ["up", "parent"]}.get(name, [name]):
            copies[other].wait()

    lower_body(
        position(), order, count_ref, parent_ref, x_ref, basis_ref, up_ref, outs, g_ref, leaf_ref, ready
    )


def lower_warm_kernel(order, count_ref, parent_ref, x_ref, basis_ref, up_ref, *refs):
    n = len(order)
    outs = refs[:n]
    g_ref, leaf_ref = refs[n:]
    lower_body(
        position(), order, count_ref, parent_ref, x_ref, basis_ref, up_ref, outs, g_ref, leaf_ref, lambda name: None
    )


def lower(order, cold, count, parents, x, basis, up):
    boxes, dirs, rows, leaf = basis.shape
    pairs, dirs_up, rank, _ = up.shape
    smem = pl.BlockSpec(memory_space=pltpu.SMEM)
    vmem = pl.BlockSpec(memory_space=pltpu.VMEM)
    hbm = pl.BlockSpec(memory_space=pltpu.HBM)
    scratch = [
        pltpu.VMEM((boxes * dirs, 2, rows, NRHS), F32),
        pltpu.VMEM((pairs, dirs, 4 * rank, NRHS), BF16),
    ]
    if cold:
        scratch += [
            pltpu.SMEM(count.shape, jnp.int32),
            pltpu.SMEM(parents.shape, jnp.int32),
            pltpu.VMEM(x.shape, BF16),
            pltpu.VMEM(basis.shape, BF16),
            pltpu.VMEM(up.shape, BF16),
            pltpu.SemaphoreType.DMA((4 + boxes,)),
        ]
    block = jax.ShapeDtypeStruct((pairs, dirs_up // len(order), rank, NRHS), BF16)
    return pl.pallas_call(
        functools.partial(lower_cold_kernel if cold else lower_warm_kernel, order),
        out_shape=[block] * len(order),
        in_specs=[hbm] * 5 if cold else [smem, smem, vmem, vmem, vmem],
        out_specs=[vmem] * len(order),
        scratch_shapes=scratch,
        compiler_params=pltpu.CompilerParams(vmem_limit_bytes=32 * 1024 * 1024),
        cost_estimate=pl.CostEstimate(
            flops=400_000_000, bytes_accessed=2_800_000, transcendentals=0
        ),
        name="lower_cold" if cold else "lower_warm",
    )(count, parents, x, basis, up)


def gather_mids(order, mids, spread_ref):
    me = position()
    pairs, local, rank, _ = mids[0].shape
    for mid_ref, k in zip(mids, order):
        source = jnp.bitwise_xor(me, k)
        for p in range(pairs):
            for h in range(local):
                mid = mid_ref[p, h]
                spread_ref[source * pairs + p, h, :rank] = mid
                spread_ref[source * pairs + p, h, rank:] = turn(mid.astype(F32)).astype(BF16)


def upper_half(perm_ref, spread_ref, down_ref, row_ref, h):
    groups = down_ref.shape[0]
    rank = spread_ref.shape[2] // 2
    tops = ([], [])
    for q in range(groups):
        parts = [spread_ref[perm_ref[2 * q + s], h] for s in range(2)]
        top = jnp.dot(
            down_ref[q, h], jnp.concatenate(parts, axis=0), preferred_element_type=F32
        )
        for t in range(2):
            piece = top[t * rank : (t + 1) * rank]
            tops[t].extend([piece.astype(BF16), turn(piece).astype(BF16)])
    results = []
    for t in range(2):
        rows = jnp.concatenate([row_ref[h, t, q] for q in range(groups)], axis=1)
        results.append(
            jnp.dot(rows, jnp.concatenate(tops[t], axis=0), preferred_element_type=F32)
        )
    return results


def upper_first_kernel(order, perm_ref, down_ref, row_ref, *refs):
    n = len(order)
    mids, out_ref, spread_ref = refs[:n], refs[n], refs[n + 1]
    gather_mids(order, mids, spread_ref)
    for h in range(out_ref.shape[0]):
        results = upper_half(perm_ref, spread_ref, down_ref, row_ref, h)
        for t in range(2):
            out_ref[h, t] = results[t].astype(BF16)


def upper_last_kernel(order, own_first, perm_ref, down_ref, row_ref, held_ref, *refs):
    n = len(order)
    mids, out_ref, spread_ref, mix_ref = refs[:n], refs[n], refs[n + 1], refs[n + 2]
    leaf = held_ref.shape[2]
    gather_mids(order, mids, spread_ref)
    if own_first:
        swap = lax.axis_index("rhs") == 1
    for h in range(out_ref.shape[0]):
        results = upper_half(perm_ref, spread_ref, down_ref, row_ref, h)
        for t in range(2):
            low = held_ref[h, t].astype(F32)
            high = results[t]
            if own_first:
                low, high = jnp.where(swap, high, low), jnp.where(swap, low, high)
            lane = lax.broadcasted_iota(jnp.int32, low.shape, 1)
            left = lane < HALF
            real = jnp.where(left, low, pltpu.roll(high, HALF, 1))
            imag = jnp.where(left, pltpu.roll(low, HALF, 1), high)
            mix_ref[h, t, pl.ds(0, leaf, stride=2), :] = real
            mix_ref[h, t, pl.ds(1, leaf, stride=2), :] = imag
            out_ref[h, t] = mix_ref[h, t].astype(BF16)


def upper(order, perm, mids, down, row, held, own_first):
    groups, local, _, width = down.shape
    leaf = row.shape[3]
    smem = pl.BlockSpec(memory_space=pltpu.SMEM)
    vmem = pl.BlockSpec(memory_space=pltpu.VMEM)
    params = dict(
        out_specs=vmem,
        compiler_params=pltpu.CompilerParams(vmem_limit_bytes=32 * 1024 * 1024),
        cost_estimate=pl.CostEstimate(
            flops=400_000_000, bytes_accessed=2_800_000, transcendentals=0
        ),
    )
    spread = pltpu.VMEM((2 * groups, local, width // 2, NRHS), BF16)
    n = len(mids)
    if held is None:
        return pl.pallas_call(
            functools.partial(upper_first_kernel, order),
            out_shape=jax.ShapeDtypeStruct((local, 2, leaf, NRHS), BF16),
            in_specs=[smem] + [vmem] * (2 + n),
            scratch_shapes=[spread],
            name="upper_first",
            **params,
        )(perm, down, row, *mids)
    return pl.pallas_call(
        functools.partial(upper_last_kernel, order, own_first),
        out_shape=jax.ShapeDtypeStruct((local, 2, 2 * leaf, NRHS), BF16),
        in_specs=[smem] + [vmem] * (3 + n),
        scratch_shapes=[spread, pltpu.VMEM((local, 2, 2 * leaf, NRHS), F32)],
        name="upper_last",
        **params,
    )(perm, down, row, held, *mids)


def on_device(
    dests, x_panels, leaf_basis, leaf_count, parent_map, up_transfer, mid_perm, down_transfer, row_basis
):
    boxes, directions, rank, _, leaf = leaf_basis.shape
    basis = leaf_basis.reshape(boxes, directions, rank * 2, leaf)
    groups, _, local = down_transfer.shape[:3]
    down = down_transfer.reshape(groups, local, 2 * rank, 4 * rank)
    row = row_basis.reshape(local, 2, groups, leaf, 2 * rank)
    flipped = jnp.transpose(x_panels, (0, 2, 3, 1))
    own_first = flipped.shape[2] == HALF
    order = tuple(range(dests - 1, -1, -1))
    if own_first:
        halves = [flipped, lax.ppermute(flipped, "rhs", [(0, 1), (1, 0)])]
    else:
        whole = lax.all_gather(flipped, "rhs", axis=2, tiled=True)
        halves = [whole[:, :, :HALF], whole[:, :, HALF:]]
    arrived = []
    for i, half in enumerate(halves):
        x = half.reshape(boxes, 2 * HALF, leaf)
        mids = lower(order, i == 0, leaf_count, parent_map, x, basis, up_transfer)
        if i == 0:
            mids, halves[1] = lax.optimization_barrier((mids, halves[1]))
        moved = []
        for mid, k in zip(mids, order):
            if k:
                pairs = [(m, m ^ k) for m in range(dests)]
                mid = lax.ppermute(mid, ("blk", "sub"), pairs)
            moved.append(mid)
        arrived.append(moved)
    held = upper(order, mid_perm, arrived[0], down, row, None, own_first)
    result = upper(order, mid_perm, arrived[1], down, row, held, own_first)
    return result.reshape(1, local, 2, leaf, 2, NRHS)


def solution(mesh):
    dests = mesh.shape["blk"] * mesh.shape["sub"]
    return jax.shard_map(
        functools.partial(on_device, dests),
        mesh=mesh,
        in_specs=(
            P(("grp", "blk", "sub"), None, None, "rhs"),
            P(("blk", "sub"), "rhs", None, None, None),
            P(("blk", "sub")),
            P("rhs"),
            P(("blk", "sub"), "rhs", None, None),
            P(),
            P(None, "rhs", ("blk", "sub"), None, None, None),
            P("rhs", ("blk", "sub"), None, None, None, None),
        ),
        out_specs=P(("grp", "rhs"), ("blk", "sub"), None, None, None, None),
        check_vma=False,
    )
```

time: 50.9 us -> 41.3 us (0.81)
  waiting for transfers between devices: 23.2 us -> 7.49 us
  starting transfers between devices: 11.5 us -> 19.1 us
  local copies, waits for them, and re-layouts: 5.39 us -> 4.62 us
  Pallas kernels: 10.3 us -> 9.78 us
    all_to_all x2 -> x0, waiting for transfers between devices: 20.2 us -> none  [on_device(): lax.all_to_all(mid, ('blk', 'sub'), split_axis=0, concat_axis=0, tiled=True)]
    ppermute x1 -> x15, starting transfers between devices: 1.56 us -> 19.1 us  [the longest x14 16.2 us: on_device(): mid = lax.ppermute(mid, ('blk', 'sub'), pairs)]
    all_to_all x2 -> x0, starting transfers between devices: 9.95 us -> none  [on_device(): lax.all_to_all(mid, ('blk', 'sub'), split_axis=0, concat_axis=0, tiled=True)]
    ppermute x1 -> x15, waiting for transfers between devices: 2.94 us -> 7.49 us  [the longest x14 7.49 us: on_device(): mid = lax.ppermute(mid, ('blk', 'sub'), pairs)]
    unnamed x24 -> x20, local copies, waits for them, and re-layouts: 5.39 us -> 4.62 us
    pallas_call x4, Pallas kernels: 10.3 us -> 9.78 us  [the longest x2 4.28 us: lower(): pl.pallas_call(functools.partial(lower_cold_kernel if cold else lower_war...]
  transfers between devices with their start and end apart: 3 -> 15, of which waited for: 3 -> 5; matrix products, arithmetic and copies ran while one was open for 0% -> 0% of each run, Pallas kernels for 9% -> 16%
where the time goes in v2:
time: 41.3 us; the launch traced here: 41.1 us
  starting transfers between devices  19.1 us (46%)
  Pallas kernels  9.78 us (24%)
  waiting for transfers between devices  7.49 us (18%)
  local copies, waits for them, and re-layouts  4.62 us (11%)
    ppermute x14, starting transfers between devices, on_device(): mid = lax.ppermute(mid, ('blk', 'sub'), pairs)  16.2 us
    ppermute x14, waiting for transfers between devices, on_device(): mid = lax.ppermute(mid, ('blk', 'sub'), pairs)  7.49 us
    unnamed x20, local copies, waits for them, and re-layouts  4.62 us
    pallas_call x2, Pallas kernels, lower(): pl.pallas_call(functools.partial(lower_cold_kernel if cold else lower_war...  4.28 us
    pallas_call x1, Pallas kernels, upper(): pl.pallas_call(functools.partial(upper_last_kernel, order, own_first), ou...  3.24 us
    ppermute x1, starting transfers between devices, on_device(): halves = [flipped, lax.ppermute(flipped, 'rhs', [(0, 1), (1, 0)])]  2.94 us
    pallas_call x1, Pallas kernels, upper(): pl.pallas_call(functools.partial(upper_first_kernel, order), out_shape=ja...  2.27 us
  transfers between devices with their start and end apart: 15, of which 5 were waited for; matrix products, arithmetic and copies ran while one was open for 0% of the time, Pallas kernels for 16%

profile of v2, /device:TPU:0, one launch (start us, length us, event | category | flops | bytes accessed | tf_op | source)
XLA Modules:
  0.0 41.1 jit_solution(5617270859108980880)
XLA Ops:
  0.0 2.9 %collective-permute-start = (bf16[2,2,64,128]{3,2,1,0:T(8,128)(2,1)}, bf16[2,2,64,128]{3,2,1,0:T(8,128)(2,1)S(1)}, u32[]{:S(2)}, u32[]{:S(2)}) collective-permute-start(bf16[2,2,64,128]{3,2,1,0:T(8,128)(2,1)} %bitcast.14), channel_id=1, source_target_pairs={{0,2},{2,0},{1,3},{3,1},{4,6},{6,4},{5,7},{7,5},{8,10},{10,8},{9,1... | collective-permute-start | bytes 196616 | tf_op jit(solution)/shard_map/ppermute | solution.py:245
  2.9 0.7 %copy-done.8 = s32[2]{0:T(128)S(1)} copy-done((s32[2]{0:T(128)S(1)}, s32[2]{0:T(128)}, u32[]{:S(2)}) %copy-start.8) | copy-done | bytes 32
  3.6 0.0 copy-done.9
  3.6 1.2 %copy-done.2 = bf16[2,16,64,2,128]{4,3,2,1,0:T(2,128)(2,1)S(1)} copy-done((bf16[2,16,64,2,128]{4,3,2,1,0:T(2,128)(2,1)S(1)}, bf16[2,16,64,2,128]{4,3,2,1,0:T(2,128)(2,1)}, u32[]{:S(2)}) %copy-start.2) | copy-done | bytes 1048600
  4.8 1.2 %copy-done.4 = bf16[1,32,64,256]{3,2,1,0:T(8,128)(2,1)S(1)} copy-done((bf16[1,32,64,256]{3,2,1,0:T(8,128)(2,1)S(1)}, bf16[1,32,64,256]{3,2,1,0:T(8,128)(2,1)}, u32[]{:S(2)}) %copy-start.4) | copy-done | bytes 1048600
  6.1 0.8 %copy-done.6 = bf16[2,128,2,64]{1,3,2,0:T(8,128)(2,1)S(1)} copy-done((bf16[2,128,2,64]{1,3,2,0:T(8,128)(2,1)S(1)}, bf16[2,128,2,64]{1,3,2,0:T(8,128)(2,1)}, u32[]{:S(2)}) %copy-start.6) | copy-done | bytes 65560
  6.9 2.3 %lower_cold.1 = (bf16[1,4,64,128]{3,2,1,0:T(8,128)(2,1)S(1)}, bf16[1,4,64,128]{3,2,1,0:T(8,128)(2,1)S(1)}, bf16[1,4,64,128]{3,2,1,0:T(8,128)(2,1)S(1)}, bf16[1,4...) custom-call(s32[2]{0:T(128)S(1)} %copy-done.8, ...), custom_call_target="tpu_custom_call" | custom-call | flops 400000000 | bytes 2800000 | tf_op jit(solution)/shard_map/lower_cold/pallas_call | solution.py:120
  9.2 0.0 collective-permute-done
  9.2 2.8 %collective-permute-start.1 = (bf16[1,4,64,128]{3,2,1,0:T(8,128)(2,1)S(1)}, bf16[1,4,64,128]{3,2,1,0:T(8,128)(2,1)S(1)}, u32[]{:S(2)}, u32[]{:S(2)}) collective-permute-start(bf16[1,4,64,128]{3,2,1,0:T(8,128)(2,1)S(1)} %get-tuple-element.38), channel_id=1, source_target_pairs={{0,13},{1,12},{4,9},{5,8},{8,5},{9,4},{12,1},{13,0},{2,15},{3,14},... | collective-permute-start | bytes 196616 | tf_op jit(solution)/shard_map/ppermute | solution.py:259
  12.1 0.9 %collective-permute-start.2 = (bf16[1,4,64,128]{3,2,1,0:T(8,128)(2,1)S(1)}, bf16[1,4,64,128]{3,2,1,0:T(8,128)(2,1)S(1)}, u32[]{:S(2)}, u32[]{:S(2)}) collective-permute-start(bf16[1,4,64,128]{3,2,1,0:T(8,128)(2,1)S(1)} %get-tuple-element.39), channel_id=1, source_target_pairs={{0,12},{1,13},{4,8},{5,9},{8,4},{9,5},{12,0},{13,1},{2,14},{3,15},... | collective-permute-start | bytes 196616 | tf_op jit(solution)/shard_map/ppermute | solution.py:259
  13.0 0.4 collective-permute-start.3
  13.4 2.2 %collective-permute-start.4 = (bf16[1,4,64,128]{3,2,1,0:T(8,128)(2,1)S(1)}, bf16[1,4,64,128]{3,2,1,0:T(8,128)(2,1)S(1)}, u32[]{:S(2)}, u32[]{:S(2)}) collective-permute-start(bf16[1,4,64,128]{3,2,1,0:T(8,128)(2,1)S(1)} %get-tuple-element.41), channel_id=1, source_target_pairs={{0,8},{1,9},{4,12},{5,13},{8,0},{9,1},{12,4},{13,5},{2,10},{3,11},... | collective-permute-start | bytes 196616 | tf_op jit(solution)/shard_map/ppermute | solution.py:259
  15.6 0.9 %collective-permute-start.5 = (bf16[1,4,64,128]{3,2,1,0:T(8,128)(2,1)S(1)}, bf16[1,4,64,128]{3,2,1,0:T(8,128)(2,1)S(1)}, u32[]{:S(2)}, u32[]{:S(2)}) collective-permute-start(bf16[1,4,64,128]{3,2,1,0:T(8,128)(2,1)S(1)} %get-tuple-element.42), channel_id=1, source_target_pairs={{0,5},{1,4},{4,1},{5,0},{8,13},{9,12},{12,9},{13,8},{2,7},{3,6},{6... | collective-permute-start | bytes 196616 | tf_op jit(solution)/shard_map/ppermute | solution.py:259
  16.5 2.0 %lower_warm.1 = (bf16[1,4,64,128]{3,2,1,0:T(8,128)(2,1)S(1)}, bf16[1,4,64,128]{3,2,1,0:T(8,128)(2,1)S(1)}, bf16[1,4,64,128]{3,2,1,0:T(8,128)(2,1)S(1)}, bf16[1,4...) custom-call(s32[2]{0:T(128)S(1)} %copy-done.8, ...), custom_call_target="tpu_custom_call" | custom-call | flops 400000000 | bytes 2800000 | tf_op jit(solution)/shard_map/lower_warm/pallas_call | solution.py:120
  18.5 0.0 collective-permute-done.1.refs_0_
  18.5 1.0 %collective-permute-start.6 = (bf16[1,4,64,128]{3,2,1,0:T(8,128)(2,1)S(1)}, bf16[1,4,64,128]{3,2,1,0:T(8,128)(2,1)S(1)}, u32[]{:S(2)}, u32[]{:S(2)}) collective-permute-start(bf16[1,4,64,128]{3,2,1,0:T(8,128)(2,1)S(1)} %get-tuple-element.43), channel_id=1, source_target_pairs={{0,4},{1,5},{4,0},{5,1},{8,12},{9,13},{12,8},{13,9},{2,6},{3,7},{6... | collective-permute-start | bytes 196616 | tf_op jit(solution)/shard_map/ppermute | solution.py:259
  19.4 0.0 collective-permute-start.7
  19.5 3.6 %collective-permute-done.3.refs_2_ = bf16[1,4,64,128]{3,2,1,0:T(8,128)(2,1)S(1)} collective-permute-done((bf16[1,4,64,128]{3,2,1,0:T(8,128)(2,1)S(1)}, bf16[1,4,64,128]{3,2,1,0:T(8,128)(2,1)S(1)}, u32[]{:S(2)}, u32[]{:S(2)}) %collective-permute-start.3) | collective-permute-done | bytes 65568 | tf_op jit(solution)/shard_map/ppermute | solution.py:259
  23.1 1.7 %collective-permute-start.8 = (bf16[1,4,64,128]{3,2,1,0:T(8,128)(2,1)S(1)}, bf16[1,4,64,128]{3,2,1,0:T(8,128)(2,1)S(1)}, u32[]{:S(2)}, u32[]{:S(2)}) collective-permute-start(bf16[1,4,64,128]{3,2,1,0:T(8,128)(2,1)S(1)} %get-tuple-element.47), channel_id=1, source_target_pairs={{0,13},{1,12},{4,9},{5,8},{8,5},{9,4},{12,1},{13,0},{2,15},{3,14},... | collective-permute-start | bytes 196616 | tf_op jit(solution)/shard_map/ppermute | solution.py:259
  24.8 0.0 collective-permute-done.4.refs_3_
  24.8 1.8 %collective-permute-start.9 = (bf16[1,4,64,128]{3,2,1,0:T(8,128)(2,1)S(1)}, bf16[1,4,64,128]{3,2,1,0:T(8,128)(2,1)S(1)}, u32[]{:S(2)}, u32[]{:S(2)}) collective-permute-start(bf16[1,4,64,128]{3,2,1,0:T(8,128)(2,1)S(1)} %get-tuple-element.48), channel_id=1, source_target_pairs={{0,12},{1,13},{4,8},{5,9},{8,4},{9,5},{12,0},{13,1},{2,14},{3,15},... | collective-permute-start | bytes 196616 | tf_op jit(solution)/shard_map/ppermute | solution.py:259
  26.6 2.7 %collective-permute-start.11 = (bf16[1,4,64,128]{3,2,1,0:T(8,128)(2,1)S(1)}, bf16[1,4,64,128]{3,2,1,0:T(8,128)(2,1)S(1)}, u32[]{:S(2)}, u32[]{:S(2)}) collective-permute-start(bf16[1,4,64,128]{3,2,1,0:T(8,128)(2,1)S(1)} %get-tuple-element.50), channel_id=1, source_target_pairs={{0,8},{1,9},{4,12},{5,13},{8,0},{9,1},{12,4},{13,5},{2,10},{3,11},... | collective-permute-start | bytes 196616 | tf_op jit(solution)/shard_map/ppermute | solution.py:259
  29.3 0.0 collective-permute-start.12
  29.3 1.7 %collective-permute-start.13 = (bf16[1,4,64,128]{3,2,1,0:T(8,128)(2,1)S(1)}, bf16[1,4,64,128]{3,2,1,0:T(8,128)(2,1)S(1)}, u32[]{:S(2)}, u32[]{:S(2)}) collective-permute-start(bf16[1,4,64,128]{3,2,1,0:T(8,128)(2,1)S(1)} %get-tuple-element.52), channel_id=1, source_target_pairs={{0,4},{1,5},{4,0},{5,1},{8,12},{9,13},{12,8},{13,9},{2,6},{3,7},{6... | collective-permute-start | bytes 196616 | tf_op jit(solution)/shard_map/ppermute | solution.py:259
  31.0 0.6 %collective-permute-done.9.refs_1_ = bf16[1,4,64,128]{3,2,1,0:T(8,128)(2,1)S(1)} collective-permute-done((bf16[1,4,64,128]{3,2,1,0:T(8,128)(2,1)S(1)}, bf16[1,4,64,128]{3,2,1,0:T(8,128)(2,1)S(1)}, u32[]{:S(2)}, u32[]{:S(2)}) %collective-permute-start.9) | collective-permute-done | bytes 65568 | tf_op jit(solution)/shard_map/ppermute | solution.py:259
  31.6 0.0 collective-permute-start.14
  31.6 0.6 %copy-done.7 = s32[8]{0:T(128)S(1)} copy-done((s32[8]{0:T(128)S(1)}, s32[8]{0:T(128)}, u32[]{:S(2)}) %copy-start.7) | copy-done | bytes 56
  32.3 2.3 %upper_first.1.held_ref = bf16[4,2,128,128]{3,2,1,0:T(8,128)(2,1)S(1)} custom-call(s32[8]{0:T(128)S(1)} %copy-done.7, bf16[4,4,128,256]{3,2,1,0:T(8,128)(2,1)S(1)} %bitcast.8, bf16[4,2,4,128,128]{4,3,2,1,0:T(8,128)(2,1)S(1)} %bitcast.10, bf16[1,4,64,128]{3,2,1,0:T(8,128)(2,1)S(1)} %collective-permute-done.1.refs_0_, ...), custom_call_target="tpu_custom_call" | custom-call | flops 400000000 | bytes 2800000 | tf_op jit(solution)/shard_map/upper_first/pallas_call | solution.py:215
  34.5 1.3 %collective-permute-done.10.refs_2_ = bf16[1,4,64,128]{3,2,1,0:T(8,128)(2,1)S(1)} collective-permute-done((bf16[1,4,64,128]{3,2,1,0:T(8,128)(2,1)S(1)}, bf16[1,4,64,128]{3,2,1,0:T(8,128)(2,1)S(1)}, u32[]{:S(2)}, u32[]{:S(2)}) %collective-permute-start.10) | collective-permute-done | bytes 65568 | tf_op jit(solution)/shard_map/ppermute | solution.py:259
  35.8 1.4 %collective-permute-done.11.refs_3_ = bf16[1,4,64,128]{3,2,1,0:T(8,128)(2,1)S(1)} collective-permute-done((bf16[1,4,64,128]{3,2,1,0:T(8,128)(2,1)S(1)}, bf16[1,4,64,128]{3,2,1,0:T(8,128)(2,1)S(1)}, u32[]{:S(2)}, u32[]{:S(2)}) %collective-permute-start.11) | collective-permute-done | bytes 65568 | tf_op jit(solution)/shard_map/ppermute | solution.py:259
  37.3 0.5 %collective-permute-done.13.refs_5_ = bf16[1,4,64,128]{3,2,1,0:T(8,128)(2,1)S(1)} collective-permute-done((bf16[1,4,64,128]{3,2,1,0:T(8,128)(2,1)S(1)}, bf16[1,4,64,128]{3,2,1,0:T(8,128)(2,1)S(1)}, u32[]{:S(2)}, u32[]{:S(2)}) %collective-permute-start.13) | collective-permute-done | bytes 65568 | tf_op jit(solution)/shard_map/ppermute | solution.py:259
  37.8 3.2 %upper_last.1 = bf16[4,2,256,128]{3,2,1,0:T(8,128)(2,1)} custom-call(s32[8]{0:T(128)S(1)} %copy-done.7, bf16[4,4,128,256]{3,2,1,0:T(8,128)(2,1)S(1)} %bitcast.9, bf16[4,2,4,128,128]{4,3,2,1,0:T(8,128)(2,1)S(1)} %bitcast.11, bf16[4,2,128,128]{3,2,1,0:T(8,128)(2,1)S(1)} %upper_first.1.held_ref, bf16[1,4,64,128]{3,2,1,0:T(8,128)(2,1)S(1)} %collective-permute-done.8.refs_0_, ...), custom_call_target="tpu_custom_call" | custom-call | flops 400000000 | bytes 2800000 | tf_op jit(solution)/shard_map/upper_last/pallas_call | solution.py:223
  (22 shorter events, 0.0 us)
Async XLA Ops:
  0.0 9.2 %collective-permute-start = (bf16[2,2,64,128]{3,2,1,0:T(8,128)(2,1)}, bf16[2,2,64,128]{3,2,1,0:T(8,128)(2,1)S(1)}, u32[]{:S(2)}, u32[]{:S(2)}) collective-permute-start(bf16[2,2,64,128]{3,2,1,0:T(8,128)(2,1)} %bitcast.14), channel_id=1, source_target_pairs={{0,2},{2,0},{1,3},{3,1},{4,6},{6,4},{5,7},{7,5},{8,10},{10,8},{9,1... | collective-permute-start | bytes 196616 | tf_op jit(solution)/shard_map/ppermute | solution.py:245
  2.9 0.7 %copy-start.8 = (s32[2]{0:T(128)S(1)}, s32[2]{0:T(128)}, u32[]{:S(2)}) copy-start(s32[2]{0:T(128)} %count_ref.1) | copy-start | bytes 28
  2.9 0.7 %copy-start.9 = (s32[32]{0:T(128)S(1)}, s32[32]{0:T(128)}, u32[]{:S(2)}) copy-start(s32[32]{0:T(128)} %parent_ref.1) | copy-start | bytes 388
  3.6 1.2 %copy-start.2 = (bf16[2,16,64,2,128]{4,3,2,1,0:T(2,128)(2,1)S(1)}, bf16[2,16,64,2,128]{4,3,2,1,0:T(2,128)(2,1)}, u32[]{:S(2)}) copy-start(bf16[2,16,64,2,128]{4,3,2,1,0:T(2,128)(2,1)} %param.9) | copy-start | bytes 3145732
  4.8 1.2 %copy-start.4 = (bf16[1,32,64,256]{3,2,1,0:T(8,128)(2,1)S(1)}, bf16[1,32,64,256]{3,2,1,0:T(8,128)(2,1)}, u32[]{:S(2)}) copy-start(bf16[1,32,64,256]{3,2,1,0:T(8,128)(2,1)} %up_ref.1) | copy-start | bytes 3145732
  6.1 0.8 %copy-start.6 = (bf16[2,128,2,64]{1,3,2,0:T(8,128)(2,1)S(1)}, bf16[2,128,2,64]{1,3,2,0:T(8,128)(2,1)}, u32[]{:S(2)}) copy-start(bf16[2,128,2,64]{1,3,2,0:T(8,128)(2,1)} %param.8) | copy-start | bytes 196612
  6.9 9.6 %copy-start.3 = (bf16[2,16,64,2,128]{4,3,2,1,0:T(2,128)(2,1)S(1)}, bf16[2,16,64,2,128]{4,3,2,1,0:T(2,128)(2,1)}, u32[]{:S(2)}) copy-start(bf16[2,16,64,2,128]{4,3,2,1,0:T(2,128)(2,1)} %param.9) | copy-start | bytes 3145732
  6.9 9.6 %copy-start.5 = (bf16[1,32,64,256]{3,2,1,0:T(8,128)(2,1)S(1)}, bf16[1,32,64,256]{3,2,1,0:T(8,128)(2,1)}, u32[]{:S(2)}) copy-start(bf16[1,32,64,256]{3,2,1,0:T(8,128)(2,1)} %up_ref.1) | copy-start | bytes 3145732
  9.2 9.2 %collective-permute-start.1 = (bf16[1,4,64,128]{3,2,1,0:T(8,128)(2,1)S(1)}, bf16[1,4,64,128]{3,2,1,0:T(8,128)(2,1)S(1)}, u32[]{:S(2)}, u32[]{:S(2)}) collective-permute-start(bf16[1,4,64,128]{3,2,1,0:T(8,128)(2,1)S(1)} %get-tuple-element.38), channel_id=1, source_target_pairs={{0,13},{1,12},{4,9},{5,8},{8,5},{9,4},{12,1},{13,0},{2,15},{3,14},... | collective-permute-start | bytes 196616 | tf_op jit(solution)/shard_map/ppermute | solution.py:259
  12.1 7.4 %collective-permute-start.2 = (bf16[1,4,64,128]{3,2,1,0:T(8,128)(2,1)S(1)}, bf16[1,4,64,128]{3,2,1,0:T(8,128)(2,1)S(1)}, u32[]{:S(2)}, u32[]{:S(2)}) collective-permute-start(bf16[1,4,64,128]{3,2,1,0:T(8,128)(2,1)S(1)} %get-tuple-element.39), channel_id=1, source_target_pairs={{0,12},{1,13},{4,8},{5,9},{8,4},{9,5},{12,0},{13,1},{2,14},{3,15},... | collective-permute-start | bytes 196616 | tf_op jit(solution)/shard_map/ppermute | solution.py:259
  13.0 10.1 %collective-permute-start.3 = (bf16[1,4,64,128]{3,2,1,0:T(8,128)(2,1)S(1)}, bf16[1,4,64,128]{3,2,1,0:T(8,128)(2,1)S(1)}, u32[]{:S(2)}, u32[]{:S(2)}) collective-permute-start(bf16[1,4,64,128]{3,2,1,0:T(8,128)(2,1)S(1)} %get-tuple-element.40), channel_id=1, source_target_pairs={{0,9},{1,8},{4,13},{5,12},{8,1},{9,0},{12,5},{13,4},{2,11},{3,10},... | collective-permute-start | bytes 196616 | tf_op jit(solution)/shard_map/ppermute | solution.py:259
  13.4 11.4 %collective-permute-start.4 = (bf16[1,4,64,128]{3,2,1,0:T(8,128)(2,1)S(1)}, bf16[1,4,64,128]{3,2,1,0:T(8,128)(2,1)S(1)}, u32[]{:S(2)}, u32[]{:S(2)}) collective-permute-start(bf16[1,4,64,128]{3,2,1,0:T(8,128)(2,1)S(1)} %get-tuple-element.41), channel_id=1, source_target_pairs={{0,8},{1,9},{4,12},{5,13},{8,0},{9,1},{12,4},{13,5},{2,10},{3,11},... | collective-permute-start | bytes 196616 | tf_op jit(solution)/shard_map/ppermute | solution.py:259
  15.6 11.1 %collective-permute-start.5 = (bf16[1,4,64,128]{3,2,1,0:T(8,128)(2,1)S(1)}, bf16[1,4,64,128]{3,2,1,0:T(8,128)(2,1)S(1)}, u32[]{:S(2)}, u32[]{:S(2)}) collective-permute-start(bf16[1,4,64,128]{3,2,1,0:T(8,128)(2,1)S(1)} %get-tuple-element.42), channel_id=1, source_target_pairs={{0,5},{1,4},{4,1},{5,0},{8,13},{9,12},{12,9},{13,8},{2,7},{3,6},{6... | collective-permute-start | bytes 196616 | tf_op jit(solution)/shard_map/ppermute | solution.py:259
  16.5 15.1 %copy-start = (bf16[4,1,4,2,64,256]{5,4,3,2,1,0:T(8,128)(2,1)S(1)}, bf16[4,1,4,2,64,256]{5,4,3,2,1,0:T(8,128)(2,1)}, u32[]{:S(2)}) copy-start(bf16[4,1,4,2,64,256]{5,4,3,2,1,0:T(8,128)(2,1)} %param.14) | copy-start | bytes 3145732
  16.5 15.1 %copy-start.1 = (bf16[1,4,2,4,128,128]{5,4,3,2,1,0:T(8,128)(2,1)S(1)}, bf16[1,4,2,4,128,128]{5,4,3,2,1,0:T(8,128)(2,1)}, u32[]{:S(2)}) copy-start(bf16[1,4,2,4,128,128]{5,4,3,2,1,0:T(8,128)(2,1)} %param.15) | copy-start | bytes 3145732
  18.5 8.1 %collective-permute-start.6 = (bf16[1,4,64,128]{3,2,1,0:T(8,128)(2,1)S(1)}, bf16[1,4,64,128]{3,2,1,0:T(8,128)(2,1)S(1)}, u32[]{:S(2)}, u32[]{:S(2)}) collective-permute-start(bf16[1,4,64,128]{3,2,1,0:T(8,128)(2,1)S(1)} %get-tuple-element.43), channel_id=1, source_target_pairs={{0,4},{1,5},{4,0},{5,1},{8,12},{9,13},{12,8},{13,9},{2,6},{3,7},{6... | collective-permute-start | bytes 196616 | tf_op jit(solution)/shard_map/ppermute | solution.py:259
  19.4 9.9 %collective-permute-start.7 = (bf16[1,4,64,128]{3,2,1,0:T(8,128)(2,1)S(1)}, bf16[1,4,64,128]{3,2,1,0:T(8,128)(2,1)S(1)}, u32[]{:S(2)}, u32[]{:S(2)}) collective-permute-start(bf16[1,4,64,128]{3,2,1,0:T(8,128)(2,1)S(1)} %get-tuple-element.44), channel_id=1, source_target_pairs={{0,1},{1,0},{4,5},{5,4},{8,9},{9,8},{12,13},{13,12},{2,3},{3,2},{6... | collective-permute-start | bytes 196616 | tf_op jit(solution)/shard_map/ppermute | solution.py:259
  23.1 6.2 %collective-permute-start.8 = (bf16[1,4,64,128]{3,2,1,0:T(8,128)(2,1)S(1)}, bf16[1,4,64,128]{3,2,1,0:T(8,128)(2,1)S(1)}, u32[]{:S(2)}, u32[]{:S(2)}) collective-permute-start(bf16[1,4,64,128]{3,2,1,0:T(8,128)(2,1)S(1)} %get-tuple-element.47), channel_id=1, source_target_pairs={{0,13},{1,12},{4,9},{5,8},{8,5},{9,4},{12,1},{13,0},{2,15},{3,14},... | collective-permute-start | bytes 196616 | tf_op jit(solution)/shard_map/ppermute | solution.py:259
  24.8 6.8 %collective-permute-start.9 = (bf16[1,4,64,128]{3,2,1,0:T(8,128)(2,1)S(1)}, bf16[1,4,64,128]{3,2,1,0:T(8,128)(2,1)S(1)}, u32[]{:S(2)}, u32[]{:S(2)}) collective-permute-start(bf16[1,4,64,128]{3,2,1,0:T(8,128)(2,1)S(1)} %get-tuple-element.48), channel_id=1, source_target_pairs={{0,12},{1,13},{4,8},{5,9},{8,4},{9,5},{12,0},{13,1},{2,14},{3,15},... | collective-permute-start | bytes 196616 | tf_op jit(solution)/shard_map/ppermute | solution.py:259
  26.6 9.2 %collective-permute-start.10 = (bf16[1,4,64,128]{3,2,1,0:T(8,128)(2,1)S(1)}, bf16[1,4,64,128]{3,2,1,0:T(8,128)(2,1)S(1)}, u32[]{:S(2)}, u32[]{:S(2)}) collective-permute-start(bf16[1,4,64,128]{3,2,1,0:T(8,128)(2,1)S(1)} %get-tuple-element.49), channel_id=1, source_target_pairs={{0,9},{1,8},{4,13},{5,12},{8,1},{9,0},{12,5},{13,4},{2,11},{3,10},... | collective-permute-start | bytes 196616 | tf_op jit(solution)/shard_map/ppermute | solution.py:259
  26.6 10.6 %collective-permute-start.11 = (bf16[1,4,64,128]{3,2,1,0:T(8,128)(2,1)S(1)}, bf16[1,4,64,128]{3,2,1,0:T(8,128)(2,1)S(1)}, u32[]{:S(2)}, u32[]{:S(2)}) collective-permute-start(bf16[1,4,64,128]{3,2,1,0:T(8,128)(2,1)S(1)} %get-tuple-element.50), channel_id=1, source_target_pairs={{0,8},{1,9},{4,12},{5,13},{8,0},{9,1},{12,4},{13,5},{2,10},{3,11},... | collective-permute-start | bytes 196616 | tf_op jit(solution)/shard_map/ppermute | solution.py:259
  29.3 8.0 %collective-permute-start.12 = (bf16[1,4,64,128]{3,2,1,0:T(8,128)(2,1)S(1)}, bf16[1,4,64,128]{3,2,1,0:T(8,128)(2,1)S(1)}, u32[]{:S(2)}, u32[]{:S(2)}) collective-permute-start(bf16[1,4,64,128]{3,2,1,0:T(8,128)(2,1)S(1)} %get-tuple-element.51), channel_id=1, source_target_pairs={{0,5},{1,4},{4,1},{5,0},{8,13},{9,12},{12,9},{13,8},{2,7},{3,6},{6... | collective-permute-start | bytes 196616 | tf_op jit(solution)/shard_map/ppermute | solution.py:259
  29.3 8.5 %collective-permute-start.13 = (bf16[1,4,64,128]{3,2,1,0:T(8,128)(2,1)S(1)}, bf16[1,4,64,128]{3,2,1,0:T(8,128)(2,1)S(1)}, u32[]{:S(2)}, u32[]{:S(2)}) collective-permute-start(bf16[1,4,64,128]{3,2,1,0:T(8,128)(2,1)S(1)} %get-tuple-element.52), channel_id=1, source_target_pairs={{0,4},{1,5},{4,0},{5,1},{8,12},{9,13},{12,8},{13,9},{2,6},{3,7},{6... | collective-permute-start | bytes 196616 | tf_op jit(solution)/shard_map/ppermute | solution.py:259
  31.6 6.2 %collective-permute-start.14 = (bf16[1,4,64,128]{3,2,1,0:T(8,128)(2,1)S(1)}, bf16[1,4,64,128]{3,2,1,0:T(8,128)(2,1)S(1)}, u32[]{:S(2)}, u32[]{:S(2)}) collective-permute-start(bf16[1,4,64,128]{3,2,1,0:T(8,128)(2,1)S(1)} %get-tuple-element.53), channel_id=1, source_target_pairs={{0,1},{1,0},{4,5},{5,4},{8,9},{9,8},{12,13},{13,12},{2,3},{3,2},{6... | collective-permute-start | bytes 196616 | tf_op jit(solution)/shard_map/ppermute | solution.py:259
  31.6 0.7 %copy-start.7 = (s32[8]{0:T(128)S(1)}, s32[8]{0:T(128)}, u32[]{:S(2)}) copy-start(s32[8]{0:T(128)} %perm_ref.3) | copy-start | bytes 100

commit v3 on v2

v3 whole, which is shorter than its diff:
```python
import functools

import jax
import jax.numpy as jnp
from jax import lax
from jax.experimental import pallas as pl
from jax.experimental.pallas import tpu as pltpu
from jax.sharding import PartitionSpec as P

NRHS = 128
HALF = 64
F32 = jnp.float32
BF16 = jnp.bfloat16


def turn(values):
    lane = lax.broadcasted_iota(jnp.int32, values.shape, 1)
    rolled = pltpu.roll(values, HALF, 1)
    return jnp.where(lane < HALF, -rolled, rolled)


def lower_body(jobs, count_ref, parent_ref, x_ref, basis_ref, up_ref, g_ref, leaf_ref, ready):
    boxes, dirs, rows, _ = basis_ref.shape
    rank = rows // 2
    first = lax.axis_index("rhs") * dirs
    even = pl.ds(0, rank, stride=2)
    odd = pl.ds(1, rank, stride=2)
    ready("start")
    for b in range(boxes):
        ready(b)
        x = x_ref[b]
        spread = jnp.concatenate([x, -x[HALF:], x[:HALF]], axis=0)
        for d in range(dirs):
            slot = b * dirs + d
            g = lax.dot_general(
                basis_ref[b, d], spread, (((1,), (1,)), ((), ())), preferred_element_type=F32
            )
            g_ref[slot, 0] = g[:, :NRHS]
            g_ref[slot, 1] = g[:, NRHS:]
            plain = g_ref[slot, 0, even, :] + g_ref[slot, 1, odd, :]
            turned = g_ref[slot, 1, even, :] - g_ref[slot, 0, odd, :]
            live = first + d < count_ref[b]
            plain = jnp.where(live, plain, jnp.zeros_like(plain)).astype(BF16)
            turned = jnp.where(live, turned, jnp.zeros_like(turned)).astype(BF16)
            base = (b % 2) * 2 * rank
            leaf_ref[b // 2, d, base : base + rank, :] = plain
            leaf_ref[b // 2, d, base + rank : base + 2 * rank, :] = turned
    ready("up")
    for out_ref, p, j in jobs:
        mid = jnp.dot(up_ref[p, j], leaf_ref[p, parent_ref[j]], preferred_element_type=F32)
        out_ref[...] = mid.astype(BF16)


def both_cores(order):
    return [(k, which) for k in order for which in (0, 1)]


def target(k, which, h, local):
    z = jnp.bitwise_xor(lax.axis_index("blk"), k)
    core = jnp.bitwise_xor(lax.axis_index("sub"), which)
    return (z * 2 + core) * local + h


def lower_cold_kernel(order, count_hbm, parent_hbm, x_hbm, basis_hbm, up_hbm, *refs):
    n = len(order)
    outs = refs[:n]
    g_ref, leaf_ref, count_ref, parent_ref, x_ref, basis_ref, up_ref, sems = refs[n:]
    boxes = basis_ref.shape[0]
    pairs, local = outs[0].shape[1:3]
    copies = {
        "x": pltpu.make_async_copy(x_hbm, x_ref, sems.at[0]),
        "count": pltpu.make_async_copy(count_hbm, count_ref, sems.at[1]),
        "parent": pltpu.make_async_copy(parent_hbm, parent_ref, sems.at[2]),
        "up": pltpu.make_async_copy(up_hbm, up_ref, sems.at[3]),
    }
    for b in range(boxes):
        copies[b] = pltpu.make_async_copy(basis_hbm.at[b], basis_ref.at[b], sems.at[4 + b])
    for name in ["x", 0, "count"] + list(range(1, boxes)) + ["up", "parent"]:
        copies[name].start()

    def ready(name):
        for other in {"start": ["x", "count"], "up": ["up", "parent"]}.get(name, [name]):
            copies[other].wait()

    jobs = [
        (out.at[which, p, h], p, target(k, which, h, local))
        for out, k in zip(outs, order)
        for which in range(2)
        for p in range(pairs)
        for h in range(local)
    ]
    lower_body(jobs, count_ref, parent_ref, x_ref, basis_ref, up_ref, g_ref, leaf_ref, ready)


def lower_warm_kernel(routes, count_ref, parent_ref, x_ref, basis_ref, up_ref, *refs):
    n = len(routes)
    outs = refs[:n]
    g_ref, leaf_ref = refs[n:]
    pairs, local = outs[0].shape[:2]
    jobs = [
        (out.at[p, h], p, target(k, which, h, local))
        for out, (k, which) in zip(outs, routes)
        for p in range(pairs)
        for h in range(local)
    ]
    lower_body(
        jobs, count_ref, parent_ref, x_ref, basis_ref, up_ref, g_ref, leaf_ref, lambda name: None
    )


def lower(order, cold, count, parents, x, basis, up):
    boxes, dirs, rows, leaf = basis.shape
    pairs, dirs_up, rank, _ = up.shape
    local = dirs_up // (2 * len(order))
    args = [count, parents, x, basis, up]
    smem = pl.BlockSpec(memory_space=pltpu.SMEM)
    vmem = pl.BlockSpec(memory_space=pltpu.VMEM)
    hbm = pl.BlockSpec(memory_space=pltpu.HBM)
    scratch = [
        pltpu.VMEM((boxes * dirs, 2, rows, NRHS), F32),
        pltpu.VMEM((pairs, dirs, 4 * rank, NRHS), BF16),
    ]
    if cold:
        scratch += [
            pltpu.SMEM(count.shape, jnp.int32),
            pltpu.SMEM(parents.shape, jnp.int32),
            pltpu.VMEM(x.shape, BF16),
            pltpu.VMEM(basis.shape, BF16),
            pltpu.VMEM(up.shape, BF16),
            pltpu.SemaphoreType.DMA((4 + boxes,)),
        ]
        kernel = functools.partial(lower_cold_kernel, order)
        blocks = [pltpu.VMEM((2, pairs, local, rank, NRHS), BF16)] * len(order)
        args = [pltpu.with_memory_space_constraint(arg, pltpu.HBM) for arg in args]
    else:
        routes = both_cores(order)
        kernel = functools.partial(lower_warm_kernel, routes)
        blocks = [pltpu.VMEM((pairs, local, rank, NRHS), BF16)] * len(routes)
    return pl.pallas_call(
        kernel,
        out_shape=blocks,
        in_specs=[hbm] * 5 if cold else [smem, smem, vmem, vmem, vmem],
        out_specs=[vmem] * len(blocks),
        scratch_shapes=scratch,
        compiler_params=pltpu.CompilerParams(
            vmem_limit_bytes=32 * 1024 * 1024
        ),
        cost_estimate=pl.CostEstimate(
            flops=1_000_000, bytes_accessed=10_000, transcendentals=0
        ),
        name="lower_cold" if cold else "lower_warm",
    )(*args)


def collect_kernel(first_ref, second_ref, *refs):
    ins, out_ref = refs[:-1], refs[-1]
    for i, ref in enumerate(ins):
        out_ref[i] = ref[1]


def collect(after, blocks):
    vmem = pl.BlockSpec(memory_space=pltpu.VMEM)
    return pl.pallas_call(
        collect_kernel,
        out_shape=jax.ShapeDtypeStruct((len(blocks),) + blocks[0].shape[1:], BF16),
        in_specs=[pl.BlockSpec(memory_space=pl.ANY)] * 2 + [vmem] * len(blocks),
        out_specs=vmem,
        name="collect",
    )(*after, *blocks)


def spread_mid(mid_ref, k, which, spread_ref):
    pairs, local, rank, _ = mid_ref.shape
    z = jnp.bitwise_xor(lax.axis_index("blk"), k)
    core = jnp.bitwise_xor(lax.axis_index("sub"), which)
    for p in range(pairs):
        source = (z * 2 + core) * pairs + p
        for h in range(local):
            mid = mid_ref[p, h]
            spread_ref[source, h, :rank] = mid
            spread_ref[source, h, rank:] = turn(mid.astype(F32)).astype(BF16)


def upper_half(perm_ref, spread_ref, down_ref, row_ref, h):
    groups = down_ref.shape[0]
    rank = spread_ref.shape[2] // 2
    tops = ([], [])
    for q in range(groups):
        parts = [spread_ref[perm_ref[2 * q + s], h] for s in range(2)]
        top = jnp.dot(
            down_ref[q, h], jnp.concatenate(parts, axis=0), preferred_element_type=F32
        )
        for t in range(2):
            piece = top[t * rank : (t + 1) * rank]
            tops[t].extend([piece.astype(BF16), turn(piece).astype(BF16)])
    results = []
    for t in range(2):
        rows = jnp.concatenate([row_ref[h, t, q] for q in range(groups)], axis=1)
        results.append(
            jnp.dot(rows, jnp.concatenate(tops[t], axis=0), preferred_element_type=F32)
        )
    return results


def upper_first_kernel(order, perm_ref, down_ref, row_ref, got_ref, *refs):
    n = len(order)
    mids, out_ref, spread_ref = refs[:n], refs[n], refs[n + 1]
    for i, k in enumerate(order):
        spread_mid(mids[i].at[0], k, 0, spread_ref)
        spread_mid(got_ref.at[i], k, 1, spread_ref)
    for h in range(out_ref.shape[0]):
        results = upper_half(perm_ref, spread_ref, down_ref, row_ref, h)
        for t in range(2):
            out_ref[h, t] = results[t].astype(BF16)


def upper_last_kernel(order, own_first, perm_ref, down_ref, row_ref, held_ref, *refs):
    routes = both_cores(order)
    n = len(routes)
    mids, out_ref, spread_ref, mix_ref = refs[:n], refs[n], refs[n + 1], refs[n + 2]
    leaf = held_ref.shape[2]
    for mid_ref, (k, which) in zip(mids, routes):
        spread_mid(mid_ref, k, which, spread_ref)
    if own_first:
        swap = lax.axis_index("rhs") == 1
    for h in range(out_ref.shape[0]):
        results = upper_half(perm_ref, spread_ref, down_ref, row_ref, h)
        for t in range(2):
            low = held_ref[h, t].astype(F32)
            high = results[t]
            if own_first:
                low, high = jnp.where(swap, high, low), jnp.where(swap, low, high)
            lane = lax.broadcasted_iota(jnp.int32, low.shape, 1)
            left = lane < HALF
            real = jnp.where(left, low, pltpu.roll(high, HALF, 1))
            imag = jnp.where(left, pltpu.roll(low, HALF, 1), high)
            mix_ref[h, t, pl.ds(0, leaf, stride=2), :] = real
            mix_ref[h, t, pl.ds(1, leaf, stride=2), :] = imag
            out_ref[h, t] = mix_ref[h, t].astype(BF16)


def upper(order, perm, mids, down, row, other, last, own_first):
    groups, local, _, width = down.shape
    leaf = row.shape[3]
    smem = pl.BlockSpec(memory_space=pltpu.SMEM)
    vmem = pl.BlockSpec(memory_space=pltpu.VMEM)
    spread = pltpu.VMEM((2 * groups, local, width // 2, NRHS), BF16)
    if last:
        kernel = functools.partial(upper_last_kernel, order, own_first)
        rows = 2 * leaf
        scratch = [spread, pltpu.VMEM((local, 2, rows, NRHS), F32)]
    else:
        kernel = functools.partial(upper_first_kernel, order)
        rows = leaf
        scratch = [spread]
    return pl.pallas_call(
        kernel,
        out_shape=jax.ShapeDtypeStruct((local, 2, rows, NRHS), BF16),
        in_specs=[smem] + [vmem] * (3 + len(mids)),
        out_specs=vmem,
        scratch_shapes=scratch,
        compiler_params=pltpu.CompilerParams(vmem_limit_bytes=32 * 1024 * 1024),
        cost_estimate=pl.CostEstimate(
            flops=1_000_000, bytes_accessed=10_000, transcendentals=0
        ),
        name="upper_last" if last else "upper_first",
    )(perm, down, row, other, *mids)


def along_blk(blocks, order):
    moved = []
    for block, k in zip(blocks, order):
        if k:
            block = lax.ppermute(block, "blk", [(m, m ^ k) for m in range(len(order))])
        moved.append(block)
    return moved


def direct(blocks, order):
    moved = []
    for block, (k, which) in zip(blocks, both_cores(order)):
        code = 2 * k + which
        if code:
            pairs = [(m, m ^ code) for m in range(2 * len(order))]
            block = lax.ppermute(block, ("blk", "sub"), pairs)
        moved.append(block)
    return moved


def on_device(
    columns, x_panels, leaf_basis, leaf_count, parent_map, up_transfer, mid_perm, down_transfer, row_basis
):
    boxes, directions, rank, _, leaf = leaf_basis.shape
    basis = leaf_basis.reshape(boxes, directions, rank * 2, leaf)
    groups, _, local = down_transfer.shape[:3]
    down = down_transfer.reshape(groups, local, 2 * rank, 4 * rank)
    row = row_basis.reshape(local, 2, groups, leaf, 2 * rank)
    flipped = jnp.transpose(x_panels, (0, 2, 3, 1))
    own_first = flipped.shape[2] == HALF
    order = tuple(range(columns - 1, -1, -1))
    swap = [(0, 1), (1, 0)]
    if own_first:
        first, second = flipped, flipped
    else:
        whole = lax.all_gather(flipped, "rhs", axis=2, tiled=True)
        first, second = whole[:, :, :HALF], whole[:, :, HALF:]
    first = first.reshape(boxes, 2 * HALF, leaf)
    blocks = lower(order, True, leaf_count, parent_map, first, basis, up_transfer)
    if own_first:
        blocks, second = lax.optimization_barrier((blocks, second))
        second = lax.ppermute(second, "rhs", swap)
    moved = along_blk(blocks, order)
    second = second.reshape(boxes, 2 * HALF, leaf)
    blocks = lower(order, False, leaf_count, parent_map, second, basis, up_transfer)
    blocks = direct(blocks, order)
    got = lax.ppermute(collect(blocks[:2], moved), "sub", swap)
    held = upper(order, mid_perm, moved, down, row, got, False, own_first)
    result = upper(order, mid_perm, blocks, down, row, held, True, own_first)
    return result.reshape(1, local, 2, leaf, 2, NRHS)


def solution(mesh):
    return jax.shard_map(
        functools.partial(on_device, mesh.shape["blk"]),
        mesh=mesh,
        in_specs=(
            P(("grp", "blk", "sub"), None, None, "rhs"),
            P(("blk", "sub"), "rhs", None, None, None),
            P(("blk", "sub")),
            P("rhs"),
            P(("blk", "sub"), "rhs", None, None),
            P(),
            P(None, "rhs", ("blk", "sub"), None, None, None),
            P("rhs", ("blk", "sub"), None, None, None, None),
        ),
        out_specs=P(("grp", "rhs"), ("blk", "sub"), None, None, None, None),
        check_vma=False,
    )
```

time: 41.3 us -> 41.3 us (level)
  starting transfers between devices: 19.1 us -> 16 us
  Pallas kernels: 9.78 us -> 12.1 us
  waiting for transfers between devices: 7.49 us -> 8.12 us
    ppermute x15 -> x12, starting transfers between devices: 19.1 us -> 16 us  [the longest x7 8.57 us: direct(): block = lax.ppermute(block, ('blk', 'sub'), pairs)]
    pallas_call x4 -> x5, Pallas kernels: 9.78 us -> 12.1 us  [the longest x2 5.48 us: upper(): pl.pallas_call(kernel, out_shape=jax.ShapeDtypeStruct((local, 2, rows, NR...]
    ppermute x15 -> x12, waiting for transfers between devices: 7.49 us -> 8.12 us  [the longest x3 8.1 us: along_blk(): block = lax.ppermute(block, 'blk', [(m, m ^ k) for m in range(len(order))])]
    unnamed x20 -> x40, local copies, waits for them, and re-layouts: 4.62 us -> 4.72 us
  transfers between devices with their start and end apart: 15 -> 12, of which waited for: 5 -> 1; matrix products, arithmetic and copies ran while one was open for 0% -> 0% of each run, Pallas kernels for 16% -> 10%
where the time goes in v3:
time: 41.3 us; the launch traced here: 41.2 us
  starting transfers between devices  16 us (39%)
  Pallas kernels  12.1 us (29%)
  waiting for transfers between devices  8.12 us (20%)
  local copies, waits for them, and re-layouts  4.72 us (11%)
    ppermute x7, starting transfers between devices, direct(): block = lax.ppermute(block, ('blk', 'sub'), pairs)  8.57 us
    ppermute x3, waiting for transfers between devices, along_blk(): block = lax.ppermute(block, 'blk', [(m, m ^ k) for m in range(len(order))])  8.1 us
    pallas_call x2, Pallas kernels, upper(): pl.pallas_call(kernel, out_shape=jax.ShapeDtypeStruct((local, 2, rows, NR...  5.48 us
    pallas_call x2, Pallas kernels, lower(): pl.pallas_call(kernel, out_shape=blocks, in_specs=[hbm] * 5 if cold else...  4.83 us
    unnamed x40, local copies, waits for them, and re-layouts  4.72 us
    ppermute x3, starting transfers between devices, along_blk(): block = lax.ppermute(block, 'blk', [(m, m ^ k) for m in range(len(order))])  4.39 us
    ppermute x1, starting transfers between devices, on_device(): second = lax.ppermute(second, 'rhs', swap)  3.01 us
    pallas_call x1, Pallas kernels, collect(): pl.pallas_call(collect_kernel, out_shape=jax.ShapeDtypeStruct((len(blocks...  1.81 us
  transfers between devices with their start and end apart: 12, of which 1 were waited for; matrix products, arithmetic and copies ran while one was open for 0% of the time, Pallas kernels for 10%

profile of v3, /device:TPU:0, one launch (start us, length us, event | category | flops | bytes accessed | tf_op | source)
XLA Modules:
  0.0 41.2 jit_solution(8583190261002015308)
XLA Ops:
  0.0 2.9 %lower_cold.1 = (bf16[2,1,4,64,128]{4,3,2,1,0:T(8,128)(2,1)S(1)}, bf16[2,1,4,64,128]{4,3,2,1,0:T(8,128)(2,1)S(1)}, bf16[2,1,4,64,128]{4,3,2,1,0:T(8,128)(2,1)S(1)}, bf16[2,1,4,64,128]{4,3,2,1,0:T(8,128)(2,1)S(1)}) custom-call(s32[2]{0:T(128)} %count_ref.1, s32[32]{0:T(128)} %parent_ref.1, bf16[2,128,128]{2,1,0:T(8,128)(2,1)} %bitcast.15, ...), custom_call_target="tpu_custom_call" | custom-call | flops 1000000 | bytes 10000 | tf_op jit(solution)/shard_map/lower_cold/pallas_call | solution.py:139
  2.9 0.0 copy-start.17
  2.9 0.0 copy-start.18
  2.9 3.0 %collective-permute-start = (bf16[2,2,64,128]{3,2,1,0:T(8,128)(2,1)S(1)}, bf16[2,2,64,128]{3,2,1,0:T(8,128)(2,1)S(1)}, u32[]{:S(2)}, u32[]{:S(2)}) collective-permute-start(bf16[2,2,64,128]{3,2,1,0:T(8,128)(2,1)S(1)} %bitcast.16), channel_id=1, source_target_pairs={{0,2},{2,0},{1,3},{3,1},{4,6},{6,4},{5,7},{7,5},{8,10},{10,8},{9,1... | collective-permute-start | bytes 196616 | tf_op jit(solution)/shard_map/ppermute | solution.py:311
  5.9 3.6 %collective-permute-start.3 = (bf16[2,1,4,64,128]{4,3,2,1,0:T(8,128)(2,1)S(1)}, bf16[2,1,4,64,128]{4,3,2,1,0:T(8,128)(2,1)S(1)}, u32[]{:S(2)}, u32[]{:S(2)}) collective-permute-start(bf16[2,1,4,64,128]{4,3,2,1,0:T(8,128)(2,1)S(1)} %get-tuple-element.29), channel_id=1, source_target_pairs={{0,12},{4,8},{8,4},{12,0},{1,13},{5,9},{9,5},{13,1},{2,14},{6,10},... | collective-permute-start | bytes 393224 | tf_op jit(solution)/shard_map/ppermute | solution.py:274
  9.5 0.0 collective-permute-start.4
  9.6 0.8 %collective-permute-start.5 = (bf16[2,1,4,64,128]{4,3,2,1,0:T(8,128)(2,1)S(1)}, bf16[2,1,4,64,128]{4,3,2,1,0:T(8,128)(2,1)S(1)}, u32[]{:S(2)}, u32[]{:S(2)}) collective-permute-start(bf16[2,1,4,64,128]{4,3,2,1,0:T(8,128)(2,1)S(1)} %get-tuple-element.31), channel_id=1, source_target_pairs={{0,4},{4,0},{8,12},{12,8},{1,5},{5,1},{9,13},{13,9},{2,6},{6,2},{1... | collective-permute-start | bytes 393224 | tf_op jit(solution)/shard_map/ppermute | solution.py:274
  10.3 0.0 collective-permute-done
  10.4 0.0 copy-start
  10.4 0.0 copy-start.1
  10.4 2.0 %lower_warm.1 = (bf16[1,4,64,128]{3,2,1,0:T(8,128)(2,1)S(1)}, bf16[1,4,64,128]{3,2,1,0:T(8,128)(2,1)S(1)}, bf16[1,4,64,128]{3,2,1,0:T(8,128)(2,1)S(1)}, bf16[1,4...) custom-call(s32[2]{0:T(128)S(1)} %copy-done.17, ...), custom_call_target="tpu_custom_call" | custom-call | flops 1000000 | bytes 10000 | tf_op jit(solution)/shard_map/lower_warm/pallas_call | solution.py:139
  12.4 3.7 %collective-permute-start.1 = (bf16[1,4,64,128]{3,2,1,0:T(8,128)(2,1)S(1)}, bf16[1,4,64,128]{3,2,1,0:T(8,128)(2,1)S(1)}, u32[]{:S(2)}, u32[]{:S(2)}) collective-permute-start(bf16[1,4,64,128]{3,2,1,0:T(8,128)(2,1)S(1)} %get-tuple-element.27), channel_id=1, source_target_pairs={{0,12},{1,13},{4,8},{5,9},{8,4},{9,5},{12,0},{13,1},{2,14},{3,15},... | collective-permute-start | bytes 196616 | tf_op jit(solution)/shard_map/ppermute | solution.py:285
  16.0 0.0 collective-permute-start.2
  16.0 0.0 collective-permute-done.3.refs_0_
  16.1 8.1 %collective-permute-done.4.refs_1_ = bf16[2,1,4,64,128]{4,3,2,1,0:T(8,128)(2,1)S(1)} collective-permute-done((bf16[2,1,4,64,128]{4,3,2,1,0:T(8,128)(2,1)S(1)}, bf16[2,1,4,64,128]{4,3,2,1,0:T(8,128)(2,1)S(1)}, u32[]{:S(2)}, u32[]{:S(2)}) %collective-permute-start.4) | collective-permute-done | bytes 131104 | tf_op jit(solution)/shard_map/ppermute | solution.py:274
  24.2 0.0 collective-permute-done.5.refs_2_
  24.2 0.6 %copy-done.8 = bf16[2,1,4,64,128]{4,3,2,1,0:T(8,128)(2,1)} copy-done((bf16[2,1,4,64,128]{4,3,2,1,0:T(8,128)(2,1)}, bf16[2,1,4,64,128]{4,3,2,1,0:T(8,128)(2,1)S(1)}, u32[]{:S(2)}) %copy-start.8) | copy-done | bytes 131096
  24.8 0.1 copy-done.10
  24.9 0.0 copy-done.12
  24.9 0.6 %copy-done.14 = bf16[1,4,64,128]{3,2,1,0:T(8,128)(2,1)} copy-done((bf16[1,4,64,128]{3,2,1,0:T(8,128)(2,1)}, bf16[1,4,64,128]{3,2,1,0:T(8,128)(2,1)S(1)}, u32[]{:S(2)}) %copy-start.14) | copy-done | bytes 65560
  25.5 1.8 %collect.1 = bf16[4,1,4,64,128]{4,3,2,1,0:T(8,128)(2,1)} custom-call(bf16[1,4,64,128]{3,2,1,0:T(8,128)(2,1)} %copy-done.12, bf16[1,4,64,128]{3,2,1,0:T(8,128)(2,1)} %copy-done.14, bf16[2,1,4,64,128]{4,3,2,1,0:T(8,128)(2,1)} %copy-done.6, bf16[2,1,4,64,128]{4,3,2,1,0:T(8,128)(2,1)} %copy-done.8, bf16[2,1,4,64,128]{4,3,2,1,0:T(8,128)(2,1)} %copy-done.10, ...), custom_call_target="tpu_custom_call" | custom-call | tf_op jit(solution)/shard_map/collect/pallas_call | solution.py:163
  27.3 2.6 %collective-permute-start.7 = (bf16[1,4,64,128]{3,2,1,0:T(8,128)(2,1)S(1)}, bf16[1,4,64,128]{3,2,1,0:T(8,128)(2,1)S(1)}, u32[]{:S(2)}, u32[]{:S(2)}) collective-permute-start(bf16[1,4,64,128]{3,2,1,0:T(8,128)(2,1)S(1)} %get-tuple-element.33), channel_id=1, source_target_pairs={{0,8},{1,9},{4,12},{5,13},{8,0},{9,1},{12,4},{13,5},{2,10},{3,11},... | collective-permute-start | bytes 196616 | tf_op jit(solution)/shard_map/ppermute | solution.py:285
  29.9 0.2 collective-permute-start.8
  30.1 1.6 %collective-permute-start.9 = (bf16[1,4,64,128]{3,2,1,0:T(8,128)(2,1)S(1)}, bf16[1,4,64,128]{3,2,1,0:T(8,128)(2,1)S(1)}, u32[]{:S(2)}, u32[]{:S(2)}) collective-permute-start(bf16[1,4,64,128]{3,2,1,0:T(8,128)(2,1)S(1)} %get-tuple-element.35), channel_id=1, source_target_pairs={{0,4},{1,5},{4,0},{5,1},{8,12},{9,13},{12,8},{13,9},{2,6},{3,7},{6... | collective-permute-start | bytes 196616 | tf_op jit(solution)/shard_map/ppermute | solution.py:285
  31.6 0.1 collective-permute-start.10
  31.7 0.5 %collective-permute-start.11 = (bf16[1,4,64,128]{3,2,1,0:T(8,128)(2,1)S(1)}, bf16[1,4,64,128]{3,2,1,0:T(8,128)(2,1)S(1)}, u32[]{:S(2)}, u32[]{:S(2)}) collective-permute-start(bf16[1,4,64,128]{3,2,1,0:T(8,128)(2,1)S(1)} %get-tuple-element.38), channel_id=1, source_target_pairs={{0,1},{1,0},{4,5},{5,4},{8,9},{9,8},{12,13},{13,12},{2,3},{3,2},{6... | collective-permute-start | bytes 196616 | tf_op jit(solution)/shard_map/ppermute | solution.py:285
  32.2 0.6 %copy-done.16 = s32[8]{0:T(128)S(1)} copy-done((s32[8]{0:T(128)S(1)}, s32[8]{0:T(128)}, u32[]{:S(2)}) %copy-start.16) | copy-done | bytes 56
  32.9 0.9 %copy-done.7 = bf16[2,1,4,64,128]{4,3,2,1,0:T(8,128)(2,1)S(1)} copy-done((bf16[2,1,4,64,128]{4,3,2,1,0:T(8,128)(2,1)S(1)}, bf16[2,1,4,64,128]{4,3,2,1,0:T(8,128)(2,1)}, u32[]{:S(2)}) %copy-start.7) | copy-done | bytes 131096
  33.8 0.9 %copy-done.9 = bf16[2,1,4,64,128]{4,3,2,1,0:T(8,128)(2,1)S(1)} copy-done((bf16[2,1,4,64,128]{4,3,2,1,0:T(8,128)(2,1)S(1)}, bf16[2,1,4,64,128]{4,3,2,1,0:T(8,128)(2,1)}, u32[]{:S(2)}) %copy-start.9) | copy-done | bytes 131096
  34.7 0.9 %copy-done.11 = bf16[2,1,4,64,128]{4,3,2,1,0:T(8,128)(2,1)S(1)} copy-done((bf16[2,1,4,64,128]{4,3,2,1,0:T(8,128)(2,1)S(1)}, bf16[2,1,4,64,128]{4,3,2,1,0:T(8,128)(2,1)}, u32[]{:S(2)}) %copy-start.11) | copy-done | bytes 131096
  35.6 2.3 %upper_first.1.held_ref = bf16[4,2,128,128]{3,2,1,0:T(8,128)(2,1)S(1)} custom-call(s32[8]{0:T(128)S(1)} %copy-done.16, bf16[4,4,128,256]{3,2,1,0:T(8,128)(2,1)S(1)} %bitcast.8, bf16[4,2,4,128,128]{4,3,2,1,0:T(8,128)(2,1)S(1)} %bitcast.10, bf16[4,1,4,64,128]{4,3,2,1,0:T(8,128)(2,1)S(1)} %collective-permute-done.6.got_ref, ...), custom_call_target="tpu_custom_call" | custom-call | flops 1000000 | bytes 10000 | tf_op jit(solution)/shard_map/upper_first/pallas_call | solution.py:256
  37.9 3.2 %upper_last.1 = bf16[4,2,256,128]{3,2,1,0:T(8,128)(2,1)} custom-call(s32[8]{0:T(128)S(1)} %copy-done.16, bf16[4,4,128,256]{3,2,1,0:T(8,128)(2,1)S(1)} %bitcast.9, bf16[4,2,4,128,128]{4,3,2,1,0:T(8,128)(2,1)S(1)} %bitcast.11, bf16[4,2,128,128]{3,2,1,0:T(8,128)(2,1)S(1)} %upper_first.1.held_ref, bf16[1,4,64,128]{3,2,1,0:T(8,128)(2,1)S(1)} %copy-done.13, ...), custom_call_target="tpu_custom_call" | custom-call | flops 1000000 | bytes 10000 | tf_op jit(solution)/shard_map/upper_last/pallas_call | solution.py:256
  (37 shorter events, 0.1 us)
Async XLA Ops:
  0.0 2.9 %copy-start.19 = (bf16[2,128,2,64]{1,3,2,0:T(8,128)(2,1)S(1)}, bf16[2,128,2,64]{1,3,2,0:T(8,128)(2,1)}, u32[]{:S(2)}) copy-start(bf16[2,128,2,64]{1,3,2,0:T(8,128)(2,1)} %param.8) | copy-start | bytes 196612
  0.0 10.3 %copy-start.2 = (bf16[2,16,64,2,128]{4,3,2,1,0:T(2,128)(2,1)S(1)}, bf16[2,16,64,2,128]{4,3,2,1,0:T(2,128)(2,1)}, u32[]{:S(2)}) copy-start(bf16[2,16,64,2,128]{4,3,2,1,0:T(2,128)(2,1)} %param.9) | copy-start | bytes 3145732
  0.0 10.3 %copy-start.3 = (bf16[1,32,64,256]{3,2,1,0:T(8,128)(2,1)S(1)}, bf16[1,32,64,256]{3,2,1,0:T(8,128)(2,1)}, u32[]{:S(2)}) copy-start(bf16[1,32,64,256]{3,2,1,0:T(8,128)(2,1)} %up_ref.1) | copy-start | bytes 3145732
  2.9 9.5 %copy-start.4 = (bf16[2,1,4,64,128]{4,3,2,1,0:T(8,128)(2,1)}, bf16[2,1,4,64,128]{4,3,2,1,0:T(8,128)(2,1)S(1)}, u32[]{:S(2)}) copy-start(bf16[2,1,4,64,128]{4,3,2,1,0:T(8,128)(2,1)S(1)} %get-tuple-element.32.refs_3_) | copy-start | bytes 393220
  2.9 7.4 %copy-start.17 = (s32[2]{0:T(128)S(1)}, s32[2]{0:T(128)}, u32[]{:S(2)}) copy-start(s32[2]{0:T(128)} %count_ref.1) | copy-start | bytes 28
  2.9 7.4 %copy-start.18 = (s32[32]{0:T(128)S(1)}, s32[32]{0:T(128)}, u32[]{:S(2)}) copy-start(s32[32]{0:T(128)} %parent_ref.1) | copy-start | bytes 388
  2.9 7.4 %collective-permute-start = (bf16[2,2,64,128]{3,2,1,0:T(8,128)(2,1)S(1)}, bf16[2,2,64,128]{3,2,1,0:T(8,128)(2,1)S(1)}, u32[]{:S(2)}, u32[]{:S(2)}) collective-permute-start(bf16[2,2,64,128]{3,2,1,0:T(8,128)(2,1)S(1)} %bitcast.16), channel_id=1, source_target_pairs={{0,2},{2,0},{1,3},{3,1},{4,6},{6,4},{5,7},{7,5},{8,10},{10,8},{9,1... | collective-permute-start | bytes 196616 | tf_op jit(solution)/shard_map/ppermute | solution.py:311
  5.9 10.1 %collective-permute-start.3 = (bf16[2,1,4,64,128]{4,3,2,1,0:T(8,128)(2,1)S(1)}, bf16[2,1,4,64,128]{4,3,2,1,0:T(8,128)(2,1)S(1)}, u32[]{:S(2)}, u32[]{:S(2)}) collective-permute-start(bf16[2,1,4,64,128]{4,3,2,1,0:T(8,128)(2,1)S(1)} %get-tuple-element.29), channel_id=1, source_target_pairs={{0,12},{4,8},{8,4},{12,0},{1,13},{5,9},{9,5},{13,1},{2,14},{6,10},... | collective-permute-start | bytes 393224 | tf_op jit(solution)/shard_map/ppermute | solution.py:274
  9.5 14.6 %collective-permute-start.4 = (bf16[2,1,4,64,128]{4,3,2,1,0:T(8,128)(2,1)S(1)}, bf16[2,1,4,64,128]{4,3,2,1,0:T(8,128)(2,1)S(1)}, u32[]{:S(2)}, u32[]{:S(2)}) collective-permute-start(bf16[2,1,4,64,128]{4,3,2,1,0:T(8,128)(2,1)S(1)} %get-tuple-element.30), channel_id=1, source_target_pairs={{0,8},{4,12},{8,0},{12,4},{1,9},{5,13},{9,1},{13,5},{2,10},{6,14},... | collective-permute-start | bytes 393224 | tf_op jit(solution)/shard_map/ppermute | solution.py:274
  9.6 14.6 %collective-permute-start.5 = (bf16[2,1,4,64,128]{4,3,2,1,0:T(8,128)(2,1)S(1)}, bf16[2,1,4,64,128]{4,3,2,1,0:T(8,128)(2,1)S(1)}, u32[]{:S(2)}, u32[]{:S(2)}) collective-permute-start(bf16[2,1,4,64,128]{4,3,2,1,0:T(8,128)(2,1)S(1)} %get-tuple-element.31), channel_id=1, source_target_pairs={{0,4},{4,0},{8,12},{12,8},{1,5},{5,1},{9,13},{13,9},{2,6},{6,2},{1... | collective-permute-start | bytes 393224 | tf_op jit(solution)/shard_map/ppermute | solution.py:274
  10.4 21.9 %copy-start = (bf16[4,1,4,2,64,256]{5,4,3,2,1,0:T(8,128)(2,1)S(1)}, bf16[4,1,4,2,64,256]{5,4,3,2,1,0:T(8,128)(2,1)}, u32[]{:S(2)}) copy-start(bf16[4,1,4,2,64,256]{5,4,3,2,1,0:T(8,128)(2,1)} %param.14) | copy-start | bytes 3145732
  10.4 21.8 %copy-start.1 = (bf16[1,4,2,4,128,128]{5,4,3,2,1,0:T(8,128)(2,1)S(1)}, bf16[1,4,2,4,128,128]{5,4,3,2,1,0:T(8,128)(2,1)}, u32[]{:S(2)}) copy-start(bf16[1,4,2,4,128,128]{5,4,3,2,1,0:T(8,128)(2,1)} %param.15) | copy-start | bytes 3145732
  12.4 11.8 %collective-permute-start.1 = (bf16[1,4,64,128]{3,2,1,0:T(8,128)(2,1)S(1)}, bf16[1,4,64,128]{3,2,1,0:T(8,128)(2,1)S(1)}, u32[]{:S(2)}, u32[]{:S(2)}) collective-permute-start(bf16[1,4,64,128]{3,2,1,0:T(8,128)(2,1)S(1)} %get-tuple-element.27), channel_id=1, source_target_pairs={{0,12},{1,13},{4,8},{5,9},{8,4},{9,5},{12,0},{13,1},{2,14},{3,15},... | collective-permute-start | bytes 196616 | tf_op jit(solution)/shard_map/ppermute | solution.py:285
  16.0 16.2 %copy-start.5 = (bf16[2,1,4,64,128]{4,3,2,1,0:T(8,128)(2,1)S(1)}, bf16[2,1,4,64,128]{4,3,2,1,0:T(8,128)(2,1)}, u32[]{:S(2)}) copy-start(bf16[2,1,4,64,128]{4,3,2,1,0:T(8,128)(2,1)} %copy-done.4) | copy-start | bytes 393220
  16.0 8.1 %collective-permute-start.2 = (bf16[1,4,64,128]{3,2,1,0:T(8,128)(2,1)S(1)}, bf16[1,4,64,128]{3,2,1,0:T(8,128)(2,1)S(1)}, u32[]{:S(2)}, u32[]{:S(2)}) collective-permute-start(bf16[1,4,64,128]{3,2,1,0:T(8,128)(2,1)S(1)} %get-tuple-element.28), channel_id=1, source_target_pairs={{0,13},{1,12},{4,9},{5,8},{8,5},{9,4},{12,1},{13,0},{2,15},{3,14},... | collective-permute-start | bytes 196616 | tf_op jit(solution)/shard_map/ppermute | solution.py:285
  16.0 8.1 %copy-start.6 = (bf16[2,1,4,64,128]{4,3,2,1,0:T(8,128)(2,1)}, bf16[2,1,4,64,128]{4,3,2,1,0:T(8,128)(2,1)S(1)}, u32[]{:S(2)}) copy-start(bf16[2,1,4,64,128]{4,3,2,1,0:T(8,128)(2,1)S(1)} %collective-permute-done.3.refs_0_) | copy-start | bytes 393220
  24.2 0.6 %copy-start.8 = (bf16[2,1,4,64,128]{4,3,2,1,0:T(8,128)(2,1)}, bf16[2,1,4,64,128]{4,3,2,1,0:T(8,128)(2,1)S(1)}, u32[]{:S(2)}) copy-start(bf16[2,1,4,64,128]{4,3,2,1,0:T(8,128)(2,1)S(1)} %collective-permute-done.4.refs_1_) | copy-start | bytes 393220
  24.2 0.7 %copy-start.10 = (bf16[2,1,4,64,128]{4,3,2,1,0:T(8,128)(2,1)}, bf16[2,1,4,64,128]{4,3,2,1,0:T(8,128)(2,1)S(1)}, u32[]{:S(2)}) copy-start(bf16[2,1,4,64,128]{4,3,2,1,0:T(8,128)(2,1)S(1)} %collective-permute-done.5.refs_2_) | copy-start | bytes 393220
  24.2 0.7 %copy-start.12 = (bf16[1,4,64,128]{3,2,1,0:T(8,128)(2,1)}, bf16[1,4,64,128]{3,2,1,0:T(8,128)(2,1)S(1)}, u32[]{:S(2)}) copy-start(bf16[1,4,64,128]{3,2,1,0:T(8,128)(2,1)S(1)} %collective-permute-done.1.first_ref.refs_0_) | copy-start | bytes 196612
  24.9 0.6 %copy-start.14 = (bf16[1,4,64,128]{3,2,1,0:T(8,128)(2,1)}, bf16[1,4,64,128]{3,2,1,0:T(8,128)(2,1)S(1)}, u32[]{:S(2)}) copy-start(bf16[1,4,64,128]{3,2,1,0:T(8,128)(2,1)S(1)} %collective-permute-done.2.second_ref.refs_1_) | copy-start | bytes 196612
  27.3 4.4 %collective-permute-start.6 = (bf16[4,1,4,64,128]{4,3,2,1,0:T(8,128)(2,1)}, bf16[4,1,4,64,128]{4,3,2,1,0:T(8,128)(2,1)S(1)}, u32[]{:S(2)}, u32[]{:S(2)}) collective-permute-start(bf16[4,1,4,64,128]{4,3,2,1,0:T(8,128)(2,1)} %collect.1), channel_id=1, source_target_pairs={{0,1},{1,0},{2,3},{3,2},{4,5},{5,4},{6,7},{7,6},{8,9},{9,8},{10,11... | collective-permute-start | bytes 786440 | tf_op jit(solution)/shard_map/ppermute | solution.py:316
  27.3 10.5 %collective-permute-start.7 = (bf16[1,4,64,128]{3,2,1,0:T(8,128)(2,1)S(1)}, bf16[1,4,64,128]{3,2,1,0:T(8,128)(2,1)S(1)}, u32[]{:S(2)}, u32[]{:S(2)}) collective-permute-start(bf16[1,4,64,128]{3,2,1,0:T(8,128)(2,1)S(1)} %get-tuple-element.33), channel_id=1, source_target_pairs={{0,8},{1,9},{4,12},{5,13},{8,0},{9,1},{12,4},{13,5},{2,10},{3,11},... | collective-permute-start | bytes 196616 | tf_op jit(solution)/shard_map/ppermute | solution.py:285
  29.9 8.0 %collective-permute-start.8 = (bf16[1,4,64,128]{3,2,1,0:T(8,128)(2,1)S(1)}, bf16[1,4,64,128]{3,2,1,0:T(8,128)(2,1)S(1)}, u32[]{:S(2)}, u32[]{:S(2)}) collective-permute-start(bf16[1,4,64,128]{3,2,1,0:T(8,128)(2,1)S(1)} %get-tuple-element.34), channel_id=1, source_target_pairs={{0,9},{1,8},{4,13},{5,12},{8,1},{9,0},{12,5},{13,4},{2,11},{3,10},... | collective-permute-start | bytes 196616 | tf_op jit(solution)/shard_map/ppermute | solution.py:285
  30.1 7.8 %collective-permute-start.9 = (bf16[1,4,64,128]{3,2,1,0:T(8,128)(2,1)S(1)}, bf16[1,4,64,128]{3,2,1,0:T(8,128)(2,1)S(1)}, u32[]{:S(2)}, u32[]{:S(2)}) collective-permute-start(bf16[1,4,64,128]{3,2,1,0:T(8,128)(2,1)S(1)} %get-tuple-element.35), channel_id=1, source_target_pairs={{0,4},{1,5},{4,0},{5,1},{8,12},{9,13},{12,8},{13,9},{2,6},{3,7},{6... | collective-permute-start | bytes 196616 | tf_op jit(solution)/shard_map/ppermute | solution.py:285
  31.6 6.2 %collective-permute-start.10 = (bf16[1,4,64,128]{3,2,1,0:T(8,128)(2,1)S(1)}, bf16[1,4,64,128]{3,2,1,0:T(8,128)(2,1)S(1)}, u32[]{:S(2)}, u32[]{:S(2)}) collective-permute-start(bf16[1,4,64,128]{3,2,1,0:T(8,128)(2,1)S(1)} %get-tuple-element.36), channel_id=1, source_target_pairs={{0,5},{1,4},{4,1},{5,0},{8,13},{9,12},{12,9},{13,8},{2,7},{3,6},{6... | collective-permute-start | bytes 196616 | tf_op jit(solution)/shard_map/ppermute | solution.py:285
  31.7 6.2 %collective-permute-start.11 = (bf16[1,4,64,128]{3,2,1,0:T(8,128)(2,1)S(1)}, bf16[1,4,64,128]{3,2,1,0:T(8,128)(2,1)S(1)}, u32[]{:S(2)}, u32[]{:S(2)}) collective-permute-start(bf16[1,4,64,128]{3,2,1,0:T(8,128)(2,1)S(1)} %get-tuple-element.38), channel_id=1, source_target_pairs={{0,1},{1,0},{4,5},{5,4},{8,9},{9,8},{12,13},{13,12},{2,3},{3,2},{6... | collective-permute-start | bytes 196616 | tf_op jit(solution)/shard_map/ppermute | solution.py:285
  32.2 0.7 %copy-start.16 = (s32[8]{0:T(128)S(1)}, s32[8]{0:T(128)}, u32[]{:S(2)}) copy-start(s32[8]{0:T(128)} %perm_ref.3) | copy-start | bytes 100
  32.9 0.9 %copy-start.7 = (bf16[2,1,4,64,128]{4,3,2,1,0:T(8,128)(2,1)S(1)}, bf16[2,1,4,64,128]{4,3,2,1,0:T(8,128)(2,1)}, u32[]{:S(2)}) copy-start(bf16[2,1,4,64,128]{4,3,2,1,0:T(8,128)(2,1)} %copy-done.6) | copy-start | bytes 393220
  33.8 0.9 %copy-start.9 = (bf16[2,1,4,64,128]{4,3,2,1,0:T(8,128)(2,1)S(1)}, bf16[2,1,4,64,128]{4,3,2,1,0:T(8,128)(2,1)}, u32[]{:S(2)}) copy-start(bf16[2,1,4,64,128]{4,3,2,1,0:T(8,128)(2,1)} %copy-done.8) | copy-start | bytes 393220
  34.7 0.9 %copy-start.11 = (bf16[2,1,4,64,128]{4,3,2,1,0:T(8,128)(2,1)S(1)}, bf16[2,1,4,64,128]{4,3,2,1,0:T(8,128)(2,1)}, u32[]{:S(2)}) copy-start(bf16[2,1,4,64,128]{4,3,2,1,0:T(8,128)(2,1)} %copy-done.10) | copy-start | bytes 393220
  35.6 2.3 %copy-start.13 = (bf16[1,4,64,128]{3,2,1,0:T(8,128)(2,1)S(1)}, bf16[1,4,64,128]{3,2,1,0:T(8,128)(2,1)}, u32[]{:S(2)}) copy-start(bf16[1,4,64,128]{3,2,1,0:T(8,128)(2,1)} %copy-done.12) | copy-start | bytes 196612
  35.6 2.3 %copy-start.15 = (bf16[1,4,64,128]{3,2,1,0:T(8,128)(2,1)S(1)}, bf16[1,4,64,128]{3,2,1,0:T(8,128)(2,1)}, u32[]{:S(2)}) copy-start(bf16[1,4,64,128]{3,2,1,0:T(8,128)(2,1)} %copy-done.14) | copy-start | bytes 196612

commit v4 on v0

v4 whole, which is shorter than its diff:
```python
import functools

import jax
import jax.numpy as jnp
from jax import lax
from jax.experimental import pallas as pl
from jax.experimental.pallas import tpu as pltpu
from jax.sharding import PartitionSpec as P

NRHS = 128
F32 = jnp.float32
BF16 = jnp.bfloat16
PARAMS = pltpu.CompilerParams(vmem_limit_bytes=32 * 1024 * 1024)
COST = pl.CostEstimate(flops=1_000_000, bytes_accessed=10_000, transcendentals=0)


def both_cores(steps):
    return [(k, which) for k in steps for which in (0, 1)]


def partner(k, which):
    z = jnp.bitwise_xor(lax.axis_index("blk"), k)
    core = jnp.bitwise_xor(lax.axis_index("sub"), which)
    return z * 2 + core


def load_kernel(basis_hbm, up_hbm, basis_ref, up_ref, sems):
    copies = [
        pltpu.make_async_copy(basis_hbm, basis_ref, sems.at[0]),
        pltpu.make_async_copy(up_hbm, up_ref, sems.at[1]),
    ]
    for copy in copies:
        copy.start()
    for copy in copies:
        copy.wait()


def load(*arrays):
    return pl.pallas_call(
        load_kernel,
        out_shape=[pltpu.VMEM(array.shape, array.dtype) for array in arrays],
        in_specs=[pl.BlockSpec(memory_space=pltpu.HBM)] * len(arrays),
        out_specs=[pl.BlockSpec(memory_space=pltpu.VMEM)] * len(arrays),
        scratch_shapes=[pltpu.SemaphoreType.DMA((len(arrays),))],
        compiler_params=PARAMS,
        cost_estimate=COST,
        name="load",
    )(*[pltpu.with_memory_space_constraint(array, pltpu.HBM) for array in arrays])


def up_stage(outs, routes, parent_ref, up_ref, leaf_ref):
    pairs, local = outs[0].shape[:2]
    for out, (k, which) in zip(outs, routes):
        dest = partner(k, which)
        for p in range(pairs):
            for h in range(local):
                j = dest * local + h
                mid = jnp.dot(
                    up_ref[p, j], leaf_ref[p, parent_ref[j]], preferred_element_type=F32
                )
                out[p, h] = mid.astype(BF16)


def lower_kernel(routes, count_ref, parent_ref, *refs):
    n = len(routes)
    xs, (basis_ref, up_ref) = refs[: -n - 4], refs[-n - 4 : -n - 2]
    outs, leaf_ref, g_ref = refs[-n - 2 : -2], refs[-2], refs[-1]
    boxes, dirs, rows, _ = basis_ref.shape
    rank = rows // 2
    first = lax.axis_index("rhs") * dirs
    even = pl.ds(0, rank, stride=2)
    odd = pl.ds(1, rank, stride=2)
    for b in range(boxes):
        if len(xs) == 2:
            own, other = xs[0][b], xs[1][b]
            swap = lax.axis_index("rhs") == 1
            low, high = jnp.where(swap, other, own), jnp.where(swap, own, other)
            spread = jnp.concatenate([low[0], high[0], low[1], high[1]], axis=0)
        else:
            spread = jnp.concatenate([xs[0][b, 0], xs[0][b, 1]], axis=0)
        for d in range(dirs):
            slot = b * dirs + d
            g = lax.dot_general(
                basis_ref[b, d], spread, (((1,), (1,)), ((), ())), preferred_element_type=F32
            )
            g_ref[slot, 0] = g[:, :NRHS]
            g_ref[slot, 1] = g[:, NRHS:]
            real = g_ref[slot, 0, even, :] - g_ref[slot, 1, odd, :]
            imag = g_ref[slot, 1, even, :] + g_ref[slot, 0, odd, :]
            live = first + d < count_ref[b]
            real = jnp.where(live, real, jnp.zeros_like(real)).astype(BF16)
            imag = jnp.where(live, imag, jnp.zeros_like(imag)).astype(BF16)
            base = (b % 2) * 2 * rank
            leaf_ref[b // 2, d, base : base + rank, :NRHS] = real
            leaf_ref[b // 2, d, base : base + rank, NRHS:] = imag
            leaf_ref[b // 2, d, base + rank : base + 2 * rank, :NRHS] = -imag
            leaf_ref[b // 2, d, base + rank : base + 2 * rank, NRHS:] = real
    up_stage(outs, routes, parent_ref, up_ref, leaf_ref)


def lower(routes, dests, count, parents, xs, basis, up):
    boxes, dirs, rows, _ = basis.shape
    pairs, dirs_up, rank, _ = up.shape
    block = pltpu.VMEM((pairs, dirs_up // dests, rank, 2 * NRHS), BF16)
    smem = pl.BlockSpec(memory_space=pltpu.SMEM)
    vmem = pl.BlockSpec(memory_space=pltpu.VMEM)
    return pl.pallas_call(
        functools.partial(lower_kernel, routes),
        out_shape=[block] * len(routes) + [pltpu.VMEM((pairs, dirs, 4 * rank, 2 * NRHS), BF16)],
        in_specs=[smem, smem] + [vmem] * (2 + len(xs)),
        out_specs=[vmem] * (len(routes) + 1),
        scratch_shapes=[pltpu.VMEM((boxes * dirs, 2, rows, NRHS), F32)],
        compiler_params=PARAMS,
        cost_estimate=COST,
        name="lower",
    )(count, parents, *xs, basis, up)


def rest_kernel(routes, parent_ref, up_ref, leaf_ref, *outs):
    up_stage(outs, routes, parent_ref, up_ref, leaf_ref)


def rest(routes, dests, parents, up, leaf):
    pairs, dirs_up, rank, _ = up.shape
    block = pltpu.VMEM((pairs, dirs_up // dests, rank, 2 * NRHS), BF16)
    smem = pl.BlockSpec(memory_space=pltpu.SMEM)
    vmem = pl.BlockSpec(memory_space=pltpu.VMEM)
    return pl.pallas_call(
        functools.partial(rest_kernel, routes),
        out_shape=[block] * len(routes),
        in_specs=[smem, vmem, vmem],
        out_specs=[vmem] * len(routes),
        compiler_params=PARAMS,
        cost_estimate=COST,
        name="rest",
    )(parents, up, leaf)


def upper_kernel(routes, perm_hbm, down_ref, row_ref, *refs):
    n = len(routes)
    mids = refs[:n]
    out_hbm, spread_ref, mix_ref, out_ref, perm_ref, sems = refs[n:]
    groups, local = down_ref.shape[:2]
    rank = spread_ref.shape[2] // 2
    leaf = row_ref.shape[3]
    fetch = pltpu.make_async_copy(perm_hbm, perm_ref, sems.at[local])
    fetch.start()
    for mid_ref, (k, which) in zip(mids, routes):
        pairs = mid_ref.shape[0]
        for p in range(pairs):
            source = partner(k, which) * pairs + p
            for h in range(local):
                mid = mid_ref[p, h]
                spread_ref[source, h, :rank] = mid
                spread_ref[source, h, rank:, :NRHS] = -mid[:, NRHS:]
                spread_ref[source, h, rank:, NRHS:] = mid[:, :NRHS]
    fetch.wait()
    copies = []
    for h in range(local):
        tops = ([], [])
        for q in range(groups):
            parts = [spread_ref[perm_ref[2 * q + s], h] for s in range(2)]
            top = jnp.dot(
                down_ref[q, h], jnp.concatenate(parts, axis=0), preferred_element_type=F32
            ).astype(BF16)
            for t in range(2):
                piece = top[t * rank : (t + 1) * rank]
                tops[t].append(piece)
                tops[t].append(jnp.concatenate([-piece[:, NRHS:], piece[:, :NRHS]], axis=1))
        for t in range(2):
            rows = jnp.concatenate([row_ref[h, t, q] for q in range(groups)], axis=1)
            field = jnp.dot(rows, jnp.concatenate(tops[t], axis=0), preferred_element_type=F32)
            mix_ref[h, t, pl.ds(0, leaf, stride=2), :] = field[:, :NRHS]
            mix_ref[h, t, pl.ds(1, leaf, stride=2), :] = field[:, NRHS:]
            out_ref[h, t] = mix_ref[h, t].astype(BF16)
        copies.append(pltpu.make_async_copy(out_ref.at[h], out_hbm.at[h], sems.at[h]))
        copies[-1].start()
    for copy in copies:
        copy.wait()


def upper(routes, perm, down, row, mids):
    groups, local, _, width = down.shape
    leaf = row.shape[3]
    vmem = pl.BlockSpec(memory_space=pltpu.VMEM)
    hbm = pl.BlockSpec(memory_space=pltpu.HBM)
    shape = (local, 2, 2 * leaf, NRHS)
    return pl.pallas_call(
        functools.partial(upper_kernel, routes),
        out_shape=jax.ShapeDtypeStruct(shape, BF16),
        in_specs=[hbm] + [vmem] * (2 + len(mids)),
        out_specs=hbm,
        scratch_shapes=[
            pltpu.VMEM((2 * groups, local, width // 2, 2 * NRHS), BF16),
            pltpu.VMEM(shape, F32),
            pltpu.VMEM(shape, BF16),
            pltpu.SMEM(perm.shape, jnp.int32),
            pltpu.SemaphoreType.DMA((local + 1,)),
        ],
        compiler_params=PARAMS,
        cost_estimate=COST,
        name="upper",
    )(pltpu.with_memory_space_constraint(perm, pltpu.HBM), down, row, *mids)


def send(block, route, dests):
    code = 2 * route[0] + route[1]
    if not code:
        return block
    return lax.ppermute(block, ("blk", "sub"), [(m, m ^ code) for m in range(dests)])


def on_device(
    columns, x_panels, leaf_basis, leaf_count, parent_map, up_transfer, mid_perm, down_transfer, row_basis
):
    boxes, directions, rank, _, leaf = leaf_basis.shape
    basis = leaf_basis.reshape(boxes, directions, rank * 2, leaf)
    groups, _, local = down_transfer.shape[:3]
    down = down_transfer.reshape(groups, local, 2 * rank, 4 * rank)
    row = row_basis.reshape(local, 2, groups, leaf, 2 * rank)
    x = jnp.transpose(x_panels, (0, 2, 3, 1))
    if 2 * x.shape[2] == NRHS:
        xs = [x, lax.ppermute(x, "rhs", [(0, 1), (1, 0)])]
    else:
        xs = [lax.all_gather(x, "rhs", axis=2, tiled=True)]
    basis, up = load(basis, up_transfer)
    dests = 2 * columns
    routes = both_cores(range(columns - 1, -1, -1))
    *early, leaf_coef = lower(routes[:2], dests, leaf_count, parent_map, xs, basis, up)
    late = rest(routes[2:], dests, parent_map, up, leaf_coef)
    mids = [send(block, route, dests) for block, route in zip([*early, *late], routes)]
    result = upper(routes, mid_perm, down, row, mids)
    return result.reshape(1, local, 2, leaf, 2, NRHS)


def solution(mesh):
    return jax.shard_map(
        functools.partial(on_device, mesh.shape["blk"]),
        mesh=mesh,
        in_specs=(
            P(("grp", "blk", "sub"), None, None, "rhs"),
            P(("blk", "sub"), "rhs", None, None, None),
            P(("blk", "sub")),
            P("rhs"),
            P(("blk", "sub"), "rhs", None, None),
            P(),
            P(None, "rhs", ("blk", "sub"), None, None, None),
            P("rhs", ("blk", "sub"), None, None, None, None),
        ),
        out_specs=P(("grp", "rhs"), ("blk", "sub"), None, None, None, None),
        check_vma=False,
    )
```

time: 116 us -> 36 us (0.31)
  the two profiles are of different devices: /device:TPU:0 before, /device:TPU:1 now
where the time goes in v4:
time: 36 us; the launch traced here: 35.8 us
  starting transfers between devices  20.5 us (57%)
  waiting for transfers between devices  7.91 us (22%)
  Pallas kernels  7.3 us (20%)
    ppermute x7, starting transfers between devices, send(): lax.ppermute(block, ('blk', 'sub'), [(m, m ^ code) for m in range(dests)])  18.4 us
    ppermute x7, waiting for transfers between devices, send(): lax.ppermute(block, ('blk', 'sub'), [(m, m ^ code) for m in range(dests)])  7.61 us
    pallas_call x1, Pallas kernels, upper(): pl.pallas_call(functools.partial(upper_kernel, routes), out_shape=jax.Sha...  2.65 us
    ppermute x1, starting transfers between devices, on_device(): xs = [x, lax.ppermute(x, 'rhs', [(0, 1), (1, 0)])]  2.11 us
    pallas_call x1, Pallas kernels, lower(): pl.pallas_call(functools.partial(lower_kernel, routes), out_shape=[block]...  1.88 us
    pallas_call x1, Pallas kernels, load(): pl.pallas_call(load_kernel, out_shape=[pltpu.VMEM(array.shape, array.dtyp...  1.56 us
    pallas_call x1, Pallas kernels, rest(): pl.pallas_call(functools.partial(rest_kernel, routes), out_shape=[block]...  1.21 us
  transfers between devices with their start and end apart: 8, of which 4 were waited for; matrix products, arithmetic and copies ran while one was open for 0% of the time, Pallas kernels for 8%

profile of v4, /device:TPU:1, one launch (start us, length us, event | category | flops | bytes accessed | tf_op | source)
XLA Modules:
  0.0 35.8 jit_solution(10125361825026758415)
XLA Ops:
  0.0 0.0 copy-start.2
  0.0 0.0 copy-start.3
  0.0 0.0 copy-start.4
  0.0 2.1 %collective-permute-start = (bf16[2,2,64,128]{3,2,1,0:T(8,128)(2,1)}, bf16[2,2,64,128]{3,2,1,0:T(8,128)(2,1)S(1)}, u32[]{:S(2)}, u32[]{:S(2)}) collective-permute-start(bf16[2,2,64,128]{3,2,1,0:T(8,128)(2,1)} %bitcast.7), channel_id=1, source_target_pairs={{0,2},{2,0},{1,3},{3,1},{4,6},{6,4},{5,7},{7,5},{8,10},{10,8},{9,1... | collective-permute-start | bytes 196616 | tf_op jit(solution)/shard_map/ppermute | solution.py:223
  2.1 1.6 %load.1 = (bf16[2,16,128,128]{3,2,1,0:T(8,128)(2,1)S(1)}, bf16[1,32,64,256]{3,2,1,0:T(8,128)(2,1)S(1)}) custom-call(bf16[2,16,128,128]{3,2,1,0:T(8,128)(2,1)} %bitcast.9, bf16[1,32,64,256]{3,2,1,0:T(8,128)(2,1)} %up_hbm.1), custom_call_target="tpu_custom_call" | custom-call | flops 1000000 | bytes 10000 | tf_op jit(solution)/shard_map/load/pallas_call | solution.py:39
  3.7 0.3 collective-permute-done.refs_1_
  4.0 0.0 copy-done.2
  4.0 0.0 copy-done.3
  4.0 0.0 copy-done.4
  4.0 1.9 %lower.1 = (bf16[1,4,64,256]{3,2,1,0:T(8,128)(2,1)S(1)}, bf16[1,4,64,256]{3,2,1,0:T(8,128)(2,1)S(1)}, bf16[1,16,256,256]{3,2,1,0:T(8,128)(2,1)S(1)}) custom-call(s32[2]{0:T(128)S(1)} %copy-done.4, s32[32]{0:T(128)S(1)} %copy-done.3, bf16[2,2,64,128]{3,2,1,0:T(8,128)(2,1)S(1)} %bitcast.8, bf16[2,2,64,128]{3,2,1,0:T(8,128)(2,1)S(1)} %collective-permute-done.refs_1_, ...), custom_call_target="tpu_custom_call" | custom-call | flops 1000000 | bytes 10000 | tf_op jit(solution)/shard_map/lower/pallas_call | solution.py:107
  5.9 0.0 copy-start
  5.9 0.0 copy-start.1
  5.9 3.6 %collective-permute-start.1 = (bf16[1,4,64,256]{3,2,1,0:T(8,128)(2,1)S(1)}, bf16[1,4,64,256]{3,2,1,0:T(8,128)(2,1)S(1)}, u32[]{:S(2)}, u32[]{:S(2)}) collective-permute-start(bf16[1,4,64,256]{3,2,1,0:T(8,128)(2,1)S(1)} %get-tuple-element.18), channel_id=1, source_target_pairs={{0,12},{1,13},{4,8},{5,9},{8,4},{9,5},{12,0},{13,1},{2,14},{3,15},... | collective-permute-start | bytes 393224 | tf_op jit(solution)/shard_map/ppermute | solution.py:210
  9.5 1.8 %collective-permute-start.2 = (bf16[1,4,64,256]{3,2,1,0:T(8,128)(2,1)S(1)}, bf16[1,4,64,256]{3,2,1,0:T(8,128)(2,1)S(1)}, u32[]{:S(2)}, u32[]{:S(2)}) collective-permute-start(bf16[1,4,64,256]{3,2,1,0:T(8,128)(2,1)S(1)} %get-tuple-element.19), channel_id=1, source_target_pairs={{0,13},{1,12},{4,9},{5,8},{8,5},{9,4},{12,1},{13,0},{2,15},{3,14},... | collective-permute-start | bytes 393224 | tf_op jit(solution)/shard_map/ppermute | solution.py:210
  11.3 1.2 %rest.1 = (bf16[1,4,64,256]{3,2,1,0:T(8,128)(2,1)S(1)}, bf16[1,4,64,256]{3,2,1,0:T(8,128)(2,1)S(1)}, bf16[1,4,64,256]{3,2,1,0:T(8,128)(2,1)S(1)}, bf16[1,4,64,25...) custom-call(s32[32]{0:T(128)S(1)} %copy-done.3, ...), custom_call_target="tpu_custom_call" | custom-call | flops 1000000 | bytes 10000 | tf_op jit(solution)/shard_map/rest/pallas_call | solution.py:128
  12.5 0.7 %collective-permute-start.3 = (bf16[1,4,64,256]{3,2,1,0:T(8,128)(2,1)S(1)}, bf16[1,4,64,256]{3,2,1,0:T(8,128)(2,1)S(1)}, u32[]{:S(2)}, u32[]{:S(2)}) collective-permute-start(bf16[1,4,64,256]{3,2,1,0:T(8,128)(2,1)S(1)} %get-tuple-element.21), channel_id=1, source_target_pairs={{0,8},{1,9},{4,12},{5,13},{8,0},{9,1},{12,4},{13,5},{2,10},{3,11},... | collective-permute-start | bytes 393224 | tf_op jit(solution)/shard_map/ppermute | solution.py:210
  13.3 2.2 %collective-permute-start.4 = (bf16[1,4,64,256]{3,2,1,0:T(8,128)(2,1)S(1)}, bf16[1,4,64,256]{3,2,1,0:T(8,128)(2,1)S(1)}, u32[]{:S(2)}, u32[]{:S(2)}) collective-permute-start(bf16[1,4,64,256]{3,2,1,0:T(8,128)(2,1)S(1)} %get-tuple-element.22), channel_id=1, source_target_pairs={{0,9},{1,8},{4,13},{5,12},{8,1},{9,0},{12,5},{13,4},{2,11},{3,10},... | collective-permute-start | bytes 393224 | tf_op jit(solution)/shard_map/ppermute | solution.py:210
  15.5 0.9 %collective-permute-start.5 = (bf16[1,4,64,256]{3,2,1,0:T(8,128)(2,1)S(1)}, bf16[1,4,64,256]{3,2,1,0:T(8,128)(2,1)S(1)}, u32[]{:S(2)}, u32[]{:S(2)}) collective-permute-start(bf16[1,4,64,256]{3,2,1,0:T(8,128)(2,1)S(1)} %get-tuple-element.23), channel_id=1, source_target_pairs={{0,4},{1,5},{4,0},{5,1},{8,12},{9,13},{12,8},{13,9},{2,6},{3,7},{6... | collective-permute-start | bytes 393224 | tf_op jit(solution)/shard_map/ppermute | solution.py:210
  16.4 0.0 collective-permute-done.1.refs_0_
  16.4 9.2 %collective-permute-start.6 = (bf16[1,4,64,256]{3,2,1,0:T(8,128)(2,1)S(1)}, bf16[1,4,64,256]{3,2,1,0:T(8,128)(2,1)S(1)}, u32[]{:S(2)}, u32[]{:S(2)}) collective-permute-start(bf16[1,4,64,256]{3,2,1,0:T(8,128)(2,1)S(1)} %get-tuple-element.24), channel_id=1, source_target_pairs={{0,5},{1,4},{4,1},{5,0},{8,13},{9,12},{12,9},{13,8},{2,7},{3,6},{6... | collective-permute-start | bytes 393224 | tf_op jit(solution)/shard_map/ppermute | solution.py:210
  25.6 0.0 collective-permute-done.2.refs_1_
  25.6 0.0 collective-permute-start.7
  25.6 3.0 %collective-permute-done.3.refs_2_ = bf16[1,4,64,256]{3,2,1,0:T(8,128)(2,1)S(1)} collective-permute-done((bf16[1,4,64,256]{3,2,1,0:T(8,128)(2,1)S(1)}, bf16[1,4,64,256]{3,2,1,0:T(8,128)(2,1)S(1)}, u32[]{:S(2)}, u32[]{:S(2)}) %collective-permute-start.3) | collective-permute-done | bytes 131104 | tf_op jit(solution)/shard_map/ppermute | solution.py:210
  28.6 3.6 %collective-permute-done.4.refs_3_ = bf16[1,4,64,256]{3,2,1,0:T(8,128)(2,1)S(1)} collective-permute-done((bf16[1,4,64,256]{3,2,1,0:T(8,128)(2,1)S(1)}, bf16[1,4,64,256]{3,2,1,0:T(8,128)(2,1)S(1)}, u32[]{:S(2)}, u32[]{:S(2)}) %collective-permute-start.4) | collective-permute-done | bytes 131104 | tf_op jit(solution)/shard_map/ppermute | solution.py:210
  32.2 0.0 collective-permute-done.5.refs_4_
  32.2 0.9 %collective-permute-done.6.refs_5_ = bf16[1,4,64,256]{3,2,1,0:T(8,128)(2,1)S(1)} collective-permute-done((bf16[1,4,64,256]{3,2,1,0:T(8,128)(2,1)S(1)}, bf16[1,4,64,256]{3,2,1,0:T(8,128)(2,1)S(1)}, u32[]{:S(2)}, u32[]{:S(2)}) %collective-permute-start.6) | collective-permute-done | bytes 131104 | tf_op jit(solution)/shard_map/ppermute | solution.py:210
  33.2 0.0 collective-permute-done.7.refs_7_
  33.2 0.0 copy-done
  33.2 0.0 copy-done.1
  33.2 2.7 %upper.1 = bf16[4,2,256,128]{3,2,1,0:T(8,128)(2,1)} custom-call(s32[8]{0:T(128)} %perm_hbm.1, bf16[4,4,128,256]{3,2,1,0:T(8,128)(2,1)S(1)} %bitcast.5, bf16[4,2,4,128,128]{4,3,2,1,0:T(8,128)(2,1)S(1)} %bitcast.6, bf16[1,4,64,256]{3,2,1,0:T(8,128)(2,1)S(1)} %collective-permute-done.1.refs_0_, bf16[1,4,64,256]{3,2,1,0:T(8,128)(2,1)S(1)} %collective-permute-done.2.refs_1_, ...), custom_call_target="tpu_custom_call" | custom-call | flops 1000000 | bytes 10000 | tf_op jit(solution)/shard_map/upper/pallas_call | solution.py:188
Async XLA Ops:
  0.0 4.0 %copy-start.2 = (bf16[2,128,2,64]{1,3,2,0:T(8,128)(2,1)S(1)}, bf16[2,128,2,64]{1,3,2,0:T(8,128)(2,1)}, u32[]{:S(2)}) copy-start(bf16[2,128,2,64]{1,3,2,0:T(8,128)(2,1)} %param.8) | copy-start | bytes 196612
  0.0 4.0 %copy-start.3 = (s32[32]{0:T(128)S(1)}, s32[32]{0:T(128)}, u32[]{:S(2)}) copy-start(s32[32]{0:T(128)} %parent_ref.3) | copy-start | bytes 388
  0.0 4.0 %copy-start.4 = (s32[2]{0:T(128)S(1)}, s32[2]{0:T(128)}, u32[]{:S(2)}) copy-start(s32[2]{0:T(128)} %count_ref.1) | copy-start | bytes 28
  0.0 4.0 %collective-permute-start = (bf16[2,2,64,128]{3,2,1,0:T(8,128)(2,1)}, bf16[2,2,64,128]{3,2,1,0:T(8,128)(2,1)S(1)}, u32[]{:S(2)}, u32[]{:S(2)}) collective-permute-start(bf16[2,2,64,128]{3,2,1,0:T(8,128)(2,1)} %bitcast.7), channel_id=1, source_target_pairs={{0,2},{2,0},{1,3},{3,1},{4,6},{6,4},{5,7},{7,5},{8,10},{10,8},{9,1... | collective-permute-start | bytes 196616 | tf_op jit(solution)/shard_map/ppermute | solution.py:223
  5.9 27.3 %copy-start = (bf16[4,1,4,2,64,256]{5,4,3,2,1,0:T(8,128)(2,1)S(1)}, bf16[4,1,4,2,64,256]{5,4,3,2,1,0:T(8,128)(2,1)}, u32[]{:S(2)}) copy-start(bf16[4,1,4,2,64,256]{5,4,3,2,1,0:T(8,128)(2,1)} %param.14) | copy-start | bytes 3145732
  5.9 27.3 %copy-start.1 = (bf16[1,4,2,4,128,128]{5,4,3,2,1,0:T(8,128)(2,1)S(1)}, bf16[1,4,2,4,128,128]{5,4,3,2,1,0:T(8,128)(2,1)}, u32[]{:S(2)}) copy-start(bf16[1,4,2,4,128,128]{5,4,3,2,1,0:T(8,128)(2,1)} %param.15) | copy-start | bytes 3145732
  5.9 10.5 %collective-permute-start.1 = (bf16[1,4,64,256]{3,2,1,0:T(8,128)(2,1)S(1)}, bf16[1,4,64,256]{3,2,1,0:T(8,128)(2,1)S(1)}, u32[]{:S(2)}, u32[]{:S(2)}) collective-permute-start(bf16[1,4,64,256]{3,2,1,0:T(8,128)(2,1)S(1)} %get-tuple-element.18), channel_id=1, source_target_pairs={{0,12},{1,13},{4,8},{5,9},{8,4},{9,5},{12,0},{13,1},{2,14},{3,15},... | collective-permute-start | bytes 393224 | tf_op jit(solution)/shard_map/ppermute | solution.py:210
  9.5 16.0 %collective-permute-start.2 = (bf16[1,4,64,256]{3,2,1,0:T(8,128)(2,1)S(1)}, bf16[1,4,64,256]{3,2,1,0:T(8,128)(2,1)S(1)}, u32[]{:S(2)}, u32[]{:S(2)}) collective-permute-start(bf16[1,4,64,256]{3,2,1,0:T(8,128)(2,1)S(1)} %get-tuple-element.19), channel_id=1, source_target_pairs={{0,13},{1,12},{4,9},{5,8},{8,5},{9,4},{12,1},{13,0},{2,15},{3,14},... | collective-permute-start | bytes 393224 | tf_op jit(solution)/shard_map/ppermute | solution.py:210
  12.5 16.0 %collective-permute-start.3 = (bf16[1,4,64,256]{3,2,1,0:T(8,128)(2,1)S(1)}, bf16[1,4,64,256]{3,2,1,0:T(8,128)(2,1)S(1)}, u32[]{:S(2)}, u32[]{:S(2)}) collective-permute-start(bf16[1,4,64,256]{3,2,1,0:T(8,128)(2,1)S(1)} %get-tuple-element.21), channel_id=1, source_target_pairs={{0,8},{1,9},{4,12},{5,13},{8,0},{9,1},{12,4},{13,5},{2,10},{3,11},... | collective-permute-start | bytes 393224 | tf_op jit(solution)/shard_map/ppermute | solution.py:210
  13.3 19.0 %collective-permute-start.4 = (bf16[1,4,64,256]{3,2,1,0:T(8,128)(2,1)S(1)}, bf16[1,4,64,256]{3,2,1,0:T(8,128)(2,1)S(1)}, u32[]{:S(2)}, u32[]{:S(2)}) collective-permute-start(bf16[1,4,64,256]{3,2,1,0:T(8,128)(2,1)S(1)} %get-tuple-element.22), channel_id=1, source_target_pairs={{0,9},{1,8},{4,13},{5,12},{8,1},{9,0},{12,5},{13,4},{2,11},{3,10},... | collective-permute-start | bytes 393224 | tf_op jit(solution)/shard_map/ppermute | solution.py:210
  15.5 16.8 %collective-permute-start.5 = (bf16[1,4,64,256]{3,2,1,0:T(8,128)(2,1)S(1)}, bf16[1,4,64,256]{3,2,1,0:T(8,128)(2,1)S(1)}, u32[]{:S(2)}, u32[]{:S(2)}) collective-permute-start(bf16[1,4,64,256]{3,2,1,0:T(8,128)(2,1)S(1)} %get-tuple-element.23), channel_id=1, source_target_pairs={{0,4},{1,5},{4,0},{5,1},{8,12},{9,13},{12,8},{13,9},{2,6},{3,7},{6... | collective-permute-start | bytes 393224 | tf_op jit(solution)/shard_map/ppermute | solution.py:210
  16.4 16.8 %collective-permute-start.6 = (bf16[1,4,64,256]{3,2,1,0:T(8,128)(2,1)S(1)}, bf16[1,4,64,256]{3,2,1,0:T(8,128)(2,1)S(1)}, u32[]{:S(2)}, u32[]{:S(2)}) collective-permute-start(bf16[1,4,64,256]{3,2,1,0:T(8,128)(2,1)S(1)} %get-tuple-element.24), channel_id=1, source_target_pairs={{0,5},{1,4},{4,1},{5,0},{8,13},{9,12},{12,9},{13,8},{2,7},{3,6},{6... | collective-permute-start | bytes 393224 | tf_op jit(solution)/shard_map/ppermute | solution.py:210
  25.6 7.6 %collective-permute-start.7 = (bf16[1,4,64,256]{3,2,1,0:T(8,128)(2,1)S(1)}, bf16[1,4,64,256]{3,2,1,0:T(8,128)(2,1)S(1)}, u32[]{:S(2)}, u32[]{:S(2)}) collective-permute-start(bf16[1,4,64,256]{3,2,1,0:T(8,128)(2,1)S(1)} %get-tuple-element.26), channel_id=1, source_target_pairs={{0,1},{1,0},{4,5},{5,4},{8,9},{9,8},{12,13},{13,12},{2,3},{3,2},{6... | collective-permute-start | bytes 393224 | tf_op jit(solution)/shard_map/ppermute | solution.py:210

commit v5 on v4

v5 whole, which is shorter than its diff:
```python
import functools

import jax
import jax.numpy as jnp
from jax import lax
from jax.experimental import pallas as pl
from jax.experimental.pallas import tpu as pltpu
from jax.sharding import PartitionSpec as P

NRHS = 128
HALF = 64
F32 = jnp.float32
BF16 = jnp.bfloat16
PARAMS = pltpu.CompilerParams(vmem_limit_bytes=32 * 1024 * 1024)
COST = pl.CostEstimate(flops=1_000_000, bytes_accessed=10_000, transcendentals=0)


def both_cores(steps):
    return [(k, which) for k in steps for which in (0, 1)]


def partner(k, which):
    z = jnp.bitwise_xor(lax.axis_index("blk"), k)
    core = jnp.bitwise_xor(lax.axis_index("sub"), which)
    return z * 2 + core


def up_stage(outs, routes, parent_ref, up_ref, leaf_ref, cut=lambda mid: mid):
    pairs, local = outs[0].shape[:2]
    for out, (k, which) in zip(outs, routes):
        dest = partner(k, which)
        for p in range(pairs):
            for h in range(local):
                j = dest * local + h
                mid = jnp.dot(
                    up_ref[p, j], leaf_ref[p, parent_ref[j]], preferred_element_type=F32
                )
                out[p, h] = cut(mid).astype(BF16)


def leaf_stage(spreads, combine, count_ref, basis_ref, g_ref, leaf_ref, ready):
    boxes, dirs, rows, _ = basis_ref.shape
    rank = rows // 2
    width = leaf_ref.shape[3]
    first = lax.axis_index("rhs") * dirs
    even = pl.ds(0, rank, stride=2)
    odd = pl.ds(1, rank, stride=2)
    for b in range(boxes):
        ready(b)
        spread = spreads(b)
        for d in range(dirs):
            slot = b * dirs + d
            g = lax.dot_general(
                basis_ref[b, d], spread, (((1,), (1,)), ((), ())), preferred_element_type=F32
            )
            g_ref[slot, 0] = g[:, :NRHS]
            g_ref[slot, 1] = g[:, NRHS:]
            live = first + d < count_ref[b]
            pieces = combine(
                [g_ref[slot, i, even, :] for i in range(2)],
                [g_ref[slot, i, odd, :] for i in range(2)],
            )
            pieces = [jnp.where(live, x, jnp.zeros_like(x)).astype(BF16) for x in pieces]
            base = (b % 2) * 2 * rank
            top, bottom = slice(base, base + rank), slice(base + rank, base + 2 * rank)
            if width == NRHS:
                leaf_ref[b // 2, d, top, :] = pieces[0]
                leaf_ref[b // 2, d, bottom, :] = pieces[1]
            else:
                leaf_ref[b // 2, d, top, :NRHS] = pieces[0]
                leaf_ref[b // 2, d, top, NRHS:] = pieces[1]
                leaf_ref[b // 2, d, bottom, :NRHS] = -pieces[1]
                leaf_ref[b // 2, d, bottom, NRHS:] = pieces[0]


def half_columns(even, odd):
    return even[0] + odd[1], even[1] - odd[0]


def all_columns(even, odd):
    return even[0] - odd[1], even[1] + odd[0]


def own_kernel(routes, count_hbm, parent_hbm, x_hbm, basis_hbm, up_hbm, *refs):
    n = len(routes)
    outs, basis_ref, up_ref = refs[:n], refs[n], refs[n + 1]
    count_ref, parent_ref, x_ref, leaf_ref, g_ref, sems = refs[n + 2 :]
    boxes = basis_ref.shape[0]
    copies = {
        "x": pltpu.make_async_copy(x_hbm, x_ref, sems.at[0]),
        "count": pltpu.make_async_copy(count_hbm, count_ref, sems.at[1]),
        "parent": pltpu.make_async_copy(parent_hbm, parent_ref, sems.at[2]),
        "up": pltpu.make_async_copy(up_hbm, up_ref, sems.at[3]),
    }
    for b in range(boxes):
        copies[b] = pltpu.make_async_copy(basis_hbm.at[b], basis_ref.at[b], sems.at[4 + b])
    for name in ["x", 0, "count"] + list(range(1, boxes)) + ["up", "parent"]:
        copies[name].start()
    copies["x"].wait()
    copies["count"].wait()

    def spreads(b):
        real, imag = x_ref[b, 0], x_ref[b, 1]
        return jnp.concatenate([real, imag, -imag, real], axis=0)

    leaf_stage(
        spreads, half_columns, count_ref, basis_ref, g_ref, leaf_ref, lambda b: copies[b].wait()
    )
    copies["up"].wait()
    copies["parent"].wait()
    up_stage(outs, routes, parent_ref, up_ref, leaf_ref)


def own(routes, dests, count, parents, x, basis, up):
    boxes, dirs, rows, _ = basis.shape
    pairs, dirs_up, rank, _ = up.shape
    block = pltpu.VMEM((pairs, dirs_up // dests, rank, NRHS), BF16)
    args = [count, parents, x, basis, up]
    return pl.pallas_call(
        functools.partial(own_kernel, routes),
        out_shape=[block] * len(routes)
        + [pltpu.VMEM(basis.shape, BF16), pltpu.VMEM(up.shape, BF16)],
        in_specs=[pl.BlockSpec(memory_space=pltpu.HBM)] * 5,
        out_specs=[pl.BlockSpec(memory_space=pltpu.VMEM)] * (len(routes) + 2),
        scratch_shapes=[
            pltpu.SMEM(count.shape, jnp.int32),
            pltpu.SMEM(parents.shape, jnp.int32),
            pltpu.VMEM(x.shape, BF16),
            pltpu.VMEM((pairs, dirs, 4 * rank, NRHS), BF16),
            pltpu.VMEM((boxes * dirs, 2, rows, NRHS), F32),
            pltpu.SemaphoreType.DMA((4 + boxes,)),
        ],
        compiler_params=PARAMS,
        cost_estimate=COST,
        name="own",
    )(*[pltpu.with_memory_space_constraint(arg, pltpu.HBM) for arg in args])


def other_columns(mid):
    left = lax.broadcasted_iota(jnp.int32, (mid.shape[0], NRHS), 1) < HALF
    real, imag = mid[:, :NRHS], mid[:, NRHS:]
    low = jnp.where(left, real, pltpu.roll(imag, HALF, 1))
    high = jnp.where(left, pltpu.roll(real, HALF, 1), imag)
    return jnp.where(lax.axis_index("rhs") == 1, low, high)


def lower_kernel(full, halved, count_ref, parent_ref, *refs):
    n, m = len(full), len(halved)
    g_ref, leaf_ref = refs[-2:]
    outs = refs[-2 - n - m : -2]
    *xs, basis_ref, up_ref = refs[: -2 - n - m]

    def spreads(b):
        if len(xs) == 1:
            return jnp.concatenate([xs[0][b, 0], xs[0][b, 1]], axis=0)
        own, other = xs[0][b], xs[1][b]
        swap = lax.axis_index("rhs") == 1
        low, high = jnp.where(swap, other, own), jnp.where(swap, own, other)
        return jnp.concatenate([low[0], high[0], low[1], high[1]], axis=0)

    leaf_stage(spreads, all_columns, count_ref, basis_ref, g_ref, leaf_ref, lambda b: None)
    up_stage(outs[:n], full, parent_ref, up_ref, leaf_ref)
    if halved:
        up_stage(outs[n:], halved, parent_ref, up_ref, leaf_ref, other_columns)


def lower(full, halved, dests, count, parents, xs, basis, up):
    boxes, dirs, rows, _ = basis.shape
    pairs, dirs_up, rank, _ = up.shape
    shape = (pairs, dirs_up // dests, rank)
    smem = pl.BlockSpec(memory_space=pltpu.SMEM)
    vmem = pl.BlockSpec(memory_space=pltpu.VMEM)
    n = len(full) + len(halved)
    return pl.pallas_call(
        functools.partial(lower_kernel, full, halved),
        out_shape=[pltpu.VMEM(shape + (2 * NRHS,), BF16)] * len(full)
        + [pltpu.VMEM(shape + (NRHS,), BF16)] * len(halved),
        in_specs=[smem, smem] + [vmem] * (2 + len(xs)),
        out_specs=[vmem] * n,
        scratch_shapes=[
            pltpu.VMEM((boxes * dirs, 2, rows, NRHS), F32),
            pltpu.VMEM((pairs, dirs, 4 * rank, 2 * NRHS), BF16),
        ],
        compiler_params=PARAMS,
        cost_estimate=COST,
        name="lower",
    )(count, parents, *xs, basis, up)


def upper_kernel(full, halved, perm_hbm, down_ref, row_ref, *refs):
    n, m = len(full), len(halved)
    mids, own_mids, other_mids = refs[:n], refs[n : n + m], refs[n + m : n + 2 * m]
    out_hbm, spread_ref, mix_ref, out_ref, perm_ref, sems = refs[n + 2 * m :]
    groups, local = down_ref.shape[:2]
    rank = spread_ref.shape[2] // 2
    leaf = row_ref.shape[3]
    fetch = pltpu.make_async_copy(perm_hbm, perm_ref, sems.at[local])
    fetch.start()

    def put(source, h, real, imag):
        spread_ref[source, h, :rank, :NRHS] = real
        spread_ref[source, h, :rank, NRHS:] = imag
        spread_ref[source, h, rank:, :NRHS] = -imag
        spread_ref[source, h, rank:, NRHS:] = real

    left = lax.broadcasted_iota(jnp.int32, (rank, NRHS), 1) < HALF
    for own_ref, other_ref, (k, which) in zip(own_mids, other_mids, halved):
        pairs = own_ref.shape[0]
        swap = lax.axis_index("rhs") == 1
        for p in range(pairs):
            for h in range(local):
                low, high = own_ref[p, h].astype(F32), other_ref[p, h].astype(F32)
                low, high = jnp.where(swap, high, low), jnp.where(swap, low, high)
                real = jnp.where(left, low, pltpu.roll(high, HALF, 1)).astype(BF16)
                imag = jnp.where(left, pltpu.roll(low, HALF, 1), high).astype(BF16)
                put(partner(k, which) * pairs + p, h, real, imag)
    for mid_ref, (k, which) in zip(mids, full):
        pairs = mid_ref.shape[0]
        for p in range(pairs):
            for h in range(local):
                mid = mid_ref[p, h]
                put(partner(k, which) * pairs + p, h, mid[:, :NRHS], mid[:, NRHS:])
    fetch.wait()
    copies = []
    for h in range(local):
        tops = ([], [])
        for q in range(groups):
            parts = [spread_ref[perm_ref[2 * q + s], h] for s in range(2)]
            top = jnp.dot(
                down_ref[q, h], jnp.concatenate(parts, axis=0), preferred_element_type=F32
            ).astype(BF16)
            for t in range(2):
                piece = top[t * rank : (t + 1) * rank]
                tops[t].append(piece)
                tops[t].append(jnp.concatenate([-piece[:, NRHS:], piece[:, :NRHS]], axis=1))
        for t in range(2):
            rows = jnp.concatenate([row_ref[h, t, q] for q in range(groups)], axis=1)
            field = jnp.dot(rows, jnp.concatenate(tops[t], axis=0), preferred_element_type=F32)
            mix_ref[h, t, pl.ds(0, leaf, stride=2), :] = field[:, :NRHS]
            mix_ref[h, t, pl.ds(1, leaf, stride=2), :] = field[:, NRHS:]
            out_ref[h, t] = mix_ref[h, t].astype(BF16)
        copies.append(pltpu.make_async_copy(out_ref.at[h], out_hbm.at[h], sems.at[h]))
        copies[-1].start()
    for copy in copies:
        copy.wait()


def upper(full, halved, perm, down, row, mids):
    groups, local, _, width = down.shape
    leaf = row.shape[3]
    vmem = pl.BlockSpec(memory_space=pltpu.VMEM)
    hbm = pl.BlockSpec(memory_space=pltpu.HBM)
    shape = (local, 2, 2 * leaf, NRHS)
    return pl.pallas_call(
        functools.partial(upper_kernel, full, halved),
        out_shape=jax.ShapeDtypeStruct(shape, BF16),
        in_specs=[hbm] + [vmem] * (2 + len(mids)),
        out_specs=hbm,
        scratch_shapes=[
            pltpu.VMEM((2 * groups, local, width // 2, 2 * NRHS), BF16),
            pltpu.VMEM(shape, F32),
            pltpu.VMEM(shape, BF16),
            pltpu.SMEM(perm.shape, jnp.int32),
            pltpu.SemaphoreType.DMA((local + 1,)),
        ],
        compiler_params=PARAMS,
        cost_estimate=COST,
        name="upper",
    )(pltpu.with_memory_space_constraint(perm, pltpu.HBM), down, row, *mids)


def send(block, route, dests):
    code = 2 * route[0] + route[1]
    if not code:
        return block
    return lax.ppermute(block, ("blk", "sub"), [(m, m ^ code) for m in range(dests)])


def on_device(
    columns, x_panels, leaf_basis, leaf_count, parent_map, up_transfer, mid_perm, down_transfer, row_basis
):
    boxes, directions, rank, _, leaf = leaf_basis.shape
    basis = leaf_basis.reshape(boxes, directions, rank * 2, leaf)
    groups, _, local = down_transfer.shape[:3]
    down = down_transfer.reshape(groups, local, 2 * rank, 4 * rank)
    row = row_basis.reshape(local, 2, groups, leaf, 2 * rank)
    x = jnp.transpose(x_panels, (0, 2, 3, 1))
    dests = 2 * columns
    full = [(2, 0), (1, 0), (0, 1), (2, 1), (1, 1), (0, 0)]
    farther = both_cores(range(columns - 1, 2, -1))
    if 2 * x.shape[2] == NRHS:
        halved = farther
        xs = [x, lax.ppermute(x, "rhs", [(0, 1), (1, 0)])]
        *own_mids, basis, up = own(halved, dests, leaf_count, parent_map, x, basis, up_transfer)
        own_mids = [send(mid, route, dests) for mid, route in zip(own_mids, halved)]
    else:
        full, halved, own_mids, up = farther + full, [], [], up_transfer
        xs = [lax.all_gather(x, "rhs", axis=2, tiled=True)]
    mids = lower(full, halved, dests, leaf_count, parent_map, xs, basis, up)
    mids = [send(mid, route, dests) for mid, route in zip(mids, full + halved)]
    n = len(full)
    result = upper(full, halved, mid_perm, down, row, [*mids[:n], *own_mids, *mids[n:]])
    return result.reshape(1, local, 2, leaf, 2, NRHS)


def solution(mesh):
    return jax.shard_map(
        functools.partial(on_device, mesh.shape["blk"]),
        mesh=mesh,
        in_specs=(
            P(("grp", "blk", "sub"), None, None, "rhs"),
            P(("blk", "sub"), "rhs", None, None, None),
            P(("blk", "sub")),
            P("rhs"),
            P(("blk", "sub"), "rhs", None, None),
            P(),
            P(None, "rhs", ("blk", "sub"), None, None, None),
            P("rhs", ("blk", "sub"), None, None, None, None),
        ),
        out_specs=P(("grp", "rhs"), ("blk", "sub"), None, None, None, None),
        check_vma=False,
    )
```

time: 36 us -> 35.1 us (0.975)
  the two profiles are of different devices: /device:TPU:1 before, /device:TPU:0 now
where the time goes in v5:
time: 35.1 us; the launch traced here: 35 us
  starting transfers between devices  15.6 us (44%)
  waiting for transfers between devices  11 us (31%)
  Pallas kernels  7.68 us (22%)
  local copies, waits for them, and re-layouts  0.66 us (2%)
    ppermute x9, starting transfers between devices, send(): lax.ppermute(block, ('blk', 'sub'), [(m, m ^ code) for m in range(dests)])  12.7 us
    ppermute x9, waiting for transfers between devices, send(): lax.ppermute(block, ('blk', 'sub'), [(m, m ^ code) for m in range(dests)])  11 us
    ppermute x1, starting transfers between devices, on_device(): xs = [x, lax.ppermute(x, 'rhs', [(0, 1), (1, 0)])]  2.94 us
    pallas_call x1, Pallas kernels, upper(): pl.pallas_call(functools.partial(upper_kernel, full, halved), out_shape=j...  2.64 us
    pallas_call x1, Pallas kernels, lower(): pl.pallas_call(functools.partial(lower_kernel, full, halved), out_shape=[...  2.52 us
    pallas_call x1, Pallas kernels, own(): pl.pallas_call(functools.partial(own_kernel, routes), out_shape=[block] *...  2.52 us
  transfers between devices with their start and end apart: 10, of which 3 were waited for; matrix products, arithmetic and copies ran while one was open for 0% of the time, Pallas kernels for 14%

profile of v5, /device:TPU:0, one launch (start us, length us, event | category | flops | bytes accessed | tf_op | source)
XLA Modules:
  0.0 35.0 jit_solution(15340725291014356781)
XLA Ops:
  0.0 2.9 %collective-permute-start = (bf16[2,2,64,128]{3,2,1,0:T(8,128)(2,1)}, bf16[2,2,64,128]{3,2,1,0:T(8,128)(2,1)S(1)}, u32[]{:S(2)}, u32[]{:S(2)}) collective-permute-start(bf16[2,2,64,128]{3,2,1,0:T(8,128)(2,1)} %bitcast.7), channel_id=1, source_target_pairs={{0,2},{2,0},{1,3},{3,1},{4,6},{6,4},{5,7},{7,5},{8,10},{10,8},{9,1... | collective-permute-start | bytes 196616 | tf_op jit(solution)/shard_map/ppermute | solution.py:293
  2.9 0.0 copy-start.2
  2.9 2.5 %own.1 = (bf16[1,4,64,128]{3,2,1,0:T(8,128)(2,1)S(1)}, bf16[1,4,64,128]{3,2,1,0:T(8,128)(2,1)S(1)}, bf16[2,16,128,128]{3,2,1,0:T(8,128)(2,1)S(1)}, bf16[1,32,64,256]{3,2,1,0:T(8,128)(2,1)S(1)}) custom-call(s32[2]{0:T(128)} %count_ref.1, s32[32]{0:T(128)} %parent_ref.1, bf16[2,2,64,128]{3,2,1,0:T(8,128)(2,1)} %bitcast.8, bf16[2,16,128,128]{3,2,1,0:T(8,128)(2,1)} %bitcast.10, ...), custom_call_target="tpu_custom_call" | custom-call | flops 1000000 | bytes 10000 | tf_op jit(solution)/shard_map/own/pallas_call | solution.py:119
  5.5 3.7 %collective-permute-start.6 = (bf16[1,4,64,128]{3,2,1,0:T(8,128)(2,1)S(1)}, bf16[1,4,64,128]{3,2,1,0:T(8,128)(2,1)S(1)}, u32[]{:S(2)}, u32[]{:S(2)}) collective-permute-start(bf16[1,4,64,128]{3,2,1,0:T(8,128)(2,1)S(1)} %get-tuple-element.25), channel_id=1, source_target_pairs={{0,12},{1,13},{4,8},{5,9},{8,4},{9,5},{12,0},{13,1},{2,14},{3,15},... | collective-permute-start | bytes 196616 | tf_op jit(solution)/shard_map/ppermute | solution.py:276
  9.1 0.0 collective-permute-start.7
  9.1 0.0 collective-permute-done.refs_1_
  9.1 0.0 copy-start.3
  9.1 0.0 copy-start.4
  9.2 0.0 copy-done.2
  9.2 0.6 %copy-done.3 = s32[2]{0:T(128)S(1)} copy-done((s32[2]{0:T(128)S(1)}, s32[2]{0:T(128)}, u32[]{:S(2)}) %copy-start.3) | copy-done | bytes 32
  9.8 0.0 copy-done.4
  9.8 0.0 copy-start
  9.8 2.5 %lower.1 = (bf16[1,4,64,256]{3,2,1,0:T(8,128)(2,1)S(1)}, bf16[1,4,64,256]{3,2,1,0:T(8,128)(2,1)S(1)}, bf16[1,4,64,256]{3,2,1,0:T(8,128)(2,1)S(1)}, bf16[1,4,64,2...) custom-call(s32[2]{0:T(128)S(1)} %copy-done.3, ...), custom_call_target="tpu_custom_call" | custom-call | flops 1000000 | bytes 10000 | tf_op jit(solution)/shard_map/lower/pallas_call | solution.py:174
  12.3 2.8 %collective-permute-start.8 = (bf16[1,4,64,128]{3,2,1,0:T(8,128)(2,1)S(1)}, bf16[1,4,64,128]{3,2,1,0:T(8,128)(2,1)S(1)}, u32[]{:S(2)}, u32[]{:S(2)}) collective-permute-start(bf16[1,4,64,128]{3,2,1,0:T(8,128)(2,1)S(1)} %get-tuple-element.27), channel_id=1, source_target_pairs={{0,12},{1,13},{4,8},{5,9},{8,4},{9,5},{12,0},{13,1},{2,14},{3,15},... | collective-permute-start | bytes 196616 | tf_op jit(solution)/shard_map/ppermute | solution.py:276
  15.1 0.9 %collective-permute-start.9 = (bf16[1,4,64,128]{3,2,1,0:T(8,128)(2,1)S(1)}, bf16[1,4,64,128]{3,2,1,0:T(8,128)(2,1)S(1)}, u32[]{:S(2)}, u32[]{:S(2)}) collective-permute-start(bf16[1,4,64,128]{3,2,1,0:T(8,128)(2,1)S(1)} %get-tuple-element.28), channel_id=1, source_target_pairs={{0,13},{1,12},{4,9},{5,8},{8,5},{9,4},{12,1},{13,0},{2,15},{3,14},... | collective-permute-start | bytes 196616 | tf_op jit(solution)/shard_map/ppermute | solution.py:276
  16.0 0.0 collective-permute-start.1
  16.0 0.0 collective-permute-done.6.refs_6_
  16.0 4.0 %collective-permute-start.2 = (bf16[1,4,64,256]{3,2,1,0:T(8,128)(2,1)S(1)}, bf16[1,4,64,256]{3,2,1,0:T(8,128)(2,1)S(1)}, u32[]{:S(2)}, u32[]{:S(2)}) collective-permute-start(bf16[1,4,64,256]{3,2,1,0:T(8,128)(2,1)S(1)} %get-tuple-element.20), channel_id=1, source_target_pairs={{0,4},{1,5},{4,0},{5,1},{8,12},{9,13},{12,8},{13,9},{2,6},{3,7},{6... | collective-permute-start | bytes 393224 | tf_op jit(solution)/shard_map/ppermute | solution.py:276
  20.1 0.0 collective-permute-done.7.refs_7_
  20.1 0.0 collective-permute-start.3
  20.1 0.0 collective-permute-done.8.refs_8_
  20.1 0.1 collective-permute-start.4
  20.2 0.6 %collective-permute-done.9.refs_9_ = bf16[1,4,64,128]{3,2,1,0:T(8,128)(2,1)S(1)} collective-permute-done((bf16[1,4,64,128]{3,2,1,0:T(8,128)(2,1)S(1)}, bf16[1,4,64,128]{3,2,1,0:T(8,128)(2,1)S(1)}, u32[]{:S(2)}, u32[]{:S(2)}) %collective-permute-start.9) | collective-permute-done | bytes 65568 | tf_op jit(solution)/shard_map/ppermute | solution.py:276
  20.8 1.2 %collective-permute-start.5 = (bf16[1,4,64,256]{3,2,1,0:T(8,128)(2,1)S(1)}, bf16[1,4,64,256]{3,2,1,0:T(8,128)(2,1)S(1)}, u32[]{:S(2)}, u32[]{:S(2)}) collective-permute-start(bf16[1,4,64,256]{3,2,1,0:T(8,128)(2,1)S(1)} %get-tuple-element.23), channel_id=1, source_target_pairs={{0,5},{1,4},{4,1},{5,0},{8,13},{9,12},{12,9},{13,8},{2,7},{3,6},{6... | collective-permute-start | bytes 393224 | tf_op jit(solution)/shard_map/ppermute | solution.py:276
  21.9 6.2 %collective-permute-done.1.refs_0_ = bf16[1,4,64,256]{3,2,1,0:T(8,128)(2,1)S(1)} collective-permute-done((bf16[1,4,64,256]{3,2,1,0:T(8,128)(2,1)S(1)}, bf16[1,4,64,256]{3,2,1,0:T(8,128)(2,1)S(1)}, u32[]{:S(2)}, u32[]{:S(2)}) %collective-permute-start.1) | collective-permute-done | bytes 131104 | tf_op jit(solution)/shard_map/ppermute | solution.py:276
  28.1 0.0 collective-permute-done.2.refs_1_
  28.1 0.0 collective-permute-done.3.refs_2_
  28.1 4.2 %collective-permute-done.4.refs_3_ = bf16[1,4,64,256]{3,2,1,0:T(8,128)(2,1)S(1)} collective-permute-done((bf16[1,4,64,256]{3,2,1,0:T(8,128)(2,1)S(1)}, bf16[1,4,64,256]{3,2,1,0:T(8,128)(2,1)S(1)}, u32[]{:S(2)}, u32[]{:S(2)}) %collective-permute-start.4) | collective-permute-done | bytes 131104 | tf_op jit(solution)/shard_map/ppermute | solution.py:276
  32.3 0.0 collective-permute-done.5.refs_4_
  32.3 0.0 copy-done
  32.3 0.0 copy-done.1
  32.3 2.6 %upper.1 = bf16[4,2,256,128]{3,2,1,0:T(8,128)(2,1)} custom-call(s32[8]{0:T(128)} %perm_hbm.1, bf16[4,4,128,256]{3,2,1,0:T(8,128)(2,1)S(1)} %bitcast.5, bf16[4,2,4,128,128]{4,3,2,1,0:T(8,128)(2,1)S(1)} %bitcast.6, bf16[1,4,64,256]{3,2,1,0:T(8,128)(2,1)S(1)} %collective-permute-done.1.refs_0_, bf16[1,4,64,256]{3,2,1,0:T(8,128)(2,1)S(1)} %collective-permute-done.2.refs_1_, ...), custom_call_target="tpu_custom_call" | custom-call | flops 1000000 | bytes 10000 | tf_op jit(solution)/shard_map/upper/pallas_call | solution.py:254
  (1 shorter events, 0.0 us)
Async XLA Ops:
  0.0 9.1 %collective-permute-start = (bf16[2,2,64,128]{3,2,1,0:T(8,128)(2,1)}, bf16[2,2,64,128]{3,2,1,0:T(8,128)(2,1)S(1)}, u32[]{:S(2)}, u32[]{:S(2)}) collective-permute-start(bf16[2,2,64,128]{3,2,1,0:T(8,128)(2,1)} %bitcast.7), channel_id=1, source_target_pairs={{0,2},{2,0},{1,3},{3,1},{4,6},{6,4},{5,7},{7,5},{8,10},{10,8},{9,1... | collective-permute-start | bytes 196616 | tf_op jit(solution)/shard_map/ppermute | solution.py:293
  2.9 6.2 %copy-start.2 = (bf16[2,128,2,64]{1,3,2,0:T(8,128)(2,1)S(1)}, bf16[2,128,2,64]{1,3,2,0:T(8,128)(2,1)}, u32[]{:S(2)}) copy-start(bf16[2,128,2,64]{1,3,2,0:T(8,128)(2,1)} %param.8) | copy-start | bytes 196612
  5.5 10.6 %collective-permute-start.6 = (bf16[1,4,64,128]{3,2,1,0:T(8,128)(2,1)S(1)}, bf16[1,4,64,128]{3,2,1,0:T(8,128)(2,1)S(1)}, u32[]{:S(2)}, u32[]{:S(2)}) collective-permute-start(bf16[1,4,64,128]{3,2,1,0:T(8,128)(2,1)S(1)} %get-tuple-element.25), channel_id=1, source_target_pairs={{0,12},{1,13},{4,8},{5,9},{8,4},{9,5},{12,0},{13,1},{2,14},{3,15},... | collective-permute-start | bytes 196616 | tf_op jit(solution)/shard_map/ppermute | solution.py:276
  9.1 10.9 %collective-permute-start.7 = (bf16[1,4,64,128]{3,2,1,0:T(8,128)(2,1)S(1)}, bf16[1,4,64,128]{3,2,1,0:T(8,128)(2,1)S(1)}, u32[]{:S(2)}, u32[]{:S(2)}) collective-permute-start(bf16[1,4,64,128]{3,2,1,0:T(8,128)(2,1)S(1)} %get-tuple-element.26), channel_id=1, source_target_pairs={{0,13},{1,12},{4,9},{5,8},{8,5},{9,4},{12,1},{13,0},{2,15},{3,14},... | collective-permute-start | bytes 196616 | tf_op jit(solution)/shard_map/ppermute | solution.py:276
  9.1 0.7 %copy-start.3 = (s32[2]{0:T(128)S(1)}, s32[2]{0:T(128)}, u32[]{:S(2)}) copy-start(s32[2]{0:T(128)} %count_ref.1) | copy-start | bytes 28
  9.1 0.7 %copy-start.4 = (s32[32]{0:T(128)S(1)}, s32[32]{0:T(128)}, u32[]{:S(2)}) copy-start(s32[32]{0:T(128)} %parent_ref.1) | copy-start | bytes 388
  9.8 22.5 %copy-start = (bf16[4,1,4,2,64,256]{5,4,3,2,1,0:T(8,128)(2,1)S(1)}, bf16[4,1,4,2,64,256]{5,4,3,2,1,0:T(8,128)(2,1)}, u32[]{:S(2)}) copy-start(bf16[4,1,4,2,64,256]{5,4,3,2,1,0:T(8,128)(2,1)} %param.14) | copy-start | bytes 3145732
  9.8 22.5 %copy-start.1 = (bf16[1,4,2,4,128,128]{5,4,3,2,1,0:T(8,128)(2,1)S(1)}, bf16[1,4,2,4,128,128]{5,4,3,2,1,0:T(8,128)(2,1)}, u32[]{:S(2)}) copy-start(bf16[1,4,2,4,128,128]{5,4,3,2,1,0:T(8,128)(2,1)} %param.15) | copy-start | bytes 3145732
  12.3 7.7 %collective-permute-start.8 = (bf16[1,4,64,128]{3,2,1,0:T(8,128)(2,1)S(1)}, bf16[1,4,64,128]{3,2,1,0:T(8,128)(2,1)S(1)}, u32[]{:S(2)}, u32[]{:S(2)}) collective-permute-start(bf16[1,4,64,128]{3,2,1,0:T(8,128)(2,1)S(1)} %get-tuple-element.27), channel_id=1, source_target_pairs={{0,12},{1,13},{4,8},{5,9},{8,4},{9,5},{12,0},{13,1},{2,14},{3,15},... | collective-permute-start | bytes 196616 | tf_op jit(solution)/shard_map/ppermute | solution.py:276
  15.1 5.6 %collective-permute-start.9 = (bf16[1,4,64,128]{3,2,1,0:T(8,128)(2,1)S(1)}, bf16[1,4,64,128]{3,2,1,0:T(8,128)(2,1)S(1)}, u32[]{:S(2)}, u32[]{:S(2)}) collective-permute-start(bf16[1,4,64,128]{3,2,1,0:T(8,128)(2,1)S(1)} %get-tuple-element.28), channel_id=1, source_target_pairs={{0,13},{1,12},{4,9},{5,8},{8,5},{9,4},{12,1},{13,0},{2,15},{3,14},... | collective-permute-start | bytes 196616 | tf_op jit(solution)/shard_map/ppermute | solution.py:276
  16.0 12.1 %collective-permute-start.1 = (bf16[1,4,64,256]{3,2,1,0:T(8,128)(2,1)S(1)}, bf16[1,4,64,256]{3,2,1,0:T(8,128)(2,1)S(1)}, u32[]{:S(2)}, u32[]{:S(2)}) collective-permute-start(bf16[1,4,64,256]{3,2,1,0:T(8,128)(2,1)S(1)} %get-tuple-element.19), channel_id=1, source_target_pairs={{0,8},{1,9},{4,12},{5,13},{8,0},{9,1},{12,4},{13,5},{2,10},{3,11},... | collective-permute-start | bytes 393224 | tf_op jit(solution)/shard_map/ppermute | solution.py:276
  16.0 12.1 %collective-permute-start.2 = (bf16[1,4,64,256]{3,2,1,0:T(8,128)(2,1)S(1)}, bf16[1,4,64,256]{3,2,1,0:T(8,128)(2,1)S(1)}, u32[]{:S(2)}, u32[]{:S(2)}) collective-permute-start(bf16[1,4,64,256]{3,2,1,0:T(8,128)(2,1)S(1)} %get-tuple-element.20), channel_id=1, source_target_pairs={{0,4},{1,5},{4,0},{5,1},{8,12},{9,13},{12,8},{13,9},{2,6},{3,7},{6... | collective-permute-start | bytes 393224 | tf_op jit(solution)/shard_map/ppermute | solution.py:276
  20.1 8.1 %collective-permute-start.3 = (bf16[1,4,64,256]{3,2,1,0:T(8,128)(2,1)S(1)}, bf16[1,4,64,256]{3,2,1,0:T(8,128)(2,1)S(1)}, u32[]{:S(2)}, u32[]{:S(2)}) collective-permute-start(bf16[1,4,64,256]{3,2,1,0:T(8,128)(2,1)S(1)} %get-tuple-element.21), channel_id=1, source_target_pairs={{0,1},{1,0},{4,5},{5,4},{8,9},{9,8},{12,13},{13,12},{2,3},{3,2},{6... | collective-permute-start | bytes 393224 | tf_op jit(solution)/shard_map/ppermute | solution.py:276
  20.1 12.2 %collective-permute-start.4 = (bf16[1,4,64,256]{3,2,1,0:T(8,128)(2,1)S(1)}, bf16[1,4,64,256]{3,2,1,0:T(8,128)(2,1)S(1)}, u32[]{:S(2)}, u32[]{:S(2)}) collective-permute-start(bf16[1,4,64,256]{3,2,1,0:T(8,128)(2,1)S(1)} %get-tuple-element.22), channel_id=1, source_target_pairs={{0,9},{1,8},{4,13},{5,12},{8,1},{9,0},{12,5},{13,4},{2,11},{3,10},... | collective-permute-start | bytes 393224 | tf_op jit(solution)/shard_map/ppermute | solution.py:276
  20.8 11.6 %collective-permute-start.5 = (bf16[1,4,64,256]{3,2,1,0:T(8,128)(2,1)S(1)}, bf16[1,4,64,256]{3,2,1,0:T(8,128)(2,1)S(1)}, u32[]{:S(2)}, u32[]{:S(2)}) collective-permute-start(bf16[1,4,64,256]{3,2,1,0:T(8,128)(2,1)S(1)} %get-tuple-element.23), channel_id=1, source_target_pairs={{0,5},{1,4},{4,1},{5,0},{8,13},{9,12},{12,9},{13,8},{2,7},{3,6},{6... | collective-permute-start | bytes 393224 | tf_op jit(solution)/shard_map/ppermute | solution.py:276

commit v6 on v5

--- a/solution.py
+++ b/solution.py
@@ -49,12 +49,15 @@
         ready(b)
         spread = spreads(b)
         for d in range(dirs):
-            slot = b * dirs + d
             g = lax.dot_general(
                 basis_ref[b, d], spread, (((1,), (1,)), ((), ())), preferred_element_type=F32
             )
-            g_ref[slot, 0] = g[:, :NRHS]
-            g_ref[slot, 1] = g[:, NRHS:]
+            g_ref[b * dirs + d, 0] = g[:, :NRHS]
+            g_ref[b * dirs + d, 1] = g[:, NRHS:]
+        if b == 0:
+            ready("count")
+        for d in range(dirs):
+            slot = b * dirs + d
             live = first + d < count_ref[b]
             pieces = combine(
                 [g_ref[slot, i, even, :] for i in range(2)],
@@ -97,14 +100,13 @@
     for name in ["x", 0, "count"] + list(range(1, boxes)) + ["up", "parent"]:
         copies[name].start()
     copies["x"].wait()
-    copies["count"].wait()
 
     def spreads(b):
         real, imag = x_ref[b, 0], x_ref[b, 1]
         return jnp.concatenate([real, imag, -imag, real], axis=0)
 
     leaf_stage(
-        spreads, half_columns, count_ref, basis_ref, g_ref, leaf_ref, lambda b: copies[b].wait()
+        spreads, half_columns, count_ref, basis_ref, g_ref, leaf_ref, lambda name: copies[name].wait()
     )
     copies["up"].wait()
     copies["parent"].wait()
@@ -144,11 +146,21 @@
     return jnp.where(lax.axis_index("rhs") == 1, low, high)
 
 
-def lower_kernel(full, halved, count_ref, parent_ref, *refs):
+def lower_kernel(full, halved, count_hbm, parent_hbm, *refs):
     n, m = len(full), len(halved)
-    g_ref, leaf_ref = refs[-2:]
-    outs = refs[-2 - n - m : -2]
-    *xs, basis_ref, up_ref = refs[: -2 - n - m]
+    g_ref, leaf_ref, count_ref, parent_ref, sems = refs[-5:]
+    outs = refs[-5 - n - m : -5]
+    *xs, basis_ref, up_ref = refs[: -5 - n - m]
+    copies = {
+        "count": pltpu.make_async_copy(count_hbm, count_ref, sems.at[0]),
+        "parent": pltpu.make_async_copy(parent_hbm, parent_ref, sems.at[1]),
+    }
+    for copy in copies.values():
+        copy.start()
+
+    def ready(name):
+        if name in copies:
+            copies[name].wait()
 
     def spreads(b):
         if len(xs) == 1:
@@ -158,7 +170,8 @@
         low, high = jnp.where(swap, other, own), jnp.where(swap, own, other)
         return jnp.concatenate([low[0], high[0], low[1], high[1]], axis=0)
 
-    leaf_stage(spreads, all_columns, count_ref, basis_ref, g_ref, leaf_ref, lambda b: None)
+    leaf_stage(spreads, all_columns, count_ref, basis_ref, g_ref, leaf_ref, ready)
+    ready("parent")
     up_stage(outs[:n], full, parent_ref, up_ref, leaf_ref)
     if halved:
         up_stage(outs[n:], halved, parent_ref, up_ref, leaf_ref, other_columns)
@@ -168,33 +181,44 @@
     boxes, dirs, rows, _ = basis.shape
     pairs, dirs_up, rank, _ = up.shape
     shape = (pairs, dirs_up // dests, rank)
-    smem = pl.BlockSpec(memory_space=pltpu.SMEM)
+    hbm = pl.BlockSpec(memory_space=pltpu.HBM)
     vmem = pl.BlockSpec(memory_space=pltpu.VMEM)
     n = len(full) + len(halved)
     return pl.pallas_call(
         functools.partial(lower_kernel, full, halved),
         out_shape=[pltpu.VMEM(shape + (2 * NRHS,), BF16)] * len(full)
         + [pltpu.VMEM(shape + (NRHS,), BF16)] * len(halved),
-        in_specs=[smem, smem] + [vmem] * (2 + len(xs)),
+        in_specs=[hbm, hbm] + [vmem] * (2 + len(xs)),
         out_specs=[vmem] * n,
         scratch_shapes=[
             pltpu.VMEM((boxes * dirs, 2, rows, NRHS), F32),
             pltpu.VMEM((pairs, dirs, 4 * rank, 2 * NRHS), BF16),
+            pltpu.SMEM(count.shape, jnp.int32),
+            pltpu.SMEM(parents.shape, jnp.int32),
+            pltpu.SemaphoreType.DMA((2,)),
         ],
         compiler_params=PARAMS,
         cost_estimate=COST,
         name="lower",
-    )(count, parents, *xs, basis, up)
-
-
-def upper_kernel(full, halved, perm_hbm, down_ref, row_ref, *refs):
+    )(*[pltpu.with_memory_space_constraint(a, pltpu.HBM) for a in (count, parents)], *xs, basis, up)
+
+
+def twist(top):
+    return jnp.concatenate([-top[:, NRHS:], top[:, :NRHS]], axis=1)
+
+
+def twisted_rows(tops):
+    return jnp.concatenate([rows for top in tops for rows in (top, twist(top))], axis=0)
+
+
+def upper_kernel(full, halved, last, perm_hbm, down_ref, row_ref, *refs):
     n, m = len(full), len(halved)
     mids, own_mids, other_mids = refs[:n], refs[n : n + m], refs[n + m : n + 2 * m]
-    out_hbm, spread_ref, mix_ref, out_ref, perm_ref, sems = refs[n + 2 * m :]
+    field_ref, top_ref, spread_ref, perm_ref, sem = refs[n + 2 * m :]
     groups, local = down_ref.shape[:2]
     rank = spread_ref.shape[2] // 2
     leaf = row_ref.shape[3]
-    fetch = pltpu.make_async_copy(perm_hbm, perm_ref, sems.at[local])
+    fetch = pltpu.make_async_copy(perm_hbm, perm_ref, sem.at[0])
     fetch.start()
 
     def put(source, h, real, imag):
@@ -205,68 +229,120 @@
 
     left = lax.broadcasted_iota(jnp.int32, (rank, NRHS), 1) < HALF
     for own_ref, other_ref, (k, which) in zip(own_mids, other_mids, halved):
-        pairs = own_ref.shape[0]
         swap = lax.axis_index("rhs") == 1
-        for p in range(pairs):
-            for h in range(local):
-                low, high = own_ref[p, h].astype(F32), other_ref[p, h].astype(F32)
-                low, high = jnp.where(swap, high, low), jnp.where(swap, low, high)
-                real = jnp.where(left, low, pltpu.roll(high, HALF, 1)).astype(BF16)
-                imag = jnp.where(left, pltpu.roll(low, HALF, 1), high).astype(BF16)
-                put(partner(k, which) * pairs + p, h, real, imag)
+        for h in range(local):
+            low, high = own_ref[0, h].astype(F32), other_ref[0, h].astype(F32)
+            low, high = jnp.where(swap, high, low), jnp.where(swap, low, high)
+            real = jnp.where(left, low, pltpu.roll(high, HALF, 1)).astype(BF16)
+            imag = jnp.where(left, pltpu.roll(low, HALF, 1), high).astype(BF16)
+            put(partner(k, which), h, real, imag)
     for mid_ref, (k, which) in zip(mids, full):
-        pairs = mid_ref.shape[0]
-        for p in range(pairs):
-            for h in range(local):
-                mid = mid_ref[p, h]
-                put(partner(k, which) * pairs + p, h, mid[:, :NRHS], mid[:, NRHS:])
+        for h in range(local):
+            mid = mid_ref[0, h]
+            put(partner(k, which), h, mid[:, :NRHS], mid[:, NRHS:])
+    missing = partner(*last)
+    for h in range(local):
+        spread_ref[missing, h] = jnp.zeros(spread_ref.shape[2:], BF16)
     fetch.wait()
-    copies = []
     for h in range(local):
         tops = ([], [])
         for q in range(groups):
-            parts = [spread_ref[perm_ref[2 * q + s], h] for s in range(2)]
+            children = [perm_ref[2 * q + s] for s in range(2)]
             top = jnp.dot(
-                down_ref[q, h], jnp.concatenate(parts, axis=0), preferred_element_type=F32
-            ).astype(BF16)
+                down_ref[q, h],
+                jnp.concatenate([spread_ref[child, h] for child in children], axis=0),
+                preferred_element_type=F32,
+            )
+            lacks = jnp.logical_or(children[0] == missing, children[1] == missing)
+            top_ref[jnp.where(lacks, 0, 1), h] = top
+            top = jnp.where(lacks, jnp.zeros_like(top), top).astype(BF16)
             for t in range(2):
-                piece = top[t * rank : (t + 1) * rank]
-                tops[t].append(piece)
-                tops[t].append(jnp.concatenate([-piece[:, NRHS:], piece[:, :NRHS]], axis=1))
+                tops[t].append(top[t * rank : (t + 1) * rank])
         for t in range(2):
             rows = jnp.concatenate([row_ref[h, t, q] for q in range(groups)], axis=1)
-            field = jnp.dot(rows, jnp.concatenate(tops[t], axis=0), preferred_element_type=F32)
-            mix_ref[h, t, pl.ds(0, leaf, stride=2), :] = field[:, :NRHS]
-            mix_ref[h, t, pl.ds(1, leaf, stride=2), :] = field[:, NRHS:]
-            out_ref[h, t] = mix_ref[h, t].astype(BF16)
-        copies.append(pltpu.make_async_copy(out_ref.at[h], out_hbm.at[h], sems.at[h]))
-        copies[-1].start()
-    for copy in copies:
-        copy.wait()
-
-
-def upper(full, halved, perm, down, row, mids):
+            field = jnp.dot(rows, twisted_rows(tops[t]), preferred_element_type=F32)
+            field_ref[h, t, pl.ds(0, leaf, stride=2), :] = field[:, :NRHS]
+            field_ref[h, t, pl.ds(1, leaf, stride=2), :] = field[:, NRHS:]
+
+
+def upper(full, halved, last, perm, down, row, mids):
     groups, local, _, width = down.shape
     leaf = row.shape[3]
+    rank = width // 4
     vmem = pl.BlockSpec(memory_space=pltpu.VMEM)
     hbm = pl.BlockSpec(memory_space=pltpu.HBM)
-    shape = (local, 2, 2 * leaf, NRHS)
     return pl.pallas_call(
-        functools.partial(upper_kernel, full, halved),
-        out_shape=jax.ShapeDtypeStruct(shape, BF16),
+        functools.partial(upper_kernel, full, halved, last),
+        out_shape=[
+            pltpu.VMEM((local, 2, 2 * leaf, NRHS), F32),
+            pltpu.VMEM((2, local, 2 * rank, 2 * NRHS), F32),
+        ],
         in_specs=[hbm] + [vmem] * (2 + len(mids)),
-        out_specs=hbm,
+        out_specs=[vmem] * 2,
         scratch_shapes=[
-            pltpu.VMEM((2 * groups, local, width // 2, 2 * NRHS), BF16),
-            pltpu.VMEM(shape, F32),
-            pltpu.VMEM(shape, BF16),
+            pltpu.VMEM((2 * groups, local, 2 * rank, 2 * NRHS), BF16),
             pltpu.SMEM(perm.shape, jnp.int32),
-            pltpu.SemaphoreType.DMA((local + 1,)),
+            pltpu.SemaphoreType.DMA((1,)),
         ],
         compiler_params=PARAMS,
         cost_estimate=COST,
         name="upper",
     )(pltpu.with_memory_space_constraint(perm, pltpu.HBM), down, row, *mids)
+
+
+def finish_kernel(last, perm_hbm, down_ref, row_ref, field_ref, top_ref, mid_ref, out_hbm, mix_ref, out_ref, perm_ref, sems):
+    groups, local = down_ref.shape[:2]
+    rank = mid_ref.shape[2]
+    leaf = row_ref.shape[3]
+    fetch = pltpu.make_async_copy(perm_hbm, perm_ref, sems.at[local])
+    fetch.start()
+    fetch.wait()
+    missing = partner(*last)
+    group, child = 0, 0
+    for i in range(2 * groups):
+        found = perm_ref[i] == missing
+        group = jnp.where(found, i // 2, group)
+        child = jnp.where(found, i % 2, child)
+    copies = []
+    for h in range(local):
+        mid = mid_ref[0, h]
+        spread = twisted_rows([mid])
+        zeros = jnp.zeros_like(spread)
+        spread = jnp.concatenate(
+            [jnp.where(child == 0, spread, zeros), jnp.where(child == 1, spread, zeros)], axis=0
+        )
+        top = top_ref[0, h] + jnp.dot(down_ref[group, h], spread, preferred_element_type=F32)
+        top = top.astype(BF16)
+        for t in range(2):
+            rows = twisted_rows([top[t * rank : (t + 1) * rank]])
+            field = jnp.dot(row_ref[h, t, group], rows, preferred_element_type=F32)
+            mix_ref[h, t, pl.ds(0, leaf, stride=2), :] = field[:, :NRHS]
+            mix_ref[h, t, pl.ds(1, leaf, stride=2), :] = field[:, NRHS:]
+            out_ref[h, t] = (field_ref[h, t] + mix_ref[h, t]).astype(BF16)
+        copies.append(pltpu.make_async_copy(out_ref.at[h], out_hbm.at[h], sems.at[h]))
+        copies[-1].start()
+    for copy in copies:
+        copy.wait()
+
+
+def finish(last, perm, down, row, field, top, mid):
+    vmem = pl.BlockSpec(memory_space=pltpu.VMEM)
+    hbm = pl.BlockSpec(memory_space=pltpu.HBM)
+    return pl.pallas_call(
+        functools.partial(finish_kernel, last),
+        out_shape=jax.ShapeDtypeStruct(field.shape, BF16),
+        in_specs=[hbm] + [vmem] * 5,
+        out_specs=hbm,
+        scratch_shapes=[
+            pltpu.VMEM(field.shape, F32),
+            pltpu.VMEM(field.shape, BF16),
+            pltpu.SMEM(perm.shape, jnp.int32),
+            pltpu.SemaphoreType.DMA((field.shape[0] + 1,)),
+        ],
+        compiler_params=PARAMS,
+        cost_estimate=COST,
+        name="finish",
+    )(pltpu.with_memory_space_constraint(perm, pltpu.HBM), down, row, field, top, mid)
 
 
 def send(block, route, dests):
@@ -286,20 +362,25 @@
     row = row_basis.reshape(local, 2, groups, leaf, 2 * rank)
     x = jnp.transpose(x_panels, (0, 2, 3, 1))
     dests = 2 * columns
-    full = [(2, 0), (1, 0), (0, 1), (2, 1), (1, 1), (0, 0)]
-    farther = both_cores(range(columns - 1, 2, -1))
+    two = both_cores((2,))
+    full = both_cores(range(columns - 1, 3, -1)) + [(3, 0), (1, 0), (0, 1), (1, 1), (0, 0)]
+    last = (3, 1)
     if 2 * x.shape[2] == NRHS:
-        halved = farther
+        halved = two
         xs = [x, lax.ppermute(x, "rhs", [(0, 1), (1, 0)])]
         *own_mids, basis, up = own(halved, dests, leaf_count, parent_map, x, basis, up_transfer)
         own_mids = [send(mid, route, dests) for mid, route in zip(own_mids, halved)]
     else:
-        full, halved, own_mids, up = farther + full, [], [], up_transfer
+        full, halved, own_mids, up = two + full, [], [], up_transfer
         xs = [lax.all_gather(x, "rhs", axis=2, tiled=True)]
-    mids = lower(full, halved, dests, leaf_count, parent_map, xs, basis, up)
-    mids = [send(mid, route, dests) for mid, route in zip(mids, full + halved)]
     n = len(full)
-    result = upper(full, halved, mid_perm, down, row, [*mids[:n], *own_mids, *mids[n:]])
+    routes = full + [last] + halved
+    mids = lower(full + [last], halved, dests, leaf_count, parent_map, xs, basis, up)
+    mids = [send(mid, route, dests) for mid, route in zip(mids, routes)]
+    field, top = upper(
+        full, halved, last, mid_perm, down, row, [*mids[:n], *own_mids, *mids[n + 1 :]]
+    )
+    result = finish(last, mid_perm, down, row, field, top, mids[n])
     return result.reshape(1, local, 2, leaf, 2, NRHS)
 
 

time: 35.1 us -> 33.2 us (0.946)
  waiting for transfers between devices: 11 us -> 8.72 us
  Pallas kernels: 7.68 us -> 9.1 us
  local copies, waits for them, and re-layouts: 0.66 us -> 0.02 us
  starting transfers between devices: 15.6 us -> 15.2 us
    ppermute x9, waiting for transfers between devices: 11 us -> 8.72 us  [send(): lax.ppermute(block, ('blk', 'sub'), [(m, m ^ code) for m in range(dests)])]
    pallas_call x1 -> x2, Pallas kernels: 2.64 us -> 4.08 us  [the longest x1 2.21 us: finish(): pl.pallas_call(functools.partial(finish_kernel, last), out_shape=jax.Shap...]
    unnamed x10 -> x6, local copies, waits for them, and re-layouts: 0.66 us -> 0.02 us
    ppermute x9, starting transfers between devices: 12.7 us -> 12.2 us  [send(): lax.ppermute(block, ('blk', 'sub'), [(m, m ^ code) for m in range(dests)])]
  transfers between devices with their start and end apart: 10 -> 10, of which waited for: 3 -> 4; matrix products, arithmetic and copies ran while one was open for 0% -> 0% of each run, Pallas kernels for 14% -> 21%
where the time goes in v6:
time: 33.2 us; the launch traced here: 33.1 us
  starting transfers between devices  15.2 us (46%)
  Pallas kernels  9.1 us (27%)
  waiting for transfers between devices  8.72 us (26%)
    ppermute x9, starting transfers between devices, send(): lax.ppermute(block, ('blk', 'sub'), [(m, m ^ code) for m in range(dests)])  12.2 us
    ppermute x9, waiting for transfers between devices, send(): lax.ppermute(block, ('blk', 'sub'), [(m, m ^ code) for m in range(dests)])  8.72 us
    ppermute x1, starting transfers between devices, on_device(): xs = [x, lax.ppermute(x, 'rhs', [(0, 1), (1, 0)])]  2.94 us
    pallas_call x1, Pallas kernels, own(): pl.pallas_call(functools.partial(own_kernel, routes), out_shape=[block] *...  2.55 us
    pallas_call x1, Pallas kernels, lower(): pl.pallas_call(functools.partial(lower_kernel, full, halved), out_shape=[...  2.47 us
    pallas_call x1, Pallas kernels, finish(): pl.pallas_call(functools.partial(finish_kernel, last), out_shape=jax.Shap...  2.21 us
    pallas_call x1, Pallas kernels, upper(): pl.pallas_call(functools.partial(upper_kernel, full, halved, last), out_s...  1.88 us
  transfers between devices with their start and end apart: 10, of which 4 were waited for; matrix products, arithmetic and copies ran while one was open for 0% of the time, Pallas kernels for 21%

profile of v6, /device:TPU:0, one launch (start us, length us, event | category | flops | bytes accessed | tf_op | source)
XLA Modules:
  0.0 33.1 jit_solution(6113367635975304320)
XLA Ops:
  0.0 2.9 %collective-permute-start = (bf16[2,2,64,128]{3,2,1,0:T(8,128)(2,1)}, bf16[2,2,64,128]{3,2,1,0:T(8,128)(2,1)S(1)}, u32[]{:S(2)}, u32[]{:S(2)}) collective-permute-start(bf16[2,2,64,128]{3,2,1,0:T(8,128)(2,1)} %bitcast.9), channel_id=1, source_target_pairs={{0,2},{2,0},{1,3},{3,1},{4,6},{6,4},{5,7},{7,5},{8,10},{10,8},{9,1... | collective-permute-start | bytes 196616 | tf_op jit(solution)/shard_map/ppermute | solution.py:370
  2.9 0.0 copy-start.2
  2.9 2.5 %own.1 = (bf16[1,4,64,128]{3,2,1,0:T(8,128)(2,1)S(1)}, bf16[1,4,64,128]{3,2,1,0:T(8,128)(2,1)S(1)}, bf16[2,16,128,128]{3,2,1,0:T(8,128)(2,1)S(1)}, bf16[1,32,64,256]{3,2,1,0:T(8,128)(2,1)S(1)}) custom-call(s32[2]{0:T(128)} %count_hbm.3, s32[32]{0:T(128)} %parent_hbm.3, bf16[2,2,64,128]{3,2,1,0:T(8,128)(2,1)} %bitcast.10, bf16[2,16,128,128]{3,2,1,0:T(8,128)(2,1)} %bitcast.12, ...), custom_call_target="tpu_custom_call" | custom-call | flops 1000000 | bytes 10000 | tf_op jit(solution)/shard_map/own/pallas_call | solution.py:121
  5.5 2.7 %collective-permute-start.5 = (bf16[1,4,64,128]{3,2,1,0:T(8,128)(2,1)S(1)}, bf16[1,4,64,128]{3,2,1,0:T(8,128)(2,1)S(1)}, u32[]{:S(2)}, u32[]{:S(2)}) collective-permute-start(bf16[1,4,64,128]{3,2,1,0:T(8,128)(2,1)S(1)} %get-tuple-element.26), channel_id=1, source_target_pairs={{0,8},{1,9},{4,12},{5,13},{8,0},{9,1},{12,4},{13,5},{2,10},{3,11},... | collective-permute-start | bytes 196616 | tf_op jit(solution)/shard_map/ppermute | solution.py:352
  8.2 0.0 collective-permute-start.6
  8.2 0.0 collective-permute-done.refs_1_
  8.2 0.0 copy-done.2
  8.2 0.0 copy-start
  8.2 0.0 copy-start.1
  8.2 2.5 %lower.1 = (bf16[1,4,64,256]{3,2,1,0:T(8,128)(2,1)S(1)}, bf16[1,4,64,256]{3,2,1,0:T(8,128)(2,1)S(1)}, bf16[1,4,64,256]{3,2,1,0:T(8,128)(2,1)S(1)}, bf16[1,4,64,2...) custom-call(s32[2]{0:T(128)} %count_hbm.3, ...), custom_call_target="tpu_custom_call" | custom-call | flops 1000000 | bytes 10000 | tf_op jit(solution)/shard_map/lower/pallas_call | solution.py:187
  10.7 1.8 %collective-permute-start.7 = (bf16[1,4,64,128]{3,2,1,0:T(8,128)(2,1)S(1)}, bf16[1,4,64,128]{3,2,1,0:T(8,128)(2,1)S(1)}, u32[]{:S(2)}, u32[]{:S(2)}) collective-permute-start(bf16[1,4,64,128]{3,2,1,0:T(8,128)(2,1)S(1)} %get-tuple-element.28), channel_id=1, source_target_pairs={{0,8},{1,9},{4,12},{5,13},{8,0},{9,1},{12,4},{13,5},{2,10},{3,11},... | collective-permute-start | bytes 196616 | tf_op jit(solution)/shard_map/ppermute | solution.py:352
  12.5 0.9 %collective-permute-start.8 = (bf16[1,4,64,128]{3,2,1,0:T(8,128)(2,1)S(1)}, bf16[1,4,64,128]{3,2,1,0:T(8,128)(2,1)S(1)}, u32[]{:S(2)}, u32[]{:S(2)}) collective-permute-start(bf16[1,4,64,128]{3,2,1,0:T(8,128)(2,1)S(1)} %get-tuple-element.29), channel_id=1, source_target_pairs={{0,9},{1,8},{4,13},{5,12},{8,1},{9,0},{12,5},{13,4},{2,11},{3,10},... | collective-permute-start | bytes 196616 | tf_op jit(solution)/shard_map/ppermute | solution.py:352
  13.4 3.6 %collective-permute-start.1 = (bf16[1,4,64,256]{3,2,1,0:T(8,128)(2,1)S(1)}, bf16[1,4,64,256]{3,2,1,0:T(8,128)(2,1)S(1)}, u32[]{:S(2)}, u32[]{:S(2)}) collective-permute-start(bf16[1,4,64,256]{3,2,1,0:T(8,128)(2,1)S(1)} %get-tuple-element.21), channel_id=1, source_target_pairs={{0,12},{1,13},{4,8},{5,9},{8,4},{9,5},{12,0},{13,1},{2,14},{3,15},... | collective-permute-start | bytes 393224 | tf_op jit(solution)/shard_map/ppermute | solution.py:352
  17.0 0.0 collective-permute-done.5.refs_5_
  17.0 0.0 collective-permute-start.2
  17.0 0.0 collective-permute-done.6.refs_6_
  17.0 0.1 collective-permute-start.3
  17.1 4.2 %collective-permute-done.7.refs_7_ = bf16[1,4,64,128]{3,2,1,0:T(8,128)(2,1)S(1)} collective-permute-done((bf16[1,4,64,128]{3,2,1,0:T(8,128)(2,1)S(1)}, bf16[1,4,64,128]{3,2,1,0:T(8,128)(2,1)S(1)}, u32[]{:S(2)}, u32[]{:S(2)}) %collective-permute-start.7) | collective-permute-done | bytes 65568 | tf_op jit(solution)/shard_map/ppermute | solution.py:352
  21.4 0.0 collective-permute-start.4
  21.4 1.5 %collective-permute-done.8.refs_8_ = bf16[1,4,64,128]{3,2,1,0:T(8,128)(2,1)S(1)} collective-permute-done((bf16[1,4,64,128]{3,2,1,0:T(8,128)(2,1)S(1)}, bf16[1,4,64,128]{3,2,1,0:T(8,128)(2,1)S(1)}, u32[]{:S(2)}, u32[]{:S(2)}) %collective-permute-start.8) | collective-permute-done | bytes 65568 | tf_op jit(solution)/shard_map/ppermute | solution.py:352
  22.9 3.1 %collective-permute-start.9 = (bf16[1,4,64,256]{3,2,1,0:T(8,128)(2,1)S(1)}, bf16[1,4,64,256]{3,2,1,0:T(8,128)(2,1)S(1)}, u32[]{:S(2)}, u32[]{:S(2)}) collective-permute-start(bf16[1,4,64,256]{3,2,1,0:T(8,128)(2,1)S(1)} %get-tuple-element.32), channel_id=1, source_target_pairs={{0,13},{1,12},{4,9},{5,8},{8,5},{9,4},{12,1},{13,0},{2,15},{3,14},... | collective-permute-start | bytes 393224 | tf_op jit(solution)/shard_map/ppermute | solution.py:352
  26.0 0.0 collective-permute-done.1.refs_0_
  26.1 0.0 collective-permute-done.2.refs_1_
  26.1 0.0 collective-permute-done.3.refs_2_
  26.1 1.5 %collective-permute-done.4.refs_3_ = bf16[1,4,64,256]{3,2,1,0:T(8,128)(2,1)S(1)} collective-permute-done((bf16[1,4,64,256]{3,2,1,0:T(8,128)(2,1)S(1)}, bf16[1,4,64,256]{3,2,1,0:T(8,128)(2,1)S(1)}, u32[]{:S(2)}, u32[]{:S(2)}) %collective-permute-start.4) | collective-permute-done | bytes 131104 | tf_op jit(solution)/shard_map/ppermute | solution.py:352
  27.6 0.0 copy-done
  27.6 0.0 copy-done.1
  27.6 1.9 %upper.1 = (f32[4,2,256,128]{3,2,1,0:T(8,128)S(1)}, f32[2,4,128,256]{3,2,1,0:T(8,128)S(1)}) custom-call(s32[8]{0:T(128)} %perm_hbm.3, bf16[4,4,128,256]{3,2,1,0:T(8,128)(2,1)S(1)} %bitcast.5, bf16[4,2,4,128,128]{4,3,2,1,0:T(8,128)(2,1)S(1)} %bitcast.7, bf16[1,4,64,256]{3,2,1,0:T(8,128)(2,1)S(1)} %collective-permute-done.1.refs_0_, ...), custom_call_target="tpu_custom_call" | custom-call | flops 1000000 | bytes 10000 | tf_op jit(solution)/shard_map/upper/pallas_call | solution.py:274
  29.5 1.4 %collective-permute-done.9.mid_ref = bf16[1,4,64,256]{3,2,1,0:T(8,128)(2,1)S(1)} collective-permute-done((bf16[1,4,64,256]{3,2,1,0:T(8,128)(2,1)S(1)}, bf16[1,4,64,256]{3,2,1,0:T(8,128)(2,1)S(1)}, u32[]{:S(2)}, u32[]{:S(2)}) %collective-permute-start.9) | collective-permute-done | bytes 131104 | tf_op jit(solution)/shard_map/ppermute | solution.py:352
  30.9 2.2 %finish.1 = bf16[4,2,256,128]{3,2,1,0:T(8,128)(2,1)} custom-call(s32[8]{0:T(128)} %perm_hbm.3, bf16[4,4,128,256]{3,2,1,0:T(8,128)(2,1)S(1)} %bitcast.6, bf16[4,2,4,128,128]{4,3,2,1,0:T(8,128)(2,1)S(1)} %bitcast.8, f32[4,2,256,128]{3,2,1,0:T(8,128)S(1)} %get-tuple-element.30.field_ref, f32[2,4,128,256]{3,2,1,0:T(8,128)S(1)} %get-tuple-element.31.top_ref, ...), custom_call_target="tpu_custom_call" | custom-call | flops 1000000 | bytes 10000 | tf_op jit(solution)/shard_map/finish/pallas_call | solution.py:331
Async XLA Ops:
  0.0 8.2 %collective-permute-start = (bf16[2,2,64,128]{3,2,1,0:T(8,128)(2,1)}, bf16[2,2,64,128]{3,2,1,0:T(8,128)(2,1)S(1)}, u32[]{:S(2)}, u32[]{:S(2)}) collective-permute-start(bf16[2,2,64,128]{3,2,1,0:T(8,128)(2,1)} %bitcast.9), channel_id=1, source_target_pairs={{0,2},{2,0},{1,3},{3,1},{4,6},{6,4},{5,7},{7,5},{8,10},{10,8},{9,1... | collective-permute-start | bytes 196616 | tf_op jit(solution)/shard_map/ppermute | solution.py:370
  2.9 5.2 %copy-start.2 = (bf16[2,128,2,64]{1,3,2,0:T(8,128)(2,1)S(1)}, bf16[2,128,2,64]{1,3,2,0:T(8,128)(2,1)}, u32[]{:S(2)}) copy-start(bf16[2,128,2,64]{1,3,2,0:T(8,128)(2,1)} %param.8) | copy-start | bytes 196612
  5.5 11.5 %collective-permute-start.5 = (bf16[1,4,64,128]{3,2,1,0:T(8,128)(2,1)S(1)}, bf16[1,4,64,128]{3,2,1,0:T(8,128)(2,1)S(1)}, u32[]{:S(2)}, u32[]{:S(2)}) collective-permute-start(bf16[1,4,64,128]{3,2,1,0:T(8,128)(2,1)S(1)} %get-tuple-element.26), channel_id=1, source_target_pairs={{0,8},{1,9},{4,12},{5,13},{8,0},{9,1},{12,4},{13,5},{2,10},{3,11},... | collective-permute-start | bytes 196616 | tf_op jit(solution)/shard_map/ppermute | solution.py:352
  8.2 8.9 %collective-permute-start.6 = (bf16[1,4,64,128]{3,2,1,0:T(8,128)(2,1)S(1)}, bf16[1,4,64,128]{3,2,1,0:T(8,128)(2,1)S(1)}, u32[]{:S(2)}, u32[]{:S(2)}) collective-permute-start(bf16[1,4,64,128]{3,2,1,0:T(8,128)(2,1)S(1)} %get-tuple-element.27), channel_id=1, source_target_pairs={{0,9},{1,8},{4,13},{5,12},{8,1},{9,0},{12,5},{13,4},{2,11},{3,10},... | collective-permute-start | bytes 196616 | tf_op jit(solution)/shard_map/ppermute | solution.py:352
  8.2 19.4 %copy-start = (bf16[4,1,4,2,64,256]{5,4,3,2,1,0:T(8,128)(2,1)S(1)}, bf16[4,1,4,2,64,256]{5,4,3,2,1,0:T(8,128)(2,1)}, u32[]{:S(2)}) copy-start(bf16[4,1,4,2,64,256]{5,4,3,2,1,0:T(8,128)(2,1)} %param.14) | copy-start | bytes 3145732
  8.2 19.4 %copy-start.1 = (bf16[1,4,2,4,128,128]{5,4,3,2,1,0:T(8,128)(2,1)S(1)}, bf16[1,4,2,4,128,128]{5,4,3,2,1,0:T(8,128)(2,1)}, u32[]{:S(2)}) copy-start(bf16[1,4,2,4,128,128]{5,4,3,2,1,0:T(8,128)(2,1)} %param.15) | copy-start | bytes 3145732
  10.7 10.7 %collective-permute-start.7 = (bf16[1,4,64,128]{3,2,1,0:T(8,128)(2,1)S(1)}, bf16[1,4,64,128]{3,2,1,0:T(8,128)(2,1)S(1)}, u32[]{:S(2)}, u32[]{:S(2)}) collective-permute-start(bf16[1,4,64,128]{3,2,1,0:T(8,128)(2,1)S(1)} %get-tuple-element.28), channel_id=1, source_target_pairs={{0,8},{1,9},{4,12},{5,13},{8,0},{9,1},{12,4},{13,5},{2,10},{3,11},... | collective-permute-start | bytes 196616 | tf_op jit(solution)/shard_map/ppermute | solution.py:352
  12.5 10.4 %collective-permute-start.8 = (bf16[1,4,64,128]{3,2,1,0:T(8,128)(2,1)S(1)}, bf16[1,4,64,128]{3,2,1,0:T(8,128)(2,1)S(1)}, u32[]{:S(2)}, u32[]{:S(2)}) collective-permute-start(bf16[1,4,64,128]{3,2,1,0:T(8,128)(2,1)S(1)} %get-tuple-element.29), channel_id=1, source_target_pairs={{0,9},{1,8},{4,13},{5,12},{8,1},{9,0},{12,5},{13,4},{2,11},{3,10},... | collective-permute-start | bytes 196616 | tf_op jit(solution)/shard_map/ppermute | solution.py:352
  13.4 12.6 %collective-permute-start.1 = (bf16[1,4,64,256]{3,2,1,0:T(8,128)(2,1)S(1)}, bf16[1,4,64,256]{3,2,1,0:T(8,128)(2,1)S(1)}, u32[]{:S(2)}, u32[]{:S(2)}) collective-permute-start(bf16[1,4,64,256]{3,2,1,0:T(8,128)(2,1)S(1)} %get-tuple-element.21), channel_id=1, source_target_pairs={{0,12},{1,13},{4,8},{5,9},{8,4},{9,5},{12,0},{13,1},{2,14},{3,15},... | collective-permute-start | bytes 393224 | tf_op jit(solution)/shard_map/ppermute | solution.py:352
  17.0 9.0 %collective-permute-start.2 = (bf16[1,4,64,256]{3,2,1,0:T(8,128)(2,1)S(1)}, bf16[1,4,64,256]{3,2,1,0:T(8,128)(2,1)S(1)}, u32[]{:S(2)}, u32[]{:S(2)}) collective-permute-start(bf16[1,4,64,256]{3,2,1,0:T(8,128)(2,1)S(1)} %get-tuple-element.22), channel_id=1, source_target_pairs={{0,4},{1,5},{4,0},{5,1},{8,12},{9,13},{12,8},{13,9},{2,6},{3,7},{6... | collective-permute-start | bytes 393224 | tf_op jit(solution)/shard_map/ppermute | solution.py:352
  17.0 9.0 %collective-permute-start.3 = (bf16[1,4,64,256]{3,2,1,0:T(8,128)(2,1)S(1)}, bf16[1,4,64,256]{3,2,1,0:T(8,128)(2,1)S(1)}, u32[]{:S(2)}, u32[]{:S(2)}) collective-permute-start(bf16[1,4,64,256]{3,2,1,0:T(8,128)(2,1)S(1)} %get-tuple-element.23), channel_id=1, source_target_pairs={{0,1},{1,0},{4,5},{5,4},{8,9},{9,8},{12,13},{13,12},{2,3},{3,2},{6... | collective-permute-start | bytes 393224 | tf_op jit(solution)/shard_map/ppermute | solution.py:352
  21.4 6.2 %collective-permute-start.4 = (bf16[1,4,64,256]{3,2,1,0:T(8,128)(2,1)S(1)}, bf16[1,4,64,256]{3,2,1,0:T(8,128)(2,1)S(1)}, u32[]{:S(2)}, u32[]{:S(2)}) collective-permute-start(bf16[1,4,64,256]{3,2,1,0:T(8,128)(2,1)S(1)} %get-tuple-element.24), channel_id=1, source_target_pairs={{0,5},{1,4},{4,1},{5,0},{8,13},{9,12},{12,9},{13,8},{2,7},{3,6},{6... | collective-permute-start | bytes 393224 | tf_op jit(solution)/shard_map/ppermute | solution.py:352
  22.9 7.9 %collective-permute-start.9 = (bf16[1,4,64,256]{3,2,1,0:T(8,128)(2,1)S(1)}, bf16[1,4,64,256]{3,2,1,0:T(8,128)(2,1)S(1)}, u32[]{:S(2)}, u32[]{:S(2)}) collective-permute-start(bf16[1,4,64,256]{3,2,1,0:T(8,128)(2,1)S(1)} %get-tuple-element.32), channel_id=1, source_target_pairs={{0,13},{1,12},{4,9},{5,8},{8,5},{9,4},{12,1},{13,0},{2,15},{3,14},... | collective-permute-start | bytes 393224 | tf_op jit(solution)/shard_map/ppermute | solution.py:352

commit v7 on v6

--- a/solution.py
+++ b/solution.py
@@ -38,6 +38,11 @@
                 out[p, h] = cut(mid).astype(BF16)
 
 
+def chunks(count):
+    middle = (count + 1) // 2
+    return [group for group in (range(middle), range(middle, count)) if group]
+
+
 def leaf_stage(spreads, combine, count_ref, basis_ref, g_ref, leaf_ref, ready):
     boxes, dirs, rows, _ = basis_ref.shape
     rank = rows // 2
@@ -45,18 +50,18 @@
     first = lax.axis_index("rhs") * dirs
     even = pl.ds(0, rank, stride=2)
     odd = pl.ds(1, rank, stride=2)
-    for b in range(boxes):
-        ready(b)
+    for b, group in [(b, group) for b in range(boxes) for group in chunks(dirs)]:
+        ready((b, group))
         spread = spreads(b)
-        for d in range(dirs):
+        for d in group:
             g = lax.dot_general(
                 basis_ref[b, d], spread, (((1,), (1,)), ((), ())), preferred_element_type=F32
             )
             g_ref[b * dirs + d, 0] = g[:, :NRHS]
             g_ref[b * dirs + d, 1] = g[:, NRHS:]
-        if b == 0:
+        if b == 0 and 0 in group:
             ready("count")
-        for d in range(dirs):
+        for d in group:
             slot = b * dirs + d
             live = first + d < count_ref[b]
             pieces = combine(
@@ -95,9 +100,11 @@
         "parent": pltpu.make_async_copy(parent_hbm, parent_ref, sems.at[2]),
         "up": pltpu.make_async_copy(up_hbm, up_ref, sems.at[3]),
     }
-    for b in range(boxes):
-        copies[b] = pltpu.make_async_copy(basis_hbm.at[b], basis_ref.at[b], sems.at[4 + b])
-    for name in ["x", 0, "count"] + list(range(1, boxes)) + ["up", "parent"]:
+    parts = [(b, group) for b in range(boxes) for group in chunks(basis_ref.shape[1])]
+    for i, (b, group) in enumerate(parts):
+        at = (b, pl.ds(group.start, len(group)))
+        copies[b, group] = pltpu.make_async_copy(basis_hbm.at[at], basis_ref.at[at], sems.at[4 + i])
+    for name in ["x", parts[0], "count", *parts[1:], "up", "parent"]:
         copies[name].start()
     copies["x"].wait()
 
@@ -130,7 +137,7 @@
             pltpu.VMEM(x.shape, BF16),
             pltpu.VMEM((pairs, dirs, 4 * rank, NRHS), BF16),
             pltpu.VMEM((boxes * dirs, 2, rows, NRHS), F32),
-            pltpu.SemaphoreType.DMA((4 + boxes,)),
+            pltpu.SemaphoreType.DMA((4 + 2 * boxes,)),
         ],
         compiler_params=PARAMS,
         cost_estimate=COST,
@@ -211,7 +218,72 @@
     return jnp.concatenate([rows for top in tops for rows in (top, twist(top))], axis=0)
 
 
-def upper_kernel(full, halved, last, perm_hbm, down_ref, row_ref, *refs):
+def late_groups(late, perm_ref, groups):
+    found = []
+    for route in late:
+        source = partner(*route)
+        group, child = 0, 0
+        for i in range(2 * groups):
+            hit = perm_ref[i] == source
+            group = jnp.where(hit, i // 2, group)
+            child = jnp.where(hit, i % 2, child)
+        found.append((group, child))
+    return found
+
+
+def prep_kernel(late, perm_hbm, down_ref, row_ref, after_ref, down_out, row_out, mix_ref, perm_ref, sem):
+    groups, local = down_ref.shape[:2]
+    leaf, width = row_ref.shape[3:]
+    fetch = pltpu.make_async_copy(perm_hbm, perm_ref, sem.at[0])
+    fetch.start()
+    fetch.wait()
+    found = late_groups(late, perm_ref, groups)
+    (group_a, _), (group_b, _) = found
+    left = lax.broadcasted_iota(jnp.int32, (leaf, width), 1) < width // 2
+    for h in range(local):
+        for i, (group, _) in enumerate(found):
+            block = down_ref[group, h]
+            rows = block.shape[0]
+            for j, (other, child) in enumerate(found):
+                part = jnp.where(child == 0, block[:, :width], block[:, width:])
+                if i != j:
+                    part = jnp.where(group == other, part, jnp.zeros_like(part))
+                if i == 1:
+                    part = jnp.where(group_a == group_b, jnp.zeros_like(part), part)
+                down_out[h, i * rows : (i + 1) * rows, j * width : (j + 1) * width] = part
+            for t in range(2):
+                block = row_ref[h, t, group].astype(F32)
+                slot = (h * 2 + t) * 2 + i
+                mix_ref[slot, pl.ds(0, leaf, stride=2), :] = jnp.where(left, block, -block)
+                mix_ref[slot, pl.ds(1, leaf, stride=2), :] = pltpu.roll(block, width // 2, 1)
+                row_out[h, t, :, i * width : (i + 1) * width] = mix_ref[slot].astype(BF16)
+
+
+def prep(late, perm, down, row, after):
+    groups, local, rows, width = down.shape
+    leaf = row.shape[3]
+    vmem = pl.BlockSpec(memory_space=pltpu.VMEM)
+    hbm = pl.BlockSpec(memory_space=pltpu.HBM)
+    return pl.pallas_call(
+        functools.partial(prep_kernel, late),
+        out_shape=[
+            pltpu.VMEM((local, 2 * rows, width), BF16),
+            pltpu.VMEM((local, 2, 2 * leaf, width), BF16),
+        ],
+        in_specs=[hbm, vmem, vmem, pl.BlockSpec(memory_space=pl.ANY)],
+        out_specs=[vmem] * 2,
+        scratch_shapes=[
+            pltpu.VMEM((4 * local, 2 * leaf, width // 2), F32),
+            pltpu.SMEM(perm.shape, jnp.int32),
+            pltpu.SemaphoreType.DMA((1,)),
+        ],
+        compiler_params=PARAMS,
+        cost_estimate=COST,
+        name="prep",
+    )(pltpu.with_memory_space_constraint(perm, pltpu.HBM), down, row, after)
+
+
+def upper_kernel(full, halved, late, perm_hbm, down_ref, row_ref, *refs):
     n, m = len(full), len(halved)
     mids, own_mids, other_mids = refs[:n], refs[n : n + m], refs[n + m : n + 2 * m]
     field_ref, top_ref, spread_ref, perm_ref, sem = refs[n + 2 * m :]
@@ -240,21 +312,23 @@
         for h in range(local):
             mid = mid_ref[0, h]
             put(partner(k, which), h, mid[:, :NRHS], mid[:, NRHS:])
-    missing = partner(*last)
+    for route in late:
+        for h in range(local):
+            spread_ref[partner(*route), h] = jnp.zeros(spread_ref.shape[2:], BF16)
     for h in range(local):
-        spread_ref[missing, h] = jnp.zeros(spread_ref.shape[2:], BF16)
+        top_ref[1, h] = jnp.zeros(top_ref.shape[2:], F32)
     fetch.wait()
+    (group_a, _), (group_b, _) = late_groups(late, perm_ref, groups)
     for h in range(local):
         tops = ([], [])
         for q in range(groups):
-            children = [perm_ref[2 * q + s] for s in range(2)]
+            parts = [spread_ref[perm_ref[2 * q + s], h] for s in range(2)]
             top = jnp.dot(
-                down_ref[q, h],
-                jnp.concatenate([spread_ref[child, h] for child in children], axis=0),
-                preferred_element_type=F32,
+                down_ref[q, h], jnp.concatenate(parts, axis=0), preferred_element_type=F32
             )
-            lacks = jnp.logical_or(children[0] == missing, children[1] == missing)
-            top_ref[jnp.where(lacks, 0, 1), h] = top
+            is_a, is_b = group_a == q, group_b == q
+            top_ref[jnp.where(is_a, 0, jnp.where(is_b, 1, 2)), h] = top
+            lacks = jnp.logical_or(is_a, is_b)
             top = jnp.where(lacks, jnp.zeros_like(top), top).astype(BF16)
             for t in range(2):
                 tops[t].append(top[t * rank : (t + 1) * rank])
@@ -265,17 +339,17 @@
             field_ref[h, t, pl.ds(1, leaf, stride=2), :] = field[:, NRHS:]
 
 
-def upper(full, halved, last, perm, down, row, mids):
+def upper(full, halved, late, perm, down, row, mids):
     groups, local, _, width = down.shape
     leaf = row.shape[3]
     rank = width // 4
     vmem = pl.BlockSpec(memory_space=pltpu.VMEM)
     hbm = pl.BlockSpec(memory_space=pltpu.HBM)
     return pl.pallas_call(
-        functools.partial(upper_kernel, full, halved, last),
+        functools.partial(upper_kernel, full, halved, late),
         out_shape=[
             pltpu.VMEM((local, 2, 2 * leaf, NRHS), F32),
-            pltpu.VMEM((2, local, 2 * rank, 2 * NRHS), F32),
+            pltpu.VMEM((3, local, 2 * rank, 2 * NRHS), F32),
         ],
         in_specs=[hbm] + [vmem] * (2 + len(mids)),
         out_specs=[vmem] * 2,
@@ -290,59 +364,44 @@
     )(pltpu.with_memory_space_constraint(perm, pltpu.HBM), down, row, *mids)
 
 
-def finish_kernel(last, perm_hbm, down_ref, row_ref, field_ref, top_ref, mid_ref, out_hbm, mix_ref, out_ref, perm_ref, sems):
-    groups, local = down_ref.shape[:2]
-    rank = mid_ref.shape[2]
-    leaf = row_ref.shape[3]
-    fetch = pltpu.make_async_copy(perm_hbm, perm_ref, sems.at[local])
-    fetch.start()
-    fetch.wait()
-    missing = partner(*last)
-    group, child = 0, 0
-    for i in range(2 * groups):
-        found = perm_ref[i] == missing
-        group = jnp.where(found, i // 2, group)
-        child = jnp.where(found, i % 2, child)
+def finish_kernel(down_ref, row_ref, field_ref, top_ref, *refs):
+    mids, (out_hbm, out_ref, sems) = refs[:-3], refs[-3:]
+    local = field_ref.shape[0]
+    rank = mids[0].shape[2]
     copies = []
-    for h in range(local):
-        mid = mid_ref[0, h]
-        spread = twisted_rows([mid])
-        zeros = jnp.zeros_like(spread)
-        spread = jnp.concatenate(
-            [jnp.where(child == 0, spread, zeros), jnp.where(child == 1, spread, zeros)], axis=0
-        )
-        top = top_ref[0, h] + jnp.dot(down_ref[group, h], spread, preferred_element_type=F32)
-        top = top.astype(BF16)
-        for t in range(2):
-            rows = twisted_rows([top[t * rank : (t + 1) * rank]])
-            field = jnp.dot(row_ref[h, t, group], rows, preferred_element_type=F32)
-            mix_ref[h, t, pl.ds(0, leaf, stride=2), :] = field[:, :NRHS]
-            mix_ref[h, t, pl.ds(1, leaf, stride=2), :] = field[:, NRHS:]
-            out_ref[h, t] = (field_ref[h, t] + mix_ref[h, t]).astype(BF16)
-        copies.append(pltpu.make_async_copy(out_ref.at[h], out_hbm.at[h], sems.at[h]))
+    for i, group in enumerate(chunks(local)):
+        for h in group:
+            spread = twisted_rows([mid[0, h] for mid in mids])
+            top = jnp.concatenate([top_ref[0, h], top_ref[1, h]], axis=0)
+            top = top + jnp.dot(down_ref[h], spread, preferred_element_type=F32)
+            top = top.astype(BF16)
+            for t in range(2):
+                pieces = [top[r : r + rank] for r in (t * rank, (2 + t) * rank)]
+                values = jnp.concatenate(
+                    [half for piece in pieces for half in (piece[:, :NRHS], piece[:, NRHS:])],
+                    axis=0,
+                )
+                field = jnp.dot(row_ref[h, t], values, preferred_element_type=F32)
+                out_ref[h, t] = (field_ref[h, t] + field).astype(BF16)
+        at = pl.ds(group.start, len(group))
+        copies.append(pltpu.make_async_copy(out_ref.at[at], out_hbm.at[at], sems.at[i]))
         copies[-1].start()
     for copy in copies:
         copy.wait()
 
 
-def finish(last, perm, down, row, field, top, mid):
+def finish(down, row, field, top, mids):
     vmem = pl.BlockSpec(memory_space=pltpu.VMEM)
-    hbm = pl.BlockSpec(memory_space=pltpu.HBM)
     return pl.pallas_call(
-        functools.partial(finish_kernel, last),
+        finish_kernel,
         out_shape=jax.ShapeDtypeStruct(field.shape, BF16),
-        in_specs=[hbm] + [vmem] * 5,
-        out_specs=hbm,
-        scratch_shapes=[
-            pltpu.VMEM(field.shape, F32),
-            pltpu.VMEM(field.shape, BF16),
-            pltpu.SMEM(perm.shape, jnp.int32),
-            pltpu.SemaphoreType.DMA((field.shape[0] + 1,)),
-        ],
+        in_specs=[vmem] * (4 + len(mids)),
+        out_specs=pl.BlockSpec(memory_space=pltpu.HBM),
+        scratch_shapes=[pltpu.VMEM(field.shape, BF16), pltpu.SemaphoreType.DMA((2,))],
         compiler_params=PARAMS,
         cost_estimate=COST,
         name="finish",
-    )(pltpu.with_memory_space_constraint(perm, pltpu.HBM), down, row, field, top, mid)
+    )(down, row, field, top, *mids)
 
 
 def send(block, route, dests):
@@ -363,8 +422,8 @@
     x = jnp.transpose(x_panels, (0, 2, 3, 1))
     dests = 2 * columns
     two = both_cores((2,))
-    full = both_cores(range(columns - 1, 3, -1)) + [(3, 0), (1, 0), (0, 1), (1, 1), (0, 0)]
-    last = (3, 1)
+    full = both_cores(range(columns - 1, 3, -1)) + [(3, 0), (1, 0), (1, 1), (0, 0)]
+    late = [(3, 1), (0, 1)]
     if 2 * x.shape[2] == NRHS:
         halved = two
         xs = [x, lax.ppermute(x, "rhs", [(0, 1), (1, 0)])]
@@ -374,13 +433,14 @@
         full, halved, own_mids, up = two + full, [], [], up_transfer
         xs = [lax.all_gather(x, "rhs", axis=2, tiled=True)]
     n = len(full)
-    routes = full + [last] + halved
-    mids = lower(full + [last], halved, dests, leaf_count, parent_map, xs, basis, up)
+    routes = full + late + halved
+    mids = lower(full + late, halved, dests, leaf_count, parent_map, xs, basis, up)
     mids = [send(mid, route, dests) for mid, route in zip(mids, routes)]
+    down_late, row_late = prep(late, mid_perm, down, row, [*own_mids, mids[0]][0])
     field, top = upper(
-        full, halved, last, mid_perm, down, row, [*mids[:n], *own_mids, *mids[n + 1 :]]
+        full, halved, late, mid_perm, down, row, [*mids[:n], *own_mids, *mids[n + 2 :]]
     )
-    result = finish(last, mid_perm, down, row, field, top, mids[n])
+    result = finish(down_late, row_late, field, top, mids[n : n + 2])
     return result.reshape(1, local, 2, leaf, 2, NRHS)
 
 

time: 33.2 us -> 34.5 us (1.039)
  Pallas kernels: 9.1 us -> 10.2 us
  starting transfers between devices: 15.2 us -> 16 us
  waiting for transfers between devices: 8.72 us -> 8.07 us
    ppermute x9, starting transfers between devices: 12.2 us -> 13 us  [send(): lax.ppermute(block, ('blk', 'sub'), [(m, m ^ code) for m in range(dests)])]
    pallas_call x2 -> x3, Pallas kernels: 4.08 us -> 4.85 us  [the longest x1 1.87 us: upper(): pl.pallas_call(functools.partial(upper_kernel, full, halved, late), out_s...]
    ppermute x9, waiting for transfers between devices: 8.72 us -> 8.07 us  [send(): lax.ppermute(block, ('blk', 'sub'), [(m, m ^ code) for m in range(dests)])]
  transfers between devices with their start and end apart: 10 -> 10, of which waited for: 4 -> 3; matrix products, arithmetic and copies ran while one was open for 0% -> 0% of each run, Pallas kernels for 21% -> 24%
where the time goes in v7:
time: 34.5 us; the launch traced here: 34.3 us
  starting transfers between devices  16 us (46%)
  Pallas kernels  10.2 us (30%)
  waiting for transfers between devices  8.07 us (23%)
    ppermute x9, starting transfers between devices, send(): lax.ppermute(block, ('blk', 'sub'), [(m, m ^ code) for m in range(dests)])  13 us
    ppermute x9, waiting for transfers between devices, send(): lax.ppermute(block, ('blk', 'sub'), [(m, m ^ code) for m in range(dests)])  8.07 us
    ppermute x1, starting transfers between devices, on_device(): xs = [x, lax.ppermute(x, 'rhs', [(0, 1), (1, 0)])]  2.94 us
    pallas_call x1, Pallas kernels, own(): pl.pallas_call(functools.partial(own_kernel, routes), out_shape=[block] *...  2.78 us
    pallas_call x1, Pallas kernels, lower(): pl.pallas_call(functools.partial(lower_kernel, full, halved), out_shape=[...  2.52 us
    pallas_call x1, Pallas kernels, upper(): pl.pallas_call(functools.partial(upper_kernel, full, halved, late), out_s...  1.87 us
    pallas_call x1, Pallas kernels, finish(): pl.pallas_call(finish_kernel, out_shape=jax.ShapeDtypeStruct(field.shape,...  1.77 us
    pallas_call x1, Pallas kernels, prep(): pl.pallas_call(functools.partial(prep_kernel, late), out_shape=[pltpu.VME...  1.22 us
  transfers between devices with their start and end apart: 10, of which 3 were waited for; matrix products, arithmetic and copies ran while one was open for 0% of the time, Pallas kernels for 24%

profile of v7, /device:TPU:0, one launch (start us, length us, event | category | flops | bytes accessed | tf_op | source)
XLA Modules:
  0.0 34.3 jit_solution(10470537050829461354)
XLA Ops:
  0.0 0.0 copy-start.2
  0.0 2.9 %collective-permute-start.1 = (bf16[2,2,64,128]{3,2,1,0:T(8,128)(2,1)}, bf16[2,2,64,128]{3,2,1,0:T(8,128)(2,1)S(1)}, u32[]{:S(2)}, u32[]{:S(2)}) collective-permute-start(bf16[2,2,64,128]{3,2,1,0:T(8,128)(2,1)} %bitcast.9), channel_id=1, source_target_pairs={{0,2},{2,0},{1,3},{3,1},{4,6},{6,4},{5,7},{7,5},{8,10},{10,8},{9,1... | collective-permute-start | bytes 196616 | tf_op jit(solution)/shard_map/ppermute | solution.py:429
  2.9 2.8 %own.1 = (bf16[1,4,64,128]{3,2,1,0:T(8,128)(2,1)S(1)}, bf16[1,4,64,128]{3,2,1,0:T(8,128)(2,1)S(1)}, bf16[2,16,128,128]{3,2,1,0:T(8,128)(2,1)S(1)}, bf16[1,32,64,256]{3,2,1,0:T(8,128)(2,1)S(1)}) custom-call(s32[2]{0:T(128)} %count_hbm.3, s32[32]{0:T(128)} %parent_hbm.3, bf16[2,2,64,128]{3,2,1,0:T(8,128)(2,1)} %bitcast.10, bf16[2,16,128,128]{3,2,1,0:T(8,128)(2,1)} %bitcast.12, ...), custom_call_target="tpu_custom_call" | custom-call | flops 1000000 | bytes 10000 | tf_op jit(solution)/shard_map/own/pallas_call | solution.py:128
  5.7 0.0 copy-start
  5.7 0.0 copy-start.1
  5.8 2.7 %collective-permute-start = (bf16[1,4,64,128]{3,2,1,0:T(8,128)(2,1)S(1)}, bf16[1,4,64,128]{3,2,1,0:T(8,128)(2,1)S(1)}, u32[]{:S(2)}, u32[]{:S(2)}) collective-permute-start(bf16[1,4,64,128]{3,2,1,0:T(8,128)(2,1)S(1)} %get-tuple-element.21), channel_id=1, source_target_pairs={{0,8},{1,9},{4,12},{5,13},{8,0},{9,1},{12,4},{13,5},{2,10},{3,11},... | collective-permute-start | bytes 196616 | tf_op jit(solution)/shard_map/ppermute | solution.py:411
  8.4 0.0 collective-permute-start.5
  8.4 0.0 collective-permute-done.1.refs_1_
  8.4 0.0 copy-done.2
  8.4 2.5 %lower.1 = (bf16[1,4,64,256]{3,2,1,0:T(8,128)(2,1)S(1)}, bf16[1,4,64,256]{3,2,1,0:T(8,128)(2,1)S(1)}, bf16[1,4,64,256]{3,2,1,0:T(8,128)(2,1)S(1)}, bf16[1,4,64,2...) custom-call(s32[2]{0:T(128)} %count_hbm.3, ...), custom_call_target="tpu_custom_call" | custom-call | flops 1000000 | bytes 10000 | tf_op jit(solution)/shard_map/lower/pallas_call | solution.py:194
  11.0 1.8 %collective-permute-start.6 = (bf16[1,4,64,128]{3,2,1,0:T(8,128)(2,1)S(1)}, bf16[1,4,64,128]{3,2,1,0:T(8,128)(2,1)S(1)}, u32[]{:S(2)}, u32[]{:S(2)}) collective-permute-start(bf16[1,4,64,128]{3,2,1,0:T(8,128)(2,1)S(1)} %get-tuple-element.31), channel_id=1, source_target_pairs={{0,8},{1,9},{4,12},{5,13},{8,0},{9,1},{12,4},{13,5},{2,10},{3,11},... | collective-permute-start | bytes 196616 | tf_op jit(solution)/shard_map/ppermute | solution.py:411
  12.8 0.9 %collective-permute-start.7 = (bf16[1,4,64,128]{3,2,1,0:T(8,128)(2,1)S(1)}, bf16[1,4,64,128]{3,2,1,0:T(8,128)(2,1)S(1)}, u32[]{:S(2)}, u32[]{:S(2)}) collective-permute-start(bf16[1,4,64,128]{3,2,1,0:T(8,128)(2,1)S(1)} %get-tuple-element.32), channel_id=1, source_target_pairs={{0,9},{1,8},{4,13},{5,12},{8,1},{9,0},{12,5},{13,4},{2,11},{3,10},... | collective-permute-start | bytes 196616 | tf_op jit(solution)/shard_map/ppermute | solution.py:411
  13.7 3.6 %collective-permute-start.2 = (bf16[1,4,64,256]{3,2,1,0:T(8,128)(2,1)S(1)}, bf16[1,4,64,256]{3,2,1,0:T(8,128)(2,1)S(1)}, u32[]{:S(2)}, u32[]{:S(2)}) collective-permute-start(bf16[1,4,64,256]{3,2,1,0:T(8,128)(2,1)S(1)} %get-tuple-element.26), channel_id=1, source_target_pairs={{0,12},{1,13},{4,8},{5,9},{8,4},{9,5},{12,0},{13,1},{2,14},{3,15},... | collective-permute-start | bytes 393224 | tf_op jit(solution)/shard_map/ppermute | solution.py:411
  17.3 0.0 collective-permute-done.after_ref.refs_4_
  17.3 0.0 collective-permute-start.3
  17.3 0.0 collective-permute-done.5.refs_5_
  17.3 0.6 %collective-permute-start.4 = (bf16[1,4,64,256]{3,2,1,0:T(8,128)(2,1)S(1)}, bf16[1,4,64,256]{3,2,1,0:T(8,128)(2,1)S(1)}, u32[]{:S(2)}, u32[]{:S(2)}) collective-permute-start(bf16[1,4,64,256]{3,2,1,0:T(8,128)(2,1)S(1)} %get-tuple-element.28), channel_id=1, source_target_pairs={{0,5},{1,4},{4,1},{5,0},{8,13},{9,12},{12,9},{13,8},{2,7},{3,6},{6... | collective-permute-start | bytes 393224 | tf_op jit(solution)/shard_map/ppermute | solution.py:411
  17.9 3.7 %collective-permute-done.6.refs_6_ = bf16[1,4,64,128]{3,2,1,0:T(8,128)(2,1)S(1)} collective-permute-done((bf16[1,4,64,128]{3,2,1,0:T(8,128)(2,1)S(1)}, bf16[1,4,64,128]{3,2,1,0:T(8,128)(2,1)S(1)}, u32[]{:S(2)}, u32[]{:S(2)}) %collective-permute-start.6) | collective-permute-done | bytes 65568 | tf_op jit(solution)/shard_map/ppermute | solution.py:411
  21.6 3.0 %collective-permute-start.8 = (bf16[1,4,64,256]{3,2,1,0:T(8,128)(2,1)S(1)}, bf16[1,4,64,256]{3,2,1,0:T(8,128)(2,1)S(1)}, u32[]{:S(2)}, u32[]{:S(2)}) collective-permute-start(bf16[1,4,64,256]{3,2,1,0:T(8,128)(2,1)S(1)} %get-tuple-element.35), channel_id=1, source_target_pairs={{0,13},{1,12},{4,9},{5,8},{8,5},{9,4},{12,1},{13,0},{2,15},{3,14},... | collective-permute-start | bytes 393224 | tf_op jit(solution)/shard_map/ppermute | solution.py:411
  24.7 0.0 collective-permute-done.7.refs_7_
  24.7 0.4 %collective-permute-start.9 = (bf16[1,4,64,256]{3,2,1,0:T(8,128)(2,1)S(1)}, bf16[1,4,64,256]{3,2,1,0:T(8,128)(2,1)S(1)}, u32[]{:S(2)}, u32[]{:S(2)}) collective-permute-start(bf16[1,4,64,256]{3,2,1,0:T(8,128)(2,1)S(1)} %get-tuple-element.36), channel_id=1, source_target_pairs={{0,1},{1,0},{4,5},{5,4},{8,9},{9,8},{12,13},{13,12},{2,3},{3,2},{6... | collective-permute-start | bytes 393224 | tf_op jit(solution)/shard_map/ppermute | solution.py:411
  25.0 0.0 copy-done
  25.0 0.0 copy-done.1
  25.1 1.2 %prep.1 = (bf16[4,256,256]{2,1,0:T(8,128)(2,1)S(1)}, bf16[4,2,256,256]{3,2,1,0:T(8,128)(2,1)S(1)}) custom-call(s32[8]{0:T(128)} %perm_hbm.3, bf16[4,4,128,256]{3,2,1,0:T(8,128)(2,1)S(1)} %bitcast.5, bf16[4,2,4,128,128]{4,3,2,1,0:T(8,128)(2,1)S(1)} %bitcast.7, bf16[1,4,64,128]{3,2,1,0:T(8,128)(2,1)S(1)} %collective-permute-done.after_ref.refs_4_), custom_call_target="tpu_custom_call" | custom-call | flops 1000000 | bytes 10000 | tf_op jit(solution)/shard_map/prep/pallas_call | solution.py:267
  26.3 0.0 collective-permute-done.2.refs_0_
  26.3 0.1 collective-permute-done.3.refs_1_
  26.3 4.3 %collective-permute-done.4.refs_2_ = bf16[1,4,64,256]{3,2,1,0:T(8,128)(2,1)S(1)} collective-permute-done((bf16[1,4,64,256]{3,2,1,0:T(8,128)(2,1)S(1)}, bf16[1,4,64,256]{3,2,1,0:T(8,128)(2,1)S(1)}, u32[]{:S(2)}, u32[]{:S(2)}) %collective-permute-start.4) | collective-permute-done | bytes 131104 | tf_op jit(solution)/shard_map/ppermute | solution.py:411
  30.7 1.9 %upper.1 = (f32[4,2,256,128]{3,2,1,0:T(8,128)S(1)}, f32[3,4,128,256]{3,2,1,0:T(8,128)S(1)}) custom-call(s32[8]{0:T(128)} %perm_hbm.3, bf16[4,4,128,256]{3,2,1,0:T(8,128)(2,1)S(1)} %bitcast.6, bf16[4,2,4,128,128]{4,3,2,1,0:T(8,128)(2,1)S(1)} %bitcast.8, bf16[1,4,64,256]{3,2,1,0:T(8,128)(2,1)S(1)} %collective-permute-done.2.refs_0_, ...), custom_call_target="tpu_custom_call" | custom-call | flops 1000000 | bytes 10000 | tf_op jit(solution)/shard_map/upper/pallas_call | solution.py:348
  32.5 0.0 collective-permute-done.8.refs_0_
  32.5 0.0 collective-permute-done.9.refs_1_
  32.5 1.8 %finish.1 = bf16[4,2,256,128]{3,2,1,0:T(8,128)(2,1)} custom-call(bf16[4,256,256]{2,1,0:T(8,128)(2,1)S(1)} %get-tuple-element.22.down_ref, bf16[4,2,256,256]{3,2,1,0:T(8,128)(2,1)S(1)} %get-tuple-element.23.row_ref, f32[4,2,256,128]{3,2,1,0:T(8,128)S(1)} %get-tuple-element.33.field_ref, f32[3,4,128,256]{3,2,1,0:T(8,128)S(1)} %get-tuple-element.34.top_ref, ...), custom_call_target="tpu_custom_call" | custom-call | flops 1000000 | bytes 10000 | tf_op jit(solution)/shard_map/finish/pallas_call | solution.py:395
Async XLA Ops:
  0.0 8.4 %copy-start.2 = (bf16[2,128,2,64]{1,3,2,0:T(8,128)(2,1)S(1)}, bf16[2,128,2,64]{1,3,2,0:T(8,128)(2,1)}, u32[]{:S(2)}) copy-start(bf16[2,128,2,64]{1,3,2,0:T(8,128)(2,1)} %param.8) | copy-start | bytes 196612
  0.0 8.4 %collective-permute-start.1 = (bf16[2,2,64,128]{3,2,1,0:T(8,128)(2,1)}, bf16[2,2,64,128]{3,2,1,0:T(8,128)(2,1)S(1)}, u32[]{:S(2)}, u32[]{:S(2)}) collective-permute-start(bf16[2,2,64,128]{3,2,1,0:T(8,128)(2,1)} %bitcast.9), channel_id=1, source_target_pairs={{0,2},{2,0},{1,3},{3,1},{4,6},{6,4},{5,7},{7,5},{8,10},{10,8},{9,1... | collective-permute-start | bytes 196616 | tf_op jit(solution)/shard_map/ppermute | solution.py:429
  5.7 19.3 %copy-start = (bf16[4,1,4,2,64,256]{5,4,3,2,1,0:T(8,128)(2,1)S(1)}, bf16[4,1,4,2,64,256]{5,4,3,2,1,0:T(8,128)(2,1)}, u32[]{:S(2)}) copy-start(bf16[4,1,4,2,64,256]{5,4,3,2,1,0:T(8,128)(2,1)} %param.14) | copy-start | bytes 3145732
  5.7 19.3 %copy-start.1 = (bf16[1,4,2,4,128,128]{5,4,3,2,1,0:T(8,128)(2,1)S(1)}, bf16[1,4,2,4,128,128]{5,4,3,2,1,0:T(8,128)(2,1)}, u32[]{:S(2)}) copy-start(bf16[1,4,2,4,128,128]{5,4,3,2,1,0:T(8,128)(2,1)} %param.15) | copy-start | bytes 3145732
  5.8 11.6 %collective-permute-start = (bf16[1,4,64,128]{3,2,1,0:T(8,128)(2,1)S(1)}, bf16[1,4,64,128]{3,2,1,0:T(8,128)(2,1)S(1)}, u32[]{:S(2)}, u32[]{:S(2)}) collective-permute-start(bf16[1,4,64,128]{3,2,1,0:T(8,128)(2,1)S(1)} %get-tuple-element.21), channel_id=1, source_target_pairs={{0,8},{1,9},{4,12},{5,13},{8,0},{9,1},{12,4},{13,5},{2,10},{3,11},... | collective-permute-start | bytes 196616 | tf_op jit(solution)/shard_map/ppermute | solution.py:411
  8.4 8.9 %collective-permute-start.5 = (bf16[1,4,64,128]{3,2,1,0:T(8,128)(2,1)S(1)}, bf16[1,4,64,128]{3,2,1,0:T(8,128)(2,1)S(1)}, u32[]{:S(2)}, u32[]{:S(2)}) collective-permute-start(bf16[1,4,64,128]{3,2,1,0:T(8,128)(2,1)S(1)} %get-tuple-element.30), channel_id=1, source_target_pairs={{0,9},{1,8},{4,13},{5,12},{8,1},{9,0},{12,5},{13,4},{2,11},{3,10},... | collective-permute-start | bytes 196616 | tf_op jit(solution)/shard_map/ppermute | solution.py:411
  11.0 10.7 %collective-permute-start.6 = (bf16[1,4,64,128]{3,2,1,0:T(8,128)(2,1)S(1)}, bf16[1,4,64,128]{3,2,1,0:T(8,128)(2,1)S(1)}, u32[]{:S(2)}, u32[]{:S(2)}) collective-permute-start(bf16[1,4,64,128]{3,2,1,0:T(8,128)(2,1)S(1)} %get-tuple-element.31), channel_id=1, source_target_pairs={{0,8},{1,9},{4,12},{5,13},{8,0},{9,1},{12,4},{13,5},{2,10},{3,11},... | collective-permute-start | bytes 196616 | tf_op jit(solution)/shard_map/ppermute | solution.py:411
  12.8 11.9 %collective-permute-start.7 = (bf16[1,4,64,128]{3,2,1,0:T(8,128)(2,1)S(1)}, bf16[1,4,64,128]{3,2,1,0:T(8,128)(2,1)S(1)}, u32[]{:S(2)}, u32[]{:S(2)}) collective-permute-start(bf16[1,4,64,128]{3,2,1,0:T(8,128)(2,1)S(1)} %get-tuple-element.32), channel_id=1, source_target_pairs={{0,9},{1,8},{4,13},{5,12},{8,1},{9,0},{12,5},{13,4},{2,11},{3,10},... | collective-permute-start | bytes 196616 | tf_op jit(solution)/shard_map/ppermute | solution.py:411
  13.7 12.5 %collective-permute-start.2 = (bf16[1,4,64,256]{3,2,1,0:T(8,128)(2,1)S(1)}, bf16[1,4,64,256]{3,2,1,0:T(8,128)(2,1)S(1)}, u32[]{:S(2)}, u32[]{:S(2)}) collective-permute-start(bf16[1,4,64,256]{3,2,1,0:T(8,128)(2,1)S(1)} %get-tuple-element.26), channel_id=1, source_target_pairs={{0,12},{1,13},{4,8},{5,9},{8,4},{9,5},{12,0},{13,1},{2,14},{3,15},... | collective-permute-start | bytes 393224 | tf_op jit(solution)/shard_map/ppermute | solution.py:411
  17.3 9.0 %collective-permute-start.3 = (bf16[1,4,64,256]{3,2,1,0:T(8,128)(2,1)S(1)}, bf16[1,4,64,256]{3,2,1,0:T(8,128)(2,1)S(1)}, u32[]{:S(2)}, u32[]{:S(2)}) collective-permute-start(bf16[1,4,64,256]{3,2,1,0:T(8,128)(2,1)S(1)} %get-tuple-element.27), channel_id=1, source_target_pairs={{0,4},{1,5},{4,0},{5,1},{8,12},{9,13},{12,8},{13,9},{2,6},{3,7},{6... | collective-permute-start | bytes 393224 | tf_op jit(solution)/shard_map/ppermute | solution.py:411
  17.3 13.3 %collective-permute-start.4 = (bf16[1,4,64,256]{3,2,1,0:T(8,128)(2,1)S(1)}, bf16[1,4,64,256]{3,2,1,0:T(8,128)(2,1)S(1)}, u32[]{:S(2)}, u32[]{:S(2)}) collective-permute-start(bf16[1,4,64,256]{3,2,1,0:T(8,128)(2,1)S(1)} %get-tuple-element.28), channel_id=1, source_target_pairs={{0,5},{1,4},{4,1},{5,0},{8,13},{9,12},{12,9},{13,8},{2,7},{3,6},{6... | collective-permute-start | bytes 393224 | tf_op jit(solution)/shard_map/ppermute | solution.py:411
  21.6 10.9 %collective-permute-start.8 = (bf16[1,4,64,256]{3,2,1,0:T(8,128)(2,1)S(1)}, bf16[1,4,64,256]{3,2,1,0:T(8,128)(2,1)S(1)}, u32[]{:S(2)}, u32[]{:S(2)}) collective-permute-start(bf16[1,4,64,256]{3,2,1,0:T(8,128)(2,1)S(1)} %get-tuple-element.35), channel_id=1, source_target_pairs={{0,13},{1,12},{4,9},{5,8},{8,5},{9,4},{12,1},{13,0},{2,15},{3,14},... | collective-permute-start | bytes 393224 | tf_op jit(solution)/shard_map/ppermute | solution.py:411
  24.7 7.9 %collective-permute-start.9 = (bf16[1,4,64,256]{3,2,1,0:T(8,128)(2,1)S(1)}, bf16[1,4,64,256]{3,2,1,0:T(8,128)(2,1)S(1)}, u32[]{:S(2)}, u32[]{:S(2)}) collective-permute-start(bf16[1,4,64,256]{3,2,1,0:T(8,128)(2,1)S(1)} %get-tuple-element.36), channel_id=1, source_target_pairs={{0,1},{1,0},{4,5},{5,4},{8,9},{9,8},{12,13},{13,12},{2,3},{3,2},{6... | collective-permute-start | bytes 393224 | tf_op jit(solution)/shard_map/ppermute | solution.py:411

commit v8 on v6

--- a/solution.py
+++ b/solution.py
@@ -36,6 +36,11 @@
                     up_ref[p, j], leaf_ref[p, parent_ref[j]], preferred_element_type=F32
                 )
                 out[p, h] = cut(mid).astype(BF16)
+
+
+def chunks(count):
+    middle = (count + 1) // 2
+    return [group for group in (range(middle), range(middle, count)) if group]
 
 
 def leaf_stage(spreads, combine, count_ref, basis_ref, g_ref, leaf_ref, ready):
@@ -211,13 +216,56 @@
     return jnp.concatenate([rows for top in tops for rows in (top, twist(top))], axis=0)
 
 
-def upper_kernel(full, halved, last, perm_hbm, down_ref, row_ref, *refs):
+def late_place(late, perm_ref, groups):
+    source = partner(*late)
+    group, child = 0, 0
+    for i in range(2 * groups):
+        hit = perm_ref[i] == source
+        group = jnp.where(hit, i // 2, group)
+        child = jnp.where(hit, i % 2, child)
+    return group, child
+
+
+def prep_kernel(late, perm_hbm, down_ref, row_ref, after_ref, down_out, row_out, perm_ref, sem):
+    groups, local = down_ref.shape[:2]
+    width = row_ref.shape[4]
+    fetch = pltpu.make_async_copy(perm_hbm, perm_ref, sem.at[0])
+    fetch.start()
+    fetch.wait()
+    group, child = late_place(late, perm_ref, groups)
+    for h in range(local):
+        block = down_ref[group, h]
+        down_out[h] = jnp.where(child == 0, block[:, :width], block[:, width:])
+        for t in range(2):
+            row_out[h, t] = row_ref[h, t, group]
+
+
+def prep(late, perm, down, row, after):
+    local, rows = down.shape[1:3]
+    leaf, width = row.shape[3:]
+    vmem = pl.BlockSpec(memory_space=pltpu.VMEM)
+    hbm = pl.BlockSpec(memory_space=pltpu.HBM)
+    return pl.pallas_call(
+        functools.partial(prep_kernel, late),
+        out_shape=[
+            pltpu.VMEM((local, rows, width), BF16),
+            pltpu.VMEM((local, 2, leaf, width), BF16),
+        ],
+        in_specs=[hbm, vmem, vmem, pl.BlockSpec(memory_space=pl.ANY)],
+        out_specs=[vmem] * 2,
+        scratch_shapes=[pltpu.SMEM(perm.shape, jnp.int32), pltpu.SemaphoreType.DMA((1,))],
+        compiler_params=PARAMS,
+        cost_estimate=COST,
+        name="prep",
+    )(pltpu.with_memory_space_constraint(perm, pltpu.HBM), down, row, after)
+
+
+def upper_kernel(full, halved, late, perm_hbm, down_ref, row_ref, *refs):
     n, m = len(full), len(halved)
     mids, own_mids, other_mids = refs[:n], refs[n : n + m], refs[n + m : n + 2 * m]
     field_ref, top_ref, spread_ref, perm_ref, sem = refs[n + 2 * m :]
     groups, local = down_ref.shape[:2]
     rank = spread_ref.shape[2] // 2
-    leaf = row_ref.shape[3]
     fetch = pltpu.make_async_copy(perm_hbm, perm_ref, sem.at[0])
     fetch.start()
 
@@ -240,41 +288,37 @@
         for h in range(local):
             mid = mid_ref[0, h]
             put(partner(k, which), h, mid[:, :NRHS], mid[:, NRHS:])
-    missing = partner(*last)
     for h in range(local):
-        spread_ref[missing, h] = jnp.zeros(spread_ref.shape[2:], BF16)
+        spread_ref[partner(*late), h] = jnp.zeros(spread_ref.shape[2:], BF16)
     fetch.wait()
+    group, _ = late_place(late, perm_ref, groups)
     for h in range(local):
         tops = ([], [])
         for q in range(groups):
-            children = [perm_ref[2 * q + s] for s in range(2)]
+            parts = [spread_ref[perm_ref[2 * q + s], h] for s in range(2)]
             top = jnp.dot(
-                down_ref[q, h],
-                jnp.concatenate([spread_ref[child, h] for child in children], axis=0),
-                preferred_element_type=F32,
+                down_ref[q, h], jnp.concatenate(parts, axis=0), preferred_element_type=F32
             )
-            lacks = jnp.logical_or(children[0] == missing, children[1] == missing)
+            lacks = group == q
             top_ref[jnp.where(lacks, 0, 1), h] = top
             top = jnp.where(lacks, jnp.zeros_like(top), top).astype(BF16)
             for t in range(2):
                 tops[t].append(top[t * rank : (t + 1) * rank])
         for t in range(2):
             rows = jnp.concatenate([row_ref[h, t, q] for q in range(groups)], axis=1)
-            field = jnp.dot(rows, twisted_rows(tops[t]), preferred_element_type=F32)
-            field_ref[h, t, pl.ds(0, leaf, stride=2), :] = field[:, :NRHS]
-            field_ref[h, t, pl.ds(1, leaf, stride=2), :] = field[:, NRHS:]
-
-
-def upper(full, halved, last, perm, down, row, mids):
+            field_ref[h, t] = jnp.dot(rows, twisted_rows(tops[t]), preferred_element_type=F32)
+
+
+def upper(full, halved, late, perm, down, row, mids):
     groups, local, _, width = down.shape
     leaf = row.shape[3]
     rank = width // 4
     vmem = pl.BlockSpec(memory_space=pltpu.VMEM)
     hbm = pl.BlockSpec(memory_space=pltpu.HBM)
     return pl.pallas_call(
-        functools.partial(upper_kernel, full, halved, last),
+        functools.partial(upper_kernel, full, halved, late),
         out_shape=[
-            pltpu.VMEM((local, 2, 2 * leaf, NRHS), F32),
+            pltpu.VMEM((local, 2, leaf, 2 * NRHS), F32),
             pltpu.VMEM((2, local, 2 * rank, 2 * NRHS), F32),
         ],
         in_specs=[hbm] + [vmem] * (2 + len(mids)),
@@ -290,59 +334,49 @@
     )(pltpu.with_memory_space_constraint(perm, pltpu.HBM), down, row, *mids)
 
 
-def finish_kernel(last, perm_hbm, down_ref, row_ref, field_ref, top_ref, mid_ref, out_hbm, mix_ref, out_ref, perm_ref, sems):
-    groups, local = down_ref.shape[:2]
+def finish_kernel(down_ref, row_ref, field_ref, top_ref, mid_ref, out_hbm, mix_ref, out_ref, sems):
+    local, _, leaf, _ = field_ref.shape
     rank = mid_ref.shape[2]
-    leaf = row_ref.shape[3]
-    fetch = pltpu.make_async_copy(perm_hbm, perm_ref, sems.at[local])
-    fetch.start()
-    fetch.wait()
-    missing = partner(*last)
-    group, child = 0, 0
-    for i in range(2 * groups):
-        found = perm_ref[i] == missing
-        group = jnp.where(found, i // 2, group)
-        child = jnp.where(found, i % 2, child)
     copies = []
-    for h in range(local):
-        mid = mid_ref[0, h]
-        spread = twisted_rows([mid])
-        zeros = jnp.zeros_like(spread)
-        spread = jnp.concatenate(
-            [jnp.where(child == 0, spread, zeros), jnp.where(child == 1, spread, zeros)], axis=0
-        )
-        top = top_ref[0, h] + jnp.dot(down_ref[group, h], spread, preferred_element_type=F32)
-        top = top.astype(BF16)
-        for t in range(2):
-            rows = twisted_rows([top[t * rank : (t + 1) * rank]])
-            field = jnp.dot(row_ref[h, t, group], rows, preferred_element_type=F32)
-            mix_ref[h, t, pl.ds(0, leaf, stride=2), :] = field[:, :NRHS]
-            mix_ref[h, t, pl.ds(1, leaf, stride=2), :] = field[:, NRHS:]
-            out_ref[h, t] = (field_ref[h, t] + mix_ref[h, t]).astype(BF16)
-        copies.append(pltpu.make_async_copy(out_ref.at[h], out_hbm.at[h], sems.at[h]))
+    for i, group in enumerate(chunks(local)):
+        for h in group:
+            top = top_ref[0, h] + jnp.dot(
+                down_ref[h], twisted_rows([mid_ref[0, h]]), preferred_element_type=F32
+            )
+            top = top.astype(BF16)
+            for t in range(2):
+                rows = twisted_rows([top[t * rank : (t + 1) * rank]])
+                field = field_ref[h, t] + jnp.dot(
+                    row_ref[h, t], rows, preferred_element_type=F32
+                )
+                mix_ref[h, t, pl.ds(0, leaf, stride=2), :] = field[:, :NRHS]
+                mix_ref[h, t, pl.ds(1, leaf, stride=2), :] = field[:, NRHS:]
+                out_ref[h, t] = mix_ref[h, t].astype(BF16)
+        at = pl.ds(group.start, len(group))
+        copies.append(pltpu.make_async_copy(out_ref.at[at], out_hbm.at[at], sems.at[i]))
         copies[-1].start()
     for copy in copies:
         copy.wait()
 
 
-def finish(last, perm, down, row, field, top, mid):
+def finish(down, row, field, top, mid):
+    local, _, leaf, _ = field.shape
+    shape = (local, 2, 2 * leaf, NRHS)
     vmem = pl.BlockSpec(memory_space=pltpu.VMEM)
-    hbm = pl.BlockSpec(memory_space=pltpu.HBM)
     return pl.pallas_call(
-        functools.partial(finish_kernel, last),
-        out_shape=jax.ShapeDtypeStruct(field.shape, BF16),
-        in_specs=[hbm] + [vmem] * 5,
-        out_specs=hbm,
+        finish_kernel,
+        out_shape=jax.ShapeDtypeStruct(shape, BF16),
+        in_specs=[vmem] * 5,
+        out_specs=pl.BlockSpec(memory_space=pltpu.HBM),
         scratch_shapes=[
-            pltpu.VMEM(field.shape, F32),
-            pltpu.VMEM(field.shape, BF16),
-            pltpu.SMEM(perm.shape, jnp.int32),
-            pltpu.SemaphoreType.DMA((field.shape[0] + 1,)),
+            pltpu.VMEM(shape, F32),
+            pltpu.VMEM(shape, BF16),
+            pltpu.SemaphoreType.DMA((2,)),
         ],
         compiler_params=PARAMS,
         cost_estimate=COST,
         name="finish",
-    )(pltpu.with_memory_space_constraint(perm, pltpu.HBM), down, row, field, top, mid)
+    )(down, row, field, top, mid)
 
 
 def send(block, route, dests):
@@ -364,7 +398,7 @@
     dests = 2 * columns
     two = both_cores((2,))
     full = both_cores(range(columns - 1, 3, -1)) + [(3, 0), (1, 0), (0, 1), (1, 1), (0, 0)]
-    last = (3, 1)
+    late = (3, 1)
     if 2 * x.shape[2] == NRHS:
         halved = two
         xs = [x, lax.ppermute(x, "rhs", [(0, 1), (1, 0)])]
@@ -374,13 +408,14 @@
         full, halved, own_mids, up = two + full, [], [], up_transfer
         xs = [lax.all_gather(x, "rhs", axis=2, tiled=True)]
     n = len(full)
-    routes = full + [last] + halved
-    mids = lower(full + [last], halved, dests, leaf_count, parent_map, xs, basis, up)
+    routes = full + [late] + halved
+    mids = lower(full + [late], halved, dests, leaf_count, parent_map, xs, basis, up)
     mids = [send(mid, route, dests) for mid, route in zip(mids, routes)]
+    down_late, row_late = prep(late, mid_perm, down, row, [*own_mids, mids[0]][0])
     field, top = upper(
-        full, halved, last, mid_perm, down, row, [*mids[:n], *own_mids, *mids[n + 1 :]]
+        full, halved, late, mid_perm, down, row, [*mids[:n], *own_mids, *mids[n + 1 :]]
     )
-    result = finish(last, mid_perm, down, row, field, top, mids[n])
+    result = finish(down_late, row_late, field, top, mids[n])
     return result.reshape(1, local, 2, leaf, 2, NRHS)
 
 

time: 33.2 us -> 32.7 us (0.985)
  waiting for transfers between devices: 8.72 us -> 7.97 us
    ppermute x9, waiting for transfers between devices: 8.72 us -> 7.97 us  [send(): lax.ppermute(block, ('blk', 'sub'), [(m, m ^ code) for m in range(dests)])]
    pallas_call x2 -> x3, Pallas kernels: 4.08 us -> 4.22 us  [the longest x1 1.86 us: upper(): pl.pallas_call(functools.partial(upper_kernel, full, halved, late), out_s...]
  transfers between devices with their start and end apart: 10 -> 10, of which waited for: 4 -> 4; matrix products, arithmetic and copies ran while one was open for 0% -> 0% of each run, Pallas kernels for 21% -> 23%
where the time goes in v8:
time: 32.7 us; the launch traced here: 32.5 us
  starting transfers between devices  15.2 us (46%)
  Pallas kernels  9.24 us (28%)
  waiting for transfers between devices  7.97 us (24%)
    ppermute x9, starting transfers between devices, send(): lax.ppermute(block, ('blk', 'sub'), [(m, m ^ code) for m in range(dests)])  12.2 us
    ppermute x9, waiting for transfers between devices, send(): lax.ppermute(block, ('blk', 'sub'), [(m, m ^ code) for m in range(dests)])  7.97 us
    ppermute x1, starting transfers between devices, on_device(): xs = [x, lax.ppermute(x, 'rhs', [(0, 1), (1, 0)])]  2.94 us
    pallas_call x1, Pallas kernels, own(): pl.pallas_call(functools.partial(own_kernel, routes), out_shape=[block] *...  2.55 us
    pallas_call x1, Pallas kernels, lower(): pl.pallas_call(functools.partial(lower_kernel, full, halved), out_shape=[...  2.47 us
    pallas_call x1, Pallas kernels, upper(): pl.pallas_call(functools.partial(upper_kernel, full, halved, late), out_s...  1.86 us
    pallas_call x1, Pallas kernels, finish(): pl.pallas_call(finish_kernel, out_shape=jax.ShapeDtypeStruct(shape, BF16)...  1.63 us
    pallas_call x1, Pallas kernels, prep(): pl.pallas_call(functools.partial(prep_kernel, late), out_shape=[pltpu.VME...  0.73 us
  transfers between devices with their start and end apart: 10, of which 4 were waited for; matrix products, arithmetic and copies ran while one was open for 0% of the time, Pallas kernels for 23%

profile of v8, /device:TPU:0, one launch (start us, length us, event | category | flops | bytes accessed | tf_op | source)
XLA Modules:
  0.0 32.5 jit_solution(3694490730726994340)
XLA Ops:
  0.0 2.9 %collective-permute-start.1 = (bf16[2,2,64,128]{3,2,1,0:T(8,128)(2,1)}, bf16[2,2,64,128]{3,2,1,0:T(8,128)(2,1)S(1)}, u32[]{:S(2)}, u32[]{:S(2)}) collective-permute-start(bf16[2,2,64,128]{3,2,1,0:T(8,128)(2,1)} %bitcast.9), channel_id=1, source_target_pairs={{0,2},{2,0},{1,3},{3,1},{4,6},{6,4},{5,7},{7,5},{8,10},{10,8},{9,1... | collective-permute-start | bytes 196616 | tf_op jit(solution)/shard_map/ppermute | solution.py:404
  2.9 0.0 copy-start.2
  2.9 2.5 %own.1 = (bf16[1,4,64,128]{3,2,1,0:T(8,128)(2,1)S(1)}, bf16[1,4,64,128]{3,2,1,0:T(8,128)(2,1)S(1)}, bf16[2,16,128,128]{3,2,1,0:T(8,128)(2,1)S(1)}, bf16[1,32,64,256]{3,2,1,0:T(8,128)(2,1)S(1)}) custom-call(s32[2]{0:T(128)} %count_hbm.3, s32[32]{0:T(128)} %parent_hbm.3, bf16[2,2,64,128]{3,2,1,0:T(8,128)(2,1)} %bitcast.10, bf16[2,16,128,128]{3,2,1,0:T(8,128)(2,1)} %bitcast.12, ...), custom_call_target="tpu_custom_call" | custom-call | flops 1000000 | bytes 10000 | tf_op jit(solution)/shard_map/own/pallas_call | solution.py:126
  5.5 2.7 %collective-permute-start = (bf16[1,4,64,128]{3,2,1,0:T(8,128)(2,1)S(1)}, bf16[1,4,64,128]{3,2,1,0:T(8,128)(2,1)S(1)}, u32[]{:S(2)}, u32[]{:S(2)}) collective-permute-start(bf16[1,4,64,128]{3,2,1,0:T(8,128)(2,1)S(1)} %get-tuple-element.21), channel_id=1, source_target_pairs={{0,8},{1,9},{4,12},{5,13},{8,0},{9,1},{12,4},{13,5},{2,10},{3,11},... | collective-permute-start | bytes 196616 | tf_op jit(solution)/shard_map/ppermute | solution.py:386
  8.2 0.0 collective-permute-start.6
  8.2 0.0 collective-permute-done.1.refs_1_
  8.2 0.0 copy-done.2
  8.2 0.0 copy-start
  8.2 0.0 copy-start.1
  8.2 2.5 %lower.1 = (bf16[1,4,64,256]{3,2,1,0:T(8,128)(2,1)S(1)}, bf16[1,4,64,256]{3,2,1,0:T(8,128)(2,1)S(1)}, bf16[1,4,64,256]{3,2,1,0:T(8,128)(2,1)S(1)}, bf16[1,4,64,2...) custom-call(s32[2]{0:T(128)} %count_hbm.3, ...), custom_call_target="tpu_custom_call" | custom-call | flops 1000000 | bytes 10000 | tf_op jit(solution)/shard_map/lower/pallas_call | solution.py:192
  10.7 1.8 %collective-permute-start.7 = (bf16[1,4,64,128]{3,2,1,0:T(8,128)(2,1)S(1)}, bf16[1,4,64,128]{3,2,1,0:T(8,128)(2,1)S(1)}, u32[]{:S(2)}, u32[]{:S(2)}) collective-permute-start(bf16[1,4,64,128]{3,2,1,0:T(8,128)(2,1)S(1)} %get-tuple-element.32), channel_id=1, source_target_pairs={{0,8},{1,9},{4,12},{5,13},{8,0},{9,1},{12,4},{13,5},{2,10},{3,11},... | collective-permute-start | bytes 196616 | tf_op jit(solution)/shard_map/ppermute | solution.py:386
  12.5 0.9 %collective-permute-start.8 = (bf16[1,4,64,128]{3,2,1,0:T(8,128)(2,1)S(1)}, bf16[1,4,64,128]{3,2,1,0:T(8,128)(2,1)S(1)}, u32[]{:S(2)}, u32[]{:S(2)}) collective-permute-start(bf16[1,4,64,128]{3,2,1,0:T(8,128)(2,1)S(1)} %get-tuple-element.33), channel_id=1, source_target_pairs={{0,9},{1,8},{4,13},{5,12},{8,1},{9,0},{12,5},{13,4},{2,11},{3,10},... | collective-permute-start | bytes 196616 | tf_op jit(solution)/shard_map/ppermute | solution.py:386
  13.4 3.6 %collective-permute-start.2 = (bf16[1,4,64,256]{3,2,1,0:T(8,128)(2,1)S(1)}, bf16[1,4,64,256]{3,2,1,0:T(8,128)(2,1)S(1)}, u32[]{:S(2)}, u32[]{:S(2)}) collective-permute-start(bf16[1,4,64,256]{3,2,1,0:T(8,128)(2,1)S(1)} %get-tuple-element.26), channel_id=1, source_target_pairs={{0,12},{1,13},{4,8},{5,9},{8,4},{9,5},{12,0},{13,1},{2,14},{3,15},... | collective-permute-start | bytes 393224 | tf_op jit(solution)/shard_map/ppermute | solution.py:386
  17.0 0.0 collective-permute-done.after_ref.refs_5_
  17.0 0.0 collective-permute-start.3
  17.0 0.0 collective-permute-done.6.refs_6_
  17.0 0.1 collective-permute-start.4
  17.1 4.2 %collective-permute-done.7.refs_7_ = bf16[1,4,64,128]{3,2,1,0:T(8,128)(2,1)S(1)} collective-permute-done((bf16[1,4,64,128]{3,2,1,0:T(8,128)(2,1)S(1)}, bf16[1,4,64,128]{3,2,1,0:T(8,128)(2,1)S(1)}, u32[]{:S(2)}, u32[]{:S(2)}) %collective-permute-start.7) | collective-permute-done | bytes 65568 | tf_op jit(solution)/shard_map/ppermute | solution.py:386
  21.4 0.0 collective-permute-start.5
  21.4 1.5 %collective-permute-done.8.refs_8_ = bf16[1,4,64,128]{3,2,1,0:T(8,128)(2,1)S(1)} collective-permute-done((bf16[1,4,64,128]{3,2,1,0:T(8,128)(2,1)S(1)}, bf16[1,4,64,128]{3,2,1,0:T(8,128)(2,1)S(1)}, u32[]{:S(2)}, u32[]{:S(2)}) %collective-permute-start.8) | collective-permute-done | bytes 65568 | tf_op jit(solution)/shard_map/ppermute | solution.py:386
  22.9 3.1 %collective-permute-start.9 = (bf16[1,4,64,256]{3,2,1,0:T(8,128)(2,1)S(1)}, bf16[1,4,64,256]{3,2,1,0:T(8,128)(2,1)S(1)}, u32[]{:S(2)}, u32[]{:S(2)}) collective-permute-start(bf16[1,4,64,256]{3,2,1,0:T(8,128)(2,1)S(1)} %get-tuple-element.36), channel_id=1, source_target_pairs={{0,13},{1,12},{4,9},{5,8},{8,5},{9,4},{12,1},{13,0},{2,15},{3,14},... | collective-permute-start | bytes 393224 | tf_op jit(solution)/shard_map/ppermute | solution.py:386
  26.0 0.0 copy-done
  26.0 0.0 copy-done.1
  26.1 0.7 %prep.1 = (bf16[4,128,128]{2,1,0:T(8,128)(2,1)S(1)}, bf16[4,2,128,128]{3,2,1,0:T(8,128)(2,1)S(1)}) custom-call(s32[8]{0:T(128)} %perm_hbm.3, bf16[4,4,128,256]{3,2,1,0:T(8,128)(2,1)S(1)} %bitcast.5, bf16[4,2,4,128,128]{4,3,2,1,0:T(8,128)(2,1)S(1)} %bitcast.7, bf16[1,4,64,128]{3,2,1,0:T(8,128)(2,1)S(1)} %collective-permute-done.after_ref.refs_5_), custom_call_target="tpu_custom_call" | custom-call | flops 1000000 | bytes 10000 | tf_op jit(solution)/shard_map/prep/pallas_call | solution.py:248
  26.8 0.0 collective-permute-done.2.refs_0_
  26.8 0.0 collective-permute-done.3.refs_1_
  26.8 0.0 collective-permute-done.4.refs_2_
  26.8 0.7 %collective-permute-done.5.refs_3_ = bf16[1,4,64,256]{3,2,1,0:T(8,128)(2,1)S(1)} collective-permute-done((bf16[1,4,64,256]{3,2,1,0:T(8,128)(2,1)S(1)}, bf16[1,4,64,256]{3,2,1,0:T(8,128)(2,1)S(1)}, u32[]{:S(2)}, u32[]{:S(2)}) %collective-permute-start.5) | collective-permute-done | bytes 131104 | tf_op jit(solution)/shard_map/ppermute | solution.py:386
  27.6 1.9 %upper.1 = (f32[4,2,128,256]{3,2,1,0:T(8,128)S(1)}, f32[2,4,128,256]{3,2,1,0:T(8,128)S(1)}) custom-call(s32[8]{0:T(128)} %perm_hbm.3, bf16[4,4,128,256]{3,2,1,0:T(8,128)(2,1)S(1)} %bitcast.6, bf16[4,2,4,128,128]{4,3,2,1,0:T(8,128)(2,1)S(1)} %bitcast.8, bf16[1,4,64,256]{3,2,1,0:T(8,128)(2,1)S(1)} %collective-permute-done.2.refs_0_, ...), custom_call_target="tpu_custom_call" | custom-call | flops 1000000 | bytes 10000 | tf_op jit(solution)/shard_map/upper/pallas_call | solution.py:318
  29.4 1.4 %collective-permute-done.9.mid_ref = bf16[1,4,64,256]{3,2,1,0:T(8,128)(2,1)S(1)} collective-permute-done((bf16[1,4,64,256]{3,2,1,0:T(8,128)(2,1)S(1)}, bf16[1,4,64,256]{3,2,1,0:T(8,128)(2,1)S(1)}, u32[]{:S(2)}, u32[]{:S(2)}) %collective-permute-start.9) | collective-permute-done | bytes 131104 | tf_op jit(solution)/shard_map/ppermute | solution.py:386
  30.9 1.6 %finish.1 = bf16[4,2,256,128]{3,2,1,0:T(8,128)(2,1)} custom-call(bf16[4,128,128]{2,1,0:T(8,128)(2,1)S(1)} %get-tuple-element.22.down_ref, bf16[4,2,128,128]{3,2,1,0:T(8,128)(2,1)S(1)} %get-tuple-element.23.row_ref, f32[4,2,128,256]{3,2,1,0:T(8,128)S(1)} %get-tuple-element.34.field_ref, f32[2,4,128,256]{3,2,1,0:T(8,128)S(1)} %get-tuple-element.35.top_ref, ...), custom_call_target="tpu_custom_call" | custom-call | flops 1000000 | bytes 10000 | tf_op jit(solution)/shard_map/finish/pallas_call | solution.py:366
Async XLA Ops:
  0.0 8.2 %collective-permute-start.1 = (bf16[2,2,64,128]{3,2,1,0:T(8,128)(2,1)}, bf16[2,2,64,128]{3,2,1,0:T(8,128)(2,1)S(1)}, u32[]{:S(2)}, u32[]{:S(2)}) collective-permute-start(bf16[2,2,64,128]{3,2,1,0:T(8,128)(2,1)} %bitcast.9), channel_id=1, source_target_pairs={{0,2},{2,0},{1,3},{3,1},{4,6},{6,4},{5,7},{7,5},{8,10},{10,8},{9,1... | collective-permute-start | bytes 196616 | tf_op jit(solution)/shard_map/ppermute | solution.py:404
  2.9 5.2 %copy-start.2 = (bf16[2,128,2,64]{1,3,2,0:T(8,128)(2,1)S(1)}, bf16[2,128,2,64]{1,3,2,0:T(8,128)(2,1)}, u32[]{:S(2)}) copy-start(bf16[2,128,2,64]{1,3,2,0:T(8,128)(2,1)} %param.8) | copy-start | bytes 196612
  5.5 11.5 %collective-permute-start = (bf16[1,4,64,128]{3,2,1,0:T(8,128)(2,1)S(1)}, bf16[1,4,64,128]{3,2,1,0:T(8,128)(2,1)S(1)}, u32[]{:S(2)}, u32[]{:S(2)}) collective-permute-start(bf16[1,4,64,128]{3,2,1,0:T(8,128)(2,1)S(1)} %get-tuple-element.21), channel_id=1, source_target_pairs={{0,8},{1,9},{4,12},{5,13},{8,0},{9,1},{12,4},{13,5},{2,10},{3,11},... | collective-permute-start | bytes 196616 | tf_op jit(solution)/shard_map/ppermute | solution.py:386
  8.2 8.9 %collective-permute-start.6 = (bf16[1,4,64,128]{3,2,1,0:T(8,128)(2,1)S(1)}, bf16[1,4,64,128]{3,2,1,0:T(8,128)(2,1)S(1)}, u32[]{:S(2)}, u32[]{:S(2)}) collective-permute-start(bf16[1,4,64,128]{3,2,1,0:T(8,128)(2,1)S(1)} %get-tuple-element.31), channel_id=1, source_target_pairs={{0,9},{1,8},{4,13},{5,12},{8,1},{9,0},{12,5},{13,4},{2,11},{3,10},... | collective-permute-start | bytes 196616 | tf_op jit(solution)/shard_map/ppermute | solution.py:386
  8.2 17.9 %copy-start = (bf16[4,1,4,2,64,256]{5,4,3,2,1,0:T(8,128)(2,1)S(1)}, bf16[4,1,4,2,64,256]{5,4,3,2,1,0:T(8,128)(2,1)}, u32[]{:S(2)}) copy-start(bf16[4,1,4,2,64,256]{5,4,3,2,1,0:T(8,128)(2,1)} %param.14) | copy-start | bytes 3145732
  8.2 17.9 %copy-start.1 = (bf16[1,4,2,4,128,128]{5,4,3,2,1,0:T(8,128)(2,1)S(1)}, bf16[1,4,2,4,128,128]{5,4,3,2,1,0:T(8,128)(2,1)}, u32[]{:S(2)}) copy-start(bf16[1,4,2,4,128,128]{5,4,3,2,1,0:T(8,128)(2,1)} %param.15) | copy-start | bytes 3145732
  10.7 10.7 %collective-permute-start.7 = (bf16[1,4,64,128]{3,2,1,0:T(8,128)(2,1)S(1)}, bf16[1,4,64,128]{3,2,1,0:T(8,128)(2,1)S(1)}, u32[]{:S(2)}, u32[]{:S(2)}) collective-permute-start(bf16[1,4,64,128]{3,2,1,0:T(8,128)(2,1)S(1)} %get-tuple-element.32), channel_id=1, source_target_pairs={{0,8},{1,9},{4,12},{5,13},{8,0},{9,1},{12,4},{13,5},{2,10},{3,11},... | collective-permute-start | bytes 196616 | tf_op jit(solution)/shard_map/ppermute | solution.py:386
  12.5 10.4 %collective-permute-start.8 = (bf16[1,4,64,128]{3,2,1,0:T(8,128)(2,1)S(1)}, bf16[1,4,64,128]{3,2,1,0:T(8,128)(2,1)S(1)}, u32[]{:S(2)}, u32[]{:S(2)}) collective-permute-start(bf16[1,4,64,128]{3,2,1,0:T(8,128)(2,1)S(1)} %get-tuple-element.33), channel_id=1, source_target_pairs={{0,9},{1,8},{4,13},{5,12},{8,1},{9,0},{12,5},{13,4},{2,11},{3,10},... | collective-permute-start | bytes 196616 | tf_op jit(solution)/shard_map/ppermute | solution.py:386
  13.4 13.3 %collective-permute-start.2 = (bf16[1,4,64,256]{3,2,1,0:T(8,128)(2,1)S(1)}, bf16[1,4,64,256]{3,2,1,0:T(8,128)(2,1)S(1)}, u32[]{:S(2)}, u32[]{:S(2)}) collective-permute-start(bf16[1,4,64,256]{3,2,1,0:T(8,128)(2,1)S(1)} %get-tuple-element.26), channel_id=1, source_target_pairs={{0,12},{1,13},{4,8},{5,9},{8,4},{9,5},{12,0},{13,1},{2,14},{3,15},... | collective-permute-start | bytes 393224 | tf_op jit(solution)/shard_map/ppermute | solution.py:386
  17.0 9.8 %collective-permute-start.3 = (bf16[1,4,64,256]{3,2,1,0:T(8,128)(2,1)S(1)}, bf16[1,4,64,256]{3,2,1,0:T(8,128)(2,1)S(1)}, u32[]{:S(2)}, u32[]{:S(2)}) collective-permute-start(bf16[1,4,64,256]{3,2,1,0:T(8,128)(2,1)S(1)} %get-tuple-element.27), channel_id=1, source_target_pairs={{0,4},{1,5},{4,0},{5,1},{8,12},{9,13},{12,8},{13,9},{2,6},{3,7},{6... | collective-permute-start | bytes 393224 | tf_op jit(solution)/shard_map/ppermute | solution.py:386
  17.0 9.8 %collective-permute-start.4 = (bf16[1,4,64,256]{3,2,1,0:T(8,128)(2,1)S(1)}, bf16[1,4,64,256]{3,2,1,0:T(8,128)(2,1)S(1)}, u32[]{:S(2)}, u32[]{:S(2)}) collective-permute-start(bf16[1,4,64,256]{3,2,1,0:T(8,128)(2,1)S(1)} %get-tuple-element.28), channel_id=1, source_target_pairs={{0,1},{1,0},{4,5},{5,4},{8,9},{9,8},{12,13},{13,12},{2,3},{3,2},{6... | collective-permute-start | bytes 393224 | tf_op jit(solution)/shard_map/ppermute | solution.py:386
  21.4 6.2 %collective-permute-start.5 = (bf16[1,4,64,256]{3,2,1,0:T(8,128)(2,1)S(1)}, bf16[1,4,64,256]{3,2,1,0:T(8,128)(2,1)S(1)}, u32[]{:S(2)}, u32[]{:S(2)}) collective-permute-start(bf16[1,4,64,256]{3,2,1,0:T(8,128)(2,1)S(1)} %get-tuple-element.29), channel_id=1, source_target_pairs={{0,5},{1,4},{4,1},{5,0},{8,13},{9,12},{12,9},{13,8},{2,7},{3,6},{6... | collective-permute-start | bytes 393224 | tf_op jit(solution)/shard_map/ppermute | solution.py:386
  22.9 7.9 %collective-permute-start.9 = (bf16[1,4,64,256]{3,2,1,0:T(8,128)(2,1)S(1)}, bf16[1,4,64,256]{3,2,1,0:T(8,128)(2,1)S(1)}, u32[]{:S(2)}, u32[]{:S(2)}) collective-permute-start(bf16[1,4,64,256]{3,2,1,0:T(8,128)(2,1)S(1)} %get-tuple-element.36), channel_id=1, source_target_pairs={{0,13},{1,12},{4,9},{5,8},{8,5},{9,4},{12,1},{13,0},{2,15},{3,14},... | collective-permute-start | bytes 393224 | tf_op jit(solution)/shard_map/ppermute | solution.py:386

commit v9 on v8

--- a/solution.py
+++ b/solution.py
@@ -89,10 +89,8 @@
     return even[0] - odd[1], even[1] + odd[0]
 
 
-def own_kernel(routes, count_hbm, parent_hbm, x_hbm, basis_hbm, up_hbm, *refs):
-    n = len(routes)
-    outs, basis_ref, up_ref = refs[:n], refs[n], refs[n + 1]
-    count_ref, parent_ref, x_ref, leaf_ref, g_ref, sems = refs[n + 2 :]
+def own_kernel(routes, count_hbm, parent_hbm, x_hbm, basis_hbm, up_hbm, out_ref, basis_ref, up_ref, *refs):
+    count_ref, parent_ref, x_ref, leaf_ref, g_ref, sems = refs
     boxes = basis_ref.shape[0]
     copies = {
         "x": pltpu.make_async_copy(x_hbm, x_ref, sems.at[0]),
@@ -115,20 +113,20 @@
     )
     copies["up"].wait()
     copies["parent"].wait()
+    outs = [out_ref.at[i] for i in range(len(routes))]
     up_stage(outs, routes, parent_ref, up_ref, leaf_ref)
 
 
 def own(routes, dests, count, parents, x, basis, up):
     boxes, dirs, rows, _ = basis.shape
     pairs, dirs_up, rank, _ = up.shape
-    block = pltpu.VMEM((pairs, dirs_up // dests, rank, NRHS), BF16)
+    block = pltpu.VMEM((len(routes), pairs, dirs_up // dests, rank, NRHS), BF16)
     args = [count, parents, x, basis, up]
     return pl.pallas_call(
         functools.partial(own_kernel, routes),
-        out_shape=[block] * len(routes)
-        + [pltpu.VMEM(basis.shape, BF16), pltpu.VMEM(up.shape, BF16)],
+        out_shape=[block, pltpu.VMEM(basis.shape, BF16), pltpu.VMEM(up.shape, BF16)],
         in_specs=[pl.BlockSpec(memory_space=pltpu.HBM)] * 5,
-        out_specs=[pl.BlockSpec(memory_space=pltpu.VMEM)] * (len(routes) + 2),
+        out_specs=[pl.BlockSpec(memory_space=pltpu.VMEM)] * 3,
         scratch_shapes=[
             pltpu.SMEM(count.shape, jnp.int32),
             pltpu.SMEM(parents.shape, jnp.int32),
@@ -152,10 +150,10 @@
 
 
 def lower_kernel(full, halved, count_hbm, parent_hbm, *refs):
-    n, m = len(full), len(halved)
+    n = len(full) + bool(halved)
     g_ref, leaf_ref, count_ref, parent_ref, sems = refs[-5:]
-    outs = refs[-5 - n - m : -5]
-    *xs, basis_ref, up_ref = refs[: -5 - n - m]
+    outs = refs[-5 - n : -5]
+    *xs, basis_ref, up_ref = refs[: -5 - n]
     copies = {
         "count": pltpu.make_async_copy(count_hbm, count_ref, sems.at[0]),
         "parent": pltpu.make_async_copy(parent_hbm, parent_ref, sems.at[1]),
@@ -177,9 +175,10 @@
 
     leaf_stage(spreads, all_columns, count_ref, basis_ref, g_ref, leaf_ref, ready)
     ready("parent")
-    up_stage(outs[:n], full, parent_ref, up_ref, leaf_ref)
     if halved:
-        up_stage(outs[n:], halved, parent_ref, up_ref, leaf_ref, other_columns)
+        halves = [outs[-1].at[i] for i in range(len(halved))]
+        up_stage(halves, halved, parent_ref, up_ref, leaf_ref, other_columns)
+    up_stage(outs[: len(full)], full, parent_ref, up_ref, leaf_ref)
 
 
 def lower(full, halved, dests, count, parents, xs, basis, up):
@@ -188,11 +187,11 @@
     shape = (pairs, dirs_up // dests, rank)
     hbm = pl.BlockSpec(memory_space=pltpu.HBM)
     vmem = pl.BlockSpec(memory_space=pltpu.VMEM)
-    n = len(full) + len(halved)
+    n = len(full) + bool(halved)
     return pl.pallas_call(
         functools.partial(lower_kernel, full, halved),
         out_shape=[pltpu.VMEM(shape + (2 * NRHS,), BF16)] * len(full)
-        + [pltpu.VMEM(shape + (NRHS,), BF16)] * len(halved),
+        + [pltpu.VMEM((len(halved),) + shape + (NRHS,), BF16)] * bool(halved),
         in_specs=[hbm, hbm] + [vmem] * (2 + len(xs)),
         out_specs=[vmem] * n,
         scratch_shapes=[
@@ -214,6 +213,24 @@
 
 def twisted_rows(tops):
     return jnp.concatenate([rows for top in tops for rows in (top, twist(top))], axis=0)
+
+
+def hand_kernel(own_ref, other_ref, out_ref):
+    out_ref[0] = own_ref[1]
+    out_ref[1] = other_ref[1]
+
+
+def hand(own, other):
+    vmem = pl.BlockSpec(memory_space=pltpu.VMEM)
+    return pl.pallas_call(
+        hand_kernel,
+        out_shape=pltpu.VMEM(own.shape, BF16),
+        in_specs=[vmem] * 2,
+        out_specs=vmem,
+        compiler_params=PARAMS,
+        cost_estimate=COST,
+        name="hand",
+    )(own, other)
 
 
 def late_place(late, perm_ref, groups):
@@ -261,9 +278,12 @@
 
 
 def upper_kernel(full, halved, late, perm_hbm, down_ref, row_ref, *refs):
-    n, m = len(full), len(halved)
-    mids, own_mids, other_mids = refs[:n], refs[n : n + m], refs[n + m : n + 2 * m]
-    field_ref, top_ref, spread_ref, perm_ref, sem = refs[n + 2 * m :]
+    n = len(full)
+    mids, (field_ref, top_ref, spread_ref, perm_ref, sem) = refs[:n], refs[-5:]
+    halves = []
+    if halved:
+        own_ref, other_ref, handed_ref = refs[n:-5]
+        halves = [(own_ref.at[0], other_ref.at[0]), (handed_ref.at[0], handed_ref.at[1])]
     groups, local = down_ref.shape[:2]
     rank = spread_ref.shape[2] // 2
     fetch = pltpu.make_async_copy(perm_hbm, perm_ref, sem.at[0])
@@ -276,7 +296,7 @@
         spread_ref[source, h, rank:, NRHS:] = real
 
     left = lax.broadcasted_iota(jnp.int32, (rank, NRHS), 1) < HALF
-    for own_ref, other_ref, (k, which) in zip(own_mids, other_mids, halved):
+    for (own_ref, other_ref), (k, which) in zip(halves, halved):
         swap = lax.axis_index("rhs") == 1
         for h in range(local):
             low, high = own_ref[0, h].astype(F32), other_ref[0, h].astype(F32)
@@ -397,24 +417,27 @@
     x = jnp.transpose(x_panels, (0, 2, 3, 1))
     dests = 2 * columns
     two = both_cores((2,))
-    full = both_cores(range(columns - 1, 3, -1)) + [(3, 0), (1, 0), (0, 1), (1, 1), (0, 0)]
+    full = both_cores(range(columns - 1, 3, -1)) + [(1, 0), (0, 1), (3, 0), (1, 1), (0, 0)]
     late = (3, 1)
-    if 2 * x.shape[2] == NRHS:
+    split = 2 * x.shape[2] == NRHS
+    swap = [(0, 1), (1, 0)]
+    if split:
         halved = two
-        xs = [x, lax.ppermute(x, "rhs", [(0, 1), (1, 0)])]
-        *own_mids, basis, up = own(halved, dests, leaf_count, parent_map, x, basis, up_transfer)
-        own_mids = [send(mid, route, dests) for mid, route in zip(own_mids, halved)]
+        xs = [x, lax.ppermute(x, "rhs", swap)]
+        own_two, basis, up = own(halved, dests, leaf_count, parent_map, x, basis, up_transfer)
+        own_two = lax.ppermute(own_two, "blk", [(m, m ^ 2) for m in range(columns)])
     else:
-        full, halved, own_mids, up = two + full, [], [], up_transfer
+        full, halved, up = two + full, [], up_transfer
         xs = [lax.all_gather(x, "rhs", axis=2, tiled=True)]
     n = len(full)
-    routes = full + [late] + halved
     mids = lower(full + [late], halved, dests, leaf_count, parent_map, xs, basis, up)
-    mids = [send(mid, route, dests) for mid, route in zip(mids, routes)]
-    down_late, row_late = prep(late, mid_perm, down, row, [*own_mids, mids[0]][0])
-    field, top = upper(
-        full, halved, late, mid_perm, down, row, [*mids[:n], *own_mids, *mids[n + 1 :]]
-    )
+    halves = []
+    if split:
+        other_two = lax.ppermute(mids[-1], "blk", [(m, m ^ 2) for m in range(columns)])
+        halves = [own_two, other_two, lax.ppermute(hand(own_two, other_two), "sub", swap)]
+    mids = [send(mid, route, dests) for mid, route in zip(mids, full + [late])]
+    down_late, row_late = prep(late, mid_perm, down, row, (halves + mids)[0])
+    field, top = upper(full, halved, late, mid_perm, down, row, [*mids[:n], *halves])
     result = finish(down_late, row_late, field, top, mids[n])
     return result.reshape(1, local, 2, leaf, 2, NRHS)
 

time: 32.7 us -> 32.6 us (level)
  the two profiles are of different devices: /device:TPU:0 before, /device:TPU:1 now
where the time goes in v9:
time: 32.6 us; the launch traced here: 32.5 us
  starting transfers between devices  21.3 us (65%)
  Pallas kernels  9.2 us (28%)
  waiting for transfers between devices  1.91 us (6%)
    ppermute x5, starting transfers between devices, send(): lax.ppermute(block, ('blk', 'sub'), [(m, m ^ code) for m in range(dests)])  13.2 us
    ppermute x1, starting transfers between devices, on_device(): lax.ppermute(hand(own_two, other_two), 'sub', swap)  3.55 us
    pallas_call x1, Pallas kernels, own(): pl.pallas_call(functools.partial(own_kernel, routes), out_shape=[block, p...  2.55 us
    pallas_call x1, Pallas kernels, lower(): pl.pallas_call(functools.partial(lower_kernel, full, halved), out_shape=[...  2.4 us
    ppermute x1, starting transfers between devices, on_device(): own_two = lax.ppermute(own_two, 'blk', [(m, m ^ 2) for m in range(columns)])  2.37 us
    ppermute x1, starting transfers between devices, on_device(): xs = [x, lax.ppermute(x, 'rhs', swap)]  2.04 us
    pallas_call x1, Pallas kernels, upper(): pl.pallas_call(functools.partial(upper_kernel, full, halved, late), out_s...  1.88 us
    ppermute x1, waiting for transfers between devices, on_device(): lax.ppermute(mids[-1], 'blk', [(m, m ^ 2) for m in range(columns)])  1.8 us
  transfers between devices with their start and end apart: 9, of which 2 were waited for; matrix products, arithmetic and copies ran while one was open for 0% of the time, Pallas kernels for 23%

profile of v9, /device:TPU:1, one launch (start us, length us, event | category | flops | bytes accessed | tf_op | source)
XLA Modules:
  0.0 32.5 jit_solution(10608108074936120441)
XLA Ops:
  0.0 2.0 %collective-permute-start.1 = (bf16[2,2,64,128]{3,2,1,0:T(8,128)(2,1)}, bf16[2,2,64,128]{3,2,1,0:T(8,128)(2,1)S(1)}, u32[]{:S(2)}, u32[]{:S(2)}) collective-permute-start(bf16[2,2,64,128]{3,2,1,0:T(8,128)(2,1)} %bitcast.9), channel_id=1, source_target_pairs={{0,2},{2,0},{1,3},{3,1},{4,6},{6,4},{5,7},{7,5},{8,10},{10,8},{9,1... | collective-permute-start | bytes 196616 | tf_op jit(solution)/shard_map/ppermute | solution.py:426
  2.0 0.0 copy-start.2
  2.0 2.5 %own.1 = (bf16[2,1,4,64,128]{4,3,2,1,0:T(8,128)(2,1)S(1)}, bf16[2,16,128,128]{3,2,1,0:T(8,128)(2,1)S(1)}, bf16[1,32,64,256]{3,2,1,0:T(8,128)(2,1)S(1)}) custom-call(s32[2]{0:T(128)} %count_hbm.3, s32[32]{0:T(128)} %parent_hbm.3, bf16[2,2,64,128]{3,2,1,0:T(8,128)(2,1)} %bitcast.10, bf16[2,16,128,128]{3,2,1,0:T(8,128)(2,1)} %bitcast.12, ...), custom_call_target="tpu_custom_call" | custom-call | flops 1000000 | bytes 10000 | tf_op jit(solution)/shard_map/own/pallas_call | solution.py:125
  4.6 2.4 %collective-permute-start = (bf16[2,1,4,64,128]{4,3,2,1,0:T(8,128)(2,1)S(1)}, bf16[2,1,4,64,128]{4,3,2,1,0:T(8,128)(2,1)S(1)}, u32[]{:S(2)}, u32[]{:S(2)}) collective-permute-start(bf16[2,1,4,64,128]{4,3,2,1,0:T(8,128)(2,1)S(1)} %get-tuple-element.19), channel_id=1, source_target_pairs={{0,8},{4,12},{8,0},{12,4},{1,9},{5,13},{9,1},{13,5},{2,10},{6,14},... | collective-permute-start | bytes 393224 | tf_op jit(solution)/shard_map/ppermute | solution.py:428
  7.0 0.0 collective-permute-done.1.refs_1_
  7.0 0.0 copy-done.2
  7.0 0.0 copy-start
  7.0 0.0 copy-start.1
  7.0 2.4 %lower.1 = (bf16[1,4,64,256]{3,2,1,0:T(8,128)(2,1)S(1)}, bf16[1,4,64,256]{3,2,1,0:T(8,128)(2,1)S(1)}, bf16[1,4,64,256]{3,2,1,0:T(8,128)(2,1)S(1)}, bf16[1,4,64,2...) custom-call(s32[2]{0:T(128)} %count_hbm.3, ...), custom_call_target="tpu_custom_call" | custom-call | flops 1000000 | bytes 10000 | tf_op jit(solution)/shard_map/lower/pallas_call | solution.py:191
  9.4 0.1 collective-permute-start.6
  9.5 1.3 %collective-permute-start.2 = (bf16[1,4,64,256]{3,2,1,0:T(8,128)(2,1)S(1)}, bf16[1,4,64,256]{3,2,1,0:T(8,128)(2,1)S(1)}, u32[]{:S(2)}, u32[]{:S(2)}) collective-permute-start(bf16[1,4,64,256]{3,2,1,0:T(8,128)(2,1)S(1)} %get-tuple-element.24), channel_id=1, source_target_pairs={{0,4},{1,5},{4,0},{5,1},{8,12},{9,13},{12,8},{13,9},{2,6},{3,7},{6... | collective-permute-start | bytes 393224 | tf_op jit(solution)/shard_map/ppermute | solution.py:406
  10.8 1.8 %collective-permute-start.3 = (bf16[1,4,64,256]{3,2,1,0:T(8,128)(2,1)S(1)}, bf16[1,4,64,256]{3,2,1,0:T(8,128)(2,1)S(1)}, u32[]{:S(2)}, u32[]{:S(2)}) collective-permute-start(bf16[1,4,64,256]{3,2,1,0:T(8,128)(2,1)S(1)} %get-tuple-element.25), channel_id=1, source_target_pairs={{0,1},{1,0},{4,5},{5,4},{8,9},{9,8},{12,13},{13,12},{2,3},{3,2},{6... | collective-permute-start | bytes 393224 | tf_op jit(solution)/shard_map/ppermute | solution.py:406
  12.6 2.2 %collective-permute-start.4 = (bf16[1,4,64,256]{3,2,1,0:T(8,128)(2,1)S(1)}, bf16[1,4,64,256]{3,2,1,0:T(8,128)(2,1)S(1)}, u32[]{:S(2)}, u32[]{:S(2)}) collective-permute-start(bf16[1,4,64,256]{3,2,1,0:T(8,128)(2,1)S(1)} %get-tuple-element.26), channel_id=1, source_target_pairs={{0,12},{1,13},{4,8},{5,9},{8,4},{9,5},{12,0},{13,1},{2,14},{3,15},... | collective-permute-start | bytes 393224 | tf_op jit(solution)/shard_map/ppermute | solution.py:406
  14.8 0.0 collective-permute-done.after_ref.own_ref.refs_5_
  14.8 2.9 %collective-permute-start.5 = (bf16[1,4,64,256]{3,2,1,0:T(8,128)(2,1)S(1)}, bf16[1,4,64,256]{3,2,1,0:T(8,128)(2,1)S(1)}, u32[]{:S(2)}, u32[]{:S(2)}) collective-permute-start(bf16[1,4,64,256]{3,2,1,0:T(8,128)(2,1)S(1)} %get-tuple-element.27), channel_id=1, source_target_pairs={{0,5},{1,4},{4,1},{5,0},{8,13},{9,12},{12,9},{13,8},{2,7},{3,6},{6... | collective-permute-start | bytes 393224 | tf_op jit(solution)/shard_map/ppermute | solution.py:406
  17.7 1.8 %collective-permute-done.6.other_ref.refs_6_ = bf16[2,1,4,64,128]{4,3,2,1,0:T(8,128)(2,1)S(1)} collective-permute-done((bf16[2,1,4,64,128]{4,3,2,1,0:T(8,128)(2,1)S(1)}, bf16[2,1,4,64,128]{4,3,2,1,0:T(8,128)(2,1)S(1)}, u32[]{:S(2)}, u32[]{:S(2)}) %collective-permute-start.6) | collective-permute-done | bytes 131104 | tf_op jit(solution)/shard_map/ppermute | solution.py:436
  19.6 3.6 %collective-permute-start.7 = (bf16[2,1,4,64,128]{4,3,2,1,0:T(8,128)(2,1)S(1)}, bf16[2,1,4,64,128]{4,3,2,1,0:T(8,128)(2,1)S(1)}, u32[]{:S(2)}, u32[]{:S(2)}) collective-permute-start(bf16[2,1,4,64,128]{4,3,2,1,0:T(8,128)(2,1)S(1)} %hand.1), channel_id=1, source_target_pairs={{0,1},{1,0},{2,3},{3,2},{4,5},{5,4},{6,7},{7,6},{8,9},{9,8},{10,11... | collective-permute-start | bytes 393224 | tf_op jit(solution)/shard_map/ppermute | solution.py:437
  23.1 0.0 collective-permute-done.2.refs_0_
  23.1 5.0 %collective-permute-start.8 = (bf16[1,4,64,256]{3,2,1,0:T(8,128)(2,1)S(1)}, bf16[1,4,64,256]{3,2,1,0:T(8,128)(2,1)S(1)}, u32[]{:S(2)}, u32[]{:S(2)}) collective-permute-start(bf16[1,4,64,256]{3,2,1,0:T(8,128)(2,1)S(1)} %get-tuple-element.32), channel_id=1, source_target_pairs={{0,13},{1,12},{4,9},{5,8},{8,5},{9,4},{12,1},{13,0},{2,15},{3,14},... | collective-permute-start | bytes 393224 | tf_op jit(solution)/shard_map/ppermute | solution.py:406
  28.1 0.0 copy-done
  28.1 0.0 copy-done.1
  28.1 0.7 %prep.1 = (bf16[4,128,128]{2,1,0:T(8,128)(2,1)S(1)}, bf16[4,2,128,128]{3,2,1,0:T(8,128)(2,1)S(1)}) custom-call(s32[8]{0:T(128)} %perm_hbm.3, bf16[4,4,128,256]{3,2,1,0:T(8,128)(2,1)S(1)} %bitcast.5, bf16[4,2,4,128,128]{4,3,2,1,0:T(8,128)(2,1)S(1)} %bitcast.7, bf16[2,1,4,64,128]{4,3,2,1,0:T(8,128)(2,1)S(1)} %collective-permute-done.after_ref.own_ref.refs_5_), custom_call_target="tpu_custom_call" | custom-call | flops 1000000 | bytes 10000 | tf_op jit(solution)/shard_map/prep/pallas_call | solution.py:265
  28.8 0.0 collective-permute-done.3.refs_1_
  28.8 0.0 collective-permute-done.4.refs_2_
  28.8 0.0 collective-permute-done.5.refs_3_
  28.9 0.0 collective-permute-done.7.refs_7_
  28.9 1.9 %upper.1 = (f32[4,2,128,256]{3,2,1,0:T(8,128)S(1)}, f32[2,4,128,256]{3,2,1,0:T(8,128)S(1)}) custom-call(s32[8]{0:T(128)} %perm_hbm.3, bf16[4,4,128,256]{3,2,1,0:T(8,128)(2,1)S(1)} %bitcast.6, bf16[4,2,4,128,128]{4,3,2,1,0:T(8,128)(2,1)S(1)} %bitcast.8, bf16[1,4,64,256]{3,2,1,0:T(8,128)(2,1)S(1)} %collective-permute-done.2.refs_0_, ...), custom_call_target="tpu_custom_call" | custom-call | flops 1000000 | bytes 10000 | tf_op jit(solution)/shard_map/upper/pallas_call | solution.py:338
  30.7 0.1 collective-permute-done.8.mid_ref
  30.8 1.6 %finish.1 = bf16[4,2,256,128]{3,2,1,0:T(8,128)(2,1)} custom-call(bf16[4,128,128]{2,1,0:T(8,128)(2,1)S(1)} %get-tuple-element.20.down_ref, bf16[4,2,128,128]{3,2,1,0:T(8,128)(2,1)S(1)} %get-tuple-element.21.row_ref, f32[4,2,128,256]{3,2,1,0:T(8,128)S(1)} %get-tuple-element.30.field_ref, f32[2,4,128,256]{3,2,1,0:T(8,128)S(1)} %get-tuple-element.31.top_ref, ...), custom_call_target="tpu_custom_call" | custom-call | flops 1000000 | bytes 10000 | tf_op jit(solution)/shard_map/finish/pallas_call | solution.py:386
  (1 shorter events, 0.0 us)
Async XLA Ops:
  0.0 7.0 %collective-permute-start.1 = (bf16[2,2,64,128]{3,2,1,0:T(8,128)(2,1)}, bf16[2,2,64,128]{3,2,1,0:T(8,128)(2,1)S(1)}, u32[]{:S(2)}, u32[]{:S(2)}) collective-permute-start(bf16[2,2,64,128]{3,2,1,0:T(8,128)(2,1)} %bitcast.9), channel_id=1, source_target_pairs={{0,2},{2,0},{1,3},{3,1},{4,6},{6,4},{5,7},{7,5},{8,10},{10,8},{9,1... | collective-permute-start | bytes 196616 | tf_op jit(solution)/shard_map/ppermute | solution.py:426
  2.0 4.9 %copy-start.2 = (bf16[2,128,2,64]{1,3,2,0:T(8,128)(2,1)S(1)}, bf16[2,128,2,64]{1,3,2,0:T(8,128)(2,1)}, u32[]{:S(2)}) copy-start(bf16[2,128,2,64]{1,3,2,0:T(8,128)(2,1)} %param.8) | copy-start | bytes 196612
  4.6 10.2 %collective-permute-start = (bf16[2,1,4,64,128]{4,3,2,1,0:T(8,128)(2,1)S(1)}, bf16[2,1,4,64,128]{4,3,2,1,0:T(8,128)(2,1)S(1)}, u32[]{:S(2)}, u32[]{:S(2)}) collective-permute-start(bf16[2,1,4,64,128]{4,3,2,1,0:T(8,128)(2,1)S(1)} %get-tuple-element.19), channel_id=1, source_target_pairs={{0,8},{4,12},{8,0},{12,4},{1,9},{5,13},{9,1},{13,5},{2,10},{6,14},... | collective-permute-start | bytes 393224 | tf_op jit(solution)/shard_map/ppermute | solution.py:428
  7.0 21.1 %copy-start = (bf16[4,1,4,2,64,256]{5,4,3,2,1,0:T(8,128)(2,1)S(1)}, bf16[4,1,4,2,64,256]{5,4,3,2,1,0:T(8,128)(2,1)}, u32[]{:S(2)}) copy-start(bf16[4,1,4,2,64,256]{5,4,3,2,1,0:T(8,128)(2,1)} %param.14) | copy-start | bytes 3145732
  7.0 21.1 %copy-start.1 = (bf16[1,4,2,4,128,128]{5,4,3,2,1,0:T(8,128)(2,1)S(1)}, bf16[1,4,2,4,128,128]{5,4,3,2,1,0:T(8,128)(2,1)}, u32[]{:S(2)}) copy-start(bf16[1,4,2,4,128,128]{5,4,3,2,1,0:T(8,128)(2,1)} %param.15) | copy-start | bytes 3145732
  9.4 10.1 %collective-permute-start.6 = (bf16[2,1,4,64,128]{4,3,2,1,0:T(8,128)(2,1)S(1)}, bf16[2,1,4,64,128]{4,3,2,1,0:T(8,128)(2,1)S(1)}, u32[]{:S(2)}, u32[]{:S(2)}) collective-permute-start(bf16[2,1,4,64,128]{4,3,2,1,0:T(8,128)(2,1)S(1)} %get-tuple-element.29), channel_id=1, source_target_pairs={{0,8},{4,12},{8,0},{12,4},{1,9},{5,13},{9,1},{13,5},{2,10},{6,14},... | collective-permute-start | bytes 393224 | tf_op jit(solution)/shard_map/ppermute | solution.py:436
  9.5 13.6 %collective-permute-start.2 = (bf16[1,4,64,256]{3,2,1,0:T(8,128)(2,1)S(1)}, bf16[1,4,64,256]{3,2,1,0:T(8,128)(2,1)S(1)}, u32[]{:S(2)}, u32[]{:S(2)}) collective-permute-start(bf16[1,4,64,256]{3,2,1,0:T(8,128)(2,1)S(1)} %get-tuple-element.24), channel_id=1, source_target_pairs={{0,4},{1,5},{4,0},{5,1},{8,12},{9,13},{12,8},{13,9},{2,6},{3,7},{6... | collective-permute-start | bytes 393224 | tf_op jit(solution)/shard_map/ppermute | solution.py:406
  10.8 18.0 %collective-permute-start.3 = (bf16[1,4,64,256]{3,2,1,0:T(8,128)(2,1)S(1)}, bf16[1,4,64,256]{3,2,1,0:T(8,128)(2,1)S(1)}, u32[]{:S(2)}, u32[]{:S(2)}) collective-permute-start(bf16[1,4,64,256]{3,2,1,0:T(8,128)(2,1)S(1)} %get-tuple-element.25), channel_id=1, source_target_pairs={{0,1},{1,0},{4,5},{5,4},{8,9},{9,8},{12,13},{13,12},{2,3},{3,2},{6... | collective-permute-start | bytes 393224 | tf_op jit(solution)/shard_map/ppermute | solution.py:406
  12.6 16.2 %collective-permute-start.4 = (bf16[1,4,64,256]{3,2,1,0:T(8,128)(2,1)S(1)}, bf16[1,4,64,256]{3,2,1,0:T(8,128)(2,1)S(1)}, u32[]{:S(2)}, u32[]{:S(2)}) collective-permute-start(bf16[1,4,64,256]{3,2,1,0:T(8,128)(2,1)S(1)} %get-tuple-element.26), channel_id=1, source_target_pairs={{0,12},{1,13},{4,8},{5,9},{8,4},{9,5},{12,0},{13,1},{2,14},{3,15},... | collective-permute-start | bytes 393224 | tf_op jit(solution)/shard_map/ppermute | solution.py:406
  14.8 14.0 %collective-permute-start.5 = (bf16[1,4,64,256]{3,2,1,0:T(8,128)(2,1)S(1)}, bf16[1,4,64,256]{3,2,1,0:T(8,128)(2,1)S(1)}, u32[]{:S(2)}, u32[]{:S(2)}) collective-permute-start(bf16[1,4,64,256]{3,2,1,0:T(8,128)(2,1)S(1)} %get-tuple-element.27), channel_id=1, source_target_pairs={{0,5},{1,4},{4,1},{5,0},{8,13},{9,12},{12,9},{13,8},{2,7},{3,6},{6... | collective-permute-start | bytes 393224 | tf_op jit(solution)/shard_map/ppermute | solution.py:406
  19.6 9.3 %collective-permute-start.7 = (bf16[2,1,4,64,128]{4,3,2,1,0:T(8,128)(2,1)S(1)}, bf16[2,1,4,64,128]{4,3,2,1,0:T(8,128)(2,1)S(1)}, u32[]{:S(2)}, u32[]{:S(2)}) collective-permute-start(bf16[2,1,4,64,128]{4,3,2,1,0:T(8,128)(2,1)S(1)} %hand.1), channel_id=1, source_target_pairs={{0,1},{1,0},{2,3},{3,2},{4,5},{5,4},{6,7},{7,6},{8,9},{9,8},{10,11... | collective-permute-start | bytes 393224 | tf_op jit(solution)/shard_map/ppermute | solution.py:437
  23.1 7.7 %collective-permute-start.8 = (bf16[1,4,64,256]{3,2,1,0:T(8,128)(2,1)S(1)}, bf16[1,4,64,256]{3,2,1,0:T(8,128)(2,1)S(1)}, u32[]{:S(2)}, u32[]{:S(2)}) collective-permute-start(bf16[1,4,64,256]{3,2,1,0:T(8,128)(2,1)S(1)} %get-tuple-element.32), channel_id=1, source_target_pairs={{0,13},{1,12},{4,9},{5,8},{8,5},{9,4},{12,1},{13,0},{2,15},{3,14},... | collective-permute-start | bytes 393224 | tf_op jit(solution)/shard_map/ppermute | solution.py:406

commit v10 on v9

--- a/solution.py
+++ b/solution.py
@@ -417,7 +417,7 @@
     x = jnp.transpose(x_panels, (0, 2, 3, 1))
     dests = 2 * columns
     two = both_cores((2,))
-    full = both_cores(range(columns - 1, 3, -1)) + [(1, 0), (0, 1), (3, 0), (1, 1), (0, 0)]
+    full = both_cores(range(columns - 1, 3, -1)) + [(0, 1), (1, 0), (3, 0), (1, 1), (0, 0)]
     late = (3, 1)
     split = 2 * x.shape[2] == NRHS
     swap = [(0, 1), (1, 0)]

time: 32.6 us -> 33 us (1.012)
  the two profiles are of different devices: /device:TPU:1 before, /device:TPU:29 now
where the time goes in v10:
time: 33 us; the launch traced here: 32.9 us
  waiting for transfers between devices  16.5 us (50%)
  Pallas kernels  9.19 us (28%)
  starting transfers between devices  7.13 us (22%)
    ppermute x5, waiting for transfers between devices, send(): lax.ppermute(block, ('blk', 'sub'), [(m, m ^ code) for m in range(dests)])  6.58 us
    ppermute x1, waiting for transfers between devices, on_device(): lax.ppermute(mids[-1], 'blk', [(m, m ^ 2) for m in range(columns)])  5.43 us
    ppermute x1, waiting for transfers between devices, on_device(): own_two = lax.ppermute(own_two, 'blk', [(m, m ^ 2) for m in range(columns)])  4.43 us
    ppermute x5, starting transfers between devices, send(): lax.ppermute(block, ('blk', 'sub'), [(m, m ^ code) for m in range(dests)])  2.77 us
    pallas_call x1, Pallas kernels, own(): pl.pallas_call(functools.partial(own_kernel, routes), out_shape=[block, p...  2.54 us
    pallas_call x1, Pallas kernels, lower(): pl.pallas_call(functools.partial(lower_kernel, full, halved), out_shape=[...  2.4 us
    ppermute x1, starting transfers between devices, on_device(): lax.ppermute(mids[-1], 'blk', [(m, m ^ 2) for m in range(columns)])  2.37 us
    pallas_call x1, Pallas kernels, upper(): pl.pallas_call(functools.partial(upper_kernel, full, halved, late), out_s...  1.87 us
  transfers between devices with their start and end apart: 9, of which 4 were waited for; matrix products, arithmetic and copies ran while one was open for 0% of the time, Pallas kernels for 23%

profile of v10, /device:TPU:29, one launch (start us, length us, event | category | flops | bytes accessed | tf_op | source)
XLA Modules:
  0.0 32.9 jit_solution(12475565622936833682)
XLA Ops:
  0.0 1.2 %collective-permute-start.1 = (bf16[2,2,64,128]{3,2,1,0:T(8,128)(2,1)}, bf16[2,2,64,128]{3,2,1,0:T(8,128)(2,1)S(1)}, u32[]{:S(2)}, u32[]{:S(2)}) collective-permute-start(bf16[2,2,64,128]{3,2,1,0:T(8,128)(2,1)} %bitcast.9), channel_id=1, source_target_pairs={{0,2},{2,0},{1,3},{3,1},{4,6},{6,4},{5,7},{7,5},{8,10},{10,8},{9,1... | collective-permute-start | bytes 196616 | tf_op jit(solution)/shard_map/ppermute | solution.py:426
  1.2 0.0 copy-start.2
  1.2 2.5 %own.1 = (bf16[2,1,4,64,128]{4,3,2,1,0:T(8,128)(2,1)S(1)}, bf16[2,16,128,128]{3,2,1,0:T(8,128)(2,1)S(1)}, bf16[1,32,64,256]{3,2,1,0:T(8,128)(2,1)S(1)}) custom-call(s32[2]{0:T(128)} %count_hbm.3, s32[32]{0:T(128)} %parent_hbm.3, bf16[2,2,64,128]{3,2,1,0:T(8,128)(2,1)} %bitcast.10, bf16[2,16,128,128]{3,2,1,0:T(8,128)(2,1)} %bitcast.12, ...), custom_call_target="tpu_custom_call" | custom-call | flops 1000000 | bytes 10000 | tf_op jit(solution)/shard_map/own/pallas_call | solution.py:125
  3.8 0.1 collective-permute-start
  3.9 0.0 collective-permute-done.1.refs_1_
  3.9 0.0 copy-done.2
  3.9 0.0 copy-start
  3.9 0.0 copy-start.1
  3.9 2.4 %lower.1 = (bf16[1,4,64,256]{3,2,1,0:T(8,128)(2,1)S(1)}, bf16[1,4,64,256]{3,2,1,0:T(8,128)(2,1)S(1)}, bf16[1,4,64,256]{3,2,1,0:T(8,128)(2,1)S(1)}, bf16[1,4,64,2...) custom-call(s32[2]{0:T(128)} %count_hbm.3, ...), custom_call_target="tpu_custom_call" | custom-call | flops 1000000 | bytes 10000 | tf_op jit(solution)/shard_map/lower/pallas_call | solution.py:191
  6.3 2.4 %collective-permute-start.6 = (bf16[2,1,4,64,128]{4,3,2,1,0:T(8,128)(2,1)S(1)}, bf16[2,1,4,64,128]{4,3,2,1,0:T(8,128)(2,1)S(1)}, u32[]{:S(2)}, u32[]{:S(2)}) collective-permute-start(bf16[2,1,4,64,128]{4,3,2,1,0:T(8,128)(2,1)S(1)} %get-tuple-element.29), channel_id=1, source_target_pairs={{0,8},{4,12},{8,0},{12,4},{1,9},{5,13},{9,1},{13,5},{2,10},{6,14},... | collective-permute-start | bytes 393224 | tf_op jit(solution)/shard_map/ppermute | solution.py:436
  8.7 1.5 %collective-permute-start.2 = (bf16[1,4,64,256]{3,2,1,0:T(8,128)(2,1)S(1)}, bf16[1,4,64,256]{3,2,1,0:T(8,128)(2,1)S(1)}, u32[]{:S(2)}, u32[]{:S(2)}) collective-permute-start(bf16[1,4,64,256]{3,2,1,0:T(8,128)(2,1)S(1)} %get-tuple-element.24), channel_id=1, source_target_pairs={{0,1},{1,0},{4,5},{5,4},{8,9},{9,8},{12,13},{13,12},{2,3},{3,2},{6... | collective-permute-start | bytes 393224 | tf_op jit(solution)/shard_map/ppermute | solution.py:406
  10.2 0.2 collective-permute-start.3
  10.4 1.1 %collective-permute-start.4 = (bf16[1,4,64,256]{3,2,1,0:T(8,128)(2,1)S(1)}, bf16[1,4,64,256]{3,2,1,0:T(8,128)(2,1)S(1)}, u32[]{:S(2)}, u32[]{:S(2)}) collective-permute-start(bf16[1,4,64,256]{3,2,1,0:T(8,128)(2,1)S(1)} %get-tuple-element.26), channel_id=1, source_target_pairs={{0,12},{1,13},{4,8},{5,9},{8,4},{9,5},{12,0},{13,1},{2,14},{3,15},... | collective-permute-start | bytes 393224 | tf_op jit(solution)/shard_map/ppermute | solution.py:406
  11.5 4.4 %collective-permute-done.after_ref.own_ref.refs_5_ = bf16[2,1,4,64,128]{4,3,2,1,0:T(8,128)(2,1)S(1)} collective-permute-done((bf16[2,1,4,64,128]{4,3,2,1,0:T(8,128)(2,1)S(1)}, bf16[2,1,4,64,128]{4,3,2,1,0:T(8,128)(2,1)S(1)}, u32[]{:S(2)}, u32[]{:S(2)}) %collective-permute-start) | collective-permute-done | bytes 131104 | tf_op jit(solution)/shard_map/ppermute | solution.py:428
  15.9 0.0 collective-permute-start.5
  15.9 5.4 %collective-permute-done.6.other_ref.refs_6_ = bf16[2,1,4,64,128]{4,3,2,1,0:T(8,128)(2,1)S(1)} collective-permute-done((bf16[2,1,4,64,128]{4,3,2,1,0:T(8,128)(2,1)S(1)}, bf16[2,1,4,64,128]{4,3,2,1,0:T(8,128)(2,1)S(1)}, u32[]{:S(2)}, u32[]{:S(2)}) %collective-permute-start.6) | collective-permute-done | bytes 131104 | tf_op jit(solution)/shard_map/ppermute | solution.py:436
  21.3 0.7 %collective-permute-start.7 = (bf16[2,1,4,64,128]{4,3,2,1,0:T(8,128)(2,1)S(1)}, bf16[2,1,4,64,128]{4,3,2,1,0:T(8,128)(2,1)S(1)}, u32[]{:S(2)}, u32[]{:S(2)}) collective-permute-start(bf16[2,1,4,64,128]{4,3,2,1,0:T(8,128)(2,1)S(1)} %hand.1), channel_id=1, source_target_pairs={{0,1},{1,0},{2,3},{3,2},{4,5},{5,4},{6,7},{7,6},{8,9},{9,8},{10,11... | collective-permute-start | bytes 393224 | tf_op jit(solution)/shard_map/ppermute | solution.py:437
  22.0 0.0 collective-permute-done.2.refs_0_
  22.0 0.0 collective-permute-start.8
  22.0 0.0 copy-done
  22.0 0.0 copy-done.1
  22.0 0.7 %prep.1 = (bf16[4,128,128]{2,1,0:T(8,128)(2,1)S(1)}, bf16[4,2,128,128]{3,2,1,0:T(8,128)(2,1)S(1)}) custom-call(s32[8]{0:T(128)} %perm_hbm.3, bf16[4,4,128,256]{3,2,1,0:T(8,128)(2,1)S(1)} %bitcast.5, bf16[4,2,4,128,128]{4,3,2,1,0:T(8,128)(2,1)S(1)} %bitcast.7, bf16[2,1,4,64,128]{4,3,2,1,0:T(8,128)(2,1)S(1)} %collective-permute-done.after_ref.own_ref.refs_5_), custom_call_target="tpu_custom_call" | custom-call | flops 1000000 | bytes 10000 | tf_op jit(solution)/shard_map/prep/pallas_call | solution.py:265
  22.7 1.0 %collective-permute-done.3.refs_1_ = bf16[1,4,64,256]{3,2,1,0:T(8,128)(2,1)S(1)} collective-permute-done((bf16[1,4,64,256]{3,2,1,0:T(8,128)(2,1)S(1)}, bf16[1,4,64,256]{3,2,1,0:T(8,128)(2,1)S(1)}, u32[]{:S(2)}, u32[]{:S(2)}) %collective-permute-start.3) | collective-permute-done | bytes 131104 | tf_op jit(solution)/shard_map/ppermute | solution.py:406
  23.7 0.0 collective-permute-done.4.refs_2_
  23.7 5.6 %collective-permute-done.5.refs_3_ = bf16[1,4,64,256]{3,2,1,0:T(8,128)(2,1)S(1)} collective-permute-done((bf16[1,4,64,256]{3,2,1,0:T(8,128)(2,1)S(1)}, bf16[1,4,64,256]{3,2,1,0:T(8,128)(2,1)S(1)}, u32[]{:S(2)}, u32[]{:S(2)}) %collective-permute-start.5) | collective-permute-done | bytes 131104 | tf_op jit(solution)/shard_map/ppermute | solution.py:406
  29.3 0.0 collective-permute-done.7.refs_7_
  29.3 1.9 %upper.1 = (f32[4,2,128,256]{3,2,1,0:T(8,128)S(1)}, f32[2,4,128,256]{3,2,1,0:T(8,128)S(1)}) custom-call(s32[8]{0:T(128)} %perm_hbm.3, bf16[4,4,128,256]{3,2,1,0:T(8,128)(2,1)S(1)} %bitcast.6, bf16[4,2,4,128,128]{4,3,2,1,0:T(8,128)(2,1)S(1)} %bitcast.8, bf16[1,4,64,256]{3,2,1,0:T(8,128)(2,1)S(1)} %collective-permute-done.2.refs_0_, ...), custom_call_target="tpu_custom_call" | custom-call | flops 1000000 | bytes 10000 | tf_op jit(solution)/shard_map/upper/pallas_call | solution.py:338
  31.2 0.0 collective-permute-done.8.mid_ref
  31.2 1.6 %finish.1 = bf16[4,2,256,128]{3,2,1,0:T(8,128)(2,1)} custom-call(bf16[4,128,128]{2,1,0:T(8,128)(2,1)S(1)} %get-tuple-element.20.down_ref, bf16[4,2,128,128]{3,2,1,0:T(8,128)(2,1)S(1)} %get-tuple-element.21.row_ref, f32[4,2,128,256]{3,2,1,0:T(8,128)S(1)} %get-tuple-element.30.field_ref, f32[2,4,128,256]{3,2,1,0:T(8,128)S(1)} %get-tuple-element.31.top_ref, ...), custom_call_target="tpu_custom_call" | custom-call | flops 1000000 | bytes 10000 | tf_op jit(solution)/shard_map/finish/pallas_call | solution.py:386
  (1 shorter events, 0.0 us)
Async XLA Ops:
  0.0 3.9 %collective-permute-start.1 = (bf16[2,2,64,128]{3,2,1,0:T(8,128)(2,1)}, bf16[2,2,64,128]{3,2,1,0:T(8,128)(2,1)S(1)}, u32[]{:S(2)}, u32[]{:S(2)}) collective-permute-start(bf16[2,2,64,128]{3,2,1,0:T(8,128)(2,1)} %bitcast.9), channel_id=1, source_target_pairs={{0,2},{2,0},{1,3},{3,1},{4,6},{6,4},{5,7},{7,5},{8,10},{10,8},{9,1... | collective-permute-start | bytes 196616 | tf_op jit(solution)/shard_map/ppermute | solution.py:426
  1.2 2.7 %copy-start.2 = (bf16[2,128,2,64]{1,3,2,0:T(8,128)(2,1)S(1)}, bf16[2,128,2,64]{1,3,2,0:T(8,128)(2,1)}, u32[]{:S(2)}) copy-start(bf16[2,128,2,64]{1,3,2,0:T(8,128)(2,1)} %param.8) | copy-start | bytes 196612
  3.8 12.1 %collective-permute-start = (bf16[2,1,4,64,128]{4,3,2,1,0:T(8,128)(2,1)S(1)}, bf16[2,1,4,64,128]{4,3,2,1,0:T(8,128)(2,1)S(1)}, u32[]{:S(2)}, u32[]{:S(2)}) collective-permute-start(bf16[2,1,4,64,128]{4,3,2,1,0:T(8,128)(2,1)S(1)} %get-tuple-element.19), channel_id=1, source_target_pairs={{0,8},{4,12},{8,0},{12,4},{1,9},{5,13},{9,1},{13,5},{2,10},{6,14},... | collective-permute-start | bytes 393224 | tf_op jit(solution)/shard_map/ppermute | solution.py:428
  3.9 18.1 %copy-start = (bf16[4,1,4,2,64,256]{5,4,3,2,1,0:T(8,128)(2,1)S(1)}, bf16[4,1,4,2,64,256]{5,4,3,2,1,0:T(8,128)(2,1)}, u32[]{:S(2)}) copy-start(bf16[4,1,4,2,64,256]{5,4,3,2,1,0:T(8,128)(2,1)} %param.14) | copy-start | bytes 3145732
  3.9 18.1 %copy-start.1 = (bf16[1,4,2,4,128,128]{5,4,3,2,1,0:T(8,128)(2,1)S(1)}, bf16[1,4,2,4,128,128]{5,4,3,2,1,0:T(8,128)(2,1)}, u32[]{:S(2)}) copy-start(bf16[1,4,2,4,128,128]{5,4,3,2,1,0:T(8,128)(2,1)} %param.15) | copy-start | bytes 3145732
  6.3 15.0 %collective-permute-start.6 = (bf16[2,1,4,64,128]{4,3,2,1,0:T(8,128)(2,1)S(1)}, bf16[2,1,4,64,128]{4,3,2,1,0:T(8,128)(2,1)S(1)}, u32[]{:S(2)}, u32[]{:S(2)}) collective-permute-start(bf16[2,1,4,64,128]{4,3,2,1,0:T(8,128)(2,1)S(1)} %get-tuple-element.29), channel_id=1, source_target_pairs={{0,8},{4,12},{8,0},{12,4},{1,9},{5,13},{9,1},{13,5},{2,10},{6,14},... | collective-permute-start | bytes 393224 | tf_op jit(solution)/shard_map/ppermute | solution.py:436
  8.7 13.3 %collective-permute-start.2 = (bf16[1,4,64,256]{3,2,1,0:T(8,128)(2,1)S(1)}, bf16[1,4,64,256]{3,2,1,0:T(8,128)(2,1)S(1)}, u32[]{:S(2)}, u32[]{:S(2)}) collective-permute-start(bf16[1,4,64,256]{3,2,1,0:T(8,128)(2,1)S(1)} %get-tuple-element.24), channel_id=1, source_target_pairs={{0,1},{1,0},{4,5},{5,4},{8,9},{9,8},{12,13},{13,12},{2,3},{3,2},{6... | collective-permute-start | bytes 393224 | tf_op jit(solution)/shard_map/ppermute | solution.py:406
  10.2 13.5 %collective-permute-start.3 = (bf16[1,4,64,256]{3,2,1,0:T(8,128)(2,1)S(1)}, bf16[1,4,64,256]{3,2,1,0:T(8,128)(2,1)S(1)}, u32[]{:S(2)}, u32[]{:S(2)}) collective-permute-start(bf16[1,4,64,256]{3,2,1,0:T(8,128)(2,1)S(1)} %get-tuple-element.25), channel_id=1, source_target_pairs={{0,4},{1,5},{4,0},{5,1},{8,12},{9,13},{12,8},{13,9},{2,6},{3,7},{6... | collective-permute-start | bytes 393224 | tf_op jit(solution)/shard_map/ppermute | solution.py:406
  10.4 13.4 %collective-permute-start.4 = (bf16[1,4,64,256]{3,2,1,0:T(8,128)(2,1)S(1)}, bf16[1,4,64,256]{3,2,1,0:T(8,128)(2,1)S(1)}, u32[]{:S(2)}, u32[]{:S(2)}) collective-permute-start(bf16[1,4,64,256]{3,2,1,0:T(8,128)(2,1)S(1)} %get-tuple-element.26), channel_id=1, source_target_pairs={{0,12},{1,13},{4,8},{5,9},{8,4},{9,5},{12,0},{13,1},{2,14},{3,15},... | collective-permute-start | bytes 393224 | tf_op jit(solution)/shard_map/ppermute | solution.py:406
  15.9 13.4 %collective-permute-start.5 = (bf16[1,4,64,256]{3,2,1,0:T(8,128)(2,1)S(1)}, bf16[1,4,64,256]{3,2,1,0:T(8,128)(2,1)S(1)}, u32[]{:S(2)}, u32[]{:S(2)}) collective-permute-start(bf16[1,4,64,256]{3,2,1,0:T(8,128)(2,1)S(1)} %get-tuple-element.27), channel_id=1, source_target_pairs={{0,5},{1,4},{4,1},{5,0},{8,13},{9,12},{12,9},{13,8},{2,7},{3,6},{6... | collective-permute-start | bytes 393224 | tf_op jit(solution)/shard_map/ppermute | solution.py:406
  21.3 8.0 %collective-permute-start.7 = (bf16[2,1,4,64,128]{4,3,2,1,0:T(8,128)(2,1)S(1)}, bf16[2,1,4,64,128]{4,3,2,1,0:T(8,128)(2,1)S(1)}, u32[]{:S(2)}, u32[]{:S(2)}) collective-permute-start(bf16[2,1,4,64,128]{4,3,2,1,0:T(8,128)(2,1)S(1)} %hand.1), channel_id=1, source_target_pairs={{0,1},{1,0},{2,3},{3,2},{4,5},{5,4},{6,7},{7,6},{8,9},{9,8},{10,11... | collective-permute-start | bytes 393224 | tf_op jit(solution)/shard_map/ppermute | solution.py:437
  22.0 9.2 %collective-permute-start.8 = (bf16[1,4,64,256]{3,2,1,0:T(8,128)(2,1)S(1)}, bf16[1,4,64,256]{3,2,1,0:T(8,128)(2,1)S(1)}, u32[]{:S(2)}, u32[]{:S(2)}) collective-permute-start(bf16[1,4,64,256]{3,2,1,0:T(8,128)(2,1)S(1)} %get-tuple-element.32), channel_id=1, source_target_pairs={{0,13},{1,12},{4,9},{5,8},{8,5},{9,4},{12,1},{13,0},{2,15},{3,14},... | collective-permute-start | bytes 393224 | tf_op jit(solution)/shard_map/ppermute | solution.py:406

commit v11 on v10

--- a/solution.py
+++ b/solution.py
@@ -233,28 +233,40 @@
     )(own, other)
 
 
-def late_place(late, perm_ref, groups):
-    source = partner(*late)
-    group, child = 0, 0
-    for i in range(2 * groups):
-        hit = perm_ref[i] == source
-        group = jnp.where(hit, i // 2, group)
-        child = jnp.where(hit, i % 2, child)
-    return group, child
+def late_groups(late, perm_ref, groups):
+    found = []
+    for route in late:
+        source = partner(*route)
+        group, child = 0, 0
+        for i in range(2 * groups):
+            hit = perm_ref[i] == source
+            group = jnp.where(hit, i // 2, group)
+            child = jnp.where(hit, i % 2, child)
+        found.append((group, child))
+    return found
 
 
 def prep_kernel(late, perm_hbm, down_ref, row_ref, after_ref, down_out, row_out, perm_ref, sem):
-    groups, local = down_ref.shape[:2]
+    groups, local, rows = down_ref.shape[:3]
     width = row_ref.shape[4]
     fetch = pltpu.make_async_copy(perm_hbm, perm_ref, sem.at[0])
     fetch.start()
     fetch.wait()
-    group, child = late_place(late, perm_ref, groups)
+    found = late_groups(late, perm_ref, groups)
+    same = found[0][0] == found[1][0]
     for h in range(local):
-        block = down_ref[group, h]
-        down_out[h] = jnp.where(child == 0, block[:, :width], block[:, width:])
-        for t in range(2):
-            row_out[h, t] = row_ref[h, t, group]
+        for i, (group, _) in enumerate(found):
+            block = down_ref[group, h]
+            for j, (_, child) in enumerate(found):
+                part = jnp.where(child == 0, block[:, :width], block[:, width:])
+                zeros = jnp.zeros_like(part)
+                if i == 0 and j == 1:
+                    part = jnp.where(same, part, zeros)
+                elif i == 1:
+                    part = zeros if j == 0 else jnp.where(same, zeros, part)
+                down_out[h, i * rows : (i + 1) * rows, j * width : (j + 1) * width] = part
+            for t in range(2):
+                row_out[h, t, :, i * width : (i + 1) * width] = row_ref[h, t, group]
 
 
 def prep(late, perm, down, row, after):
@@ -265,8 +277,8 @@
     return pl.pallas_call(
         functools.partial(prep_kernel, late),
         out_shape=[
-            pltpu.VMEM((local, rows, width), BF16),
-            pltpu.VMEM((local, 2, leaf, width), BF16),
+            pltpu.VMEM((local, 2 * rows, 2 * width), BF16),
+            pltpu.VMEM((local, 2, leaf, 2 * width), BF16),
         ],
         in_specs=[hbm, vmem, vmem, pl.BlockSpec(memory_space=pl.ANY)],
         out_specs=[vmem] * 2,
@@ -309,9 +321,11 @@
             mid = mid_ref[0, h]
             put(partner(k, which), h, mid[:, :NRHS], mid[:, NRHS:])
     for h in range(local):
-        spread_ref[partner(*late), h] = jnp.zeros(spread_ref.shape[2:], BF16)
+        for route in late:
+            spread_ref[partner(*route), h] = jnp.zeros(spread_ref.shape[2:], BF16)
+        top_ref[1, h] = jnp.zeros(top_ref.shape[2:], F32)
     fetch.wait()
-    group, _ = late_place(late, perm_ref, groups)
+    (group_a, _), (group_b, _) = late_groups(late, perm_ref, groups)
     for h in range(local):
         tops = ([], [])
         for q in range(groups):
@@ -319,8 +333,9 @@
             top = jnp.dot(
                 down_ref[q, h], jnp.concatenate(parts, axis=0), preferred_element_type=F32
             )
-            lacks = group == q
-            top_ref[jnp.where(lacks, 0, 1), h] = top
+            is_a, is_b = group_a == q, group_b == q
+            top_ref[jnp.where(is_a, 0, jnp.where(is_b, 1, 2)), h] = top
+            lacks = jnp.logical_or(is_a, is_b)
             top = jnp.where(lacks, jnp.zeros_like(top), top).astype(BF16)
             for t in range(2):
                 tops[t].append(top[t * rank : (t + 1) * rank])
@@ -339,7 +354,7 @@
         functools.partial(upper_kernel, full, halved, late),
         out_shape=[
             pltpu.VMEM((local, 2, leaf, 2 * NRHS), F32),
-            pltpu.VMEM((2, local, 2 * rank, 2 * NRHS), F32),
+            pltpu.VMEM((3, local, 2 * rank, 2 * NRHS), F32),
         ],
         in_specs=[hbm] + [vmem] * (2 + len(mids)),
         out_specs=[vmem] * 2,
@@ -354,18 +369,18 @@
     )(pltpu.with_memory_space_constraint(perm, pltpu.HBM), down, row, *mids)
 
 
-def finish_kernel(down_ref, row_ref, field_ref, top_ref, mid_ref, out_hbm, mix_ref, out_ref, sems):
+def finish_kernel(down_ref, row_ref, field_ref, top_ref, mid_a, mid_b, out_hbm, mix_ref, out_ref, sems):
     local, _, leaf, _ = field_ref.shape
-    rank = mid_ref.shape[2]
+    rank = mid_a.shape[2]
     copies = []
     for i, group in enumerate(chunks(local)):
         for h in group:
-            top = top_ref[0, h] + jnp.dot(
-                down_ref[h], twisted_rows([mid_ref[0, h]]), preferred_element_type=F32
+            top = jnp.concatenate([top_ref[0, h], top_ref[1, h]], axis=0) + jnp.dot(
+                down_ref[h], twisted_rows([mid_a[0, h], mid_b[0, h]]), preferred_element_type=F32
             )
             top = top.astype(BF16)
             for t in range(2):
-                rows = twisted_rows([top[t * rank : (t + 1) * rank]])
+                rows = twisted_rows([top[r : r + rank] for r in (t * rank, (2 + t) * rank)])
                 field = field_ref[h, t] + jnp.dot(
                     row_ref[h, t], rows, preferred_element_type=F32
                 )
@@ -379,14 +394,14 @@
         copy.wait()
 
 
-def finish(down, row, field, top, mid):
+def finish(down, row, field, top, mids):
     local, _, leaf, _ = field.shape
     shape = (local, 2, 2 * leaf, NRHS)
     vmem = pl.BlockSpec(memory_space=pltpu.VMEM)
     return pl.pallas_call(
         finish_kernel,
         out_shape=jax.ShapeDtypeStruct(shape, BF16),
-        in_specs=[vmem] * 5,
+        in_specs=[vmem] * 6,
         out_specs=pl.BlockSpec(memory_space=pltpu.HBM),
         scratch_shapes=[
             pltpu.VMEM(shape, F32),
@@ -396,7 +411,7 @@
         compiler_params=PARAMS,
         cost_estimate=COST,
         name="finish",
-    )(down, row, field, top, mid)
+    )(down, row, field, top, *mids)
 
 
 def send(block, route, dests):
@@ -417,8 +432,8 @@
     x = jnp.transpose(x_panels, (0, 2, 3, 1))
     dests = 2 * columns
     two = both_cores((2,))
-    full = both_cores(range(columns - 1, 3, -1)) + [(0, 1), (1, 0), (3, 0), (1, 1), (0, 0)]
-    late = (3, 1)
+    full = both_cores(range(columns - 1, 3, -1)) + [(0, 1), (1, 0), (3, 0), (0, 0)]
+    late = [(3, 1), (1, 1)]
     split = 2 * x.shape[2] == NRHS
     swap = [(0, 1), (1, 0)]
     if split:
@@ -430,15 +445,15 @@
         full, halved, up = two + full, [], up_transfer
         xs = [lax.all_gather(x, "rhs", axis=2, tiled=True)]
     n = len(full)
-    mids = lower(full + [late], halved, dests, leaf_count, parent_map, xs, basis, up)
+    mids = lower(full + late, halved, dests, leaf_count, parent_map, xs, basis, up)
     halves = []
     if split:
         other_two = lax.ppermute(mids[-1], "blk", [(m, m ^ 2) for m in range(columns)])
         halves = [own_two, other_two, lax.ppermute(hand(own_two, other_two), "sub", swap)]
-    mids = [send(mid, route, dests) for mid, route in zip(mids, full + [late])]
+    mids = [send(mid, route, dests) for mid, route in zip(mids, full + late)]
     down_late, row_late = prep(late, mid_perm, down, row, (halves + mids)[0])
     field, top = upper(full, halved, late, mid_perm, down, row, [*mids[:n], *halves])
-    result = finish(down_late, row_late, field, top, mids[n])
+    result = finish(down_late, row_late, field, top, mids[n : n + 2])
     return result.reshape(1, local, 2, leaf, 2, NRHS)
 
 

time: 33 us -> 35.8 us (1.085)
  the two profiles are of different devices: /device:TPU:29 before, /device:TPU:0 now
where the time goes in v11:
time: 35.8 us; the launch traced here: 35.6 us
  waiting for transfers between devices  13.5 us (38%)
  starting transfers between devices  13 us (36%)
  Pallas kernels  8.97 us (25%)
    ppermute x5, starting transfers between devices, send(): lax.ppermute(block, ('blk', 'sub'), [(m, m ^ code) for m in range(dests)])  6.77 us
    ppermute x1, waiting for transfers between devices, on_device(): lax.ppermute(mids[-1], 'blk', [(m, m ^ 2) for m in range(columns)])  6.49 us
    ppermute x5, waiting for transfers between devices, send(): lax.ppermute(block, ('blk', 'sub'), [(m, m ^ code) for m in range(dests)])  4.88 us
    ppermute x1, starting transfers between devices, on_device(): xs = [x, lax.ppermute(x, 'rhs', swap)]  2.94 us
    ppermute x1, starting transfers between devices, on_device(): own_two = lax.ppermute(own_two, 'blk', [(m, m ^ 2) for m in range(columns)])  2.65 us
    pallas_call x1, Pallas kernels, own(): pl.pallas_call(functools.partial(own_kernel, routes), out_shape=[block, p...  2.52 us
    pallas_call x1, Pallas kernels, lower(): pl.pallas_call(functools.partial(lower_kernel, full, halved), out_shape=[...  2.26 us
    ppermute x1, waiting for transfers between devices, on_device(): own_two = lax.ppermute(own_two, 'blk', [(m, m ^ 2) for m in range(columns)])  2.15 us
  transfers between devices with their start and end apart: 9, of which 4 were waited for; matrix products, arithmetic and copies ran while one was open for 0% of the time, Pallas kernels for 21%

profile of v11, /device:TPU:0, one launch (start us, length us, event | category | flops | bytes accessed | tf_op | source)
XLA Modules:
  0.0 35.6 jit_solution(8218944114795900628)
XLA Ops:
  0.0 0.0 copy-start.2
  0.0 2.9 %collective-permute-start.1 = (bf16[2,2,64,128]{3,2,1,0:T(8,128)(2,1)}, bf16[2,2,64,128]{3,2,1,0:T(8,128)(2,1)S(1)}, u32[]{:S(2)}, u32[]{:S(2)}) collective-permute-start(bf16[2,2,64,128]{3,2,1,0:T(8,128)(2,1)} %bitcast.9), channel_id=1, source_target_pairs={{0,2},{2,0},{1,3},{3,1},{4,6},{6,4},{5,7},{7,5},{8,10},{10,8},{9,1... | collective-permute-start | bytes 196616 | tf_op jit(solution)/shard_map/ppermute | solution.py:441
  2.9 2.5 %own.1 = (bf16[2,1,4,64,128]{4,3,2,1,0:T(8,128)(2,1)S(1)}, bf16[2,16,128,128]{3,2,1,0:T(8,128)(2,1)S(1)}, bf16[1,32,64,256]{3,2,1,0:T(8,128)(2,1)S(1)}) custom-call(s32[2]{0:T(128)} %count_hbm.3, s32[32]{0:T(128)} %parent_hbm.3, bf16[2,2,64,128]{3,2,1,0:T(8,128)(2,1)} %bitcast.10, bf16[2,16,128,128]{3,2,1,0:T(8,128)(2,1)} %bitcast.12, ...), custom_call_target="tpu_custom_call" | custom-call | flops 1000000 | bytes 10000 | tf_op jit(solution)/shard_map/own/pallas_call | solution.py:125
  5.5 0.0 copy-start
  5.5 0.0 copy-start.1
  5.5 2.6 %collective-permute-start = (bf16[2,1,4,64,128]{4,3,2,1,0:T(8,128)(2,1)S(1)}, bf16[2,1,4,64,128]{4,3,2,1,0:T(8,128)(2,1)S(1)}, u32[]{:S(2)}, u32[]{:S(2)}) collective-permute-start(bf16[2,1,4,64,128]{4,3,2,1,0:T(8,128)(2,1)S(1)} %get-tuple-element.19), channel_id=1, source_target_pairs={{0,8},{4,12},{8,0},{12,4},{1,9},{5,13},{9,1},{13,5},{2,10},{6,14},... | collective-permute-start | bytes 393224 | tf_op jit(solution)/shard_map/ppermute | solution.py:443
  8.1 0.0 collective-permute-done.1.refs_1_
  8.2 0.0 copy-done.2
  8.2 2.3 %lower.1 = (bf16[1,4,64,256]{3,2,1,0:T(8,128)(2,1)S(1)}, bf16[1,4,64,256]{3,2,1,0:T(8,128)(2,1)S(1)}, bf16[1,4,64,256]{3,2,1,0:T(8,128)(2,1)S(1)}, bf16[1,4,64,2...) custom-call(s32[2]{0:T(128)} %count_hbm.3, ...), custom_call_target="tpu_custom_call" | custom-call | flops 1000000 | bytes 10000 | tf_op jit(solution)/shard_map/lower/pallas_call | solution.py:191
  10.4 0.6 %collective-permute-start.5 = (bf16[2,1,4,64,128]{4,3,2,1,0:T(8,128)(2,1)S(1)}, bf16[2,1,4,64,128]{4,3,2,1,0:T(8,128)(2,1)S(1)}, u32[]{:S(2)}, u32[]{:S(2)}) collective-permute-start(bf16[2,1,4,64,128]{4,3,2,1,0:T(8,128)(2,1)S(1)} %get-tuple-element.28), channel_id=1, source_target_pairs={{0,8},{4,12},{8,0},{12,4},{1,9},{5,13},{9,1},{13,5},{2,10},{6,14},... | collective-permute-start | bytes 393224 | tf_op jit(solution)/shard_map/ppermute | solution.py:451
  11.0 0.0 collective-permute-start.2
  11.0 1.6 %collective-permute-start.3 = (bf16[1,4,64,256]{3,2,1,0:T(8,128)(2,1)S(1)}, bf16[1,4,64,256]{3,2,1,0:T(8,128)(2,1)S(1)}, u32[]{:S(2)}, u32[]{:S(2)}) collective-permute-start(bf16[1,4,64,256]{3,2,1,0:T(8,128)(2,1)S(1)} %get-tuple-element.25), channel_id=1, source_target_pairs={{0,4},{1,5},{4,0},{5,1},{8,12},{9,13},{12,8},{13,9},{2,6},{3,7},{6... | collective-permute-start | bytes 393224 | tf_op jit(solution)/shard_map/ppermute | solution.py:421
  12.6 2.3 %collective-permute-start.4 = (bf16[1,4,64,256]{3,2,1,0:T(8,128)(2,1)S(1)}, bf16[1,4,64,256]{3,2,1,0:T(8,128)(2,1)S(1)}, u32[]{:S(2)}, u32[]{:S(2)}) collective-permute-start(bf16[1,4,64,256]{3,2,1,0:T(8,128)(2,1)S(1)} %get-tuple-element.26), channel_id=1, source_target_pairs={{0,12},{1,13},{4,8},{5,9},{8,4},{9,5},{12,0},{13,1},{2,14},{3,15},... | collective-permute-start | bytes 393224 | tf_op jit(solution)/shard_map/ppermute | solution.py:421
  14.9 2.2 %collective-permute-done.after_ref.own_ref.refs_4_ = bf16[2,1,4,64,128]{4,3,2,1,0:T(8,128)(2,1)S(1)} collective-permute-done((bf16[2,1,4,64,128]{4,3,2,1,0:T(8,128)(2,1)S(1)}, bf16[2,1,4,64,128]{4,3,2,1,0:T(8,128)(2,1)S(1)}, u32[]{:S(2)}, u32[]{:S(2)}) %collective-permute-start) | collective-permute-done | bytes 131104 | tf_op jit(solution)/shard_map/ppermute | solution.py:443
  17.0 6.5 %collective-permute-done.5.other_ref.refs_5_ = bf16[2,1,4,64,128]{4,3,2,1,0:T(8,128)(2,1)S(1)} collective-permute-done((bf16[2,1,4,64,128]{4,3,2,1,0:T(8,128)(2,1)S(1)}, bf16[2,1,4,64,128]{4,3,2,1,0:T(8,128)(2,1)S(1)}, u32[]{:S(2)}, u32[]{:S(2)}) %collective-permute-start.5) | collective-permute-done | bytes 131104 | tf_op jit(solution)/shard_map/ppermute | solution.py:451
  23.5 0.1 collective-permute-start.6
  23.6 2.9 %collective-permute-start.7 = (bf16[1,4,64,256]{3,2,1,0:T(8,128)(2,1)S(1)}, bf16[1,4,64,256]{3,2,1,0:T(8,128)(2,1)S(1)}, u32[]{:S(2)}, u32[]{:S(2)}) collective-permute-start(bf16[1,4,64,256]{3,2,1,0:T(8,128)(2,1)S(1)} %get-tuple-element.31), channel_id=1, source_target_pairs={{0,13},{1,12},{4,9},{5,8},{8,5},{9,4},{12,1},{13,0},{2,15},{3,14},... | collective-permute-start | bytes 393224 | tf_op jit(solution)/shard_map/ppermute | solution.py:421
  26.5 0.0 collective-permute-done.2.refs_0_
  26.5 0.0 collective-permute-start.8
  26.5 0.0 copy-done
  26.5 0.0 copy-done.1
  26.5 0.9 %prep.1 = (bf16[4,256,256]{2,1,0:T(8,128)(2,1)S(1)}, bf16[4,2,128,256]{3,2,1,0:T(8,128)(2,1)S(1)}) custom-call(s32[8]{0:T(128)} %perm_hbm.3, bf16[4,4,128,256]{3,2,1,0:T(8,128)(2,1)S(1)} %bitcast.5, bf16[4,2,4,128,128]{4,3,2,1,0:T(8,128)(2,1)S(1)} %bitcast.7, bf16[2,1,4,64,128]{4,3,2,1,0:T(8,128)(2,1)S(1)} %collective-permute-done.after_ref.own_ref.refs_4_), custom_call_target="tpu_custom_call" | custom-call | flops 1000000 | bytes 10000 | tf_op jit(solution)/shard_map/prep/pallas_call | solution.py:277
  27.4 0.0 collective-permute-done.3.refs_1_
  27.4 0.0 collective-permute-done.4.refs_2_
  27.4 0.0 collective-permute-done.6.refs_6_
  27.4 1.9 %upper.1 = (f32[4,2,128,256]{3,2,1,0:T(8,128)S(1)}, f32[3,4,128,256]{3,2,1,0:T(8,128)S(1)}) custom-call(s32[8]{0:T(128)} %perm_hbm.3, bf16[4,4,128,256]{3,2,1,0:T(8,128)(2,1)S(1)} %bitcast.6, bf16[4,2,4,128,128]{4,3,2,1,0:T(8,128)(2,1)S(1)} %bitcast.8, bf16[1,4,64,256]{3,2,1,0:T(8,128)(2,1)S(1)} %collective-permute-done.2.refs_0_, ...), custom_call_target="tpu_custom_call" | custom-call | flops 1000000 | bytes 10000 | tf_op jit(solution)/shard_map/upper/pallas_call | solution.py:353
  29.3 1.6 %collective-permute-done.7.mid_a = bf16[1,4,64,256]{3,2,1,0:T(8,128)(2,1)S(1)} collective-permute-done((bf16[1,4,64,256]{3,2,1,0:T(8,128)(2,1)S(1)}, bf16[1,4,64,256]{3,2,1,0:T(8,128)(2,1)S(1)}, u32[]{:S(2)}, u32[]{:S(2)}) %collective-permute-start.7) | collective-permute-done | bytes 131104 | tf_op jit(solution)/shard_map/ppermute | solution.py:421
  30.9 3.3 %collective-permute-done.8.mid_b = bf16[1,4,64,256]{3,2,1,0:T(8,128)(2,1)S(1)} collective-permute-done((bf16[1,4,64,256]{3,2,1,0:T(8,128)(2,1)S(1)}, bf16[1,4,64,256]{3,2,1,0:T(8,128)(2,1)S(1)}, u32[]{:S(2)}, u32[]{:S(2)}) %collective-permute-start.8) | collective-permute-done | bytes 131104 | tf_op jit(solution)/shard_map/ppermute | solution.py:421
  34.2 1.4 %finish.1 = bf16[4,2,256,128]{3,2,1,0:T(8,128)(2,1)} custom-call(bf16[4,256,256]{2,1,0:T(8,128)(2,1)S(1)} %get-tuple-element.20.down_ref, bf16[4,2,128,256]{3,2,1,0:T(8,128)(2,1)S(1)} %get-tuple-element.21.row_ref, f32[4,2,128,256]{3,2,1,0:T(8,128)S(1)} %get-tuple-element.29.field_ref, f32[3,4,128,256]{3,2,1,0:T(8,128)S(1)} %get-tuple-element.30.top_ref, ...), custom_call_target="tpu_custom_call" | custom-call | flops 1000000 | bytes 10000 | tf_op jit(solution)/shard_map/finish/pallas_call | solution.py:401
  (1 shorter events, 0.0 us)
Async XLA Ops:
  0.0 8.2 %copy-start.2 = (bf16[2,128,2,64]{1,3,2,0:T(8,128)(2,1)S(1)}, bf16[2,128,2,64]{1,3,2,0:T(8,128)(2,1)}, u32[]{:S(2)}) copy-start(bf16[2,128,2,64]{1,3,2,0:T(8,128)(2,1)} %param.8) | copy-start | bytes 196612
  0.0 8.1 %collective-permute-start.1 = (bf16[2,2,64,128]{3,2,1,0:T(8,128)(2,1)}, bf16[2,2,64,128]{3,2,1,0:T(8,128)(2,1)S(1)}, u32[]{:S(2)}, u32[]{:S(2)}) collective-permute-start(bf16[2,2,64,128]{3,2,1,0:T(8,128)(2,1)} %bitcast.9), channel_id=1, source_target_pairs={{0,2},{2,0},{1,3},{3,1},{4,6},{6,4},{5,7},{7,5},{8,10},{10,8},{9,1... | collective-permute-start | bytes 196616 | tf_op jit(solution)/shard_map/ppermute | solution.py:441
  5.5 21.0 %copy-start = (bf16[4,1,4,2,64,256]{5,4,3,2,1,0:T(8,128)(2,1)S(1)}, bf16[4,1,4,2,64,256]{5,4,3,2,1,0:T(8,128)(2,1)}, u32[]{:S(2)}) copy-start(bf16[4,1,4,2,64,256]{5,4,3,2,1,0:T(8,128)(2,1)} %param.14) | copy-start | bytes 3145732
  5.5 21.0 %copy-start.1 = (bf16[1,4,2,4,128,128]{5,4,3,2,1,0:T(8,128)(2,1)S(1)}, bf16[1,4,2,4,128,128]{5,4,3,2,1,0:T(8,128)(2,1)}, u32[]{:S(2)}) copy-start(bf16[1,4,2,4,128,128]{5,4,3,2,1,0:T(8,128)(2,1)} %param.15) | copy-start | bytes 3145732
  5.5 11.5 %collective-permute-start = (bf16[2,1,4,64,128]{4,3,2,1,0:T(8,128)(2,1)S(1)}, bf16[2,1,4,64,128]{4,3,2,1,0:T(8,128)(2,1)S(1)}, u32[]{:S(2)}, u32[]{:S(2)}) collective-permute-start(bf16[2,1,4,64,128]{4,3,2,1,0:T(8,128)(2,1)S(1)} %get-tuple-element.19), channel_id=1, source_target_pairs={{0,8},{4,12},{8,0},{12,4},{1,9},{5,13},{9,1},{13,5},{2,10},{6,14},... | collective-permute-start | bytes 393224 | tf_op jit(solution)/shard_map/ppermute | solution.py:443
  10.4 13.1 %collective-permute-start.5 = (bf16[2,1,4,64,128]{4,3,2,1,0:T(8,128)(2,1)S(1)}, bf16[2,1,4,64,128]{4,3,2,1,0:T(8,128)(2,1)S(1)}, u32[]{:S(2)}, u32[]{:S(2)}) collective-permute-start(bf16[2,1,4,64,128]{4,3,2,1,0:T(8,128)(2,1)S(1)} %get-tuple-element.28), channel_id=1, source_target_pairs={{0,8},{4,12},{8,0},{12,4},{1,9},{5,13},{9,1},{13,5},{2,10},{6,14},... | collective-permute-start | bytes 393224 | tf_op jit(solution)/shard_map/ppermute | solution.py:451
  11.0 15.5 %collective-permute-start.2 = (bf16[1,4,64,256]{3,2,1,0:T(8,128)(2,1)S(1)}, bf16[1,4,64,256]{3,2,1,0:T(8,128)(2,1)S(1)}, u32[]{:S(2)}, u32[]{:S(2)}) collective-permute-start(bf16[1,4,64,256]{3,2,1,0:T(8,128)(2,1)S(1)} %get-tuple-element.24), channel_id=1, source_target_pairs={{0,1},{1,0},{4,5},{5,4},{8,9},{9,8},{12,13},{13,12},{2,3},{3,2},{6... | collective-permute-start | bytes 393224 | tf_op jit(solution)/shard_map/ppermute | solution.py:421
  11.0 16.4 %collective-permute-start.3 = (bf16[1,4,64,256]{3,2,1,0:T(8,128)(2,1)S(1)}, bf16[1,4,64,256]{3,2,1,0:T(8,128)(2,1)S(1)}, u32[]{:S(2)}, u32[]{:S(2)}) collective-permute-start(bf16[1,4,64,256]{3,2,1,0:T(8,128)(2,1)S(1)} %get-tuple-element.25), channel_id=1, source_target_pairs={{0,4},{1,5},{4,0},{5,1},{8,12},{9,13},{12,8},{13,9},{2,6},{3,7},{6... | collective-permute-start | bytes 393224 | tf_op jit(solution)/shard_map/ppermute | solution.py:421
  12.6 14.8 %collective-permute-start.4 = (bf16[1,4,64,256]{3,2,1,0:T(8,128)(2,1)S(1)}, bf16[1,4,64,256]{3,2,1,0:T(8,128)(2,1)S(1)}, u32[]{:S(2)}, u32[]{:S(2)}) collective-permute-start(bf16[1,4,64,256]{3,2,1,0:T(8,128)(2,1)S(1)} %get-tuple-element.26), channel_id=1, source_target_pairs={{0,12},{1,13},{4,8},{5,9},{8,4},{9,5},{12,0},{13,1},{2,14},{3,15},... | collective-permute-start | bytes 393224 | tf_op jit(solution)/shard_map/ppermute | solution.py:421
  23.5 3.9 %collective-permute-start.6 = (bf16[2,1,4,64,128]{4,3,2,1,0:T(8,128)(2,1)S(1)}, bf16[2,1,4,64,128]{4,3,2,1,0:T(8,128)(2,1)S(1)}, u32[]{:S(2)}, u32[]{:S(2)}) collective-permute-start(bf16[2,1,4,64,128]{4,3,2,1,0:T(8,128)(2,1)S(1)} %hand.1), channel_id=1, source_target_pairs={{0,1},{1,0},{2,3},{3,2},{4,5},{5,4},{6,7},{7,6},{8,9},{9,8},{10,11... | collective-permute-start | bytes 393224 | tf_op jit(solution)/shard_map/ppermute | solution.py:452
  23.6 7.3 %collective-permute-start.7 = (bf16[1,4,64,256]{3,2,1,0:T(8,128)(2,1)S(1)}, bf16[1,4,64,256]{3,2,1,0:T(8,128)(2,1)S(1)}, u32[]{:S(2)}, u32[]{:S(2)}) collective-permute-start(bf16[1,4,64,256]{3,2,1,0:T(8,128)(2,1)S(1)} %get-tuple-element.31), channel_id=1, source_target_pairs={{0,13},{1,12},{4,9},{5,8},{8,5},{9,4},{12,1},{13,0},{2,15},{3,14},... | collective-permute-start | bytes 393224 | tf_op jit(solution)/shard_map/ppermute | solution.py:421
  26.5 7.7 %collective-permute-start.8 = (bf16[1,4,64,256]{3,2,1,0:T(8,128)(2,1)S(1)}, bf16[1,4,64,256]{3,2,1,0:T(8,128)(2,1)S(1)}, u32[]{:S(2)}, u32[]{:S(2)}) collective-permute-start(bf16[1,4,64,256]{3,2,1,0:T(8,128)(2,1)S(1)} %get-tuple-element.32), channel_id=1, source_target_pairs={{0,5},{1,4},{4,1},{5,0},{8,13},{9,12},{12,9},{13,8},{2,7},{3,6},{6... | collective-permute-start | bytes 393224 | tf_op jit(solution)/shard_map/ppermute | solution.py:421

commit v12 on v11

--- a/solution.py
+++ b/solution.py
@@ -89,8 +89,10 @@
     return even[0] - odd[1], even[1] + odd[0]
 
 
-def own_kernel(routes, count_hbm, parent_hbm, x_hbm, basis_hbm, up_hbm, out_ref, basis_ref, up_ref, *refs):
-    count_ref, parent_ref, x_ref, leaf_ref, g_ref, sems = refs
+def own_kernel(routes, count_hbm, parent_hbm, x_hbm, basis_hbm, up_hbm, *refs):
+    n = len(routes)
+    outs, basis_ref, up_ref = refs[:n], refs[n], refs[n + 1]
+    count_ref, parent_ref, x_ref, leaf_ref, g_ref, sems = refs[n + 2 :]
     boxes = basis_ref.shape[0]
     copies = {
         "x": pltpu.make_async_copy(x_hbm, x_ref, sems.at[0]),
@@ -102,31 +104,32 @@
         copies[b] = pltpu.make_async_copy(basis_hbm.at[b], basis_ref.at[b], sems.at[4 + b])
     for name in ["x", 0, "count"] + list(range(1, boxes)) + ["up", "parent"]:
         copies[name].start()
-    copies["x"].wait()
+    for name in ["x", "count", *range(boxes)]:
+        copies[name].wait()
 
     def spreads(b):
         real, imag = x_ref[b, 0], x_ref[b, 1]
         return jnp.concatenate([real, imag, -imag, real], axis=0)
 
     leaf_stage(
-        spreads, half_columns, count_ref, basis_ref, g_ref, leaf_ref, lambda name: copies[name].wait()
+        spreads, half_columns, count_ref, basis_ref, g_ref, leaf_ref, lambda name: None
     )
     copies["up"].wait()
     copies["parent"].wait()
-    outs = [out_ref.at[i] for i in range(len(routes))]
     up_stage(outs, routes, parent_ref, up_ref, leaf_ref)
 
 
 def own(routes, dests, count, parents, x, basis, up):
     boxes, dirs, rows, _ = basis.shape
     pairs, dirs_up, rank, _ = up.shape
-    block = pltpu.VMEM((len(routes), pairs, dirs_up // dests, rank, NRHS), BF16)
+    block = pltpu.VMEM((pairs, dirs_up // dests, rank, NRHS), BF16)
     args = [count, parents, x, basis, up]
     return pl.pallas_call(
         functools.partial(own_kernel, routes),
-        out_shape=[block, pltpu.VMEM(basis.shape, BF16), pltpu.VMEM(up.shape, BF16)],
+        out_shape=[block] * len(routes)
+        + [pltpu.VMEM(basis.shape, BF16), pltpu.VMEM(up.shape, BF16)],
         in_specs=[pl.BlockSpec(memory_space=pltpu.HBM)] * 5,
-        out_specs=[pl.BlockSpec(memory_space=pltpu.VMEM)] * 3,
+        out_specs=[pl.BlockSpec(memory_space=pltpu.VMEM)] * (len(routes) + 2),
         scratch_shapes=[
             pltpu.SMEM(count.shape, jnp.int32),
             pltpu.SMEM(parents.shape, jnp.int32),
@@ -150,10 +153,10 @@
 
 
 def lower_kernel(full, halved, count_hbm, parent_hbm, *refs):
-    n = len(full) + bool(halved)
+    n, m = len(full), len(halved)
     g_ref, leaf_ref, count_ref, parent_ref, sems = refs[-5:]
-    outs = refs[-5 - n : -5]
-    *xs, basis_ref, up_ref = refs[: -5 - n]
+    outs = refs[-5 - n - m : -5]
+    *xs, basis_ref, up_ref = refs[: -5 - n - m]
     copies = {
         "count": pltpu.make_async_copy(count_hbm, count_ref, sems.at[0]),
         "parent": pltpu.make_async_copy(parent_hbm, parent_ref, sems.at[1]),
@@ -175,10 +178,9 @@
 
     leaf_stage(spreads, all_columns, count_ref, basis_ref, g_ref, leaf_ref, ready)
     ready("parent")
+    up_stage(outs[:n], full, parent_ref, up_ref, leaf_ref)
     if halved:
-        halves = [outs[-1].at[i] for i in range(len(halved))]
-        up_stage(halves, halved, parent_ref, up_ref, leaf_ref, other_columns)
-    up_stage(outs[: len(full)], full, parent_ref, up_ref, leaf_ref)
+        up_stage(outs[n:], halved, parent_ref, up_ref, leaf_ref, other_columns)
 
 
 def lower(full, halved, dests, count, parents, xs, basis, up):
@@ -187,11 +189,11 @@
     shape = (pairs, dirs_up // dests, rank)
     hbm = pl.BlockSpec(memory_space=pltpu.HBM)
     vmem = pl.BlockSpec(memory_space=pltpu.VMEM)
-    n = len(full) + bool(halved)
+    n = len(full) + len(halved)
     return pl.pallas_call(
         functools.partial(lower_kernel, full, halved),
         out_shape=[pltpu.VMEM(shape + (2 * NRHS,), BF16)] * len(full)
-        + [pltpu.VMEM((len(halved),) + shape + (NRHS,), BF16)] * bool(halved),
+        + [pltpu.VMEM(shape + (NRHS,), BF16)] * len(halved),
         in_specs=[hbm, hbm] + [vmem] * (2 + len(xs)),
         out_specs=[vmem] * n,
         scratch_shapes=[
@@ -213,24 +215,6 @@
 
 def twisted_rows(tops):
     return jnp.concatenate([rows for top in tops for rows in (top, twist(top))], axis=0)
-
-
-def hand_kernel(own_ref, other_ref, out_ref):
-    out_ref[0] = own_ref[1]
-    out_ref[1] = other_ref[1]
-
-
-def hand(own, other):
-    vmem = pl.BlockSpec(memory_space=pltpu.VMEM)
-    return pl.pallas_call(
-        hand_kernel,
-        out_shape=pltpu.VMEM(own.shape, BF16),
-        in_specs=[vmem] * 2,
-        out_specs=vmem,
-        compiler_params=PARAMS,
-        cost_estimate=COST,
-        name="hand",
-    )(own, other)
 
 
 def late_groups(late, perm_ref, groups):
@@ -290,12 +274,9 @@
 
 
 def upper_kernel(full, halved, late, perm_hbm, down_ref, row_ref, *refs):
-    n = len(full)
-    mids, (field_ref, top_ref, spread_ref, perm_ref, sem) = refs[:n], refs[-5:]
-    halves = []
-    if halved:
-        own_ref, other_ref, handed_ref = refs[n:-5]
-        halves = [(own_ref.at[0], other_ref.at[0]), (handed_ref.at[0], handed_ref.at[1])]
+    n, m = len(full), len(halved)
+    mids, own_mids, other_mids = refs[:n], refs[n : n + m], refs[n + m : n + 2 * m]
+    field_ref, top_ref, spread_ref, perm_ref, sem = refs[n + 2 * m :]
     groups, local = down_ref.shape[:2]
     rank = spread_ref.shape[2] // 2
     fetch = pltpu.make_async_copy(perm_hbm, perm_ref, sem.at[0])
@@ -308,7 +289,7 @@
         spread_ref[source, h, rank:, NRHS:] = real
 
     left = lax.broadcasted_iota(jnp.int32, (rank, NRHS), 1) < HALF
-    for (own_ref, other_ref), (k, which) in zip(halves, halved):
+    for own_ref, other_ref, (k, which) in zip(own_mids, other_mids, halved):
         swap = lax.axis_index("rhs") == 1
         for h in range(local):
             low, high = own_ref[0, h].astype(F32), other_ref[0, h].astype(F32)
@@ -432,27 +413,24 @@
     x = jnp.transpose(x_panels, (0, 2, 3, 1))
     dests = 2 * columns
     two = both_cores((2,))
-    full = both_cores(range(columns - 1, 3, -1)) + [(0, 1), (1, 0), (3, 0), (0, 0)]
-    late = [(3, 1), (1, 1)]
-    split = 2 * x.shape[2] == NRHS
-    swap = [(0, 1), (1, 0)]
-    if split:
+    full = both_cores(range(columns - 1, 3, -1)) + [(3, 0), (1, 0), (0, 1), (0, 0)]
+    late = [(1, 1), (3, 1)]
+    if 2 * x.shape[2] == NRHS:
         halved = two
-        xs = [x, lax.ppermute(x, "rhs", swap)]
-        own_two, basis, up = own(halved, dests, leaf_count, parent_map, x, basis, up_transfer)
-        own_two = lax.ppermute(own_two, "blk", [(m, m ^ 2) for m in range(columns)])
+        xs = [x, lax.ppermute(x, "rhs", [(0, 1), (1, 0)])]
+        *own_mids, basis, up = own(halved, dests, leaf_count, parent_map, x, basis, up_transfer)
+        own_mids = [send(mid, route, dests) for mid, route in zip(own_mids, halved)]
     else:
-        full, halved, up = two + full, [], up_transfer
+        full, halved, own_mids, up = two + full, [], [], up_transfer
         xs = [lax.all_gather(x, "rhs", axis=2, tiled=True)]
     n = len(full)
+    routes = full + late + halved
     mids = lower(full + late, halved, dests, leaf_count, parent_map, xs, basis, up)
-    halves = []
-    if split:
-        other_two = lax.ppermute(mids[-1], "blk", [(m, m ^ 2) for m in range(columns)])
-        halves = [own_two, other_two, lax.ppermute(hand(own_two, other_two), "sub", swap)]
-    mids = [send(mid, route, dests) for mid, route in zip(mids, full + late)]
-    down_late, row_late = prep(late, mid_perm, down, row, (halves + mids)[0])
-    field, top = upper(full, halved, late, mid_perm, down, row, [*mids[:n], *halves])
+    mids = [send(mid, route, dests) for mid, route in zip(mids, routes)]
+    down_late, row_late = prep(late, mid_perm, down, row, [*own_mids, mids[0]][0])
+    field, top = upper(
+        full, halved, late, mid_perm, down, row, [*mids[:n], *own_mids, *mids[n + 2 :]]
+    )
     result = finish(down_late, row_late, field, top, mids[n : n + 2])
     return result.reshape(1, local, 2, leaf, 2, NRHS)
 

time: 35.8 us -> 32.3 us (0.902)
  waiting for transfers between devices: 13.5 us -> 7.86 us
  starting transfers between devices: 13 us -> 15.1 us
    ppermute x4 -> x1, waiting for transfers between devices: 8.65 us -> 0.01 us  [on_device(): xs = [x, lax.ppermute(x, 'rhs', [(0, 1), (1, 0)])]]
    ppermute x5 -> x9, starting transfers between devices: 6.77 us -> 12.2 us  [send(): lax.ppermute(block, ('blk', 'sub'), [(m, m ^ code) for m in range(dests)])]
    ppermute x4 -> x1, starting transfers between devices: 6.22 us -> 2.94 us  [on_device(): xs = [x, lax.ppermute(x, 'rhs', [(0, 1), (1, 0)])]]
    ppermute x5 -> x9, waiting for transfers between devices: 4.88 us -> 7.86 us  [send(): lax.ppermute(block, ('blk', 'sub'), [(m, m ^ code) for m in range(dests)])]
    pallas_call x2 -> x1, Pallas kernels: 2.53 us -> 2.47 us  [own(): pl.pallas_call(functools.partial(own_kernel, routes), out_shape=[block] *...]
  transfers between devices with their start and end apart: 9 -> 10, of which waited for: 4 -> 3; matrix products, arithmetic and copies ran while one was open for 0% -> 0% of each run, Pallas kernels for 21% -> 24%
where the time goes in v12:
time: 32.3 us; the launch traced here: 32.1 us
  starting transfers between devices  15.1 us (47%)
  Pallas kernels  8.99 us (28%)
  waiting for transfers between devices  7.86 us (24%)
    ppermute x9, starting transfers between devices, send(): lax.ppermute(block, ('blk', 'sub'), [(m, m ^ code) for m in range(dests)])  12.2 us
    ppermute x9, waiting for transfers between devices, send(): lax.ppermute(block, ('blk', 'sub'), [(m, m ^ code) for m in range(dests)])  7.86 us
    ppermute x1, starting transfers between devices, on_device(): xs = [x, lax.ppermute(x, 'rhs', [(0, 1), (1, 0)])]  2.94 us
    pallas_call x1, Pallas kernels, own(): pl.pallas_call(functools.partial(own_kernel, routes), out_shape=[block] *...  2.47 us
    pallas_call x1, Pallas kernels, lower(): pl.pallas_call(functools.partial(lower_kernel, full, halved), out_shape=[...  2.34 us
    pallas_call x1, Pallas kernels, upper(): pl.pallas_call(functools.partial(upper_kernel, full, halved, late), out_s...  1.88 us
    pallas_call x1, Pallas kernels, finish(): pl.pallas_call(finish_kernel, out_shape=jax.ShapeDtypeStruct(shape, BF16)...  1.44 us
    pallas_call x1, Pallas kernels, prep(): pl.pallas_call(functools.partial(prep_kernel, late), out_shape=[pltpu.VME...  0.85 us
  transfers between devices with their start and end apart: 10, of which 3 were waited for; matrix products, arithmetic and copies ran while one was open for 0% of the time, Pallas kernels for 24%

profile of v12, /device:TPU:0, one launch (start us, length us, event | category | flops | bytes accessed | tf_op | source)
XLA Modules:
  0.0 32.1 jit_solution(7867343384765314643)
XLA Ops:
  0.0 0.0 copy-start.2
  0.0 2.9 %collective-permute-start.1 = (bf16[2,2,64,128]{3,2,1,0:T(8,128)(2,1)}, bf16[2,2,64,128]{3,2,1,0:T(8,128)(2,1)S(1)}, u32[]{:S(2)}, u32[]{:S(2)}) collective-permute-start(bf16[2,2,64,128]{3,2,1,0:T(8,128)(2,1)} %bitcast.9), channel_id=1, source_target_pairs={{0,2},{2,0},{1,3},{3,1},{4,6},{6,4},{5,7},{7,5},{8,10},{10,8},{9,1... | collective-permute-start | bytes 196616 | tf_op jit(solution)/shard_map/ppermute | solution.py:420
  2.9 2.5 %own.1 = (bf16[1,4,64,128]{3,2,1,0:T(8,128)(2,1)S(1)}, bf16[1,4,64,128]{3,2,1,0:T(8,128)(2,1)S(1)}, bf16[2,16,128,128]{3,2,1,0:T(8,128)(2,1)S(1)}, bf16[1,32,64,256]{3,2,1,0:T(8,128)(2,1)S(1)}) custom-call(s32[2]{0:T(128)} %count_hbm.3, s32[32]{0:T(128)} %parent_hbm.3, bf16[2,2,64,128]{3,2,1,0:T(8,128)(2,1)} %bitcast.10, bf16[2,16,128,128]{3,2,1,0:T(8,128)(2,1)} %bitcast.12, ...), custom_call_target="tpu_custom_call" | custom-call | flops 1000000 | bytes 10000 | tf_op jit(solution)/shard_map/own/pallas_call | solution.py:127
  5.4 0.0 copy-start
  5.4 0.0 copy-start.1
  5.4 2.6 %collective-permute-start = (bf16[1,4,64,128]{3,2,1,0:T(8,128)(2,1)S(1)}, bf16[1,4,64,128]{3,2,1,0:T(8,128)(2,1)S(1)}, u32[]{:S(2)}, u32[]{:S(2)}) collective-permute-start(bf16[1,4,64,128]{3,2,1,0:T(8,128)(2,1)S(1)} %get-tuple-element.21), channel_id=1, source_target_pairs={{0,8},{1,9},{4,12},{5,13},{8,0},{9,1},{12,4},{13,5},{2,10},{3,11},... | collective-permute-start | bytes 196616 | tf_op jit(solution)/shard_map/ppermute | solution.py:402
  8.1 0.0 collective-permute-start.5
  8.1 0.0 collective-permute-done.1.refs_1_
  8.1 0.0 copy-done.2
  8.1 2.3 %lower.1 = (bf16[1,4,64,256]{3,2,1,0:T(8,128)(2,1)S(1)}, bf16[1,4,64,256]{3,2,1,0:T(8,128)(2,1)S(1)}, bf16[1,4,64,256]{3,2,1,0:T(8,128)(2,1)S(1)}, bf16[1,4,64,2...) custom-call(s32[2]{0:T(128)} %count_hbm.3, ...), custom_call_target="tpu_custom_call" | custom-call | flops 1000000 | bytes 10000 | tf_op jit(solution)/shard_map/lower/pallas_call | solution.py:193
  10.5 1.9 %collective-permute-start.6 = (bf16[1,4,64,128]{3,2,1,0:T(8,128)(2,1)S(1)}, bf16[1,4,64,128]{3,2,1,0:T(8,128)(2,1)S(1)}, u32[]{:S(2)}, u32[]{:S(2)}) collective-permute-start(bf16[1,4,64,128]{3,2,1,0:T(8,128)(2,1)S(1)} %get-tuple-element.31), channel_id=1, source_target_pairs={{0,8},{1,9},{4,12},{5,13},{8,0},{9,1},{12,4},{13,5},{2,10},{3,11},... | collective-permute-start | bytes 196616 | tf_op jit(solution)/shard_map/ppermute | solution.py:402
  12.3 0.9 %collective-permute-start.7 = (bf16[1,4,64,128]{3,2,1,0:T(8,128)(2,1)S(1)}, bf16[1,4,64,128]{3,2,1,0:T(8,128)(2,1)S(1)}, u32[]{:S(2)}, u32[]{:S(2)}) collective-permute-start(bf16[1,4,64,128]{3,2,1,0:T(8,128)(2,1)S(1)} %get-tuple-element.32), channel_id=1, source_target_pairs={{0,9},{1,8},{4,13},{5,12},{8,1},{9,0},{12,5},{13,4},{2,11},{3,10},... | collective-permute-start | bytes 196616 | tf_op jit(solution)/shard_map/ppermute | solution.py:402
  13.2 3.6 %collective-permute-start.2 = (bf16[1,4,64,256]{3,2,1,0:T(8,128)(2,1)S(1)}, bf16[1,4,64,256]{3,2,1,0:T(8,128)(2,1)S(1)}, u32[]{:S(2)}, u32[]{:S(2)}) collective-permute-start(bf16[1,4,64,256]{3,2,1,0:T(8,128)(2,1)S(1)} %get-tuple-element.26), channel_id=1, source_target_pairs={{0,12},{1,13},{4,8},{5,9},{8,4},{9,5},{12,0},{13,1},{2,14},{3,15},... | collective-permute-start | bytes 393224 | tf_op jit(solution)/shard_map/ppermute | solution.py:402
  16.8 0.0 collective-permute-done.after_ref.refs_4_
  16.8 0.0 collective-permute-start.3
  16.8 0.0 collective-permute-done.5.refs_5_
  16.8 0.1 collective-permute-start.4
  16.9 4.4 %collective-permute-done.6.refs_6_ = bf16[1,4,64,128]{3,2,1,0:T(8,128)(2,1)S(1)} collective-permute-done((bf16[1,4,64,128]{3,2,1,0:T(8,128)(2,1)S(1)}, bf16[1,4,64,128]{3,2,1,0:T(8,128)(2,1)S(1)}, u32[]{:S(2)}, u32[]{:S(2)}) %collective-permute-start.6) | collective-permute-done | bytes 65568 | tf_op jit(solution)/shard_map/ppermute | solution.py:402
  21.3 0.0 collective-permute-start.8
  21.3 1.4 %collective-permute-done.7.refs_7_ = bf16[1,4,64,128]{3,2,1,0:T(8,128)(2,1)S(1)} collective-permute-done((bf16[1,4,64,128]{3,2,1,0:T(8,128)(2,1)S(1)}, bf16[1,4,64,128]{3,2,1,0:T(8,128)(2,1)S(1)}, u32[]{:S(2)}, u32[]{:S(2)}) %collective-permute-start.7) | collective-permute-done | bytes 65568 | tf_op jit(solution)/shard_map/ppermute | solution.py:402
  22.7 3.1 %collective-permute-start.9 = (bf16[1,4,64,256]{3,2,1,0:T(8,128)(2,1)S(1)}, bf16[1,4,64,256]{3,2,1,0:T(8,128)(2,1)S(1)}, u32[]{:S(2)}, u32[]{:S(2)}) collective-permute-start(bf16[1,4,64,256]{3,2,1,0:T(8,128)(2,1)S(1)} %get-tuple-element.36), channel_id=1, source_target_pairs={{0,13},{1,12},{4,9},{5,8},{8,5},{9,4},{12,1},{13,0},{2,15},{3,14},... | collective-permute-start | bytes 393224 | tf_op jit(solution)/shard_map/ppermute | solution.py:402
  25.8 0.0 copy-done
  25.8 0.0 copy-done.1
  25.8 0.9 %prep.1 = (bf16[4,256,256]{2,1,0:T(8,128)(2,1)S(1)}, bf16[4,2,128,256]{3,2,1,0:T(8,128)(2,1)S(1)}) custom-call(s32[8]{0:T(128)} %perm_hbm.3, bf16[4,4,128,256]{3,2,1,0:T(8,128)(2,1)S(1)} %bitcast.5, bf16[4,2,4,128,128]{4,3,2,1,0:T(8,128)(2,1)S(1)} %bitcast.7, bf16[1,4,64,128]{3,2,1,0:T(8,128)(2,1)S(1)} %collective-permute-done.after_ref.refs_4_), custom_call_target="tpu_custom_call" | custom-call | flops 1000000 | bytes 10000 | tf_op jit(solution)/shard_map/prep/pallas_call | solution.py:261
  26.7 0.0 collective-permute-done.2.refs_0_
  26.7 0.0 collective-permute-done.3.refs_1_
  26.7 0.0 collective-permute-done.4.refs_2_
  26.7 1.9 %upper.1 = (f32[4,2,128,256]{3,2,1,0:T(8,128)S(1)}, f32[3,4,128,256]{3,2,1,0:T(8,128)S(1)}) custom-call(s32[8]{0:T(128)} %perm_hbm.3, bf16[4,4,128,256]{3,2,1,0:T(8,128)(2,1)S(1)} %bitcast.6, bf16[4,2,4,128,128]{4,3,2,1,0:T(8,128)(2,1)S(1)} %bitcast.8, bf16[1,4,64,256]{3,2,1,0:T(8,128)(2,1)S(1)} %collective-permute-done.2.refs_0_, ...), custom_call_target="tpu_custom_call" | custom-call | flops 1000000 | bytes 10000 | tf_op jit(solution)/shard_map/upper/pallas_call | solution.py:334
  28.6 0.0 collective-permute-done.8.mid_a
  28.6 2.0 %collective-permute-done.9.mid_b = bf16[1,4,64,256]{3,2,1,0:T(8,128)(2,1)S(1)} collective-permute-done((bf16[1,4,64,256]{3,2,1,0:T(8,128)(2,1)S(1)}, bf16[1,4,64,256]{3,2,1,0:T(8,128)(2,1)S(1)}, u32[]{:S(2)}, u32[]{:S(2)}) %collective-permute-start.9) | collective-permute-done | bytes 131104 | tf_op jit(solution)/shard_map/ppermute | solution.py:402
  30.7 1.4 %finish.1 = bf16[4,2,256,128]{3,2,1,0:T(8,128)(2,1)} custom-call(bf16[4,256,256]{2,1,0:T(8,128)(2,1)S(1)} %get-tuple-element.22.down_ref, bf16[4,2,128,256]{3,2,1,0:T(8,128)(2,1)S(1)} %get-tuple-element.23.row_ref, f32[4,2,128,256]{3,2,1,0:T(8,128)S(1)} %get-tuple-element.33.field_ref, f32[3,4,128,256]{3,2,1,0:T(8,128)S(1)} %get-tuple-element.34.top_ref, ...), custom_call_target="tpu_custom_call" | custom-call | flops 1000000 | bytes 10000 | tf_op jit(solution)/shard_map/finish/pallas_call | solution.py:382
Async XLA Ops:
  0.0 8.1 %copy-start.2 = (bf16[2,128,2,64]{1,3,2,0:T(8,128)(2,1)S(1)}, bf16[2,128,2,64]{1,3,2,0:T(8,128)(2,1)}, u32[]{:S(2)}) copy-start(bf16[2,128,2,64]{1,3,2,0:T(8,128)(2,1)} %param.8) | copy-start | bytes 196612
  0.0 8.1 %collective-permute-start.1 = (bf16[2,2,64,128]{3,2,1,0:T(8,128)(2,1)}, bf16[2,2,64,128]{3,2,1,0:T(8,128)(2,1)S(1)}, u32[]{:S(2)}, u32[]{:S(2)}) collective-permute-start(bf16[2,2,64,128]{3,2,1,0:T(8,128)(2,1)} %bitcast.9), channel_id=1, source_target_pairs={{0,2},{2,0},{1,3},{3,1},{4,6},{6,4},{5,7},{7,5},{8,10},{10,8},{9,1... | collective-permute-start | bytes 196616 | tf_op jit(solution)/shard_map/ppermute | solution.py:420
  5.4 20.4 %copy-start = (bf16[4,1,4,2,64,256]{5,4,3,2,1,0:T(8,128)(2,1)S(1)}, bf16[4,1,4,2,64,256]{5,4,3,2,1,0:T(8,128)(2,1)}, u32[]{:S(2)}) copy-start(bf16[4,1,4,2,64,256]{5,4,3,2,1,0:T(8,128)(2,1)} %param.14) | copy-start | bytes 3145732
  5.4 20.4 %copy-start.1 = (bf16[1,4,2,4,128,128]{5,4,3,2,1,0:T(8,128)(2,1)S(1)}, bf16[1,4,2,4,128,128]{5,4,3,2,1,0:T(8,128)(2,1)}, u32[]{:S(2)}) copy-start(bf16[1,4,2,4,128,128]{5,4,3,2,1,0:T(8,128)(2,1)} %param.15) | copy-start | bytes 3145732
  5.4 11.4 %collective-permute-start = (bf16[1,4,64,128]{3,2,1,0:T(8,128)(2,1)S(1)}, bf16[1,4,64,128]{3,2,1,0:T(8,128)(2,1)S(1)}, u32[]{:S(2)}, u32[]{:S(2)}) collective-permute-start(bf16[1,4,64,128]{3,2,1,0:T(8,128)(2,1)S(1)} %get-tuple-element.21), channel_id=1, source_target_pairs={{0,8},{1,9},{4,12},{5,13},{8,0},{9,1},{12,4},{13,5},{2,10},{3,11},... | collective-permute-start | bytes 196616 | tf_op jit(solution)/shard_map/ppermute | solution.py:402
  8.1 8.7 %collective-permute-start.5 = (bf16[1,4,64,128]{3,2,1,0:T(8,128)(2,1)S(1)}, bf16[1,4,64,128]{3,2,1,0:T(8,128)(2,1)S(1)}, u32[]{:S(2)}, u32[]{:S(2)}) collective-permute-start(bf16[1,4,64,128]{3,2,1,0:T(8,128)(2,1)S(1)} %get-tuple-element.30), channel_id=1, source_target_pairs={{0,9},{1,8},{4,13},{5,12},{8,1},{9,0},{12,5},{13,4},{2,11},{3,10},... | collective-permute-start | bytes 196616 | tf_op jit(solution)/shard_map/ppermute | solution.py:402
  10.5 10.9 %collective-permute-start.6 = (bf16[1,4,64,128]{3,2,1,0:T(8,128)(2,1)S(1)}, bf16[1,4,64,128]{3,2,1,0:T(8,128)(2,1)S(1)}, u32[]{:S(2)}, u32[]{:S(2)}) collective-permute-start(bf16[1,4,64,128]{3,2,1,0:T(8,128)(2,1)S(1)} %get-tuple-element.31), channel_id=1, source_target_pairs={{0,8},{1,9},{4,12},{5,13},{8,0},{9,1},{12,4},{13,5},{2,10},{3,11},... | collective-permute-start | bytes 196616 | tf_op jit(solution)/shard_map/ppermute | solution.py:402
  12.3 10.4 %collective-permute-start.7 = (bf16[1,4,64,128]{3,2,1,0:T(8,128)(2,1)S(1)}, bf16[1,4,64,128]{3,2,1,0:T(8,128)(2,1)S(1)}, u32[]{:S(2)}, u32[]{:S(2)}) collective-permute-start(bf16[1,4,64,128]{3,2,1,0:T(8,128)(2,1)S(1)} %get-tuple-element.32), channel_id=1, source_target_pairs={{0,9},{1,8},{4,13},{5,12},{8,1},{9,0},{12,5},{13,4},{2,11},{3,10},... | collective-permute-start | bytes 196616 | tf_op jit(solution)/shard_map/ppermute | solution.py:402
  13.2 13.5 %collective-permute-start.2 = (bf16[1,4,64,256]{3,2,1,0:T(8,128)(2,1)S(1)}, bf16[1,4,64,256]{3,2,1,0:T(8,128)(2,1)S(1)}, u32[]{:S(2)}, u32[]{:S(2)}) collective-permute-start(bf16[1,4,64,256]{3,2,1,0:T(8,128)(2,1)S(1)} %get-tuple-element.26), channel_id=1, source_target_pairs={{0,12},{1,13},{4,8},{5,9},{8,4},{9,5},{12,0},{13,1},{2,14},{3,15},... | collective-permute-start | bytes 393224 | tf_op jit(solution)/shard_map/ppermute | solution.py:402
  16.8 9.9 %collective-permute-start.3 = (bf16[1,4,64,256]{3,2,1,0:T(8,128)(2,1)S(1)}, bf16[1,4,64,256]{3,2,1,0:T(8,128)(2,1)S(1)}, u32[]{:S(2)}, u32[]{:S(2)}) collective-permute-start(bf16[1,4,64,256]{3,2,1,0:T(8,128)(2,1)S(1)} %get-tuple-element.27), channel_id=1, source_target_pairs={{0,4},{1,5},{4,0},{5,1},{8,12},{9,13},{12,8},{13,9},{2,6},{3,7},{6... | collective-permute-start | bytes 393224 | tf_op jit(solution)/shard_map/ppermute | solution.py:402
  16.8 9.9 %collective-permute-start.4 = (bf16[1,4,64,256]{3,2,1,0:T(8,128)(2,1)S(1)}, bf16[1,4,64,256]{3,2,1,0:T(8,128)(2,1)S(1)}, u32[]{:S(2)}, u32[]{:S(2)}) collective-permute-start(bf16[1,4,64,256]{3,2,1,0:T(8,128)(2,1)S(1)} %get-tuple-element.28), channel_id=1, source_target_pairs={{0,1},{1,0},{4,5},{5,4},{8,9},{9,8},{12,13},{13,12},{2,3},{3,2},{6... | collective-permute-start | bytes 393224 | tf_op jit(solution)/shard_map/ppermute | solution.py:402
  21.3 7.3 %collective-permute-start.8 = (bf16[1,4,64,256]{3,2,1,0:T(8,128)(2,1)S(1)}, bf16[1,4,64,256]{3,2,1,0:T(8,128)(2,1)S(1)}, u32[]{:S(2)}, u32[]{:S(2)}) collective-permute-start(bf16[1,4,64,256]{3,2,1,0:T(8,128)(2,1)S(1)} %get-tuple-element.35), channel_id=1, source_target_pairs={{0,5},{1,4},{4,1},{5,0},{8,13},{9,12},{12,9},{13,8},{2,7},{3,6},{6... | collective-permute-start | bytes 393224 | tf_op jit(solution)/shard_map/ppermute | solution.py:402
  22.7 8.0 %collective-permute-start.9 = (bf16[1,4,64,256]{3,2,1,0:T(8,128)(2,1)S(1)}, bf16[1,4,64,256]{3,2,1,0:T(8,128)(2,1)S(1)}, u32[]{:S(2)}, u32[]{:S(2)}) collective-permute-start(bf16[1,4,64,256]{3,2,1,0:T(8,128)(2,1)S(1)} %get-tuple-element.36), channel_id=1, source_target_pairs={{0,13},{1,12},{4,9},{5,8},{8,5},{9,4},{12,1},{13,0},{2,15},{3,14},... | collective-permute-start | bytes 393224 | tf_op jit(solution)/shard_map/ppermute | solution.py:402

commit v13 on v12

--- a/solution.py
+++ b/solution.py
@@ -414,7 +414,7 @@
     dests = 2 * columns
     two = both_cores((2,))
     full = both_cores(range(columns - 1, 3, -1)) + [(3, 0), (1, 0), (0, 1), (0, 0)]
-    late = [(1, 1), (3, 1)]
+    late = [(3, 1), (1, 1)]
     if 2 * x.shape[2] == NRHS:
         halved = two
         xs = [x, lax.ppermute(x, "rhs", [(0, 1), (1, 0)])]

time: 32.3 us -> 33.3 us (1.031)
  waiting for transfers between devices: 7.86 us -> 9.11 us
    ppermute x9, waiting for transfers between devices: 7.86 us -> 9.11 us  [send(): lax.ppermute(block, ('blk', 'sub'), [(m, m ^ code) for m in range(dests)])]
  transfers between devices with their start and end apart: 10 -> 10, of which waited for: 3 -> 4; matrix products, arithmetic and copies ran while one was open for 0% -> 0% of each run, Pallas kernels for 24% -> 23%
where the time goes in v13:
time: 33.3 us; the launch traced here: 33.1 us
  starting transfers between devices  14.9 us (45%)
  waiting for transfers between devices  9.11 us (27%)
  Pallas kernels  8.98 us (27%)
    ppermute x9, starting transfers between devices, send(): lax.ppermute(block, ('blk', 'sub'), [(m, m ^ code) for m in range(dests)])  12 us
    ppermute x9, waiting for transfers between devices, send(): lax.ppermute(block, ('blk', 'sub'), [(m, m ^ code) for m in range(dests)])  9.11 us
    ppermute x1, starting transfers between devices, on_device(): xs = [x, lax.ppermute(x, 'rhs', [(0, 1), (1, 0)])]  2.94 us
    pallas_call x1, Pallas kernels, own(): pl.pallas_call(functools.partial(own_kernel, routes), out_shape=[block] *...  2.47 us
    pallas_call x1, Pallas kernels, lower(): pl.pallas_call(functools.partial(lower_kernel, full, halved), out_shape=[...  2.34 us
    pallas_call x1, Pallas kernels, upper(): pl.pallas_call(functools.partial(upper_kernel, full, halved, late), out_s...  1.87 us
    pallas_call x1, Pallas kernels, finish(): pl.pallas_call(finish_kernel, out_shape=jax.ShapeDtypeStruct(shape, BF16)...  1.44 us
    pallas_call x1, Pallas kernels, prep(): pl.pallas_call(functools.partial(prep_kernel, late), out_shape=[pltpu.VME...  0.86 us
  transfers between devices with their start and end apart: 10, of which 4 were waited for; matrix products, arithmetic and copies ran while one was open for 0% of the time, Pallas kernels for 23%

profile of v13, /device:TPU:0, one launch (start us, length us, event | category | flops | bytes accessed | tf_op | source)
XLA Modules:
  0.0 33.1 jit_solution(4735923519636597295)
XLA Ops:
  0.0 0.0 copy-start.2
  0.0 2.9 %collective-permute-start.1 = (bf16[2,2,64,128]{3,2,1,0:T(8,128)(2,1)}, bf16[2,2,64,128]{3,2,1,0:T(8,128)(2,1)S(1)}, u32[]{:S(2)}, u32[]{:S(2)}) collective-permute-start(bf16[2,2,64,128]{3,2,1,0:T(8,128)(2,1)} %bitcast.9), channel_id=1, source_target_pairs={{0,2},{2,0},{1,3},{3,1},{4,6},{6,4},{5,7},{7,5},{8,10},{10,8},{9,1... | collective-permute-start | bytes 196616 | tf_op jit(solution)/shard_map/ppermute | solution.py:420
  2.9 2.5 %own.1 = (bf16[1,4,64,128]{3,2,1,0:T(8,128)(2,1)S(1)}, bf16[1,4,64,128]{3,2,1,0:T(8,128)(2,1)S(1)}, bf16[2,16,128,128]{3,2,1,0:T(8,128)(2,1)S(1)}, bf16[1,32,64,256]{3,2,1,0:T(8,128)(2,1)S(1)}) custom-call(s32[2]{0:T(128)} %count_hbm.3, s32[32]{0:T(128)} %parent_hbm.3, bf16[2,2,64,128]{3,2,1,0:T(8,128)(2,1)} %bitcast.10, bf16[2,16,128,128]{3,2,1,0:T(8,128)(2,1)} %bitcast.12, ...), custom_call_target="tpu_custom_call" | custom-call | flops 1000000 | bytes 10000 | tf_op jit(solution)/shard_map/own/pallas_call | solution.py:127
  5.4 0.0 copy-start
  5.4 0.0 copy-start.1
  5.4 2.6 %collective-permute-start = (bf16[1,4,64,128]{3,2,1,0:T(8,128)(2,1)S(1)}, bf16[1,4,64,128]{3,2,1,0:T(8,128)(2,1)S(1)}, u32[]{:S(2)}, u32[]{:S(2)}) collective-permute-start(bf16[1,4,64,128]{3,2,1,0:T(8,128)(2,1)S(1)} %get-tuple-element.21), channel_id=1, source_target_pairs={{0,8},{1,9},{4,12},{5,13},{8,0},{9,1},{12,4},{13,5},{2,10},{3,11},... | collective-permute-start | bytes 196616 | tf_op jit(solution)/shard_map/ppermute | solution.py:402
  8.1 0.0 collective-permute-start.5
  8.1 0.0 collective-permute-done.1.refs_1_
  8.1 0.0 copy-done.2
  8.1 2.3 %lower.1 = (bf16[1,4,64,256]{3,2,1,0:T(8,128)(2,1)S(1)}, bf16[1,4,64,256]{3,2,1,0:T(8,128)(2,1)S(1)}, bf16[1,4,64,256]{3,2,1,0:T(8,128)(2,1)S(1)}, bf16[1,4,64,2...) custom-call(s32[2]{0:T(128)} %count_hbm.3, ...), custom_call_target="tpu_custom_call" | custom-call | flops 1000000 | bytes 10000 | tf_op jit(solution)/shard_map/lower/pallas_call | solution.py:193
  10.5 1.9 %collective-permute-start.6 = (bf16[1,4,64,128]{3,2,1,0:T(8,128)(2,1)S(1)}, bf16[1,4,64,128]{3,2,1,0:T(8,128)(2,1)S(1)}, u32[]{:S(2)}, u32[]{:S(2)}) collective-permute-start(bf16[1,4,64,128]{3,2,1,0:T(8,128)(2,1)S(1)} %get-tuple-element.31), channel_id=1, source_target_pairs={{0,8},{1,9},{4,12},{5,13},{8,0},{9,1},{12,4},{13,5},{2,10},{3,11},... | collective-permute-start | bytes 196616 | tf_op jit(solution)/shard_map/ppermute | solution.py:402
  12.3 0.9 %collective-permute-start.7 = (bf16[1,4,64,128]{3,2,1,0:T(8,128)(2,1)S(1)}, bf16[1,4,64,128]{3,2,1,0:T(8,128)(2,1)S(1)}, u32[]{:S(2)}, u32[]{:S(2)}) collective-permute-start(bf16[1,4,64,128]{3,2,1,0:T(8,128)(2,1)S(1)} %get-tuple-element.32), channel_id=1, source_target_pairs={{0,9},{1,8},{4,13},{5,12},{8,1},{9,0},{12,5},{13,4},{2,11},{3,10},... | collective-permute-start | bytes 196616 | tf_op jit(solution)/shard_map/ppermute | solution.py:402
  13.2 3.6 %collective-permute-start.2 = (bf16[1,4,64,256]{3,2,1,0:T(8,128)(2,1)S(1)}, bf16[1,4,64,256]{3,2,1,0:T(8,128)(2,1)S(1)}, u32[]{:S(2)}, u32[]{:S(2)}) collective-permute-start(bf16[1,4,64,256]{3,2,1,0:T(8,128)(2,1)S(1)} %get-tuple-element.26), channel_id=1, source_target_pairs={{0,12},{1,13},{4,8},{5,9},{8,4},{9,5},{12,0},{13,1},{2,14},{3,15},... | collective-permute-start | bytes 393224 | tf_op jit(solution)/shard_map/ppermute | solution.py:402
  16.8 0.0 collective-permute-done.after_ref.refs_4_
  16.8 0.0 collective-permute-start.3
  16.8 0.0 collective-permute-done.5.refs_5_
  16.8 0.1 collective-permute-start.4
  16.9 4.4 %collective-permute-done.6.refs_6_ = bf16[1,4,64,128]{3,2,1,0:T(8,128)(2,1)S(1)} collective-permute-done((bf16[1,4,64,128]{3,2,1,0:T(8,128)(2,1)S(1)}, bf16[1,4,64,128]{3,2,1,0:T(8,128)(2,1)S(1)}, u32[]{:S(2)}, u32[]{:S(2)}) %collective-permute-start.6) | collective-permute-done | bytes 65568 | tf_op jit(solution)/shard_map/ppermute | solution.py:402
  21.3 2.9 %collective-permute-start.8 = (bf16[1,4,64,256]{3,2,1,0:T(8,128)(2,1)S(1)}, bf16[1,4,64,256]{3,2,1,0:T(8,128)(2,1)S(1)}, u32[]{:S(2)}, u32[]{:S(2)}) collective-permute-start(bf16[1,4,64,256]{3,2,1,0:T(8,128)(2,1)S(1)} %get-tuple-element.35), channel_id=1, source_target_pairs={{0,13},{1,12},{4,9},{5,8},{8,5},{9,4},{12,1},{13,0},{2,15},{3,14},... | collective-permute-start | bytes 393224 | tf_op jit(solution)/shard_map/ppermute | solution.py:402
  24.2 0.0 collective-permute-done.7.refs_7_
  24.2 0.0 collective-permute-start.9
  24.2 0.0 copy-done
  24.2 0.0 copy-done.1
  24.2 0.9 %prep.1 = (bf16[4,256,256]{2,1,0:T(8,128)(2,1)S(1)}, bf16[4,2,128,256]{3,2,1,0:T(8,128)(2,1)S(1)}) custom-call(s32[8]{0:T(128)} %perm_hbm.3, bf16[4,4,128,256]{3,2,1,0:T(8,128)(2,1)S(1)} %bitcast.5, bf16[4,2,4,128,128]{4,3,2,1,0:T(8,128)(2,1)S(1)} %bitcast.7, bf16[1,4,64,128]{3,2,1,0:T(8,128)(2,1)S(1)} %collective-permute-done.after_ref.refs_4_), custom_call_target="tpu_custom_call" | custom-call | flops 1000000 | bytes 10000 | tf_op jit(solution)/shard_map/prep/pallas_call | solution.py:261
  25.1 0.0 collective-permute-done.2.refs_0_
  25.1 0.2 collective-permute-done.3.refs_1_
  25.2 0.0 collective-permute-done.4.refs_2_
  25.2 1.9 %upper.1 = (f32[4,2,128,256]{3,2,1,0:T(8,128)S(1)}, f32[3,4,128,256]{3,2,1,0:T(8,128)S(1)}) custom-call(s32[8]{0:T(128)} %perm_hbm.3, bf16[4,4,128,256]{3,2,1,0:T(8,128)(2,1)S(1)} %bitcast.6, bf16[4,2,4,128,128]{4,3,2,1,0:T(8,128)(2,1)S(1)} %bitcast.8, bf16[1,4,64,256]{3,2,1,0:T(8,128)(2,1)S(1)} %collective-permute-done.2.refs_0_, ...), custom_call_target="tpu_custom_call" | custom-call | flops 1000000 | bytes 10000 | tf_op jit(solution)/shard_map/upper/pallas_call | solution.py:334
  27.1 1.9 %collective-permute-done.8.mid_a = bf16[1,4,64,256]{3,2,1,0:T(8,128)(2,1)S(1)} collective-permute-done((bf16[1,4,64,256]{3,2,1,0:T(8,128)(2,1)S(1)}, bf16[1,4,64,256]{3,2,1,0:T(8,128)(2,1)S(1)}, u32[]{:S(2)}, u32[]{:S(2)}) %collective-permute-start.8) | collective-permute-done | bytes 131104 | tf_op jit(solution)/shard_map/ppermute | solution.py:402
  29.0 2.7 %collective-permute-done.9.mid_b = bf16[1,4,64,256]{3,2,1,0:T(8,128)(2,1)S(1)} collective-permute-done((bf16[1,4,64,256]{3,2,1,0:T(8,128)(2,1)S(1)}, bf16[1,4,64,256]{3,2,1,0:T(8,128)(2,1)S(1)}, u32[]{:S(2)}, u32[]{:S(2)}) %collective-permute-start.9) | collective-permute-done | bytes 131104 | tf_op jit(solution)/shard_map/ppermute | solution.py:402
  31.7 1.4 %finish.1 = bf16[4,2,256,128]{3,2,1,0:T(8,128)(2,1)} custom-call(bf16[4,256,256]{2,1,0:T(8,128)(2,1)S(1)} %get-tuple-element.22.down_ref, bf16[4,2,128,256]{3,2,1,0:T(8,128)(2,1)S(1)} %get-tuple-element.23.row_ref, f32[4,2,128,256]{3,2,1,0:T(8,128)S(1)} %get-tuple-element.33.field_ref, f32[3,4,128,256]{3,2,1,0:T(8,128)S(1)} %get-tuple-element.34.top_ref, ...), custom_call_target="tpu_custom_call" | custom-call | flops 1000000 | bytes 10000 | tf_op jit(solution)/shard_map/finish/pallas_call | solution.py:382
Async XLA Ops:
  0.0 8.1 %copy-start.2 = (bf16[2,128,2,64]{1,3,2,0:T(8,128)(2,1)S(1)}, bf16[2,128,2,64]{1,3,2,0:T(8,128)(2,1)}, u32[]{:S(2)}) copy-start(bf16[2,128,2,64]{1,3,2,0:T(8,128)(2,1)} %param.8) | copy-start | bytes 196612
  0.0 8.1 %collective-permute-start.1 = (bf16[2,2,64,128]{3,2,1,0:T(8,128)(2,1)}, bf16[2,2,64,128]{3,2,1,0:T(8,128)(2,1)S(1)}, u32[]{:S(2)}, u32[]{:S(2)}) collective-permute-start(bf16[2,2,64,128]{3,2,1,0:T(8,128)(2,1)} %bitcast.9), channel_id=1, source_target_pairs={{0,2},{2,0},{1,3},{3,1},{4,6},{6,4},{5,7},{7,5},{8,10},{10,8},{9,1... | collective-permute-start | bytes 196616 | tf_op jit(solution)/shard_map/ppermute | solution.py:420
  5.4 18.8 %copy-start = (bf16[4,1,4,2,64,256]{5,4,3,2,1,0:T(8,128)(2,1)S(1)}, bf16[4,1,4,2,64,256]{5,4,3,2,1,0:T(8,128)(2,1)}, u32[]{:S(2)}) copy-start(bf16[4,1,4,2,64,256]{5,4,3,2,1,0:T(8,128)(2,1)} %param.14) | copy-start | bytes 3145732
  5.4 18.8 %copy-start.1 = (bf16[1,4,2,4,128,128]{5,4,3,2,1,0:T(8,128)(2,1)S(1)}, bf16[1,4,2,4,128,128]{5,4,3,2,1,0:T(8,128)(2,1)}, u32[]{:S(2)}) copy-start(bf16[1,4,2,4,128,128]{5,4,3,2,1,0:T(8,128)(2,1)} %param.15) | copy-start | bytes 3145732
  5.4 11.4 %collective-permute-start = (bf16[1,4,64,128]{3,2,1,0:T(8,128)(2,1)S(1)}, bf16[1,4,64,128]{3,2,1,0:T(8,128)(2,1)S(1)}, u32[]{:S(2)}, u32[]{:S(2)}) collective-permute-start(bf16[1,4,64,128]{3,2,1,0:T(8,128)(2,1)S(1)} %get-tuple-element.21), channel_id=1, source_target_pairs={{0,8},{1,9},{4,12},{5,13},{8,0},{9,1},{12,4},{13,5},{2,10},{3,11},... | collective-permute-start | bytes 196616 | tf_op jit(solution)/shard_map/ppermute | solution.py:402
  8.1 8.7 %collective-permute-start.5 = (bf16[1,4,64,128]{3,2,1,0:T(8,128)(2,1)S(1)}, bf16[1,4,64,128]{3,2,1,0:T(8,128)(2,1)S(1)}, u32[]{:S(2)}, u32[]{:S(2)}) collective-permute-start(bf16[1,4,64,128]{3,2,1,0:T(8,128)(2,1)S(1)} %get-tuple-element.30), channel_id=1, source_target_pairs={{0,9},{1,8},{4,13},{5,12},{8,1},{9,0},{12,5},{13,4},{2,11},{3,10},... | collective-permute-start | bytes 196616 | tf_op jit(solution)/shard_map/ppermute | solution.py:402
  10.5 10.9 %collective-permute-start.6 = (bf16[1,4,64,128]{3,2,1,0:T(8,128)(2,1)S(1)}, bf16[1,4,64,128]{3,2,1,0:T(8,128)(2,1)S(1)}, u32[]{:S(2)}, u32[]{:S(2)}) collective-permute-start(bf16[1,4,64,128]{3,2,1,0:T(8,128)(2,1)S(1)} %get-tuple-element.31), channel_id=1, source_target_pairs={{0,8},{1,9},{4,12},{5,13},{8,0},{9,1},{12,4},{13,5},{2,10},{3,11},... | collective-permute-start | bytes 196616 | tf_op jit(solution)/shard_map/ppermute | solution.py:402
  12.3 11.9 %collective-permute-start.7 = (bf16[1,4,64,128]{3,2,1,0:T(8,128)(2,1)S(1)}, bf16[1,4,64,128]{3,2,1,0:T(8,128)(2,1)S(1)}, u32[]{:S(2)}, u32[]{:S(2)}) collective-permute-start(bf16[1,4,64,128]{3,2,1,0:T(8,128)(2,1)S(1)} %get-tuple-element.32), channel_id=1, source_target_pairs={{0,9},{1,8},{4,13},{5,12},{8,1},{9,0},{12,5},{13,4},{2,11},{3,10},... | collective-permute-start | bytes 196616 | tf_op jit(solution)/shard_map/ppermute | solution.py:402
  13.2 11.8 %collective-permute-start.2 = (bf16[1,4,64,256]{3,2,1,0:T(8,128)(2,1)S(1)}, bf16[1,4,64,256]{3,2,1,0:T(8,128)(2,1)S(1)}, u32[]{:S(2)}, u32[]{:S(2)}) collective-permute-start(bf16[1,4,64,256]{3,2,1,0:T(8,128)(2,1)S(1)} %get-tuple-element.26), channel_id=1, source_target_pairs={{0,12},{1,13},{4,8},{5,9},{8,4},{9,5},{12,0},{13,1},{2,14},{3,15},... | collective-permute-start | bytes 393224 | tf_op jit(solution)/shard_map/ppermute | solution.py:402
  16.8 8.4 %collective-permute-start.3 = (bf16[1,4,64,256]{3,2,1,0:T(8,128)(2,1)S(1)}, bf16[1,4,64,256]{3,2,1,0:T(8,128)(2,1)S(1)}, u32[]{:S(2)}, u32[]{:S(2)}) collective-permute-start(bf16[1,4,64,256]{3,2,1,0:T(8,128)(2,1)S(1)} %get-tuple-element.27), channel_id=1, source_target_pairs={{0,4},{1,5},{4,0},{5,1},{8,12},{9,13},{12,8},{13,9},{2,6},{3,7},{6... | collective-permute-start | bytes 393224 | tf_op jit(solution)/shard_map/ppermute | solution.py:402
  16.8 8.4 %collective-permute-start.4 = (bf16[1,4,64,256]{3,2,1,0:T(8,128)(2,1)S(1)}, bf16[1,4,64,256]{3,2,1,0:T(8,128)(2,1)S(1)}, u32[]{:S(2)}, u32[]{:S(2)}) collective-permute-start(bf16[1,4,64,256]{3,2,1,0:T(8,128)(2,1)S(1)} %get-tuple-element.28), channel_id=1, source_target_pairs={{0,1},{1,0},{4,5},{5,4},{8,9},{9,8},{12,13},{13,12},{2,3},{3,2},{6... | collective-permute-start | bytes 393224 | tf_op jit(solution)/shard_map/ppermute | solution.py:402
  21.3 7.7 %collective-permute-start.8 = (bf16[1,4,64,256]{3,2,1,0:T(8,128)(2,1)S(1)}, bf16[1,4,64,256]{3,2,1,0:T(8,128)(2,1)S(1)}, u32[]{:S(2)}, u32[]{:S(2)}) collective-permute-start(bf16[1,4,64,256]{3,2,1,0:T(8,128)(2,1)S(1)} %get-tuple-element.35), channel_id=1, source_target_pairs={{0,13},{1,12},{4,9},{5,8},{8,5},{9,4},{12,1},{13,0},{2,15},{3,14},... | collective-permute-start | bytes 393224 | tf_op jit(solution)/shard_map/ppermute | solution.py:402
  24.2 7.5 %collective-permute-start.9 = (bf16[1,4,64,256]{3,2,1,0:T(8,128)(2,1)S(1)}, bf16[1,4,64,256]{3,2,1,0:T(8,128)(2,1)S(1)}, u32[]{:S(2)}, u32[]{:S(2)}) collective-permute-start(bf16[1,4,64,256]{3,2,1,0:T(8,128)(2,1)S(1)} %get-tuple-element.36), channel_id=1, source_target_pairs={{0,5},{1,4},{4,1},{5,0},{8,13},{9,12},{12,9},{13,8},{2,7},{3,6},{6... | collective-permute-start | bytes 393224 | tf_op jit(solution)/shard_map/ppermute | solution.py:402

commit v14 on v12

--- a/solution.py
+++ b/solution.py
@@ -102,21 +102,46 @@
     }
     for b in range(boxes):
         copies[b] = pltpu.make_async_copy(basis_hbm.at[b], basis_ref.at[b], sems.at[4 + b])
-    for name in ["x", 0, "count"] + list(range(1, boxes)) + ["up", "parent"]:
+    for name in ["x", "count", "parent", *range(boxes), "up"]:
         copies[name].start()
-    for name in ["x", "count", *range(boxes)]:
+    for name in ["x", "count", "parent", *range(boxes)]:
         copies[name].wait()
-
-    def spreads(b):
+    spreads = []
+    for b in range(boxes):
         real, imag = x_ref[b, 0], x_ref[b, 1]
-        return jnp.concatenate([real, imag, -imag, real], axis=0)
-
-    leaf_stage(
-        spreads, half_columns, count_ref, basis_ref, g_ref, leaf_ref, lambda name: None
-    )
+        spreads.append(jnp.concatenate([real, imag, -imag, real], axis=0))
+    pairs, local, rank = outs[0].shape[:3]
+    first = lax.axis_index("rhs") * basis_ref.shape[1]
+    even = pl.ds(0, rank, stride=2)
+    odd = pl.ds(1, rank, stride=2)
+    jobs = [
+        (out, p, h, partner(k, which) * local + h)
+        for out, (k, which) in zip(outs, routes)
+        for p in range(pairs)
+        for h in range(local)
+    ]
+    for i, (_, p, _, j) in enumerate(jobs):
+        d = parent_ref[j]
+        for child in range(2):
+            b, slot = 2 * p + child, 2 * i + child
+            g = lax.dot_general(
+                basis_ref[b, d], spreads[b], (((1,), (1,)), ((), ())), preferred_element_type=F32
+            )
+            g_ref[slot, 0] = g[:, :NRHS]
+            g_ref[slot, 1] = g[:, NRHS:]
+            live = first + d < count_ref[b]
+            pieces = half_columns(
+                [g_ref[slot, c, even, :] for c in range(2)],
+                [g_ref[slot, c, odd, :] for c in range(2)],
+            )
+            for c, piece in enumerate(pieces):
+                piece = jnp.where(live, piece, jnp.zeros_like(piece)).astype(BF16)
+                base = (2 * child + c) * rank
+                leaf_ref[i, base : base + rank, :] = piece
     copies["up"].wait()
-    copies["parent"].wait()
-    up_stage(outs, routes, parent_ref, up_ref, leaf_ref)
+    for i, (out, p, h, j) in enumerate(jobs):
+        mid = jnp.dot(up_ref[p, j], leaf_ref[i], preferred_element_type=F32)
+        out[p, h] = mid.astype(BF16)
 
 
 def own(routes, dests, count, parents, x, basis, up):
@@ -124,6 +149,7 @@
     pairs, dirs_up, rank, _ = up.shape
     block = pltpu.VMEM((pairs, dirs_up // dests, rank, NRHS), BF16)
     args = [count, parents, x, basis, up]
+    jobs = len(routes) * pairs * (dirs_up // dests)
     return pl.pallas_call(
         functools.partial(own_kernel, routes),
         out_shape=[block] * len(routes)
@@ -134,8 +160,8 @@
             pltpu.SMEM(count.shape, jnp.int32),
             pltpu.SMEM(parents.shape, jnp.int32),
             pltpu.VMEM(x.shape, BF16),
-            pltpu.VMEM((pairs, dirs, 4 * rank, NRHS), BF16),
-            pltpu.VMEM((boxes * dirs, 2, rows, NRHS), F32),
+            pltpu.VMEM((jobs, 4 * rank, NRHS), BF16),
+            pltpu.VMEM((2 * jobs, 2, rows, NRHS), F32),
             pltpu.SemaphoreType.DMA((4 + boxes,)),
         ],
         compiler_params=PARAMS,

time: 32.3 us -> 31.9 us (0.988)
  Pallas kernels: 8.99 us -> 8.57 us
    pallas_call x1, Pallas kernels: 2.47 us -> 2.06 us  [own(): pl.pallas_call(functools.partial(own_kernel, routes), out_shape=[block] *...]
  transfers between devices with their start and end apart: 10 -> 10, of which waited for: 3 -> 3; matrix products, arithmetic and copies ran while one was open for 0% -> 0% of each run, Pallas kernels for 24% -> 22%
where the time goes in v14:
time: 31.9 us; the launch traced here: 31.7 us
  starting transfers between devices  15.2 us (48%)
  Pallas kernels  8.57 us (27%)
  waiting for transfers between devices  7.85 us (25%)
    ppermute x9, starting transfers between devices, send(): lax.ppermute(block, ('blk', 'sub'), [(m, m ^ code) for m in range(dests)])  12.2 us
    ppermute x9, waiting for transfers between devices, send(): lax.ppermute(block, ('blk', 'sub'), [(m, m ^ code) for m in range(dests)])  7.84 us
    ppermute x1, starting transfers between devices, on_device(): xs = [x, lax.ppermute(x, 'rhs', [(0, 1), (1, 0)])]  2.94 us
    pallas_call x1, Pallas kernels, lower(): pl.pallas_call(functools.partial(lower_kernel, full, halved), out_shape=[...  2.34 us
    pallas_call x1, Pallas kernels, own(): pl.pallas_call(functools.partial(own_kernel, routes), out_shape=[block] *...  2.06 us
    pallas_call x1, Pallas kernels, upper(): pl.pallas_call(functools.partial(upper_kernel, full, halved, late), out_s...  1.88 us
    pallas_call x1, Pallas kernels, finish(): pl.pallas_call(finish_kernel, out_shape=jax.ShapeDtypeStruct(shape, BF16)...  1.44 us
    pallas_call x1, Pallas kernels, prep(): pl.pallas_call(functools.partial(prep_kernel, late), out_shape=[pltpu.VME...  0.85 us
  transfers between devices with their start and end apart: 10, of which 3 were waited for; matrix products, arithmetic and copies ran while one was open for 0% of the time, Pallas kernels for 22%

profile of v14, /device:TPU:0, one launch (start us, length us, event | category | flops | bytes accessed | tf_op | source)
XLA Modules:
  0.0 31.7 jit_solution(5125493777911492101)
XLA Ops:
  0.0 0.0 copy-start.2
  0.0 2.9 %collective-permute-start.1 = (bf16[2,2,64,128]{3,2,1,0:T(8,128)(2,1)}, bf16[2,2,64,128]{3,2,1,0:T(8,128)(2,1)S(1)}, u32[]{:S(2)}, u32[]{:S(2)}) collective-permute-start(bf16[2,2,64,128]{3,2,1,0:T(8,128)(2,1)} %bitcast.9), channel_id=1, source_target_pairs={{0,2},{2,0},{1,3},{3,1},{4,6},{6,4},{5,7},{7,5},{8,10},{10,8},{9,1... | collective-permute-start | bytes 196616 | tf_op jit(solution)/shard_map/ppermute | solution.py:446
  2.9 2.1 %own.1 = (bf16[1,4,64,128]{3,2,1,0:T(8,128)(2,1)S(1)}, bf16[1,4,64,128]{3,2,1,0:T(8,128)(2,1)S(1)}, bf16[2,16,128,128]{3,2,1,0:T(8,128)(2,1)S(1)}, bf16[1,32,64,256]{3,2,1,0:T(8,128)(2,1)S(1)}) custom-call(s32[2]{0:T(128)} %count_hbm.3, s32[32]{0:T(128)} %parent_hbm.3, bf16[2,2,64,128]{3,2,1,0:T(8,128)(2,1)} %bitcast.10, bf16[2,16,128,128]{3,2,1,0:T(8,128)(2,1)} %bitcast.12, ...), custom_call_target="tpu_custom_call" | custom-call | flops 1000000 | bytes 10000 | tf_op jit(solution)/shard_map/own/pallas_call | solution.py:153
  5.0 0.0 copy-start
  5.0 0.0 copy-start.1
  5.0 2.7 %collective-permute-start = (bf16[1,4,64,128]{3,2,1,0:T(8,128)(2,1)S(1)}, bf16[1,4,64,128]{3,2,1,0:T(8,128)(2,1)S(1)}, u32[]{:S(2)}, u32[]{:S(2)}) collective-permute-start(bf16[1,4,64,128]{3,2,1,0:T(8,128)(2,1)S(1)} %get-tuple-element.21), channel_id=1, source_target_pairs={{0,8},{1,9},{4,12},{5,13},{8,0},{9,1},{12,4},{13,5},{2,10},{3,11},... | collective-permute-start | bytes 196616 | tf_op jit(solution)/shard_map/ppermute | solution.py:428
  7.7 0.0 collective-permute-start.5
  7.7 0.0 collective-permute-done.1.refs_1_
  7.7 0.0 copy-done.2
  7.7 2.3 %lower.1 = (bf16[1,4,64,256]{3,2,1,0:T(8,128)(2,1)S(1)}, bf16[1,4,64,256]{3,2,1,0:T(8,128)(2,1)S(1)}, bf16[1,4,64,256]{3,2,1,0:T(8,128)(2,1)S(1)}, bf16[1,4,64,2...) custom-call(s32[2]{0:T(128)} %count_hbm.3, ...), custom_call_target="tpu_custom_call" | custom-call | flops 1000000 | bytes 10000 | tf_op jit(solution)/shard_map/lower/pallas_call | solution.py:219
  10.0 1.9 %collective-permute-start.6 = (bf16[1,4,64,128]{3,2,1,0:T(8,128)(2,1)S(1)}, bf16[1,4,64,128]{3,2,1,0:T(8,128)(2,1)S(1)}, u32[]{:S(2)}, u32[]{:S(2)}) collective-permute-start(bf16[1,4,64,128]{3,2,1,0:T(8,128)(2,1)S(1)} %get-tuple-element.31), channel_id=1, source_target_pairs={{0,8},{1,9},{4,12},{5,13},{8,0},{9,1},{12,4},{13,5},{2,10},{3,11},... | collective-permute-start | bytes 196616 | tf_op jit(solution)/shard_map/ppermute | solution.py:428
  11.9 0.9 %collective-permute-start.7 = (bf16[1,4,64,128]{3,2,1,0:T(8,128)(2,1)S(1)}, bf16[1,4,64,128]{3,2,1,0:T(8,128)(2,1)S(1)}, u32[]{:S(2)}, u32[]{:S(2)}) collective-permute-start(bf16[1,4,64,128]{3,2,1,0:T(8,128)(2,1)S(1)} %get-tuple-element.32), channel_id=1, source_target_pairs={{0,9},{1,8},{4,13},{5,12},{8,1},{9,0},{12,5},{13,4},{2,11},{3,10},... | collective-permute-start | bytes 196616 | tf_op jit(solution)/shard_map/ppermute | solution.py:428
  12.8 3.6 %collective-permute-start.2 = (bf16[1,4,64,256]{3,2,1,0:T(8,128)(2,1)S(1)}, bf16[1,4,64,256]{3,2,1,0:T(8,128)(2,1)S(1)}, u32[]{:S(2)}, u32[]{:S(2)}) collective-permute-start(bf16[1,4,64,256]{3,2,1,0:T(8,128)(2,1)S(1)} %get-tuple-element.26), channel_id=1, source_target_pairs={{0,12},{1,13},{4,8},{5,9},{8,4},{9,5},{12,0},{13,1},{2,14},{3,15},... | collective-permute-start | bytes 393224 | tf_op jit(solution)/shard_map/ppermute | solution.py:428
  16.4 0.0 collective-permute-done.after_ref.refs_4_
  16.4 0.0 collective-permute-start.3
  16.4 0.0 collective-permute-done.5.refs_5_
  16.4 0.1 collective-permute-start.4
  16.5 4.4 %collective-permute-done.6.refs_6_ = bf16[1,4,64,128]{3,2,1,0:T(8,128)(2,1)S(1)} collective-permute-done((bf16[1,4,64,128]{3,2,1,0:T(8,128)(2,1)S(1)}, bf16[1,4,64,128]{3,2,1,0:T(8,128)(2,1)S(1)}, u32[]{:S(2)}, u32[]{:S(2)}) %collective-permute-start.6) | collective-permute-done | bytes 65568 | tf_op jit(solution)/shard_map/ppermute | solution.py:428
  20.9 0.0 collective-permute-start.8
  20.9 1.4 %collective-permute-done.7.refs_7_ = bf16[1,4,64,128]{3,2,1,0:T(8,128)(2,1)S(1)} collective-permute-done((bf16[1,4,64,128]{3,2,1,0:T(8,128)(2,1)S(1)}, bf16[1,4,64,128]{3,2,1,0:T(8,128)(2,1)S(1)}, u32[]{:S(2)}, u32[]{:S(2)}) %collective-permute-start.7) | collective-permute-done | bytes 65568 | tf_op jit(solution)/shard_map/ppermute | solution.py:428
  22.3 3.1 %collective-permute-start.9 = (bf16[1,4,64,256]{3,2,1,0:T(8,128)(2,1)S(1)}, bf16[1,4,64,256]{3,2,1,0:T(8,128)(2,1)S(1)}, u32[]{:S(2)}, u32[]{:S(2)}) collective-permute-start(bf16[1,4,64,256]{3,2,1,0:T(8,128)(2,1)S(1)} %get-tuple-element.36), channel_id=1, source_target_pairs={{0,13},{1,12},{4,9},{5,8},{8,5},{9,4},{12,1},{13,0},{2,15},{3,14},... | collective-permute-start | bytes 393224 | tf_op jit(solution)/shard_map/ppermute | solution.py:428
  25.4 0.0 copy-done
  25.4 0.0 copy-done.1
  25.4 0.9 %prep.1 = (bf16[4,256,256]{2,1,0:T(8,128)(2,1)S(1)}, bf16[4,2,128,256]{3,2,1,0:T(8,128)(2,1)S(1)}) custom-call(s32[8]{0:T(128)} %perm_hbm.3, bf16[4,4,128,256]{3,2,1,0:T(8,128)(2,1)S(1)} %bitcast.5, bf16[4,2,4,128,128]{4,3,2,1,0:T(8,128)(2,1)S(1)} %bitcast.7, bf16[1,4,64,128]{3,2,1,0:T(8,128)(2,1)S(1)} %collective-permute-done.after_ref.refs_4_), custom_call_target="tpu_custom_call" | custom-call | flops 1000000 | bytes 10000 | tf_op jit(solution)/shard_map/prep/pallas_call | solution.py:287
  26.3 0.0 collective-permute-done.2.refs_0_
  26.3 0.0 collective-permute-done.3.refs_1_
  26.3 0.0 collective-permute-done.4.refs_2_
  26.3 1.9 %upper.1 = (f32[4,2,128,256]{3,2,1,0:T(8,128)S(1)}, f32[3,4,128,256]{3,2,1,0:T(8,128)S(1)}) custom-call(s32[8]{0:T(128)} %perm_hbm.3, bf16[4,4,128,256]{3,2,1,0:T(8,128)(2,1)S(1)} %bitcast.6, bf16[4,2,4,128,128]{4,3,2,1,0:T(8,128)(2,1)S(1)} %bitcast.8, bf16[1,4,64,256]{3,2,1,0:T(8,128)(2,1)S(1)} %collective-permute-done.2.refs_0_, ...), custom_call_target="tpu_custom_call" | custom-call | flops 1000000 | bytes 10000 | tf_op jit(solution)/shard_map/upper/pallas_call | solution.py:360
  28.2 0.0 collective-permute-done.8.mid_a
  28.2 2.0 %collective-permute-done.9.mid_b = bf16[1,4,64,256]{3,2,1,0:T(8,128)(2,1)S(1)} collective-permute-done((bf16[1,4,64,256]{3,2,1,0:T(8,128)(2,1)S(1)}, bf16[1,4,64,256]{3,2,1,0:T(8,128)(2,1)S(1)}, u32[]{:S(2)}, u32[]{:S(2)}) %collective-permute-start.9) | collective-permute-done | bytes 131104 | tf_op jit(solution)/shard_map/ppermute | solution.py:428
  30.3 1.4 %finish.1 = bf16[4,2,256,128]{3,2,1,0:T(8,128)(2,1)} custom-call(bf16[4,256,256]{2,1,0:T(8,128)(2,1)S(1)} %get-tuple-element.22.down_ref, bf16[4,2,128,256]{3,2,1,0:T(8,128)(2,1)S(1)} %get-tuple-element.23.row_ref, f32[4,2,128,256]{3,2,1,0:T(8,128)S(1)} %get-tuple-element.33.field_ref, f32[3,4,128,256]{3,2,1,0:T(8,128)S(1)} %get-tuple-element.34.top_ref, ...), custom_call_target="tpu_custom_call" | custom-call | flops 1000000 | bytes 10000 | tf_op jit(solution)/shard_map/finish/pallas_call | solution.py:408
Async XLA Ops:
  0.0 7.7 %copy-start.2 = (bf16[2,128,2,64]{1,3,2,0:T(8,128)(2,1)S(1)}, bf16[2,128,2,64]{1,3,2,0:T(8,128)(2,1)}, u32[]{:S(2)}) copy-start(bf16[2,128,2,64]{1,3,2,0:T(8,128)(2,1)} %param.8) | copy-start | bytes 196612
  0.0 7.7 %collective-permute-start.1 = (bf16[2,2,64,128]{3,2,1,0:T(8,128)(2,1)}, bf16[2,2,64,128]{3,2,1,0:T(8,128)(2,1)S(1)}, u32[]{:S(2)}, u32[]{:S(2)}) collective-permute-start(bf16[2,2,64,128]{3,2,1,0:T(8,128)(2,1)} %bitcast.9), channel_id=1, source_target_pairs={{0,2},{2,0},{1,3},{3,1},{4,6},{6,4},{5,7},{7,5},{8,10},{10,8},{9,1... | collective-permute-start | bytes 196616 | tf_op jit(solution)/shard_map/ppermute | solution.py:446
  5.0 20.4 %copy-start = (bf16[4,1,4,2,64,256]{5,4,3,2,1,0:T(8,128)(2,1)S(1)}, bf16[4,1,4,2,64,256]{5,4,3,2,1,0:T(8,128)(2,1)}, u32[]{:S(2)}) copy-start(bf16[4,1,4,2,64,256]{5,4,3,2,1,0:T(8,128)(2,1)} %param.14) | copy-start | bytes 3145732
  5.0 20.4 %copy-start.1 = (bf16[1,4,2,4,128,128]{5,4,3,2,1,0:T(8,128)(2,1)S(1)}, bf16[1,4,2,4,128,128]{5,4,3,2,1,0:T(8,128)(2,1)}, u32[]{:S(2)}) copy-start(bf16[1,4,2,4,128,128]{5,4,3,2,1,0:T(8,128)(2,1)} %param.15) | copy-start | bytes 3145732
  5.0 11.4 %collective-permute-start = (bf16[1,4,64,128]{3,2,1,0:T(8,128)(2,1)S(1)}, bf16[1,4,64,128]{3,2,1,0:T(8,128)(2,1)S(1)}, u32[]{:S(2)}, u32[]{:S(2)}) collective-permute-start(bf16[1,4,64,128]{3,2,1,0:T(8,128)(2,1)S(1)} %get-tuple-element.21), channel_id=1, source_target_pairs={{0,8},{1,9},{4,12},{5,13},{8,0},{9,1},{12,4},{13,5},{2,10},{3,11},... | collective-permute-start | bytes 196616 | tf_op jit(solution)/shard_map/ppermute | solution.py:428
  7.7 8.7 %collective-permute-start.5 = (bf16[1,4,64,128]{3,2,1,0:T(8,128)(2,1)S(1)}, bf16[1,4,64,128]{3,2,1,0:T(8,128)(2,1)S(1)}, u32[]{:S(2)}, u32[]{:S(2)}) collective-permute-start(bf16[1,4,64,128]{3,2,1,0:T(8,128)(2,1)S(1)} %get-tuple-element.30), channel_id=1, source_target_pairs={{0,9},{1,8},{4,13},{5,12},{8,1},{9,0},{12,5},{13,4},{2,11},{3,10},... | collective-permute-start | bytes 196616 | tf_op jit(solution)/shard_map/ppermute | solution.py:428
  10.0 10.8 %collective-permute-start.6 = (bf16[1,4,64,128]{3,2,1,0:T(8,128)(2,1)S(1)}, bf16[1,4,64,128]{3,2,1,0:T(8,128)(2,1)S(1)}, u32[]{:S(2)}, u32[]{:S(2)}) collective-permute-start(bf16[1,4,64,128]{3,2,1,0:T(8,128)(2,1)S(1)} %get-tuple-element.31), channel_id=1, source_target_pairs={{0,8},{1,9},{4,12},{5,13},{8,0},{9,1},{12,4},{13,5},{2,10},{3,11},... | collective-permute-start | bytes 196616 | tf_op jit(solution)/shard_map/ppermute | solution.py:428
  11.9 10.4 %collective-permute-start.7 = (bf16[1,4,64,128]{3,2,1,0:T(8,128)(2,1)S(1)}, bf16[1,4,64,128]{3,2,1,0:T(8,128)(2,1)S(1)}, u32[]{:S(2)}, u32[]{:S(2)}) collective-permute-start(bf16[1,4,64,128]{3,2,1,0:T(8,128)(2,1)S(1)} %get-tuple-element.32), channel_id=1, source_target_pairs={{0,9},{1,8},{4,13},{5,12},{8,1},{9,0},{12,5},{13,4},{2,11},{3,10},... | collective-permute-start | bytes 196616 | tf_op jit(solution)/shard_map/ppermute | solution.py:428
  12.8 13.5 %collective-permute-start.2 = (bf16[1,4,64,256]{3,2,1,0:T(8,128)(2,1)S(1)}, bf16[1,4,64,256]{3,2,1,0:T(8,128)(2,1)S(1)}, u32[]{:S(2)}, u32[]{:S(2)}) collective-permute-start(bf16[1,4,64,256]{3,2,1,0:T(8,128)(2,1)S(1)} %get-tuple-element.26), channel_id=1, source_target_pairs={{0,12},{1,13},{4,8},{5,9},{8,4},{9,5},{12,0},{13,1},{2,14},{3,15},... | collective-permute-start | bytes 393224 | tf_op jit(solution)/shard_map/ppermute | solution.py:428
  16.4 9.9 %collective-permute-start.3 = (bf16[1,4,64,256]{3,2,1,0:T(8,128)(2,1)S(1)}, bf16[1,4,64,256]{3,2,1,0:T(8,128)(2,1)S(1)}, u32[]{:S(2)}, u32[]{:S(2)}) collective-permute-start(bf16[1,4,64,256]{3,2,1,0:T(8,128)(2,1)S(1)} %get-tuple-element.27), channel_id=1, source_target_pairs={{0,4},{1,5},{4,0},{5,1},{8,12},{9,13},{12,8},{13,9},{2,6},{3,7},{6... | collective-permute-start | bytes 393224 | tf_op jit(solution)/shard_map/ppermute | solution.py:428
  16.4 9.9 %collective-permute-start.4 = (bf16[1,4,64,256]{3,2,1,0:T(8,128)(2,1)S(1)}, bf16[1,4,64,256]{3,2,1,0:T(8,128)(2,1)S(1)}, u32[]{:S(2)}, u32[]{:S(2)}) collective-permute-start(bf16[1,4,64,256]{3,2,1,0:T(8,128)(2,1)S(1)} %get-tuple-element.28), channel_id=1, source_target_pairs={{0,1},{1,0},{4,5},{5,4},{8,9},{9,8},{12,13},{13,12},{2,3},{3,2},{6... | collective-permute-start | bytes 393224 | tf_op jit(solution)/shard_map/ppermute | solution.py:428
  20.9 7.3 %collective-permute-start.8 = (bf16[1,4,64,256]{3,2,1,0:T(8,128)(2,1)S(1)}, bf16[1,4,64,256]{3,2,1,0:T(8,128)(2,1)S(1)}, u32[]{:S(2)}, u32[]{:S(2)}) collective-permute-start(bf16[1,4,64,256]{3,2,1,0:T(8,128)(2,1)S(1)} %get-tuple-element.35), channel_id=1, source_target_pairs={{0,5},{1,4},{4,1},{5,0},{8,13},{9,12},{12,9},{13,8},{2,7},{3,6},{6... | collective-permute-start | bytes 393224 | tf_op jit(solution)/shard_map/ppermute | solution.py:428
  22.3 8.0 %collective-permute-start.9 = (bf16[1,4,64,256]{3,2,1,0:T(8,128)(2,1)S(1)}, bf16[1,4,64,256]{3,2,1,0:T(8,128)(2,1)S(1)}, u32[]{:S(2)}, u32[]{:S(2)}) collective-permute-start(bf16[1,4,64,256]{3,2,1,0:T(8,128)(2,1)S(1)} %get-tuple-element.36), channel_id=1, source_target_pairs={{0,13},{1,12},{4,9},{5,8},{8,5},{9,4},{12,1},{13,0},{2,15},{3,14},... | collective-permute-start | bytes 393224 | tf_op jit(solution)/shard_map/ppermute | solution.py:428

commit v15 on v14

--- a/solution.py
+++ b/solution.py
@@ -379,21 +379,21 @@
 def finish_kernel(down_ref, row_ref, field_ref, top_ref, mid_a, mid_b, out_hbm, mix_ref, out_ref, sems):
     local, _, leaf, _ = field_ref.shape
     rank = mid_a.shape[2]
+    for h in range(local):
+        top = jnp.concatenate([top_ref[0, h], top_ref[1, h]], axis=0) + jnp.dot(
+            down_ref[h], twisted_rows([mid_a[0, h], mid_b[0, h]]), preferred_element_type=F32
+        )
+        top = top.astype(BF16)
+        for t in range(2):
+            rows = twisted_rows([top[r : r + rank] for r in (t * rank, (2 + t) * rank)])
+            field = field_ref[h, t] + jnp.dot(
+                row_ref[h, t], rows, preferred_element_type=F32
+            )
+            mix_ref[h, t, pl.ds(0, leaf, stride=2), :] = field[:, :NRHS]
+            mix_ref[h, t, pl.ds(1, leaf, stride=2), :] = field[:, NRHS:]
+            out_ref[h, t] = mix_ref[h, t].astype(BF16)
     copies = []
     for i, group in enumerate(chunks(local)):
-        for h in group:
-            top = jnp.concatenate([top_ref[0, h], top_ref[1, h]], axis=0) + jnp.dot(
-                down_ref[h], twisted_rows([mid_a[0, h], mid_b[0, h]]), preferred_element_type=F32
-            )
-            top = top.astype(BF16)
-            for t in range(2):
-                rows = twisted_rows([top[r : r + rank] for r in (t * rank, (2 + t) * rank)])
-                field = field_ref[h, t] + jnp.dot(
-                    row_ref[h, t], rows, preferred_element_type=F32
-                )
-                mix_ref[h, t, pl.ds(0, leaf, stride=2), :] = field[:, :NRHS]
-                mix_ref[h, t, pl.ds(1, leaf, stride=2), :] = field[:, NRHS:]
-                out_ref[h, t] = mix_ref[h, t].astype(BF16)
         at = pl.ds(group.start, len(group))
         copies.append(pltpu.make_async_copy(out_ref.at[at], out_hbm.at[at], sems.at[i]))
         copies[-1].start()

time: 31.9 us -> 31.9 us (level)
  no operation moved by 1% of the time
where the time goes in v15:
time: 31.9 us; the launch traced here: 31.8 us
  starting transfers between devices  15.2 us (48%)
  Pallas kernels  8.65 us (27%)
  waiting for transfers between devices  7.85 us (25%)
    ppermute x9, starting transfers between devices, send(): lax.ppermute(block, ('blk', 'sub'), [(m, m ^ code) for m in range(dests)])  12.2 us
    ppermute x9, waiting for transfers between devices, send(): lax.ppermute(block, ('blk', 'sub'), [(m, m ^ code) for m in range(dests)])  7.84 us
    ppermute x1, starting transfers between devices, on_device(): xs = [x, lax.ppermute(x, 'rhs', [(0, 1), (1, 0)])]  2.94 us
    pallas_call x1, Pallas kernels, lower(): pl.pallas_call(functools.partial(lower_kernel, full, halved), out_shape=[...  2.34 us
    pallas_call x1, Pallas kernels, own(): pl.pallas_call(functools.partial(own_kernel, routes), out_shape=[block] *...  2.06 us
    pallas_call x1, Pallas kernels, upper(): pl.pallas_call(functools.partial(upper_kernel, full, halved, late), out_s...  1.88 us
    pallas_call x1, Pallas kernels, finish(): pl.pallas_call(finish_kernel, out_shape=jax.ShapeDtypeStruct(shape, BF16)...  1.52 us
    pallas_call x1, Pallas kernels, prep(): pl.pallas_call(functools.partial(prep_kernel, late), out_shape=[pltpu.VME...  0.85 us
  transfers between devices with their start and end apart: 10, of which 3 were waited for; matrix products, arithmetic and copies ran while one was open for 0% of the time, Pallas kernels for 22%

profile of v15, /device:TPU:0, one launch (start us, length us, event | category | flops | bytes accessed | tf_op | source)
XLA Modules:
  0.0 31.8 jit_solution(7376083016004023486)
XLA Ops:
  0.0 0.0 copy-start.2
  0.0 2.9 %collective-permute-start.1 = (bf16[2,2,64,128]{3,2,1,0:T(8,128)(2,1)}, bf16[2,2,64,128]{3,2,1,0:T(8,128)(2,1)S(1)}, u32[]{:S(2)}, u32[]{:S(2)}) collective-permute-start(bf16[2,2,64,128]{3,2,1,0:T(8,128)(2,1)} %bitcast.9), channel_id=1, source_target_pairs={{0,2},{2,0},{1,3},{3,1},{4,6},{6,4},{5,7},{7,5},{8,10},{10,8},{9,1... | collective-permute-start | bytes 196616 | tf_op jit(solution)/shard_map/ppermute | solution.py:446
  2.9 2.1 %own.1 = (bf16[1,4,64,128]{3,2,1,0:T(8,128)(2,1)S(1)}, bf16[1,4,64,128]{3,2,1,0:T(8,128)(2,1)S(1)}, bf16[2,16,128,128]{3,2,1,0:T(8,128)(2,1)S(1)}, bf16[1,32,64,256]{3,2,1,0:T(8,128)(2,1)S(1)}) custom-call(s32[2]{0:T(128)} %count_hbm.3, s32[32]{0:T(128)} %parent_hbm.3, bf16[2,2,64,128]{3,2,1,0:T(8,128)(2,1)} %bitcast.10, bf16[2,16,128,128]{3,2,1,0:T(8,128)(2,1)} %bitcast.12, ...), custom_call_target="tpu_custom_call" | custom-call | flops 1000000 | bytes 10000 | tf_op jit(solution)/shard_map/own/pallas_call | solution.py:153
  5.0 0.0 copy-start
  5.0 0.0 copy-start.1
  5.0 2.7 %collective-permute-start = (bf16[1,4,64,128]{3,2,1,0:T(8,128)(2,1)S(1)}, bf16[1,4,64,128]{3,2,1,0:T(8,128)(2,1)S(1)}, u32[]{:S(2)}, u32[]{:S(2)}) collective-permute-start(bf16[1,4,64,128]{3,2,1,0:T(8,128)(2,1)S(1)} %get-tuple-element.21), channel_id=1, source_target_pairs={{0,8},{1,9},{4,12},{5,13},{8,0},{9,1},{12,4},{13,5},{2,10},{3,11},... | collective-permute-start | bytes 196616 | tf_op jit(solution)/shard_map/ppermute | solution.py:428
  7.7 0.0 collective-permute-start.5
  7.7 0.0 collective-permute-done.1.refs_1_
  7.7 0.0 copy-done.2
  7.7 2.3 %lower.1 = (bf16[1,4,64,256]{3,2,1,0:T(8,128)(2,1)S(1)}, bf16[1,4,64,256]{3,2,1,0:T(8,128)(2,1)S(1)}, bf16[1,4,64,256]{3,2,1,0:T(8,128)(2,1)S(1)}, bf16[1,4,64,2...) custom-call(s32[2]{0:T(128)} %count_hbm.3, ...), custom_call_target="tpu_custom_call" | custom-call | flops 1000000 | bytes 10000 | tf_op jit(solution)/shard_map/lower/pallas_call | solution.py:219
  10.0 1.9 %collective-permute-start.6 = (bf16[1,4,64,128]{3,2,1,0:T(8,128)(2,1)S(1)}, bf16[1,4,64,128]{3,2,1,0:T(8,128)(2,1)S(1)}, u32[]{:S(2)}, u32[]{:S(2)}) collective-permute-start(bf16[1,4,64,128]{3,2,1,0:T(8,128)(2,1)S(1)} %get-tuple-element.31), channel_id=1, source_target_pairs={{0,8},{1,9},{4,12},{5,13},{8,0},{9,1},{12,4},{13,5},{2,10},{3,11},... | collective-permute-start | bytes 196616 | tf_op jit(solution)/shard_map/ppermute | solution.py:428
  11.9 0.9 %collective-permute-start.7 = (bf16[1,4,64,128]{3,2,1,0:T(8,128)(2,1)S(1)}, bf16[1,4,64,128]{3,2,1,0:T(8,128)(2,1)S(1)}, u32[]{:S(2)}, u32[]{:S(2)}) collective-permute-start(bf16[1,4,64,128]{3,2,1,0:T(8,128)(2,1)S(1)} %get-tuple-element.32), channel_id=1, source_target_pairs={{0,9},{1,8},{4,13},{5,12},{8,1},{9,0},{12,5},{13,4},{2,11},{3,10},... | collective-permute-start | bytes 196616 | tf_op jit(solution)/shard_map/ppermute | solution.py:428
  12.8 3.6 %collective-permute-start.2 = (bf16[1,4,64,256]{3,2,1,0:T(8,128)(2,1)S(1)}, bf16[1,4,64,256]{3,2,1,0:T(8,128)(2,1)S(1)}, u32[]{:S(2)}, u32[]{:S(2)}) collective-permute-start(bf16[1,4,64,256]{3,2,1,0:T(8,128)(2,1)S(1)} %get-tuple-element.26), channel_id=1, source_target_pairs={{0,12},{1,13},{4,8},{5,9},{8,4},{9,5},{12,0},{13,1},{2,14},{3,15},... | collective-permute-start | bytes 393224 | tf_op jit(solution)/shard_map/ppermute | solution.py:428
  16.4 0.0 collective-permute-done.after_ref.refs_4_
  16.4 0.0 collective-permute-start.3
  16.4 0.0 collective-permute-done.5.refs_5_
  16.4 0.1 collective-permute-start.4
  16.5 4.4 %collective-permute-done.6.refs_6_ = bf16[1,4,64,128]{3,2,1,0:T(8,128)(2,1)S(1)} collective-permute-done((bf16[1,4,64,128]{3,2,1,0:T(8,128)(2,1)S(1)}, bf16[1,4,64,128]{3,2,1,0:T(8,128)(2,1)S(1)}, u32[]{:S(2)}, u32[]{:S(2)}) %collective-permute-start.6) | collective-permute-done | bytes 65568 | tf_op jit(solution)/shard_map/ppermute | solution.py:428
  20.9 0.0 collective-permute-start.8
  20.9 1.4 %collective-permute-done.7.refs_7_ = bf16[1,4,64,128]{3,2,1,0:T(8,128)(2,1)S(1)} collective-permute-done((bf16[1,4,64,128]{3,2,1,0:T(8,128)(2,1)S(1)}, bf16[1,4,64,128]{3,2,1,0:T(8,128)(2,1)S(1)}, u32[]{:S(2)}, u32[]{:S(2)}) %collective-permute-start.7) | collective-permute-done | bytes 65568 | tf_op jit(solution)/shard_map/ppermute | solution.py:428
  22.3 3.1 %collective-permute-start.9 = (bf16[1,4,64,256]{3,2,1,0:T(8,128)(2,1)S(1)}, bf16[1,4,64,256]{3,2,1,0:T(8,128)(2,1)S(1)}, u32[]{:S(2)}, u32[]{:S(2)}) collective-permute-start(bf16[1,4,64,256]{3,2,1,0:T(8,128)(2,1)S(1)} %get-tuple-element.36), channel_id=1, source_target_pairs={{0,13},{1,12},{4,9},{5,8},{8,5},{9,4},{12,1},{13,0},{2,15},{3,14},... | collective-permute-start | bytes 393224 | tf_op jit(solution)/shard_map/ppermute | solution.py:428
  25.4 0.0 copy-done
  25.4 0.0 copy-done.1
  25.4 0.9 %prep.1 = (bf16[4,256,256]{2,1,0:T(8,128)(2,1)S(1)}, bf16[4,2,128,256]{3,2,1,0:T(8,128)(2,1)S(1)}) custom-call(s32[8]{0:T(128)} %perm_hbm.3, bf16[4,4,128,256]{3,2,1,0:T(8,128)(2,1)S(1)} %bitcast.5, bf16[4,2,4,128,128]{4,3,2,1,0:T(8,128)(2,1)S(1)} %bitcast.7, bf16[1,4,64,128]{3,2,1,0:T(8,128)(2,1)S(1)} %collective-permute-done.after_ref.refs_4_), custom_call_target="tpu_custom_call" | custom-call | flops 1000000 | bytes 10000 | tf_op jit(solution)/shard_map/prep/pallas_call | solution.py:287
  26.3 0.0 collective-permute-done.2.refs_0_
  26.3 0.0 collective-permute-done.3.refs_1_
  26.3 0.0 collective-permute-done.4.refs_2_
  26.3 1.9 %upper.1 = (f32[4,2,128,256]{3,2,1,0:T(8,128)S(1)}, f32[3,4,128,256]{3,2,1,0:T(8,128)S(1)}) custom-call(s32[8]{0:T(128)} %perm_hbm.3, bf16[4,4,128,256]{3,2,1,0:T(8,128)(2,1)S(1)} %bitcast.6, bf16[4,2,4,128,128]{4,3,2,1,0:T(8,128)(2,1)S(1)} %bitcast.8, bf16[1,4,64,256]{3,2,1,0:T(8,128)(2,1)S(1)} %collective-permute-done.2.refs_0_, ...), custom_call_target="tpu_custom_call" | custom-call | flops 1000000 | bytes 10000 | tf_op jit(solution)/shard_map/upper/pallas_call | solution.py:360
  28.2 0.0 collective-permute-done.8.mid_a
  28.2 2.0 %collective-permute-done.9.mid_b = bf16[1,4,64,256]{3,2,1,0:T(8,128)(2,1)S(1)} collective-permute-done((bf16[1,4,64,256]{3,2,1,0:T(8,128)(2,1)S(1)}, bf16[1,4,64,256]{3,2,1,0:T(8,128)(2,1)S(1)}, u32[]{:S(2)}, u32[]{:S(2)}) %collective-permute-start.9) | collective-permute-done | bytes 131104 | tf_op jit(solution)/shard_map/ppermute | solution.py:428
  30.3 1.5 %finish.1 = bf16[4,2,256,128]{3,2,1,0:T(8,128)(2,1)} custom-call(bf16[4,256,256]{2,1,0:T(8,128)(2,1)S(1)} %get-tuple-element.22.down_ref, bf16[4,2,128,256]{3,2,1,0:T(8,128)(2,1)S(1)} %get-tuple-element.23.row_ref, f32[4,2,128,256]{3,2,1,0:T(8,128)S(1)} %get-tuple-element.33.field_ref, f32[3,4,128,256]{3,2,1,0:T(8,128)S(1)} %get-tuple-element.34.top_ref, ...), custom_call_target="tpu_custom_call" | custom-call | flops 1000000 | bytes 10000 | tf_op jit(solution)/shard_map/finish/pallas_call | solution.py:408
Async XLA Ops:
  0.0 7.7 %copy-start.2 = (bf16[2,128,2,64]{1,3,2,0:T(8,128)(2,1)S(1)}, bf16[2,128,2,64]{1,3,2,0:T(8,128)(2,1)}, u32[]{:S(2)}) copy-start(bf16[2,128,2,64]{1,3,2,0:T(8,128)(2,1)} %param.8) | copy-start | bytes 196612
  0.0 7.7 %collective-permute-start.1 = (bf16[2,2,64,128]{3,2,1,0:T(8,128)(2,1)}, bf16[2,2,64,128]{3,2,1,0:T(8,128)(2,1)S(1)}, u32[]{:S(2)}, u32[]{:S(2)}) collective-permute-start(bf16[2,2,64,128]{3,2,1,0:T(8,128)(2,1)} %bitcast.9), channel_id=1, source_target_pairs={{0,2},{2,0},{1,3},{3,1},{4,6},{6,4},{5,7},{7,5},{8,10},{10,8},{9,1... | collective-permute-start | bytes 196616 | tf_op jit(solution)/shard_map/ppermute | solution.py:446
  5.0 20.4 %copy-start = (bf16[4,1,4,2,64,256]{5,4,3,2,1,0:T(8,128)(2,1)S(1)}, bf16[4,1,4,2,64,256]{5,4,3,2,1,0:T(8,128)(2,1)}, u32[]{:S(2)}) copy-start(bf16[4,1,4,2,64,256]{5,4,3,2,1,0:T(8,128)(2,1)} %param.14) | copy-start | bytes 3145732
  5.0 20.4 %copy-start.1 = (bf16[1,4,2,4,128,128]{5,4,3,2,1,0:T(8,128)(2,1)S(1)}, bf16[1,4,2,4,128,128]{5,4,3,2,1,0:T(8,128)(2,1)}, u32[]{:S(2)}) copy-start(bf16[1,4,2,4,128,128]{5,4,3,2,1,0:T(8,128)(2,1)} %param.15) | copy-start | bytes 3145732
  5.0 11.4 %collective-permute-start = (bf16[1,4,64,128]{3,2,1,0:T(8,128)(2,1)S(1)}, bf16[1,4,64,128]{3,2,1,0:T(8,128)(2,1)S(1)}, u32[]{:S(2)}, u32[]{:S(2)}) collective-permute-start(bf16[1,4,64,128]{3,2,1,0:T(8,128)(2,1)S(1)} %get-tuple-element.21), channel_id=1, source_target_pairs={{0,8},{1,9},{4,12},{5,13},{8,0},{9,1},{12,4},{13,5},{2,10},{3,11},... | collective-permute-start | bytes 196616 | tf_op jit(solution)/shard_map/ppermute | solution.py:428
  7.7 8.7 %collective-permute-start.5 = (bf16[1,4,64,128]{3,2,1,0:T(8,128)(2,1)S(1)}, bf16[1,4,64,128]{3,2,1,0:T(8,128)(2,1)S(1)}, u32[]{:S(2)}, u32[]{:S(2)}) collective-permute-start(bf16[1,4,64,128]{3,2,1,0:T(8,128)(2,1)S(1)} %get-tuple-element.30), channel_id=1, source_target_pairs={{0,9},{1,8},{4,13},{5,12},{8,1},{9,0},{12,5},{13,4},{2,11},{3,10},... | collective-permute-start | bytes 196616 | tf_op jit(solution)/shard_map/ppermute | solution.py:428
  10.0 10.8 %collective-permute-start.6 = (bf16[1,4,64,128]{3,2,1,0:T(8,128)(2,1)S(1)}, bf16[1,4,64,128]{3,2,1,0:T(8,128)(2,1)S(1)}, u32[]{:S(2)}, u32[]{:S(2)}) collective-permute-start(bf16[1,4,64,128]{3,2,1,0:T(8,128)(2,1)S(1)} %get-tuple-element.31), channel_id=1, source_target_pairs={{0,8},{1,9},{4,12},{5,13},{8,0},{9,1},{12,4},{13,5},{2,10},{3,11},... | collective-permute-start | bytes 196616 | tf_op jit(solution)/shard_map/ppermute | solution.py:428
  11.9 10.4 %collective-permute-start.7 = (bf16[1,4,64,128]{3,2,1,0:T(8,128)(2,1)S(1)}, bf16[1,4,64,128]{3,2,1,0:T(8,128)(2,1)S(1)}, u32[]{:S(2)}, u32[]{:S(2)}) collective-permute-start(bf16[1,4,64,128]{3,2,1,0:T(8,128)(2,1)S(1)} %get-tuple-element.32), channel_id=1, source_target_pairs={{0,9},{1,8},{4,13},{5,12},{8,1},{9,0},{12,5},{13,4},{2,11},{3,10},... | collective-permute-start | bytes 196616 | tf_op jit(solution)/shard_map/ppermute | solution.py:428
  12.8 13.5 %collective-permute-start.2 = (bf16[1,4,64,256]{3,2,1,0:T(8,128)(2,1)S(1)}, bf16[1,4,64,256]{3,2,1,0:T(8,128)(2,1)S(1)}, u32[]{:S(2)}, u32[]{:S(2)}) collective-permute-start(bf16[1,4,64,256]{3,2,1,0:T(8,128)(2,1)S(1)} %get-tuple-element.26), channel_id=1, source_target_pairs={{0,12},{1,13},{4,8},{5,9},{8,4},{9,5},{12,0},{13,1},{2,14},{3,15},... | collective-permute-start | bytes 393224 | tf_op jit(solution)/shard_map/ppermute | solution.py:428
  16.4 9.9 %collective-permute-start.3 = (bf16[1,4,64,256]{3,2,1,0:T(8,128)(2,1)S(1)}, bf16[1,4,64,256]{3,2,1,0:T(8,128)(2,1)S(1)}, u32[]{:S(2)}, u32[]{:S(2)}) collective-permute-start(bf16[1,4,64,256]{3,2,1,0:T(8,128)(2,1)S(1)} %get-tuple-element.27), channel_id=1, source_target_pairs={{0,4},{1,5},{4,0},{5,1},{8,12},{9,13},{12,8},{13,9},{2,6},{3,7},{6... | collective-permute-start | bytes 393224 | tf_op jit(solution)/shard_map/ppermute | solution.py:428
  16.4 9.9 %collective-permute-start.4 = (bf16[1,4,64,256]{3,2,1,0:T(8,128)(2,1)S(1)}, bf16[1,4,64,256]{3,2,1,0:T(8,128)(2,1)S(1)}, u32[]{:S(2)}, u32[]{:S(2)}) collective-permute-start(bf16[1,4,64,256]{3,2,1,0:T(8,128)(2,1)S(1)} %get-tuple-element.28), channel_id=1, source_target_pairs={{0,1},{1,0},{4,5},{5,4},{8,9},{9,8},{12,13},{13,12},{2,3},{3,2},{6... | collective-permute-start | bytes 393224 | tf_op jit(solution)/shard_map/ppermute | solution.py:428
  20.9 7.3 %collective-permute-start.8 = (bf16[1,4,64,256]{3,2,1,0:T(8,128)(2,1)S(1)}, bf16[1,4,64,256]{3,2,1,0:T(8,128)(2,1)S(1)}, u32[]{:S(2)}, u32[]{:S(2)}) collective-permute-start(bf16[1,4,64,256]{3,2,1,0:T(8,128)(2,1)S(1)} %get-tuple-element.35), channel_id=1, source_target_pairs={{0,5},{1,4},{4,1},{5,0},{8,13},{9,12},{12,9},{13,8},{2,7},{3,6},{6... | collective-permute-start | bytes 393224 | tf_op jit(solution)/shard_map/ppermute | solution.py:428
  22.3 8.0 %collective-permute-start.9 = (bf16[1,4,64,256]{3,2,1,0:T(8,128)(2,1)S(1)}, bf16[1,4,64,256]{3,2,1,0:T(8,128)(2,1)S(1)}, u32[]{:S(2)}, u32[]{:S(2)}) collective-permute-start(bf16[1,4,64,256]{3,2,1,0:T(8,128)(2,1)S(1)} %get-tuple-element.36), channel_id=1, source_target_pairs={{0,13},{1,12},{4,9},{5,8},{8,5},{9,4},{12,1},{13,0},{2,15},{3,14},... | collective-permute-start | bytes 393224 | tf_op jit(solution)/shard_map/ppermute | solution.py:428

commit v16 on v15

--- a/solution.py
+++ b/solution.py
@@ -101,10 +101,14 @@
         "up": pltpu.make_async_copy(up_hbm, up_ref, sems.at[3]),
     }
     for b in range(boxes):
-        copies[b] = pltpu.make_async_copy(basis_hbm.at[b], basis_ref.at[b], sems.at[4 + b])
-    for name in ["x", "count", "parent", *range(boxes), "up"]:
+        for i, group in enumerate(chunks(basis_ref.shape[1])):
+            at = (b, pl.ds(group.start, len(group)))
+            sem = sems.at[4 + 2 * b + i]
+            copies[b, i] = pltpu.make_async_copy(basis_hbm.at[at], basis_ref.at[at], sem)
+    first_ones = [name for name in copies if name != "up"]
+    for name in first_ones + ["up"]:
         copies[name].start()
-    for name in ["x", "count", "parent", *range(boxes)]:
+    for name in first_ones:
         copies[name].wait()
     spreads = []
     for b in range(boxes):
@@ -162,7 +166,7 @@
             pltpu.VMEM(x.shape, BF16),
             pltpu.VMEM((jobs, 4 * rank, NRHS), BF16),
             pltpu.VMEM((2 * jobs, 2, rows, NRHS), F32),
-            pltpu.SemaphoreType.DMA((4 + boxes,)),
+            pltpu.SemaphoreType.DMA((4 + 2 * boxes,)),
         ],
         compiler_params=PARAMS,
         cost_estimate=COST,

time: 31.9 us -> 32 us (level)
  no operation moved by 1% of the time
where the time goes in v16:
time: 32 us; the launch traced here: 31.8 us
  starting transfers between devices  15.2 us (48%)
  Pallas kernels  8.66 us (27%)
  waiting for transfers between devices  7.87 us (25%)
    ppermute x9, starting transfers between devices, send(): lax.ppermute(block, ('blk', 'sub'), [(m, m ^ code) for m in range(dests)])  12.2 us
    ppermute x9, waiting for transfers between devices, send(): lax.ppermute(block, ('blk', 'sub'), [(m, m ^ code) for m in range(dests)])  7.87 us
    ppermute x1, starting transfers between devices, on_device(): xs = [x, lax.ppermute(x, 'rhs', [(0, 1), (1, 0)])]  2.94 us
    pallas_call x1, Pallas kernels, lower(): pl.pallas_call(functools.partial(lower_kernel, full, halved), out_shape=[...  2.34 us
    pallas_call x1, Pallas kernels, own(): pl.pallas_call(functools.partial(own_kernel, routes), out_shape=[block] *...  2.06 us
    pallas_call x1, Pallas kernels, upper(): pl.pallas_call(functools.partial(upper_kernel, full, halved, late), out_s...  1.88 us
    pallas_call x1, Pallas kernels, finish(): pl.pallas_call(finish_kernel, out_shape=jax.ShapeDtypeStruct(shape, BF16)...  1.53 us
    pallas_call x1, Pallas kernels, prep(): pl.pallas_call(functools.partial(prep_kernel, late), out_shape=[pltpu.VME...  0.85 us
  transfers between devices with their start and end apart: 10, of which 3 were waited for; matrix products, arithmetic and copies ran while one was open for 0% of the time, Pallas kernels for 22%

profile of v16, /device:TPU:0, one launch (start us, length us, event | category | flops | bytes accessed | tf_op | source)
XLA Modules:
  0.0 31.8 jit_solution(16917357870474309535)
XLA Ops:
  0.0 0.0 copy-start.2
  0.0 2.9 %collective-permute-start.1 = (bf16[2,2,64,128]{3,2,1,0:T(8,128)(2,1)}, bf16[2,2,64,128]{3,2,1,0:T(8,128)(2,1)S(1)}, u32[]{:S(2)}, u32[]{:S(2)}) collective-permute-start(bf16[2,2,64,128]{3,2,1,0:T(8,128)(2,1)} %bitcast.9), channel_id=1, source_target_pairs={{0,2},{2,0},{1,3},{3,1},{4,6},{6,4},{5,7},{7,5},{8,10},{10,8},{9,1... | collective-permute-start | bytes 196616 | tf_op jit(solution)/shard_map/ppermute | solution.py:450
  2.9 2.1 %own.1 = (bf16[1,4,64,128]{3,2,1,0:T(8,128)(2,1)S(1)}, bf16[1,4,64,128]{3,2,1,0:T(8,128)(2,1)S(1)}, bf16[2,16,128,128]{3,2,1,0:T(8,128)(2,1)S(1)}, bf16[1,32,64,256]{3,2,1,0:T(8,128)(2,1)S(1)}) custom-call(s32[2]{0:T(128)} %count_hbm.3, s32[32]{0:T(128)} %parent_hbm.3, bf16[2,2,64,128]{3,2,1,0:T(8,128)(2,1)} %bitcast.10, bf16[2,16,128,128]{3,2,1,0:T(8,128)(2,1)} %bitcast.12, ...), custom_call_target="tpu_custom_call" | custom-call | flops 1000000 | bytes 10000 | tf_op jit(solution)/shard_map/own/pallas_call | solution.py:157
  5.0 0.0 copy-start
  5.0 0.0 copy-start.1
  5.0 2.7 %collective-permute-start = (bf16[1,4,64,128]{3,2,1,0:T(8,128)(2,1)S(1)}, bf16[1,4,64,128]{3,2,1,0:T(8,128)(2,1)S(1)}, u32[]{:S(2)}, u32[]{:S(2)}) collective-permute-start(bf16[1,4,64,128]{3,2,1,0:T(8,128)(2,1)S(1)} %get-tuple-element.21), channel_id=1, source_target_pairs={{0,8},{1,9},{4,12},{5,13},{8,0},{9,1},{12,4},{13,5},{2,10},{3,11},... | collective-permute-start | bytes 196616 | tf_op jit(solution)/shard_map/ppermute | solution.py:432
  7.7 0.0 collective-permute-start.5
  7.7 0.0 collective-permute-done.1.refs_1_
  7.7 0.0 copy-done.2
  7.7 2.3 %lower.1 = (bf16[1,4,64,256]{3,2,1,0:T(8,128)(2,1)S(1)}, bf16[1,4,64,256]{3,2,1,0:T(8,128)(2,1)S(1)}, bf16[1,4,64,256]{3,2,1,0:T(8,128)(2,1)S(1)}, bf16[1,4,64,2...) custom-call(s32[2]{0:T(128)} %count_hbm.3, ...), custom_call_target="tpu_custom_call" | custom-call | flops 1000000 | bytes 10000 | tf_op jit(solution)/shard_map/lower/pallas_call | solution.py:223
  10.0 1.9 %collective-permute-start.6 = (bf16[1,4,64,128]{3,2,1,0:T(8,128)(2,1)S(1)}, bf16[1,4,64,128]{3,2,1,0:T(8,128)(2,1)S(1)}, u32[]{:S(2)}, u32[]{:S(2)}) collective-permute-start(bf16[1,4,64,128]{3,2,1,0:T(8,128)(2,1)S(1)} %get-tuple-element.31), channel_id=1, source_target_pairs={{0,8},{1,9},{4,12},{5,13},{8,0},{9,1},{12,4},{13,5},{2,10},{3,11},... | collective-permute-start | bytes 196616 | tf_op jit(solution)/shard_map/ppermute | solution.py:432
  11.9 0.9 %collective-permute-start.7 = (bf16[1,4,64,128]{3,2,1,0:T(8,128)(2,1)S(1)}, bf16[1,4,64,128]{3,2,1,0:T(8,128)(2,1)S(1)}, u32[]{:S(2)}, u32[]{:S(2)}) collective-permute-start(bf16[1,4,64,128]{3,2,1,0:T(8,128)(2,1)S(1)} %get-tuple-element.32), channel_id=1, source_target_pairs={{0,9},{1,8},{4,13},{5,12},{8,1},{9,0},{12,5},{13,4},{2,11},{3,10},... | collective-permute-start | bytes 196616 | tf_op jit(solution)/shard_map/ppermute | solution.py:432
  12.8 3.6 %collective-permute-start.2 = (bf16[1,4,64,256]{3,2,1,0:T(8,128)(2,1)S(1)}, bf16[1,4,64,256]{3,2,1,0:T(8,128)(2,1)S(1)}, u32[]{:S(2)}, u32[]{:S(2)}) collective-permute-start(bf16[1,4,64,256]{3,2,1,0:T(8,128)(2,1)S(1)} %get-tuple-element.26), channel_id=1, source_target_pairs={{0,12},{1,13},{4,8},{5,9},{8,4},{9,5},{12,0},{13,1},{2,14},{3,15},... | collective-permute-start | bytes 393224 | tf_op jit(solution)/shard_map/ppermute | solution.py:432
  16.4 0.0 collective-permute-done.after_ref.refs_4_
  16.4 0.0 collective-permute-start.3
  16.4 0.0 collective-permute-done.5.refs_5_
  16.4 0.1 collective-permute-start.4
  16.5 4.4 %collective-permute-done.6.refs_6_ = bf16[1,4,64,128]{3,2,1,0:T(8,128)(2,1)S(1)} collective-permute-done((bf16[1,4,64,128]{3,2,1,0:T(8,128)(2,1)S(1)}, bf16[1,4,64,128]{3,2,1,0:T(8,128)(2,1)S(1)}, u32[]{:S(2)}, u32[]{:S(2)}) %collective-permute-start.6) | collective-permute-done | bytes 65568 | tf_op jit(solution)/shard_map/ppermute | solution.py:432
  20.9 0.0 collective-permute-start.8
  20.9 1.4 %collective-permute-done.7.refs_7_ = bf16[1,4,64,128]{3,2,1,0:T(8,128)(2,1)S(1)} collective-permute-done((bf16[1,4,64,128]{3,2,1,0:T(8,128)(2,1)S(1)}, bf16[1,4,64,128]{3,2,1,0:T(8,128)(2,1)S(1)}, u32[]{:S(2)}, u32[]{:S(2)}) %collective-permute-start.7) | collective-permute-done | bytes 65568 | tf_op jit(solution)/shard_map/ppermute | solution.py:432
  22.3 3.1 %collective-permute-start.9 = (bf16[1,4,64,256]{3,2,1,0:T(8,128)(2,1)S(1)}, bf16[1,4,64,256]{3,2,1,0:T(8,128)(2,1)S(1)}, u32[]{:S(2)}, u32[]{:S(2)}) collective-permute-start(bf16[1,4,64,256]{3,2,1,0:T(8,128)(2,1)S(1)} %get-tuple-element.36), channel_id=1, source_target_pairs={{0,13},{1,12},{4,9},{5,8},{8,5},{9,4},{12,1},{13,0},{2,15},{3,14},... | collective-permute-start | bytes 393224 | tf_op jit(solution)/shard_map/ppermute | solution.py:432
  25.4 0.0 copy-done
  25.4 0.0 copy-done.1
  25.4 0.9 %prep.1 = (bf16[4,256,256]{2,1,0:T(8,128)(2,1)S(1)}, bf16[4,2,128,256]{3,2,1,0:T(8,128)(2,1)S(1)}) custom-call(s32[8]{0:T(128)} %perm_hbm.3, bf16[4,4,128,256]{3,2,1,0:T(8,128)(2,1)S(1)} %bitcast.5, bf16[4,2,4,128,128]{4,3,2,1,0:T(8,128)(2,1)S(1)} %bitcast.7, bf16[1,4,64,128]{3,2,1,0:T(8,128)(2,1)S(1)} %collective-permute-done.after_ref.refs_4_), custom_call_target="tpu_custom_call" | custom-call | flops 1000000 | bytes 10000 | tf_op jit(solution)/shard_map/prep/pallas_call | solution.py:291
  26.3 0.0 collective-permute-done.2.refs_0_
  26.3 0.0 collective-permute-done.3.refs_1_
  26.3 0.0 collective-permute-done.4.refs_2_
  26.3 1.9 %upper.1 = (f32[4,2,128,256]{3,2,1,0:T(8,128)S(1)}, f32[3,4,128,256]{3,2,1,0:T(8,128)S(1)}) custom-call(s32[8]{0:T(128)} %perm_hbm.3, bf16[4,4,128,256]{3,2,1,0:T(8,128)(2,1)S(1)} %bitcast.6, bf16[4,2,4,128,128]{4,3,2,1,0:T(8,128)(2,1)S(1)} %bitcast.8, bf16[1,4,64,256]{3,2,1,0:T(8,128)(2,1)S(1)} %collective-permute-done.2.refs_0_, ...), custom_call_target="tpu_custom_call" | custom-call | flops 1000000 | bytes 10000 | tf_op jit(solution)/shard_map/upper/pallas_call | solution.py:364
  28.2 0.0 collective-permute-done.8.mid_a
  28.2 2.0 %collective-permute-done.9.mid_b = bf16[1,4,64,256]{3,2,1,0:T(8,128)(2,1)S(1)} collective-permute-done((bf16[1,4,64,256]{3,2,1,0:T(8,128)(2,1)S(1)}, bf16[1,4,64,256]{3,2,1,0:T(8,128)(2,1)S(1)}, u32[]{:S(2)}, u32[]{:S(2)}) %collective-permute-start.9) | collective-permute-done | bytes 131104 | tf_op jit(solution)/shard_map/ppermute | solution.py:432
  30.3 1.5 %finish.1 = bf16[4,2,256,128]{3,2,1,0:T(8,128)(2,1)} custom-call(bf16[4,256,256]{2,1,0:T(8,128)(2,1)S(1)} %get-tuple-element.22.down_ref, bf16[4,2,128,256]{3,2,1,0:T(8,128)(2,1)S(1)} %get-tuple-element.23.row_ref, f32[4,2,128,256]{3,2,1,0:T(8,128)S(1)} %get-tuple-element.33.field_ref, f32[3,4,128,256]{3,2,1,0:T(8,128)S(1)} %get-tuple-element.34.top_ref, ...), custom_call_target="tpu_custom_call" | custom-call | flops 1000000 | bytes 10000 | tf_op jit(solution)/shard_map/finish/pallas_call | solution.py:412
Async XLA Ops:
  0.0 7.7 %copy-start.2 = (bf16[2,128,2,64]{1,3,2,0:T(8,128)(2,1)S(1)}, bf16[2,128,2,64]{1,3,2,0:T(8,128)(2,1)}, u32[]{:S(2)}) copy-start(bf16[2,128,2,64]{1,3,2,0:T(8,128)(2,1)} %param.8) | copy-start | bytes 196612
  0.0 7.7 %collective-permute-start.1 = (bf16[2,2,64,128]{3,2,1,0:T(8,128)(2,1)}, bf16[2,2,64,128]{3,2,1,0:T(8,128)(2,1)S(1)}, u32[]{:S(2)}, u32[]{:S(2)}) collective-permute-start(bf16[2,2,64,128]{3,2,1,0:T(8,128)(2,1)} %bitcast.9), channel_id=1, source_target_pairs={{0,2},{2,0},{1,3},{3,1},{4,6},{6,4},{5,7},{7,5},{8,10},{10,8},{9,1... | collective-permute-start | bytes 196616 | tf_op jit(solution)/shard_map/ppermute | solution.py:450
  5.0 20.4 %copy-start = (bf16[4,1,4,2,64,256]{5,4,3,2,1,0:T(8,128)(2,1)S(1)}, bf16[4,1,4,2,64,256]{5,4,3,2,1,0:T(8,128)(2,1)}, u32[]{:S(2)}) copy-start(bf16[4,1,4,2,64,256]{5,4,3,2,1,0:T(8,128)(2,1)} %param.14) | copy-start | bytes 3145732
  5.0 20.4 %copy-start.1 = (bf16[1,4,2,4,128,128]{5,4,3,2,1,0:T(8,128)(2,1)S(1)}, bf16[1,4,2,4,128,128]{5,4,3,2,1,0:T(8,128)(2,1)}, u32[]{:S(2)}) copy-start(bf16[1,4,2,4,128,128]{5,4,3,2,1,0:T(8,128)(2,1)} %param.15) | copy-start | bytes 3145732
  5.0 11.4 %collective-permute-start = (bf16[1,4,64,128]{3,2,1,0:T(8,128)(2,1)S(1)}, bf16[1,4,64,128]{3,2,1,0:T(8,128)(2,1)S(1)}, u32[]{:S(2)}, u32[]{:S(2)}) collective-permute-start(bf16[1,4,64,128]{3,2,1,0:T(8,128)(2,1)S(1)} %get-tuple-element.21), channel_id=1, source_target_pairs={{0,8},{1,9},{4,12},{5,13},{8,0},{9,1},{12,4},{13,5},{2,10},{3,11},... | collective-permute-start | bytes 196616 | tf_op jit(solution)/shard_map/ppermute | solution.py:432
  7.7 8.7 %collective-permute-start.5 = (bf16[1,4,64,128]{3,2,1,0:T(8,128)(2,1)S(1)}, bf16[1,4,64,128]{3,2,1,0:T(8,128)(2,1)S(1)}, u32[]{:S(2)}, u32[]{:S(2)}) collective-permute-start(bf16[1,4,64,128]{3,2,1,0:T(8,128)(2,1)S(1)} %get-tuple-element.30), channel_id=1, source_target_pairs={{0,9},{1,8},{4,13},{5,12},{8,1},{9,0},{12,5},{13,4},{2,11},{3,10},... | collective-permute-start | bytes 196616 | tf_op jit(solution)/shard_map/ppermute | solution.py:432
  10.0 10.8 %collective-permute-start.6 = (bf16[1,4,64,128]{3,2,1,0:T(8,128)(2,1)S(1)}, bf16[1,4,64,128]{3,2,1,0:T(8,128)(2,1)S(1)}, u32[]{:S(2)}, u32[]{:S(2)}) collective-permute-start(bf16[1,4,64,128]{3,2,1,0:T(8,128)(2,1)S(1)} %get-tuple-element.31), channel_id=1, source_target_pairs={{0,8},{1,9},{4,12},{5,13},{8,0},{9,1},{12,4},{13,5},{2,10},{3,11},... | collective-permute-start | bytes 196616 | tf_op jit(solution)/shard_map/ppermute | solution.py:432
  11.9 10.4 %collective-permute-start.7 = (bf16[1,4,64,128]{3,2,1,0:T(8,128)(2,1)S(1)}, bf16[1,4,64,128]{3,2,1,0:T(8,128)(2,1)S(1)}, u32[]{:S(2)}, u32[]{:S(2)}) collective-permute-start(bf16[1,4,64,128]{3,2,1,0:T(8,128)(2,1)S(1)} %get-tuple-element.32), channel_id=1, source_target_pairs={{0,9},{1,8},{4,13},{5,12},{8,1},{9,0},{12,5},{13,4},{2,11},{3,10},... | collective-permute-start | bytes 196616 | tf_op jit(solution)/shard_map/ppermute | solution.py:432
  12.8 13.5 %collective-permute-start.2 = (bf16[1,4,64,256]{3,2,1,0:T(8,128)(2,1)S(1)}, bf16[1,4,64,256]{3,2,1,0:T(8,128)(2,1)S(1)}, u32[]{:S(2)}, u32[]{:S(2)}) collective-permute-start(bf16[1,4,64,256]{3,2,1,0:T(8,128)(2,1)S(1)} %get-tuple-element.26), channel_id=1, source_target_pairs={{0,12},{1,13},{4,8},{5,9},{8,4},{9,5},{12,0},{13,1},{2,14},{3,15},... | collective-permute-start | bytes 393224 | tf_op jit(solution)/shard_map/ppermute | solution.py:432
  16.4 9.9 %collective-permute-start.3 = (bf16[1,4,64,256]{3,2,1,0:T(8,128)(2,1)S(1)}, bf16[1,4,64,256]{3,2,1,0:T(8,128)(2,1)S(1)}, u32[]{:S(2)}, u32[]{:S(2)}) collective-permute-start(bf16[1,4,64,256]{3,2,1,0:T(8,128)(2,1)S(1)} %get-tuple-element.27), channel_id=1, source_target_pairs={{0,4},{1,5},{4,0},{5,1},{8,12},{9,13},{12,8},{13,9},{2,6},{3,7},{6... | collective-permute-start | bytes 393224 | tf_op jit(solution)/shard_map/ppermute | solution.py:432
  16.4 9.9 %collective-permute-start.4 = (bf16[1,4,64,256]{3,2,1,0:T(8,128)(2,1)S(1)}, bf16[1,4,64,256]{3,2,1,0:T(8,128)(2,1)S(1)}, u32[]{:S(2)}, u32[]{:S(2)}) collective-permute-start(bf16[1,4,64,256]{3,2,1,0:T(8,128)(2,1)S(1)} %get-tuple-element.28), channel_id=1, source_target_pairs={{0,1},{1,0},{4,5},{5,4},{8,9},{9,8},{12,13},{13,12},{2,3},{3,2},{6... | collective-permute-start | bytes 393224 | tf_op jit(solution)/shard_map/ppermute | solution.py:432
  20.9 7.4 %collective-permute-start.8 = (bf16[1,4,64,256]{3,2,1,0:T(8,128)(2,1)S(1)}, bf16[1,4,64,256]{3,2,1,0:T(8,128)(2,1)S(1)}, u32[]{:S(2)}, u32[]{:S(2)}) collective-permute-start(bf16[1,4,64,256]{3,2,1,0:T(8,128)(2,1)S(1)} %get-tuple-element.35), channel_id=1, source_target_pairs={{0,5},{1,4},{4,1},{5,0},{8,13},{9,12},{12,9},{13,8},{2,7},{3,6},{6... | collective-permute-start | bytes 393224 | tf_op jit(solution)/shard_map/ppermute | solution.py:432
  22.3 8.0 %collective-permute-start.9 = (bf16[1,4,64,256]{3,2,1,0:T(8,128)(2,1)S(1)}, bf16[1,4,64,256]{3,2,1,0:T(8,128)(2,1)S(1)}, u32[]{:S(2)}, u32[]{:S(2)}) collective-permute-start(bf16[1,4,64,256]{3,2,1,0:T(8,128)(2,1)S(1)} %get-tuple-element.36), channel_id=1, source_target_pairs={{0,13},{1,12},{4,9},{5,8},{8,5},{9,4},{12,1},{13,0},{2,15},{3,14},... | collective-permute-start | bytes 393224 | tf_op jit(solution)/shard_map/ppermute | solution.py:432

commit v17 on v15

--- a/solution.py
+++ b/solution.py
@@ -102,7 +102,7 @@
     }
     for b in range(boxes):
         copies[b] = pltpu.make_async_copy(basis_hbm.at[b], basis_ref.at[b], sems.at[4 + b])
-    for name in ["x", "count", "parent", *range(boxes), "up"]:
+    for name in ["parent", "count", "x", *range(boxes), "up"]:
         copies[name].start()
     for name in ["x", "count", "parent", *range(boxes)]:
         copies[name].wait()

time: 31.9 us -> 32 us (level)
  no operation moved by 1% of the time
where the time goes in v17:
time: 32 us; the launch traced here: 31.8 us
  starting transfers between devices  15.2 us (48%)
  Pallas kernels  8.65 us (27%)
  waiting for transfers between devices  7.85 us (25%)
    ppermute x9, starting transfers between devices, send(): lax.ppermute(block, ('blk', 'sub'), [(m, m ^ code) for m in range(dests)])  12.2 us
    ppermute x9, waiting for transfers between devices, send(): lax.ppermute(block, ('blk', 'sub'), [(m, m ^ code) for m in range(dests)])  7.85 us
    ppermute x1, starting transfers between devices, on_device(): xs = [x, lax.ppermute(x, 'rhs', [(0, 1), (1, 0)])]  2.94 us
    pallas_call x1, Pallas kernels, lower(): pl.pallas_call(functools.partial(lower_kernel, full, halved), out_shape=[...  2.34 us
    pallas_call x1, Pallas kernels, own(): pl.pallas_call(functools.partial(own_kernel, routes), out_shape=[block] *...  2.06 us
    pallas_call x1, Pallas kernels, upper(): pl.pallas_call(functools.partial(upper_kernel, full, halved, late), out_s...  1.88 us
    pallas_call x1, Pallas kernels, finish(): pl.pallas_call(finish_kernel, out_shape=jax.ShapeDtypeStruct(shape, BF16)...  1.53 us
    pallas_call x1, Pallas kernels, prep(): pl.pallas_call(functools.partial(prep_kernel, late), out_shape=[pltpu.VME...  0.85 us
  transfers between devices with their start and end apart: 10, of which 3 were waited for; matrix products, arithmetic and copies ran while one was open for 0% of the time, Pallas kernels for 22%

profile of v17, /device:TPU:0, one launch (start us, length us, event | category | flops | bytes accessed | tf_op | source)
XLA Modules:
  0.0 31.8 jit_solution(16904147922929003013)
XLA Ops:
  0.0 0.0 copy-start.2
  0.0 2.9 %collective-permute-start.1 = (bf16[2,2,64,128]{3,2,1,0:T(8,128)(2,1)}, bf16[2,2,64,128]{3,2,1,0:T(8,128)(2,1)S(1)}, u32[]{:S(2)}, u32[]{:S(2)}) collective-permute-start(bf16[2,2,64,128]{3,2,1,0:T(8,128)(2,1)} %bitcast.9), channel_id=1, source_target_pairs={{0,2},{2,0},{1,3},{3,1},{4,6},{6,4},{5,7},{7,5},{8,10},{10,8},{9,1... | collective-permute-start | bytes 196616 | tf_op jit(solution)/shard_map/ppermute | solution.py:446
  2.9 2.1 %own.1 = (bf16[1,4,64,128]{3,2,1,0:T(8,128)(2,1)S(1)}, bf16[1,4,64,128]{3,2,1,0:T(8,128)(2,1)S(1)}, bf16[2,16,128,128]{3,2,1,0:T(8,128)(2,1)S(1)}, bf16[1,32,64,256]{3,2,1,0:T(8,128)(2,1)S(1)}) custom-call(s32[2]{0:T(128)} %count_hbm.3, s32[32]{0:T(128)} %parent_hbm.3, bf16[2,2,64,128]{3,2,1,0:T(8,128)(2,1)} %bitcast.10, bf16[2,16,128,128]{3,2,1,0:T(8,128)(2,1)} %bitcast.12, ...), custom_call_target="tpu_custom_call" | custom-call | flops 1000000 | bytes 10000 | tf_op jit(solution)/shard_map/own/pallas_call | solution.py:153
  5.0 0.0 copy-start
  5.0 0.0 copy-start.1
  5.0 2.7 %collective-permute-start = (bf16[1,4,64,128]{3,2,1,0:T(8,128)(2,1)S(1)}, bf16[1,4,64,128]{3,2,1,0:T(8,128)(2,1)S(1)}, u32[]{:S(2)}, u32[]{:S(2)}) collective-permute-start(bf16[1,4,64,128]{3,2,1,0:T(8,128)(2,1)S(1)} %get-tuple-element.21), channel_id=1, source_target_pairs={{0,8},{1,9},{4,12},{5,13},{8,0},{9,1},{12,4},{13,5},{2,10},{3,11},... | collective-permute-start | bytes 196616 | tf_op jit(solution)/shard_map/ppermute | solution.py:428
  7.7 0.0 collective-permute-start.5
  7.7 0.0 collective-permute-done.1.refs_1_
  7.7 0.0 copy-done.2
  7.7 2.3 %lower.1 = (bf16[1,4,64,256]{3,2,1,0:T(8,128)(2,1)S(1)}, bf16[1,4,64,256]{3,2,1,0:T(8,128)(2,1)S(1)}, bf16[1,4,64,256]{3,2,1,0:T(8,128)(2,1)S(1)}, bf16[1,4,64,2...) custom-call(s32[2]{0:T(128)} %count_hbm.3, ...), custom_call_target="tpu_custom_call" | custom-call | flops 1000000 | bytes 10000 | tf_op jit(solution)/shard_map/lower/pallas_call | solution.py:219
  10.0 1.9 %collective-permute-start.6 = (bf16[1,4,64,128]{3,2,1,0:T(8,128)(2,1)S(1)}, bf16[1,4,64,128]{3,2,1,0:T(8,128)(2,1)S(1)}, u32[]{:S(2)}, u32[]{:S(2)}) collective-permute-start(bf16[1,4,64,128]{3,2,1,0:T(8,128)(2,1)S(1)} %get-tuple-element.31), channel_id=1, source_target_pairs={{0,8},{1,9},{4,12},{5,13},{8,0},{9,1},{12,4},{13,5},{2,10},{3,11},... | collective-permute-start | bytes 196616 | tf_op jit(solution)/shard_map/ppermute | solution.py:428
  11.9 0.9 %collective-permute-start.7 = (bf16[1,4,64,128]{3,2,1,0:T(8,128)(2,1)S(1)}, bf16[1,4,64,128]{3,2,1,0:T(8,128)(2,1)S(1)}, u32[]{:S(2)}, u32[]{:S(2)}) collective-permute-start(bf16[1,4,64,128]{3,2,1,0:T(8,128)(2,1)S(1)} %get-tuple-element.32), channel_id=1, source_target_pairs={{0,9},{1,8},{4,13},{5,12},{8,1},{9,0},{12,5},{13,4},{2,11},{3,10},... | collective-permute-start | bytes 196616 | tf_op jit(solution)/shard_map/ppermute | solution.py:428
  12.8 3.6 %collective-permute-start.2 = (bf16[1,4,64,256]{3,2,1,0:T(8,128)(2,1)S(1)}, bf16[1,4,64,256]{3,2,1,0:T(8,128)(2,1)S(1)}, u32[]{:S(2)}, u32[]{:S(2)}) collective-permute-start(bf16[1,4,64,256]{3,2,1,0:T(8,128)(2,1)S(1)} %get-tuple-element.26), channel_id=1, source_target_pairs={{0,12},{1,13},{4,8},{5,9},{8,4},{9,5},{12,0},{13,1},{2,14},{3,15},... | collective-permute-start | bytes 393224 | tf_op jit(solution)/shard_map/ppermute | solution.py:428
  16.4 0.0 collective-permute-done.after_ref.refs_4_
  16.4 0.0 collective-permute-start.3
  16.4 0.0 collective-permute-done.5.refs_5_
  16.4 0.1 collective-permute-start.4
  16.5 4.4 %collective-permute-done.6.refs_6_ = bf16[1,4,64,128]{3,2,1,0:T(8,128)(2,1)S(1)} collective-permute-done((bf16[1,4,64,128]{3,2,1,0:T(8,128)(2,1)S(1)}, bf16[1,4,64,128]{3,2,1,0:T(8,128)(2,1)S(1)}, u32[]{:S(2)}, u32[]{:S(2)}) %collective-permute-start.6) | collective-permute-done | bytes 65568 | tf_op jit(solution)/shard_map/ppermute | solution.py:428
  20.9 0.0 collective-permute-start.8
  20.9 1.4 %collective-permute-done.7.refs_7_ = bf16[1,4,64,128]{3,2,1,0:T(8,128)(2,1)S(1)} collective-permute-done((bf16[1,4,64,128]{3,2,1,0:T(8,128)(2,1)S(1)}, bf16[1,4,64,128]{3,2,1,0:T(8,128)(2,1)S(1)}, u32[]{:S(2)}, u32[]{:S(2)}) %collective-permute-start.7) | collective-permute-done | bytes 65568 | tf_op jit(solution)/shard_map/ppermute | solution.py:428
  22.3 3.1 %collective-permute-start.9 = (bf16[1,4,64,256]{3,2,1,0:T(8,128)(2,1)S(1)}, bf16[1,4,64,256]{3,2,1,0:T(8,128)(2,1)S(1)}, u32[]{:S(2)}, u32[]{:S(2)}) collective-permute-start(bf16[1,4,64,256]{3,2,1,0:T(8,128)(2,1)S(1)} %get-tuple-element.36), channel_id=1, source_target_pairs={{0,13},{1,12},{4,9},{5,8},{8,5},{9,4},{12,1},{13,0},{2,15},{3,14},... | collective-permute-start | bytes 393224 | tf_op jit(solution)/shard_map/ppermute | solution.py:428
  25.4 0.0 copy-done
  25.4 0.0 copy-done.1
  25.4 0.9 %prep.1 = (bf16[4,256,256]{2,1,0:T(8,128)(2,1)S(1)}, bf16[4,2,128,256]{3,2,1,0:T(8,128)(2,1)S(1)}) custom-call(s32[8]{0:T(128)} %perm_hbm.3, bf16[4,4,128,256]{3,2,1,0:T(8,128)(2,1)S(1)} %bitcast.5, bf16[4,2,4,128,128]{4,3,2,1,0:T(8,128)(2,1)S(1)} %bitcast.7, bf16[1,4,64,128]{3,2,1,0:T(8,128)(2,1)S(1)} %collective-permute-done.after_ref.refs_4_), custom_call_target="tpu_custom_call" | custom-call | flops 1000000 | bytes 10000 | tf_op jit(solution)/shard_map/prep/pallas_call | solution.py:287
  26.3 0.0 collective-permute-done.2.refs_0_
  26.3 0.0 collective-permute-done.3.refs_1_
  26.3 0.0 collective-permute-done.4.refs_2_
  26.3 1.9 %upper.1 = (f32[4,2,128,256]{3,2,1,0:T(8,128)S(1)}, f32[3,4,128,256]{3,2,1,0:T(8,128)S(1)}) custom-call(s32[8]{0:T(128)} %perm_hbm.3, bf16[4,4,128,256]{3,2,1,0:T(8,128)(2,1)S(1)} %bitcast.6, bf16[4,2,4,128,128]{4,3,2,1,0:T(8,128)(2,1)S(1)} %bitcast.8, bf16[1,4,64,256]{3,2,1,0:T(8,128)(2,1)S(1)} %collective-permute-done.2.refs_0_, ...), custom_call_target="tpu_custom_call" | custom-call | flops 1000000 | bytes 10000 | tf_op jit(solution)/shard_map/upper/pallas_call | solution.py:360
  28.2 0.0 collective-permute-done.8.mid_a
  28.2 2.0 %collective-permute-done.9.mid_b = bf16[1,4,64,256]{3,2,1,0:T(8,128)(2,1)S(1)} collective-permute-done((bf16[1,4,64,256]{3,2,1,0:T(8,128)(2,1)S(1)}, bf16[1,4,64,256]{3,2,1,0:T(8,128)(2,1)S(1)}, u32[]{:S(2)}, u32[]{:S(2)}) %collective-permute-start.9) | collective-permute-done | bytes 131104 | tf_op jit(solution)/shard_map/ppermute | solution.py:428
  30.3 1.5 %finish.1 = bf16[4,2,256,128]{3,2,1,0:T(8,128)(2,1)} custom-call(bf16[4,256,256]{2,1,0:T(8,128)(2,1)S(1)} %get-tuple-element.22.down_ref, bf16[4,2,128,256]{3,2,1,0:T(8,128)(2,1)S(1)} %get-tuple-element.23.row_ref, f32[4,2,128,256]{3,2,1,0:T(8,128)S(1)} %get-tuple-element.33.field_ref, f32[3,4,128,256]{3,2,1,0:T(8,128)S(1)} %get-tuple-element.34.top_ref, ...), custom_call_target="tpu_custom_call" | custom-call | flops 1000000 | bytes 10000 | tf_op jit(solution)/shard_map/finish/pallas_call | solution.py:408
Async XLA Ops:
  0.0 7.7 %copy-start.2 = (bf16[2,128,2,64]{1,3,2,0:T(8,128)(2,1)S(1)}, bf16[2,128,2,64]{1,3,2,0:T(8,128)(2,1)}, u32[]{:S(2)}) copy-start(bf16[2,128,2,64]{1,3,2,0:T(8,128)(2,1)} %param.8) | copy-start | bytes 196612
  0.0 7.7 %collective-permute-start.1 = (bf16[2,2,64,128]{3,2,1,0:T(8,128)(2,1)}, bf16[2,2,64,128]{3,2,1,0:T(8,128)(2,1)S(1)}, u32[]{:S(2)}, u32[]{:S(2)}) collective-permute-start(bf16[2,2,64,128]{3,2,1,0:T(8,128)(2,1)} %bitcast.9), channel_id=1, source_target_pairs={{0,2},{2,0},{1,3},{3,1},{4,6},{6,4},{5,7},{7,5},{8,10},{10,8},{9,1... | collective-permute-start | bytes 196616 | tf_op jit(solution)/shard_map/ppermute | solution.py:446
  5.0 20.4 %copy-start = (bf16[4,1,4,2,64,256]{5,4,3,2,1,0:T(8,128)(2,1)S(1)}, bf16[4,1,4,2,64,256]{5,4,3,2,1,0:T(8,128)(2,1)}, u32[]{:S(2)}) copy-start(bf16[4,1,4,2,64,256]{5,4,3,2,1,0:T(8,128)(2,1)} %param.14) | copy-start | bytes 3145732
  5.0 20.4 %copy-start.1 = (bf16[1,4,2,4,128,128]{5,4,3,2,1,0:T(8,128)(2,1)S(1)}, bf16[1,4,2,4,128,128]{5,4,3,2,1,0:T(8,128)(2,1)}, u32[]{:S(2)}) copy-start(bf16[1,4,2,4,128,128]{5,4,3,2,1,0:T(8,128)(2,1)} %param.15) | copy-start | bytes 3145732
  5.0 11.4 %collective-permute-start = (bf16[1,4,64,128]{3,2,1,0:T(8,128)(2,1)S(1)}, bf16[1,4,64,128]{3,2,1,0:T(8,128)(2,1)S(1)}, u32[]{:S(2)}, u32[]{:S(2)}) collective-permute-start(bf16[1,4,64,128]{3,2,1,0:T(8,128)(2,1)S(1)} %get-tuple-element.21), channel_id=1, source_target_pairs={{0,8},{1,9},{4,12},{5,13},{8,0},{9,1},{12,4},{13,5},{2,10},{3,11},... | collective-permute-start | bytes 196616 | tf_op jit(solution)/shard_map/ppermute | solution.py:428
  7.7 8.7 %collective-permute-start.5 = (bf16[1,4,64,128]{3,2,1,0:T(8,128)(2,1)S(1)}, bf16[1,4,64,128]{3,2,1,0:T(8,128)(2,1)S(1)}, u32[]{:S(2)}, u32[]{:S(2)}) collective-permute-start(bf16[1,4,64,128]{3,2,1,0:T(8,128)(2,1)S(1)} %get-tuple-element.30), channel_id=1, source_target_pairs={{0,9},{1,8},{4,13},{5,12},{8,1},{9,0},{12,5},{13,4},{2,11},{3,10},... | collective-permute-start | bytes 196616 | tf_op jit(solution)/shard_map/ppermute | solution.py:428
  10.0 10.8 %collective-permute-start.6 = (bf16[1,4,64,128]{3,2,1,0:T(8,128)(2,1)S(1)}, bf16[1,4,64,128]{3,2,1,0:T(8,128)(2,1)S(1)}, u32[]{:S(2)}, u32[]{:S(2)}) collective-permute-start(bf16[1,4,64,128]{3,2,1,0:T(8,128)(2,1)S(1)} %get-tuple-element.31), channel_id=1, source_target_pairs={{0,8},{1,9},{4,12},{5,13},{8,0},{9,1},{12,4},{13,5},{2,10},{3,11},... | collective-permute-start | bytes 196616 | tf_op jit(solution)/shard_map/ppermute | solution.py:428
  11.9 10.4 %collective-permute-start.7 = (bf16[1,4,64,128]{3,2,1,0:T(8,128)(2,1)S(1)}, bf16[1,4,64,128]{3,2,1,0:T(8,128)(2,1)S(1)}, u32[]{:S(2)}, u32[]{:S(2)}) collective-permute-start(bf16[1,4,64,128]{3,2,1,0:T(8,128)(2,1)S(1)} %get-tuple-element.32), channel_id=1, source_target_pairs={{0,9},{1,8},{4,13},{5,12},{8,1},{9,0},{12,5},{13,4},{2,11},{3,10},... | collective-permute-start | bytes 196616 | tf_op jit(solution)/shard_map/ppermute | solution.py:428
  12.8 13.5 %collective-permute-start.2 = (bf16[1,4,64,256]{3,2,1,0:T(8,128)(2,1)S(1)}, bf16[1,4,64,256]{3,2,1,0:T(8,128)(2,1)S(1)}, u32[]{:S(2)}, u32[]{:S(2)}) collective-permute-start(bf16[1,4,64,256]{3,2,1,0:T(8,128)(2,1)S(1)} %get-tuple-element.26), channel_id=1, source_target_pairs={{0,12},{1,13},{4,8},{5,9},{8,4},{9,5},{12,0},{13,1},{2,14},{3,15},... | collective-permute-start | bytes 393224 | tf_op jit(solution)/shard_map/ppermute | solution.py:428
  16.4 9.9 %collective-permute-start.3 = (bf16[1,4,64,256]{3,2,1,0:T(8,128)(2,1)S(1)}, bf16[1,4,64,256]{3,2,1,0:T(8,128)(2,1)S(1)}, u32[]{:S(2)}, u32[]{:S(2)}) collective-permute-start(bf16[1,4,64,256]{3,2,1,0:T(8,128)(2,1)S(1)} %get-tuple-element.27), channel_id=1, source_target_pairs={{0,4},{1,5},{4,0},{5,1},{8,12},{9,13},{12,8},{13,9},{2,6},{3,7},{6... | collective-permute-start | bytes 393224 | tf_op jit(solution)/shard_map/ppermute | solution.py:428
  16.4 9.9 %collective-permute-start.4 = (bf16[1,4,64,256]{3,2,1,0:T(8,128)(2,1)S(1)}, bf16[1,4,64,256]{3,2,1,0:T(8,128)(2,1)S(1)}, u32[]{:S(2)}, u32[]{:S(2)}) collective-permute-start(bf16[1,4,64,256]{3,2,1,0:T(8,128)(2,1)S(1)} %get-tuple-element.28), channel_id=1, source_target_pairs={{0,1},{1,0},{4,5},{5,4},{8,9},{9,8},{12,13},{13,12},{2,3},{3,2},{6... | collective-permute-start | bytes 393224 | tf_op jit(solution)/shard_map/ppermute | solution.py:428
  20.9 7.3 %collective-permute-start.8 = (bf16[1,4,64,256]{3,2,1,0:T(8,128)(2,1)S(1)}, bf16[1,4,64,256]{3,2,1,0:T(8,128)(2,1)S(1)}, u32[]{:S(2)}, u32[]{:S(2)}) collective-permute-start(bf16[1,4,64,256]{3,2,1,0:T(8,128)(2,1)S(1)} %get-tuple-element.35), channel_id=1, source_target_pairs={{0,5},{1,4},{4,1},{5,0},{8,13},{9,12},{12,9},{13,8},{2,7},{3,6},{6... | collective-permute-start | bytes 393224 | tf_op jit(solution)/shard_map/ppermute | solution.py:428
  22.3 8.0 %collective-permute-start.9 = (bf16[1,4,64,256]{3,2,1,0:T(8,128)(2,1)S(1)}, bf16[1,4,64,256]{3,2,1,0:T(8,128)(2,1)S(1)}, u32[]{:S(2)}, u32[]{:S(2)}) collective-permute-start(bf16[1,4,64,256]{3,2,1,0:T(8,128)(2,1)S(1)} %get-tuple-element.36), channel_id=1, source_target_pairs={{0,13},{1,12},{4,9},{5,8},{8,5},{9,4},{12,1},{13,0},{2,15},{3,14},... | collective-permute-start | bytes 393224 | tf_op jit(solution)/shard_map/ppermute | solution.py:428

commit v18 on v14

--- a/solution.py
+++ b/solution.py
@@ -380,7 +380,8 @@
     local, _, leaf, _ = field_ref.shape
     rank = mid_a.shape[2]
     copies = []
-    for i, group in enumerate(chunks(local)):
+    stretches = [group for group in (range(local - 1), range(local - 1, local)) if group]
+    for i, group in enumerate(stretches):
         for h in group:
             top = jnp.concatenate([top_ref[0, h], top_ref[1, h]], axis=0) + jnp.dot(
                 down_ref[h], twisted_rows([mid_a[0, h], mid_b[0, h]]), preferred_element_type=F32

time: 31.9 us -> 31.8 us (level)
  no operation moved by 1% of the time
where the time goes in v18:
time: 31.8 us; the launch traced here: 31.7 us
  starting transfers between devices  15.2 us (48%)
  Pallas kernels  8.55 us (27%)
  waiting for transfers between devices  7.85 us (25%)
    ppermute x9, starting transfers between devices, send(): lax.ppermute(block, ('blk', 'sub'), [(m, m ^ code) for m in range(dests)])  12.2 us
    ppermute x9, waiting for transfers between devices, send(): lax.ppermute(block, ('blk', 'sub'), [(m, m ^ code) for m in range(dests)])  7.84 us
    ppermute x1, starting transfers between devices, on_device(): xs = [x, lax.ppermute(x, 'rhs', [(0, 1), (1, 0)])]  2.94 us
    pallas_call x1, Pallas kernels, lower(): pl.pallas_call(functools.partial(lower_kernel, full, halved), out_shape=[...  2.34 us
    pallas_call x1, Pallas kernels, own(): pl.pallas_call(functools.partial(own_kernel, routes), out_shape=[block] *...  2.06 us
    pallas_call x1, Pallas kernels, upper(): pl.pallas_call(functools.partial(upper_kernel, full, halved, late), out_s...  1.88 us
    pallas_call x1, Pallas kernels, finish(): pl.pallas_call(finish_kernel, out_shape=jax.ShapeDtypeStruct(shape, BF16)...  1.42 us
    pallas_call x1, Pallas kernels, prep(): pl.pallas_call(functools.partial(prep_kernel, late), out_shape=[pltpu.VME...  0.85 us
  transfers between devices with their start and end apart: 10, of which 3 were waited for; matrix products, arithmetic and copies ran while one was open for 0% of the time, Pallas kernels for 22%

profile of v18, /device:TPU:0, one launch (start us, length us, event | category | flops | bytes accessed | tf_op | source)
XLA Modules:
  0.0 31.7 jit_solution(15468909478879237560)
XLA Ops:
  0.0 0.0 copy-start.2
  0.0 2.9 %collective-permute-start.1 = (bf16[2,2,64,128]{3,2,1,0:T(8,128)(2,1)}, bf16[2,2,64,128]{3,2,1,0:T(8,128)(2,1)S(1)}, u32[]{:S(2)}, u32[]{:S(2)}) collective-permute-start(bf16[2,2,64,128]{3,2,1,0:T(8,128)(2,1)} %bitcast.9), channel_id=1, source_target_pairs={{0,2},{2,0},{1,3},{3,1},{4,6},{6,4},{5,7},{7,5},{8,10},{10,8},{9,1... | collective-permute-start | bytes 196616 | tf_op jit(solution)/shard_map/ppermute | solution.py:447
  2.9 2.1 %own.1 = (bf16[1,4,64,128]{3,2,1,0:T(8,128)(2,1)S(1)}, bf16[1,4,64,128]{3,2,1,0:T(8,128)(2,1)S(1)}, bf16[2,16,128,128]{3,2,1,0:T(8,128)(2,1)S(1)}, bf16[1,32,64,256]{3,2,1,0:T(8,128)(2,1)S(1)}) custom-call(s32[2]{0:T(128)} %count_hbm.3, s32[32]{0:T(128)} %parent_hbm.3, bf16[2,2,64,128]{3,2,1,0:T(8,128)(2,1)} %bitcast.10, bf16[2,16,128,128]{3,2,1,0:T(8,128)(2,1)} %bitcast.12, ...), custom_call_target="tpu_custom_call" | custom-call | flops 1000000 | bytes 10000 | tf_op jit(solution)/shard_map/own/pallas_call | solution.py:153
  5.0 0.0 copy-start
  5.0 0.0 copy-start.1
  5.0 2.7 %collective-permute-start = (bf16[1,4,64,128]{3,2,1,0:T(8,128)(2,1)S(1)}, bf16[1,4,64,128]{3,2,1,0:T(8,128)(2,1)S(1)}, u32[]{:S(2)}, u32[]{:S(2)}) collective-permute-start(bf16[1,4,64,128]{3,2,1,0:T(8,128)(2,1)S(1)} %get-tuple-element.21), channel_id=1, source_target_pairs={{0,8},{1,9},{4,12},{5,13},{8,0},{9,1},{12,4},{13,5},{2,10},{3,11},... | collective-permute-start | bytes 196616 | tf_op jit(solution)/shard_map/ppermute | solution.py:429
  7.7 0.0 collective-permute-start.5
  7.7 0.0 collective-permute-done.1.refs_1_
  7.7 0.0 copy-done.2
  7.7 2.3 %lower.1 = (bf16[1,4,64,256]{3,2,1,0:T(8,128)(2,1)S(1)}, bf16[1,4,64,256]{3,2,1,0:T(8,128)(2,1)S(1)}, bf16[1,4,64,256]{3,2,1,0:T(8,128)(2,1)S(1)}, bf16[1,4,64,2...) custom-call(s32[2]{0:T(128)} %count_hbm.3, ...), custom_call_target="tpu_custom_call" | custom-call | flops 1000000 | bytes 10000 | tf_op jit(solution)/shard_map/lower/pallas_call | solution.py:219
  10.0 1.9 %collective-permute-start.6 = (bf16[1,4,64,128]{3,2,1,0:T(8,128)(2,1)S(1)}, bf16[1,4,64,128]{3,2,1,0:T(8,128)(2,1)S(1)}, u32[]{:S(2)}, u32[]{:S(2)}) collective-permute-start(bf16[1,4,64,128]{3,2,1,0:T(8,128)(2,1)S(1)} %get-tuple-element.31), channel_id=1, source_target_pairs={{0,8},{1,9},{4,12},{5,13},{8,0},{9,1},{12,4},{13,5},{2,10},{3,11},... | collective-permute-start | bytes 196616 | tf_op jit(solution)/shard_map/ppermute | solution.py:429
  11.9 0.9 %collective-permute-start.7 = (bf16[1,4,64,128]{3,2,1,0:T(8,128)(2,1)S(1)}, bf16[1,4,64,128]{3,2,1,0:T(8,128)(2,1)S(1)}, u32[]{:S(2)}, u32[]{:S(2)}) collective-permute-start(bf16[1,4,64,128]{3,2,1,0:T(8,128)(2,1)S(1)} %get-tuple-element.32), channel_id=1, source_target_pairs={{0,9},{1,8},{4,13},{5,12},{8,1},{9,0},{12,5},{13,4},{2,11},{3,10},... | collective-permute-start | bytes 196616 | tf_op jit(solution)/shard_map/ppermute | solution.py:429
  12.8 3.6 %collective-permute-start.2 = (bf16[1,4,64,256]{3,2,1,0:T(8,128)(2,1)S(1)}, bf16[1,4,64,256]{3,2,1,0:T(8,128)(2,1)S(1)}, u32[]{:S(2)}, u32[]{:S(2)}) collective-permute-start(bf16[1,4,64,256]{3,2,1,0:T(8,128)(2,1)S(1)} %get-tuple-element.26), channel_id=1, source_target_pairs={{0,12},{1,13},{4,8},{5,9},{8,4},{9,5},{12,0},{13,1},{2,14},{3,15},... | collective-permute-start | bytes 393224 | tf_op jit(solution)/shard_map/ppermute | solution.py:429
  16.4 0.0 collective-permute-done.after_ref.refs_4_
  16.4 0.0 collective-permute-start.3
  16.4 0.0 collective-permute-done.5.refs_5_
  16.4 0.1 collective-permute-start.4
  16.5 4.4 %collective-permute-done.6.refs_6_ = bf16[1,4,64,128]{3,2,1,0:T(8,128)(2,1)S(1)} collective-permute-done((bf16[1,4,64,128]{3,2,1,0:T(8,128)(2,1)S(1)}, bf16[1,4,64,128]{3,2,1,0:T(8,128)(2,1)S(1)}, u32[]{:S(2)}, u32[]{:S(2)}) %collective-permute-start.6) | collective-permute-done | bytes 65568 | tf_op jit(solution)/shard_map/ppermute | solution.py:429
  20.9 0.0 collective-permute-start.8
  20.9 1.4 %collective-permute-done.7.refs_7_ = bf16[1,4,64,128]{3,2,1,0:T(8,128)(2,1)S(1)} collective-permute-done((bf16[1,4,64,128]{3,2,1,0:T(8,128)(2,1)S(1)}, bf16[1,4,64,128]{3,2,1,0:T(8,128)(2,1)S(1)}, u32[]{:S(2)}, u32[]{:S(2)}) %collective-permute-start.7) | collective-permute-done | bytes 65568 | tf_op jit(solution)/shard_map/ppermute | solution.py:429
  22.3 3.1 %collective-permute-start.9 = (bf16[1,4,64,256]{3,2,1,0:T(8,128)(2,1)S(1)}, bf16[1,4,64,256]{3,2,1,0:T(8,128)(2,1)S(1)}, u32[]{:S(2)}, u32[]{:S(2)}) collective-permute-start(bf16[1,4,64,256]{3,2,1,0:T(8,128)(2,1)S(1)} %get-tuple-element.36), channel_id=1, source_target_pairs={{0,13},{1,12},{4,9},{5,8},{8,5},{9,4},{12,1},{13,0},{2,15},{3,14},... | collective-permute-start | bytes 393224 | tf_op jit(solution)/shard_map/ppermute | solution.py:429
  25.4 0.0 copy-done
  25.4 0.0 copy-done.1
  25.4 0.9 %prep.1 = (bf16[4,256,256]{2,1,0:T(8,128)(2,1)S(1)}, bf16[4,2,128,256]{3,2,1,0:T(8,128)(2,1)S(1)}) custom-call(s32[8]{0:T(128)} %perm_hbm.3, bf16[4,4,128,256]{3,2,1,0:T(8,128)(2,1)S(1)} %bitcast.5, bf16[4,2,4,128,128]{4,3,2,1,0:T(8,128)(2,1)S(1)} %bitcast.7, bf16[1,4,64,128]{3,2,1,0:T(8,128)(2,1)S(1)} %collective-permute-done.after_ref.refs_4_), custom_call_target="tpu_custom_call" | custom-call | flops 1000000 | bytes 10000 | tf_op jit(solution)/shard_map/prep/pallas_call | solution.py:287
  26.3 0.0 collective-permute-done.2.refs_0_
  26.3 0.0 collective-permute-done.3.refs_1_
  26.3 0.0 collective-permute-done.4.refs_2_
  26.3 1.9 %upper.1 = (f32[4,2,128,256]{3,2,1,0:T(8,128)S(1)}, f32[3,4,128,256]{3,2,1,0:T(8,128)S(1)}) custom-call(s32[8]{0:T(128)} %perm_hbm.3, bf16[4,4,128,256]{3,2,1,0:T(8,128)(2,1)S(1)} %bitcast.6, bf16[4,2,4,128,128]{4,3,2,1,0:T(8,128)(2,1)S(1)} %bitcast.8, bf16[1,4,64,256]{3,2,1,0:T(8,128)(2,1)S(1)} %collective-permute-done.2.refs_0_, ...), custom_call_target="tpu_custom_call" | custom-call | flops 1000000 | bytes 10000 | tf_op jit(solution)/shard_map/upper/pallas_call | solution.py:360
  28.2 0.0 collective-permute-done.8.mid_a
  28.2 2.0 %collective-permute-done.9.mid_b = bf16[1,4,64,256]{3,2,1,0:T(8,128)(2,1)S(1)} collective-permute-done((bf16[1,4,64,256]{3,2,1,0:T(8,128)(2,1)S(1)}, bf16[1,4,64,256]{3,2,1,0:T(8,128)(2,1)S(1)}, u32[]{:S(2)}, u32[]{:S(2)}) %collective-permute-start.9) | collective-permute-done | bytes 131104 | tf_op jit(solution)/shard_map/ppermute | solution.py:429
  30.3 1.4 %finish.1 = bf16[4,2,256,128]{3,2,1,0:T(8,128)(2,1)} custom-call(bf16[4,256,256]{2,1,0:T(8,128)(2,1)S(1)} %get-tuple-element.22.down_ref, bf16[4,2,128,256]{3,2,1,0:T(8,128)(2,1)S(1)} %get-tuple-element.23.row_ref, f32[4,2,128,256]{3,2,1,0:T(8,128)S(1)} %get-tuple-element.33.field_ref, f32[3,4,128,256]{3,2,1,0:T(8,128)S(1)} %get-tuple-element.34.top_ref, ...), custom_call_target="tpu_custom_call" | custom-call | flops 1000000 | bytes 10000 | tf_op jit(solution)/shard_map/finish/pallas_call | solution.py:409
Async XLA Ops:
  0.0 7.7 %copy-start.2 = (bf16[2,128,2,64]{1,3,2,0:T(8,128)(2,1)S(1)}, bf16[2,128,2,64]{1,3,2,0:T(8,128)(2,1)}, u32[]{:S(2)}) copy-start(bf16[2,128,2,64]{1,3,2,0:T(8,128)(2,1)} %param.8) | copy-start | bytes 196612
  0.0 7.7 %collective-permute-start.1 = (bf16[2,2,64,128]{3,2,1,0:T(8,128)(2,1)}, bf16[2,2,64,128]{3,2,1,0:T(8,128)(2,1)S(1)}, u32[]{:S(2)}, u32[]{:S(2)}) collective-permute-start(bf16[2,2,64,128]{3,2,1,0:T(8,128)(2,1)} %bitcast.9), channel_id=1, source_target_pairs={{0,2},{2,0},{1,3},{3,1},{4,6},{6,4},{5,7},{7,5},{8,10},{10,8},{9,1... | collective-permute-start | bytes 196616 | tf_op jit(solution)/shard_map/ppermute | solution.py:447
  5.0 20.4 %copy-start = (bf16[4,1,4,2,64,256]{5,4,3,2,1,0:T(8,128)(2,1)S(1)}, bf16[4,1,4,2,64,256]{5,4,3,2,1,0:T(8,128)(2,1)}, u32[]{:S(2)}) copy-start(bf16[4,1,4,2,64,256]{5,4,3,2,1,0:T(8,128)(2,1)} %param.14) | copy-start | bytes 3145732
  5.0 20.4 %copy-start.1 = (bf16[1,4,2,4,128,128]{5,4,3,2,1,0:T(8,128)(2,1)S(1)}, bf16[1,4,2,4,128,128]{5,4,3,2,1,0:T(8,128)(2,1)}, u32[]{:S(2)}) copy-start(bf16[1,4,2,4,128,128]{5,4,3,2,1,0:T(8,128)(2,1)} %param.15) | copy-start | bytes 3145732
  5.0 11.4 %collective-permute-start = (bf16[1,4,64,128]{3,2,1,0:T(8,128)(2,1)S(1)}, bf16[1,4,64,128]{3,2,1,0:T(8,128)(2,1)S(1)}, u32[]{:S(2)}, u32[]{:S(2)}) collective-permute-start(bf16[1,4,64,128]{3,2,1,0:T(8,128)(2,1)S(1)} %get-tuple-element.21), channel_id=1, source_target_pairs={{0,8},{1,9},{4,12},{5,13},{8,0},{9,1},{12,4},{13,5},{2,10},{3,11},... | collective-permute-start | bytes 196616 | tf_op jit(solution)/shard_map/ppermute | solution.py:429
  7.7 8.7 %collective-permute-start.5 = (bf16[1,4,64,128]{3,2,1,0:T(8,128)(2,1)S(1)}, bf16[1,4,64,128]{3,2,1,0:T(8,128)(2,1)S(1)}, u32[]{:S(2)}, u32[]{:S(2)}) collective-permute-start(bf16[1,4,64,128]{3,2,1,0:T(8,128)(2,1)S(1)} %get-tuple-element.30), channel_id=1, source_target_pairs={{0,9},{1,8},{4,13},{5,12},{8,1},{9,0},{12,5},{13,4},{2,11},{3,10},... | collective-permute-start | bytes 196616 | tf_op jit(solution)/shard_map/ppermute | solution.py:429
  10.0 10.8 %collective-permute-start.6 = (bf16[1,4,64,128]{3,2,1,0:T(8,128)(2,1)S(1)}, bf16[1,4,64,128]{3,2,1,0:T(8,128)(2,1)S(1)}, u32[]{:S(2)}, u32[]{:S(2)}) collective-permute-start(bf16[1,4,64,128]{3,2,1,0:T(8,128)(2,1)S(1)} %get-tuple-element.31), channel_id=1, source_target_pairs={{0,8},{1,9},{4,12},{5,13},{8,0},{9,1},{12,4},{13,5},{2,10},{3,11},... | collective-permute-start | bytes 196616 | tf_op jit(solution)/shard_map/ppermute | solution.py:429
  11.9 10.4 %collective-permute-start.7 = (bf16[1,4,64,128]{3,2,1,0:T(8,128)(2,1)S(1)}, bf16[1,4,64,128]{3,2,1,0:T(8,128)(2,1)S(1)}, u32[]{:S(2)}, u32[]{:S(2)}) collective-permute-start(bf16[1,4,64,128]{3,2,1,0:T(8,128)(2,1)S(1)} %get-tuple-element.32), channel_id=1, source_target_pairs={{0,9},{1,8},{4,13},{5,12},{8,1},{9,0},{12,5},{13,4},{2,11},{3,10},... | collective-permute-start | bytes 196616 | tf_op jit(solution)/shard_map/ppermute | solution.py:429
  12.8 13.5 %collective-permute-start.2 = (bf16[1,4,64,256]{3,2,1,0:T(8,128)(2,1)S(1)}, bf16[1,4,64,256]{3,2,1,0:T(8,128)(2,1)S(1)}, u32[]{:S(2)}, u32[]{:S(2)}) collective-permute-start(bf16[1,4,64,256]{3,2,1,0:T(8,128)(2,1)S(1)} %get-tuple-element.26), channel_id=1, source_target_pairs={{0,12},{1,13},{4,8},{5,9},{8,4},{9,5},{12,0},{13,1},{2,14},{3,15},... | collective-permute-start | bytes 393224 | tf_op jit(solution)/shard_map/ppermute | solution.py:429
  16.4 9.9 %collective-permute-start.3 = (bf16[1,4,64,256]{3,2,1,0:T(8,128)(2,1)S(1)}, bf16[1,4,64,256]{3,2,1,0:T(8,128)(2,1)S(1)}, u32[]{:S(2)}, u32[]{:S(2)}) collective-permute-start(bf16[1,4,64,256]{3,2,1,0:T(8,128)(2,1)S(1)} %get-tuple-element.27), channel_id=1, source_target_pairs={{0,4},{1,5},{4,0},{5,1},{8,12},{9,13},{12,8},{13,9},{2,6},{3,7},{6... | collective-permute-start | bytes 393224 | tf_op jit(solution)/shard_map/ppermute | solution.py:429
  16.4 9.9 %collective-permute-start.4 = (bf16[1,4,64,256]{3,2,1,0:T(8,128)(2,1)S(1)}, bf16[1,4,64,256]{3,2,1,0:T(8,128)(2,1)S(1)}, u32[]{:S(2)}, u32[]{:S(2)}) collective-permute-start(bf16[1,4,64,256]{3,2,1,0:T(8,128)(2,1)S(1)} %get-tuple-element.28), channel_id=1, source_target_pairs={{0,1},{1,0},{4,5},{5,4},{8,9},{9,8},{12,13},{13,12},{2,3},{3,2},{6... | collective-permute-start | bytes 393224 | tf_op jit(solution)/shard_map/ppermute | solution.py:429
  20.9 7.3 %collective-permute-start.8 = (bf16[1,4,64,256]{3,2,1,0:T(8,128)(2,1)S(1)}, bf16[1,4,64,256]{3,2,1,0:T(8,128)(2,1)S(1)}, u32[]{:S(2)}, u32[]{:S(2)}) collective-permute-start(bf16[1,4,64,256]{3,2,1,0:T(8,128)(2,1)S(1)} %get-tuple-element.35), channel_id=1, source_target_pairs={{0,5},{1,4},{4,1},{5,0},{8,13},{9,12},{12,9},{13,8},{2,7},{3,6},{6... | collective-permute-start | bytes 393224 | tf_op jit(solution)/shard_map/ppermute | solution.py:429
  22.3 8.0 %collective-permute-start.9 = (bf16[1,4,64,256]{3,2,1,0:T(8,128)(2,1)S(1)}, bf16[1,4,64,256]{3,2,1,0:T(8,128)(2,1)S(1)}, u32[]{:S(2)}, u32[]{:S(2)}) collective-permute-start(bf16[1,4,64,256]{3,2,1,0:T(8,128)(2,1)S(1)} %get-tuple-element.36), channel_id=1, source_target_pairs={{0,13},{1,12},{4,9},{5,8},{8,5},{9,4},{12,1},{13,0},{2,15},{3,14},... | collective-permute-start | bytes 393224 | tf_op jit(solution)/shard_map/ppermute | solution.py:429
